TPU v7x, 256 devices: a whole 4x4x8 slice. The times are simulated.
256 devices in a mesh: wide: 64 (over z_hi, y, x), narrow: 4 (over z_lo, core).
Axes of the slice: x: 4, y: 4, z: 8 (z_hi: 4, z_lo: 2; z = z_hi * 2 + z_lo), core: 2. Of those that a mesh axis runs over, the one named last changes fastest.
Arguments:
- inputs: bfloat16 [1, 64, 32, 16, 512], P(None, 'wide', 'narrow'), may hold values from -6 to 6
- norm_params: float32 [2, 512], replicated, may hold values from -1 to 1.5
- w_qkv: bfloat16 [512, 1536], replicated, may hold values from -2 to 2
- w_proj: bfloat16 [512, 512], replicated, may hold values from -0.25 to 0.25
- upstream: bfloat16 [1, 64, 32, 16, 512], P(None, 'wide', 'narrow'), may hold values from -16 to 16
Outputs:
- output: bfloat16 [1, 64, 32, 16, 512], P(None, 'wide', 'narrow')
- grad_inputs: bfloat16 [1, 64, 32, 16, 512], P(None, 'wide', 'narrow')
- grad_qkv: float32 [512, 1536], P(None, 'wide')
- grad_proj: float32 [512, 512], P(None, 'wide')
- grad_norm: float32 [2, 512], P(None, 'wide')
All inputs are finite; a program needn't handle non-finite values.
Results may differ from a plain program's by a relative error of at most 0.023.
The roundings to bfloat16 on the way count: a program that leaves them out, or rounds other values in their place, can miss the bound.
Values may be sent and summed in bfloat16 or wider, within the bound.
No kernel may reach another device: no remote copies, remote signals or barrier semaphores. Data moves between devices by JAX's collectives and lax.ppermute only.
A program may use at most 128 MiB of HBM per device.

v0:
```python
import jax
import jax.numpy as jnp
from jax import lax
from jax.sharding import PartitionSpec as P

HEADS = 16
HEAD_DIM = 32
WIN = 8


def from_behind(value, axis, steps):
    count = lax.axis_size(axis)
    pairs = [(source, (source + steps) % count) for source in range(count)]
    return lax.ppermute(value, axis, pairs)


def from_partner(shard, axis, apart):
    return lax.ppermute(shard, axis, [(i, i ^ 1 << apart) for i in range(lax.axis_size(axis))])


def normalize(field_in, norm_params):
    floats = field_in.astype(jnp.float32)
    average = jnp.mean(floats, -1, keepdims=True)
    centered = floats - average
    variance = jnp.mean(centered * centered, -1, keepdims=True)
    inv_scale = lax.rsqrt(variance + 1e-05)
    unit_field = centered * inv_scale
    return (unit_field, inv_scale, unit_field * norm_params[0] + norm_params[1])


def normalize_back(d_normed, unit_field, inv_scale, norm_params):
    d_unit = d_normed * norm_params[0]
    first_mean = jnp.mean(d_unit, -1, keepdims=True)
    second_mean = jnp.mean(d_unit * unit_field, -1, keepdims=True)
    return inv_scale * (d_unit - first_mean - unit_field * second_mean)


def region_of(coords, count):
    return jnp.where(coords < count - WIN, 0, jnp.where(coords < count - WIN // 2, 1, 2)).astype(
        jnp.int32
    )


def split_heads(rows):
    return rows.reshape(rows.shape[:-1] + (HEADS, HEAD_DIM))


def merge_heads(rows):
    return rows.reshape(rows.shape[:-2] + (HEADS * HEAD_DIM,))


def attend(queries, key_rows, value_rows, same_label, upstream_att):
    scaling = HEAD_DIM ** (-0.5)
    allowed = jnp.expand_dims(same_label, -3)
    scores = (
        jnp.einsum("...qhd,...khd->...hqk", queries, key_rows, preferred_element_type=jnp.float32)
        * scaling
    )
    scores = jnp.where(allowed, scores, -1e30)
    highest = jnp.max(scores, -1, keepdims=True)
    weights = jnp.where(allowed, jnp.exp(scores - highest), 0.0)
    attention = weights / jnp.sum(weights, -1, keepdims=True)
    attention_low = attention.astype(jnp.bfloat16)
    attended = jnp.einsum(
        "...hqk,...khd->...qhd", attention_low, value_rows, preferred_element_type=jnp.float32
    ).astype(jnp.bfloat16)
    d_attention = jnp.einsum(
        "...qhd,...khd->...hqk", upstream_att, value_rows, preferred_element_type=jnp.float32
    )
    row_inner = jnp.sum(attention * d_attention, -1, keepdims=True)
    d_scores = (attention * (d_attention - row_inner) * scaling).astype(jnp.bfloat16)
    d_query = jnp.einsum(
        "...hqk,...khd->...qhd", d_scores, key_rows, preferred_element_type=jnp.float32
    )
    d_key = jnp.einsum(
        "...hqk,...qhd->...khd", d_scores, queries, preferred_element_type=jnp.float32
    )
    d_value = jnp.einsum(
        "...hqk,...qhd->...khd", attention_low, upstream_att, preferred_element_type=jnp.float32
    )
    return (attended, d_query, d_key, d_value)


def to_query(field_in):
    batches = field_in.shape[0]
    y_windows = field_in.shape[3] // WIN
    feature = field_in.shape[-1]
    split = field_in.reshape(batches, WIN, y_windows, WIN, feature)
    return split.transpose(0, 2, 1, 3, 4).reshape(batches, y_windows, WIN * WIN, feature)


def from_query(rows, token_shape):
    batches, y_windows = (rows.shape[0], rows.shape[1])
    feature = rows.shape[-1]
    split = rows.reshape(batches, y_windows, WIN, WIN, feature)
    return split.transpose(0, 2, 1, 3, 4).reshape(token_shape + (feature,))


def to_keys(window):
    slots, batches, y_cells, feature = (
        window.shape[0],
        window.shape[1],
        window.shape[4],
        window.shape[5],
    )
    split = window.reshape(slots, batches, WIN, y_cells // WIN, WIN, feature)
    return split.transpose(1, 3, 0, 2, 4, 5).reshape(
        batches, y_cells // WIN, slots * WIN * WIN, feature
    )


def from_keys(rows, token_shape):
    batches, y_windows = (rows.shape[0], rows.shape[1])
    feature = rows.shape[-1]
    split = rows.reshape(batches, y_windows, WIN, WIN, WIN, feature)
    return split.transpose(2, 0, 3, 1, 4, 5).reshape((WIN,) + token_shape + (feature,))


def roll_in(inputs, upstream):
    midway = WIN // 2
    moved = from_behind((inputs, upstream), "wide", -midway)
    leading = from_behind((moved[0][:, :, :midway], moved[1][:, :, :midway]), "narrow", -1)
    first = jnp.concatenate([moved[0][:, :, midway:], leading[0]], 2)
    second = jnp.concatenate([moved[1][:, :, midway:], leading[1]], 2)
    return (jnp.roll(first, -midway, 3), jnp.roll(second, -midway, 3))


def roll_out(field_in):
    midway = WIN // 2
    moved = from_behind(field_in, "wide", midway)
    trailing = from_behind(moved[:, :, midway:], "narrow", 1)
    joined = jnp.concatenate([trailing, moved[:, :, :midway]], 2)
    return jnp.roll(joined, midway, 3)


def window_gather(slab):
    place = lax.axis_index("wide")
    gathered = slab[None]
    for level in range(WIN.bit_length() - 1):
        partner = from_partner(gathered, "wide", level)
        upper_half = place >> level & 1 == 1
        gathered = jnp.where(
            upper_half,
            jnp.concatenate([partner, gathered], 0),
            jnp.concatenate([gathered, partner], 0),
        )
    return gathered


def window_return(partials):
    place = lax.axis_index("wide")
    for level in reversed(range(WIN.bit_length() - 1)):
        midway = partials.shape[0] // 2
        upper_half = place >> level & 1 == 1
        kept = jnp.where(upper_half, partials[midway:], partials[:midway])
        outgoing = jnp.where(upper_half, partials[:midway], partials[midway:])
        partials = kept + from_partner(outgoing, "wide", level)
    return partials[0]


def on_device(inputs, norm_params, w_qkv, w_proj, upstream):
    channels = HEADS * HEAD_DIM
    highest_precision = lax.Precision.HIGHEST
    shifted, rolled_up = roll_in(inputs, upstream)
    y_cells = shifted.shape[3]
    y_windows = y_cells // WIN
    place = lax.axis_index("wide")
    column = lax.axis_index("narrow")
    z_count = lax.axis_size("wide")
    x_count = WIN * lax.axis_size("narrow")
    steps_win = jnp.arange(WIN, dtype=jnp.int32)
    x_region = region_of(column * WIN + steps_win, x_count)
    y_region = region_of(jnp.arange(y_cells, dtype=jnp.int32), y_cells)
    key_z = region_of(place // WIN * WIN + steps_win, z_count)
    key_labels = 9 * key_z[:, None, None] + 3 * x_region[None, :, None] + y_region[None, None, :]
    key_labels = (
        key_labels.reshape(WIN, WIN, y_windows, WIN)
        .transpose(2, 0, 1, 3)
        .reshape(y_windows, WIN**3)
    )
    query_z = region_of(place, z_count)
    query_labels = 9 * query_z + 3 * x_region[:, None] + y_region[None, :]
    query_labels = (
        query_labels.reshape(WIN, y_windows, WIN).transpose(1, 0, 2).reshape(y_windows, WIN * WIN)
    )
    same_label = (query_labels[:, :, None] == key_labels[:, None, :])[None]
    unit_field, inv_scale, scaled = normalize(shifted, norm_params)
    normed = scaled.astype(jnp.bfloat16)
    token_shape = normed.shape[:-1]
    flat_normed = normed.reshape(-1, channels)
    qkv = jnp.dot(flat_normed, w_qkv, preferred_element_type=jnp.float32).astype(jnp.bfloat16)
    qkv = qkv.reshape(token_shape + (3 * channels,))
    flat_up = rolled_up.reshape(-1, channels)
    upstream_att = jnp.dot(flat_up, w_proj.T, preferred_element_type=jnp.float32).astype(
        jnp.bfloat16
    )
    upstream_att = upstream_att.reshape(token_shape + (channels,))
    queries = split_heads(to_query(qkv[..., :channels]))
    kv_window = window_gather(qkv[..., channels:])
    kv_rows = to_keys(kv_window)
    key_rows = split_heads(kv_rows[..., :channels])
    value_rows = split_heads(kv_rows[..., channels:])
    attended, d_query, d_key, d_value = attend(
        queries, key_rows, value_rows, same_label, split_heads(to_query(upstream_att))
    )
    attended = from_query(merge_heads(attended), token_shape)
    flat_dq = from_query(merge_heads(d_query), token_shape).reshape(-1, channels)
    d_kv = from_keys(jnp.concatenate([merge_heads(d_key), merge_heads(d_value)], -1), token_shape)
    flat_attended = attended.reshape(-1, channels)
    projected = jnp.dot(flat_attended, w_proj, preferred_element_type=jnp.float32).astype(
        jnp.bfloat16
    )
    projected = projected.reshape(token_shape + (channels,))
    grad_proj = jnp.dot(flat_attended.T, flat_up, preferred_element_type=jnp.float32)
    float_normed = flat_normed.astype(jnp.float32)
    float_weights = w_qkv.astype(jnp.float32)
    returned = window_return(d_kv).reshape(-1, 2 * channels)
    d_qkv = jnp.concatenate([flat_dq, returned], 1)
    grad_qkv = jnp.dot(float_normed.T, d_qkv, precision=highest_precision)
    d_normed = jnp.dot(d_qkv, float_weights.T, precision=highest_precision)
    flat_unit = unit_field.reshape(-1, channels)
    flat_inv = inv_scale.reshape(-1, 1)
    grad_norm = jnp.stack([jnp.sum(d_normed * flat_unit, 0), jnp.sum(d_normed, 0)])
    d_shifted = normalize_back(d_normed, flat_unit, flat_inv, norm_params).astype(jnp.bfloat16)
    d_shifted = d_shifted.reshape(token_shape + (channels,))
    output = (inputs.astype(jnp.float32) + roll_out(projected).astype(jnp.float32)).astype(
        jnp.bfloat16
    )
    grad_inputs = (upstream.astype(jnp.float32) + roll_out(d_shifted).astype(jnp.float32)).astype(
        jnp.bfloat16
    )
    totals = lax.psum((grad_qkv, grad_proj, grad_norm), "narrow")
    grad_qkv, grad_proj, grad_norm = (
        lax.psum_scatter(totals[0], "wide", scatter_dimension=1, tiled=True),
        lax.psum_scatter(totals[1], "wide", scatter_dimension=1, tiled=True),
        lax.psum_scatter(totals[2], "wide", scatter_dimension=1, tiled=True),
    )
    return (output, grad_inputs, grad_qkv, grad_proj, grad_norm)


def solution(mesh):
    in_specs = (
        P(None, "wide", "narrow", None, None),
        P(),
        P(),
        P(),
        P(None, "wide", "narrow", None, None),
    )
    out_specs = (
        P(None, "wide", "narrow", None, None),
        P(None, "wide", "narrow", None, None),
        P(None, "wide"),
        P(None, "wide"),
        P(None, "wide"),
    )
    return jax.shard_map(
        on_device, mesh=mesh, in_specs=in_specs, out_specs=out_specs, check_vma=False
    )
```

profile of v0, /device:TPU:1, one launch (start us, length us, event | category | flops | bytes accessed | tf_op | source)
XLA Modules:
  0.0 888.2 jit_solution(12983061260838681818)
XLA Ops:
  7.2 9.4 %collective-permute-start = (bf16[1,1,8,16,512]{4,3,2,1,0:T(8,128)(2,1)}, bf16[1,1,8,16,512]{4,3,2,1,0:T(8,128)(2,1)S(1)}, u32[]{:S(2)}, u32[]{:S(2)}) collective-permute-start(bf16[1,1,8,16,512]{4,3,2,1,0:T(8,128)(2,1)} %param.5), channel_id=1, source_target_pairs={{0,240},{4,244},{8,248},{12,252},{16,0},{20,4},{24,8},{28,12},{32,... | collective-permute-start | bytes 393224 | tf_op jit(solution)/shard_map/ppermute | solution.py:14
  17.1 0.8 fusion.55
  17.9 1.2 collective-permute-done
  19.1 5.7 collective-permute-start.1
  24.9 3.9 collective-permute-done.1
  29.8 0.8 slice_bitcast_fusion.1
  30.7 1.2 collective-permute-start.2
  32.4 4.7 collective-permute-done.2
  37.2 2.8 collective-permute-start.3
  40.1 1.5 fusion.52
  41.6 1.1 fusion.31
  42.7 9.3 %collective-permute-done.3 = bf16[2,1,1,8,16,1024]{5,4,3,0,2,1:T(8,128)(2,1)S(1)} collective-permute-done((bf16[2,1,1,8,16,1024]{5,4,3,0,2,1:T(8,128)(2,1)S(1)}, bf16[2,1,1,8,16,1024]{5,4,3,0,2,1:T(8,128)(2,1)S(1)}, u32[]{:S(2)}, u32[]{:S(2)}) %collective-permute-start.3) | collective-permute-done | bytes 524320 | tf_op jit(solution)/shard_map/ppermute | solution.py:18
  52.0 1.1 maximum_select_fusion.1
  53.2 0.7 broadcast_compare_fusion
  54.6 0.8 fusion.36
  56.0 1.1 copy.55
  57.2 0.9 slice_bitcast_fusion.3
  58.4 1.1 copy.51
  59.8 18.2 %collective-permute-done.4 = bf16[4,1,1,8,16,1024]{5,4,3,0,2,1:T(8,128)(2,1)} collective-permute-done((bf16[4,1,1,8,16,1024]{5,4,3,0,2,1:T(8,128)(2,1)}, bf16[4,1,1,8,16,1024]{5,4,3,0,2,1:T(8,128)(2,1)}, u32[]{:S(2)}, u32[]{:S(2)}) %collective-permute-start.4) | collective-permute-done | bytes 1048608 | tf_op jit(solution)/shard_map/ppermute | solution.py:18
  77.9 1.9 fusion.12
  80.0 1.2 fusion.50
  81.2 1.3 copy.50
  82.6 1.5 copy.48
  84.1 2.7 fusion.57
  86.8 4.9 fusion.56
  91.8 4.0 convolution_bitcast_fusion
  95.8 18.7 %fusion.18 = f32[1,2,512,16,32]{2,4,3,1,0:T(8,128)} fusion(bf16[2,64,16,32]{1,3,2,0:T(8,128)(2,1)S(1)} %copy-done.8, f32[2,16,64,512]{3,2,1,0:T(8,128)} %fusion.57, f32[2,16,64,512]{3,2,1,0:T(8,128)} %get-tuple-element.32, f32[2,16,64]{2,1,0:T(8,128)S(1)} %get-tuple-element.31), kind=kOutput, calls=%fused_computation.24 | convolution fusion | flops 74451456 | bytes 10625024 | tf_op jit(solution)/shard_map/...hqk,...qhd->...khd/dot_general | solution.py:75
  114.5 7.4 copy.59
  121.9 7.3 concatenate.235
  129.2 7.4 copy.61
  136.7 7.3 concatenate.236
  144.0 2.7 maximum_bitcast_fusion
  147.7 45.7 %collective-permute-done.9 = f32[4,1,1,8,16,1024]{5,4,3,0,2,1:T(8,128)S(1)} collective-permute-done((f32[4,1,1,8,16,1024]{5,4,3,0,2,1:T(8,128)S(1)}, f32[4,1,1,8,16,1024]{5,4,3,0,2,1:T(8,128)S(1)}, u32[]{:S(2)}, u32[]{:S(2)}) %collective-permute-start.9) | collective-permute-done | bytes 2097184 | tf_op jit(solution)/shard_map/ppermute | solution.py:18
  193.8 1.3 copy-done.1
  195.1 1.1 slice_select_fusion.2
  196.3 2.8 collective-permute-start.10
  199.0 0.7 fusion.24
  200.7 0.6 copy-done.5
  201.4 1.3 fusion.58
  202.8 18.3 %collective-permute-done.10 = f32[2,1,1,8,16,1024]{5,4,3,0,2,1:T(8,128)} collective-permute-done((f32[2,1,1,8,16,1024]{5,4,3,0,2,1:T(8,128)}, f32[2,1,1,8,16,1024]{5,4,3,0,2,1:T(8,128)}, u32[]{:S(2)}, u32[]{:S(2)}) %collective-permute-start.10) | collective-permute-done | bytes 1048608 | tf_op jit(solution)/shard_map/ppermute | solution.py:18
  221.0 2.1 select_add_fusion
  223.2 0.9 slice_select_fusion.3
  224.1 1.2 collective-permute-start.11
  225.3 17.5 %fusion.21 = f32[1,2,64,16,32]{2,4,3,1,0:T(8,128)S(1)} fusion(bf16[2,512,16,32]{1,3,2,0:T(8,128)(2,1)} %bitcast.133, f32[2,16,64,512]{3,2,1,0:T(8,128)} %fusion.57, f32[2,16,64,512]{3,2,1,0:T(8,128)} %get-tuple-element.32, f32[2,16,64]{2,1,0:T(8,128)S(1)} %copy-done.16), kind=kOutput, calls=%fused_computation.26 | convolution fusion | flops 74451456 | bytes 9707520 | tf_op jit(solution)/shard_map/...hqk,...khd->...qhd/dot_general | solution.py:72
  242.8 1.4 copy.56
  244.2 1.6 reshape_reshape.20
  245.9 1.1 select_add_fusion.1
  247.0 4.0 fusion.28
  251.1 1.4 convolution_convert_fusion.3
  252.4 1.1 collective-permute-start.5
  254.8 6.3 collective-permute-done.5
  261.1 3.3 collective-permute-start.6
  264.4 1.8 multiply_reduce_fusion.1
  266.8 0.7 add_convert_fusion.1
  267.5 167.7 %all-reduce = f32[2,512]{1,0:T(2,128)S(1)} all-reduce(f32[2,512]{1,0:T(2,128)S(1)} %pad_maximum_fusion.9), channel_id=4, replica_groups=mesh['wide'=64,'narrow'=4] {'wide'}, use_global_device_ids=true, to_apply=%region_14.15.clone | all-reduce | flops 1024 | bytes 8192
  435.2 26.1 %collective-permute-start.13 = (bf16[1,1,4,16,512]{4,3,2,1,0:T(8,128)(2,1)S(1)}, bf16[1,1,4,16,512]{4,3,2,1,0:T(8,128)(2,1)S(1)}, u32[]{:S(2)}, u32[]{:S(2)}) collective-permute-start(bf16[1,1,4,16,512]{4,3,2,1,0:T(8,128)(2,1)S(1)} %get-tuple-element.21), channel_id=1, source_target_pairs={{0,1},{1,2},{2,3},{3,0},{4,5},{5,6},{6,7},{7,4},{8,9},{9,10},{10,1... | collective-permute-start | bytes 196616 | tf_op jit(solution)/shard_map/ppermute | solution.py:14
  461.4 0.6 constant_dynamic-slice_fusion
  462.0 71.6 %reduce-scatter.6.cloned.1.call-done = f32[512,8]{0,1:T(8,128)} async-done(((f32[512,512]{0,1:T(8,128)}), f32[512,8]{0,1:T(8,128)}) %reduce-scatter.6.cloned.1.call-update) | async-done | bytes 16400 | tf_op jit(solution)/shard_map/reduce_scatter | solution.py:235
  533.6 301.0 %reduce-scatter.4.cloned.1.call-done = f32[512,24]{0,1:T(8,128)} async-done(((f32[512,1536]{0,1:T(8,128)}), f32[512,24]{0,1:T(8,128)}) %reduce-scatter.4.cloned.1.call-update) | async-done | bytes 49168 | tf_op jit(solution)/shard_map/reduce_scatter | solution.py:234
  834.6 0.7 add_convert_fusion
  835.3 42.4 %all-reduce.4.cloned.1.call-done = (f32[512,24]{0,1:T(8,128)}, f32[512,8]{0,1:T(8,128)}, f32[2,8]{1,0:T(2,128)}) async-done(((f32[512,24]{0,1:T(8,128)}, f32[512,8]{0,1:T(8,128)}, f32[2,8]{1,0:T(2,128)}), (f32[512,24]{0,1:T(8,128)}, f32[512,8]{0,1:T(8,128)}, f32[2,8]{1,0:T(2,128)})) %all-reduce.4.cloned.1.call-update) | async-done | bytes 65616 | tf_op jit(solution)/shard_map/psum | solution.py:232
  877.7 1.4 copy.74
  879.1 1.3 copy.75
  880.5 1.2 copy.76
  (97 shorter events, 8.0 us)
Async XLA Ops:
  7.2 22.3 %copy-start = (bf16[512,1536]{1,0:T(8,128)(2,1)S(1)}, bf16[512,1536]{1,0:T(8,128)(2,1)}, u32[]{:S(2)}) copy-start(bf16[512,1536]{1,0:T(8,128)(2,1)} %param.7) | copy-start | bytes 4718596
  7.2 526.4 %reduce-scatter.6.cloned.1.call-start = ((), (), s32[]{:S(2)}) async-start(), calls=%async_computation.3 | async-start | bytes 1064960 | tf_op jit(solution)/shard_map/reduce_scatter | solution.py:235
  7.2 11.9 %collective-permute-start = (bf16[1,1,8,16,512]{4,3,2,1,0:T(8,128)(2,1)}, bf16[1,1,8,16,512]{4,3,2,1,0:T(8,128)(2,1)S(1)}, u32[]{:S(2)}, u32[]{:S(2)}) collective-permute-start(bf16[1,1,8,16,512]{4,3,2,1,0:T(8,128)(2,1)} %param.5), channel_id=1, source_target_pairs={{0,240},{4,244},{8,248},{12,252},{16,0},{20,4},{24,8},{28,12},{32,... | collective-permute-start | bytes 393224 | tf_op jit(solution)/shard_map/ppermute | solution.py:14
  16.6 23.5 %collective-permute-start.7 = (bf16[1,1,8,16,512]{4,3,2,1,0:T(8,128)(2,1)}, bf16[1,1,8,16,512]{4,3,2,1,0:T(8,128)(2,1)}, u32[]{:S(2)}, u32[]{:S(2)}) collective-permute-start(bf16[1,1,8,16,512]{4,3,2,1,0:T(8,128)(2,1)} %param.9), channel_id=1, source_target_pairs={{0,240},{4,244},{8,248},{12,252},{16,0},{20,4},{24,8},{28,12},{32,... | collective-permute-start | bytes 393224 | tf_op jit(solution)/shard_map/ppermute | solution.py:14
  19.1 9.6 %collective-permute-start.1 = (bf16[1,1,4,16,512]{4,3,2,1,0:T(8,128)(2,1)S(1)}, bf16[1,1,4,16,512]{4,3,2,1,0:T(8,128)(2,1)S(1)}, u32[]{:S(2)}, u32[]{:S(2)}) collective-permute-start(bf16[1,1,4,16,512]{4,3,2,1,0:T(8,128)(2,1)S(1)} %get-tuple-element.28), channel_id=1, source_target_pairs={{0,3},{1,0},{2,1},{3,2},{4,7},{5,4},{6,5},{7,6},{8,11},{9,8},{10,9... | collective-permute-start | bytes 196616 | tf_op jit(solution)/shard_map/ppermute | solution.py:14
  29.4 25.9 %copy-start.4 = (bf16[128,512]{1,0:T(8,128)(2,1)}, bf16[128,512]{1,0:T(8,128)(2,1)S(1)}, u32[]{:S(2)}) copy-start(bf16[128,512]{1,0:T(8,128)(2,1)S(1)} %add_convert_fusion.2) | copy-start | bytes 393220
  29.4 25.9 %copy-start.2 = (bf16[512,512]{1,0:T(8,128)(2,1)S(1)}, bf16[512,512]{1,0:T(8,128)(2,1)}, u32[]{:S(2)}) copy-start(bf16[512,512]{1,0:T(8,128)(2,1)} %param.8) | copy-start | bytes 1572868
  29.8 0.8 copy-start.3
  30.7 6.5 collective-permute-start.2
  37.2 14.8 %collective-permute-start.3 = (bf16[2,1,1,8,16,1024]{5,4,3,0,2,1:T(8,128)(2,1)S(1)}, bf16[2,1,1,8,16,1024]{5,4,3,0,2,1:T(8,128)(2,1)S(1)}, u32[]{:S(2)}, u32[]{:S(2)}) collective-permute-start(bf16[2,1,1,8,16,1024]{5,4,3,0,2,1:T(8,128)(2,1)S(1)} %fusion.30), channel_id=1, source_target_pairs={{0,8},{4,12},{8,0},{12,4},{16,24},{20,28},{24,16},{28,20},{32,40},... | collective-permute-start | bytes 1572872 | tf_op jit(solution)/shard_map/ppermute | solution.py:18
  41.6 12.3 %copy-start.7 = (bf16[1,1,4,16,512]{4,3,2,1,0:T(8,128)(2,1)}, bf16[1,1,4,16,512]{4,3,2,1,0:T(8,128)(2,1)S(1)}, u32[]{:S(2)}) copy-start(bf16[1,1,4,16,512]{4,3,2,1,0:T(8,128)(2,1)S(1)} %get-tuple-element.23) | copy-start | bytes 196612
  41.6 12.3 %collective-permute-start.8 = (bf16[1,1,4,16,512]{4,3,2,1,0:T(8,128)(2,1)}, bf16[1,1,4,16,512]{4,3,2,1,0:T(8,128)(2,1)S(1)}, u32[]{:S(2)}, u32[]{:S(2)}) collective-permute-start(bf16[1,1,4,16,512]{4,3,2,1,0:T(8,128)(2,1)} %get-tuple-element.24), channel_id=1, source_target_pairs={{0,3},{1,0},{2,1},{3,2},{4,7},{5,4},{6,5},{7,6},{8,11},{9,8},{10,9... | collective-permute-start | bytes 196616 | tf_op jit(solution)/shard_map/ppermute | solution.py:14
  53.1 24.8 %collective-permute-start.4 = (bf16[4,1,1,8,16,1024]{5,4,3,0,2,1:T(8,128)(2,1)}, bf16[4,1,1,8,16,1024]{5,4,3,0,2,1:T(8,128)(2,1)}, u32[]{:S(2)}, u32[]{:S(2)}) collective-permute-start(bf16[4,1,1,8,16,1024]{5,4,3,0,2,1:T(8,128)(2,1)} %maximum_select_fusion.1), channel_id=1, source_target_pairs={{0,16},{4,20},{8,24},{12,28},{16,0},{20,4},{24,8},{28,12},{32,48},... | collective-permute-start | bytes 3145736 | tf_op jit(solution)/shard_map/ppermute | solution.py:18
  53.9 0.6 copy-start.9
  80.0 4.1 copy-start.6
  82.6 4.3 copy-start.8
  82.6 4.3 copy-start.12
  91.8 107.3 %copy-start.15 = (f32[2,16,64]{2,1,0:T(8,128)}, f32[2,16,64]{2,1,0:T(8,128)S(1)}, u32[]{:S(2)}) copy-start(f32[2,16,64]{2,1,0:T(8,128)S(1)} %get-tuple-element.31) | copy-start | bytes 24580
  147.3 46.1 %collective-permute-start.9 = (f32[4,1,1,8,16,1024]{5,4,3,0,2,1:T(8,128)S(1)}, f32[4,1,1,8,16,1024]{5,4,3,0,2,1:T(8,128)S(1)}, u32[]{:S(2)}, u32[]{:S(2)}) collective-permute-start(f32[4,1,1,8,16,1024]{5,4,3,0,2,1:T(8,128)S(1)} %bitcast.124), channel_id=1, source_target_pairs={{0,16},{4,20},{8,24},{12,28},{16,0},{20,4},{24,8},{28,12},{32,48},... | collective-permute-start | bytes 6291464 | tf_op jit(solution)/shard_map/ppermute | solution.py:18
  193.4 5.6 copy-start.14
  193.8 1.3 copy-start.1
  196.3 24.8 %collective-permute-start.10 = (f32[2,1,1,8,16,1024]{5,4,3,0,2,1:T(8,128)}, f32[2,1,1,8,16,1024]{5,4,3,0,2,1:T(8,128)}, u32[]{:S(2)}, u32[]{:S(2)}) collective-permute-start(f32[2,1,1,8,16,1024]{5,4,3,0,2,1:T(8,128)} %slice_select_fusion.2), channel_id=1, source_target_pairs={{0,8},{4,12},{8,0},{12,4},{16,24},{20,28},{24,16},{28,20},{32,40},... | collective-permute-start | bytes 3145736 | tf_op jit(solution)/shard_map/ppermute | solution.py:18
  200.7 24.6 %copy-start.16 = (f32[2,16,64]{2,1,0:T(8,128)S(1)}, f32[2,16,64]{2,1,0:T(8,128)}, u32[]{:S(2)}) copy-start(f32[2,16,64]{2,1,0:T(8,128)} %copy-done.15) | copy-start | bytes 24580
  200.7 0.7 copy-start.5
  202.7 631.8 %reduce-scatter.4.cloned.1.call-start = ((), (), s32[]{:S(2)}) async-start(), calls=%async_computation.2 | async-start | bytes 3194880 | tf_op jit(solution)/shard_map/reduce_scatter | solution.py:234
  224.1 21.8 %collective-permute-start.11 = (f32[1,1,1,8,16,1024]{5,4,3,0,2,1:T(8,128)}, f32[1,1,1,8,16,1024]{5,4,3,0,2,1:T(8,128)}, u32[]{:S(2)}, u32[]{:S(2)}) collective-permute-start(f32[1,1,1,8,16,1024]{5,4,3,0,2,1:T(8,128)} %slice_select_fusion.3), channel_id=1, source_target_pairs={{0,4},{4,0},{8,12},{12,8},{16,20},{20,16},{24,28},{28,24},{32,36},... | collective-permute-start | bytes 1572872 | tf_op jit(solution)/shard_map/ppermute | solution.py:18
  247.0 6.6 copy-start.13
  251.0 15.8 %copy-start.10 = (bf16[1,1,8,16,512]{4,3,2,1,0:T(8,128)(2,1)S(1)}, bf16[1,1,8,16,512]{4,3,2,1,0:T(8,128)(2,1)}, u32[]{:S(2)}) copy-start(bf16[1,1,8,16,512]{4,3,2,1,0:T(8,128)(2,1)} %param.5) | copy-start | bytes 393220
  251.0 583.6 %copy-start.11 = (bf16[1,1,8,16,512]{4,3,2,1,0:T(8,128)(2,1)S(1)}, bf16[1,1,8,16,512]{4,3,2,1,0:T(8,128)(2,1)}, u32[]{:S(2)}) copy-start(bf16[1,1,8,16,512]{4,3,2,1,0:T(8,128)(2,1)} %param.9) | copy-start | bytes 393220
  251.0 626.7 %all-reduce.4.cloned.1.call-start = ((), (), s32[]{:S(2)}) async-start(), calls=%async_computation.4 | async-start | bytes 133120 | tf_op jit(solution)/shard_map/psum | solution.py:232
  252.4 8.7 collective-permute-start.5
  261.1 5.7 collective-permute-start.6
  266.4 168.8 %collective-permute-start.12 = (bf16[1,1,8,16,512]{4,3,2,1,0:T(8,128)(2,1)S(1)}, bf16[1,1,8,16,512]{4,3,2,1,0:T(8,128)(2,1)S(1)}, u32[]{:S(2)}, u32[]{:S(2)}) collective-permute-start(bf16[1,1,8,16,512]{4,3,2,1,0:T(8,128)(2,1)S(1)} %bitcast.137), channel_id=1, source_target_pairs={{0,16},{4,20},{8,24},{12,28},{16,32},{20,36},{24,40},{28,44},{32,4... | collective-permute-start | bytes 393224 | tf_op jit(solution)/shard_map/ppermute | solution.py:14
  435.2 399.4 %collective-permute-start.13 = (bf16[1,1,4,16,512]{4,3,2,1,0:T(8,128)(2,1)S(1)}, bf16[1,1,4,16,512]{4,3,2,1,0:T(8,128)(2,1)S(1)}, u32[]{:S(2)}, u32[]{:S(2)}) collective-permute-start(bf16[1,1,4,16,512]{4,3,2,1,0:T(8,128)(2,1)S(1)} %get-tuple-element.21), channel_id=1, source_target_pairs={{0,1},{1,2},{2,3},{3,0},{4,5},{5,6},{6,7},{7,4},{8,9},{9,10},{10,1... | collective-permute-start | bytes 196616 | tf_op jit(solution)/shard_map/ppermute | solution.py:14
Sparse Core Ops, SparseCore 0:
  202.8 330.6 reduce-scatter.5
  539.1 295.4 reduce-scatter.3
  838.2 39.4 all-reduce.3
where the time goes:
time: 889 us; the launch traced here: 888 us
  waiting for transfers between devices  523 us (59%)
  blocking collectives  168 us (19%)
  matrix products  57.8 us (7%)
  starting transfers between devices  54.7 us (6%)
  local copies, waits for them, and re-layouts  53.3 us (6%)
  other arithmetic  17 us (2%)
  between operations  14.9 us (2%)
    reduce_scatter x1, waiting for transfers between devices, on_device(): lax.psum_scatter(totals[0], 'wide', scatter_dimension=1, tiled=True)  301 us
    unnamed x1, blocking collectives  168 us
    ppermute x6, waiting for transfers between devices, from_partner(): lax.ppermute(shard, axis, [(i, i ^ 1 << apart) for i in range(lax.axis_si...  96.1 us
    reduce_scatter x1, waiting for transfers between devices, on_device(): lax.psum_scatter(totals[1], 'wide', scatter_dimension=1, tiled=True)  71.6 us
    ppermute x8, starting transfers between devices, from_behind(): return lax.ppermute(value, axis, pairs)  46.2 us
    psum x1, waiting for transfers between devices, on_device(): totals = lax.psum((grad_qkv, grad_proj, grad_norm), 'narrow')  42.4 us
    dot_general x1, matrix products, attend(): jnp.einsum('...hqk,...qhd->...khd', d_scores, queries, preferred_element_...  18.7 us
  transfers between devices with their start and end apart: 17, of which 12 were waited for; matrix products, arithmetic and copies ran while one was open for 6% of the time, Pallas kernels for 0%

commit v1 on v0

v1 whole, which is shorter than its diff:
```python
import jax
import jax.numpy as jnp
from jax import lax
from jax.experimental import pallas as pl
from jax.experimental.pallas import tpu as pltpu
from jax.sharding import PartitionSpec as P

HEADS = 16
HEAD_DIM = 32
C = 512
WIN = 8
RING = 4
OWN = C // RING
SLAB = 128
TOKENS = RING * SLAB
BLOCK = 256
SCALE = HEAD_DIM**-0.5
LOG2E = 1.4426950408889634
F32 = jnp.float32
BF16 = jnp.bfloat16


def move(value, target):
    pairs = []
    for place in range(64):
        for column in range(4):
            to_place, to_column = target(place, column)
            pairs.append((place * 4 + column, (to_place % 64) * 4 + to_column % 4))
    return lax.ppermute(value, ("wide", "narrow"), pairs)


def partner_of(place):
    return place + 4 if (place // 4) % 2 else place - 4


def along_x(steps):
    return lambda p, n: (p // 4 * 4 + (p + steps) % 4, n)


def other_core(p, n):
    return (p, n ^ 1)


def plane_groups():
    return [
        [(16 * z + member) * 4 + column for member in range(16)]
        for z in range(4)
        for column in range(4)
    ]


def along_z(steps):
    return lambda p, n: (p + 16 * steps, n)


def other_z(p, n):
    return (p, n ^ 2)


def exchange(value, groups):
    return lax.all_to_all(value, ("wide", "narrow"), 0, 0, axis_index_groups=groups)


def dot(a, b):
    return lax.dot_general(a, b, (((1,), (0,)), ((), ())), preferred_element_type=F32)


def dot_nt(a, b):
    return lax.dot_general(a, b, (((1,), (1,)), ((), ())), preferred_element_type=F32)


def unit_of(rows):
    floats = rows.astype(F32)
    average = jnp.mean(floats, -1, keepdims=True)
    centered = floats - average
    variance = jnp.mean(centered * centered, -1, keepdims=True)
    inv_scale = lax.rsqrt(variance + 1e-05)
    return centered * inv_scale, inv_scale


def two_terms(value):
    high = value.astype(BF16)
    low = (value - high.astype(F32)).astype(BF16)
    return high, low


def own_columns(w_qkv, x):
    start = pl.multiple_of(OWN * x, OWN)
    return jnp.concatenate(
        [w_qkv[:, pl.ds(pl.multiple_of(start + C * third, OWN), OWN)] for third in range(3)], 1
    )


def project(parts, norm, w_qkv, w_proj, member):
    unit, _ = unit_of(jnp.concatenate([part[0] for part in parts], 0))
    normed = (unit * norm[0:1, :] + norm[1:2, :]).astype(BF16)
    qkv = dot(normed, own_columns(w_qkv, member)).astype(BF16)
    rows = w_proj[pl.ds(pl.multiple_of(OWN * member, OWN), OWN), :]
    cotangent = dot_nt(jnp.concatenate([part[1] for part in parts], 0), rows).astype(BF16)
    return normed, qkv, cotangent


def first_kernel(flags, p0, p1, p2, p3, norm, w_qkv, w_proj, normed_ref, qkv_ref, up_ref):
    normed_ref[...], qkv_ref[...], up_ref[...] = project(
        (p0, p1, p2, p3), norm, w_qkv, w_proj, flags[3]
    )


def attention_kernel(
    flags, p0, p1, p2, p3, normed0, qkv0, up0, norm, w_qkv, w_proj,
    r0, r1, r2, r3, dt_ref, at_ref, normed1,
):
    normed1[...], qkv1, up1 = project((p0, p1, p2, p3), norm, w_qkv, w_proj, flags[3])
    qkv = jnp.concatenate([qkv0[...], qkv1], 0)
    cotangent = jnp.concatenate([up0[...], up1], 0)
    queries = qkv[:, :OWN]
    keys = qkv[:, OWN : 2 * OWN]
    values = qkv[:, 2 * OWN :]
    queries_t = queries.T
    cotangent_t = cotangent.T
    keys_t = keys.T
    values_t = values.T
    head_of_lane = lax.broadcasted_iota(jnp.int32, (TOKENS, OWN), 1) // HEAD_DIM

    def label(shape, dim):
        token = lax.broadcasted_iota(jnp.int32, shape, dim)
        row = token // 256
        half = (token // 32) % 2
        low_y = (token // 4) % 2
        return row * flags[0] + half * flags[1] + low_y * flags[2]

    key_label = label((TOKENS, 1), 0)
    query_label = label((1, TOKENS), 1)
    d_key = jnp.zeros((TOKENS, OWN), F32)
    d_value = jnp.zeros((TOKENS, OWN), F32)
    for block in range(TOKENS // BLOCK):
        span = slice(block * BLOCK, (block + 1) * BLOCK)
        allowed = key_label == query_label[:, span]
        for head in range(RING):
            chosen = head_of_lane == head
            rows = slice(head * HEAD_DIM, (head + 1) * HEAD_DIM)
            key_head = jnp.where(chosen, keys, jnp.zeros_like(keys))
            value_head = jnp.where(chosen, values, jnp.zeros_like(values))
            scores = jnp.where(allowed, dot(key_head, queries_t[:, span]), -1e30)
            highest = jnp.max(scores, 0, keepdims=True)
            weights = jnp.exp2((scores - highest) * (SCALE * LOG2E))
            probs = weights * (1.0 / jnp.sum(weights, 0, keepdims=True))
            probs_low = probs.astype(BF16)
            d_probs = dot(value_head, cotangent_t[:, span])
            inner = jnp.sum(probs * d_probs, 0, keepdims=True)
            d_scores = (probs * ((d_probs - inner) * SCALE)).astype(BF16)
            at_ref[rows, span] = dot(values_t[rows], probs_low).astype(BF16)
            dt_ref[rows, span] = dot(keys_t[rows], d_scores)
            query_head = jnp.where(chosen[span], queries[span], jnp.zeros_like(queries[span]))
            cotangent_head = jnp.where(
                chosen[span], cotangent[span], jnp.zeros_like(cotangent[span])
            )
            d_key += dot(d_scores, query_head)
            d_value += dot(probs_low, cotangent_head)
    dt_ref[OWN : 2 * OWN, :] = d_key.T
    dt_ref[2 * OWN :, :] = d_value.T
    d_query = dt_ref[:OWN, :].T.astype(BF16)
    attended = at_ref[...].T
    for member, r_ref in enumerate((r0, r1, r2, r3)):
        for part in range(2):
            rows = slice(256 * part + 64 * member, 256 * part + 64 * member + 64)
            to = slice(64 * part, 64 * part + 64)
            r_ref[to, :OWN] = d_query[rows]
            r_ref[to, OWN : 2 * OWN] = d_key[rows].astype(BF16)
            r_ref[to, 2 * OWN : 3 * OWN] = d_value[rows].astype(BF16)
            r_ref[to, 3 * OWN :] = attended[rows]


def gradient_kernel(
    spot, p0, p1, p2, p3, p4, p5, p6, p7, dt_ref, at_ref, normed0, normed1, w_qkv,
    keep, send, g_ref, p_ref, n_ref,
):
    x, core = spot[0], spot[2]
    parts = (p0, p1, p2, p3, p4, p5, p6, p7)
    d_high, d_low = two_terms(dt_ref[...])
    normed = jnp.concatenate([normed0[...], normed1[...]], 0)
    g_ref[...] = dot(d_high, normed) + dot(d_low, normed)
    columns = own_columns(w_qkv, x)
    gain_row = jnp.zeros((1, C), F32)
    offset_row = jnp.zeros((1, C), F32)
    for piece in range(4):
        rows = jnp.concatenate([parts[2 * piece][0], parts[2 * piece + 1][0]], 0)
        high, low = two_terms(dt_ref[:, piece * SLAB : (piece + 1) * SLAB].T)
        d_normed = dot_nt(high, columns) + dot_nt(low, columns)
        gain_row += jnp.sum(d_normed * unit_of(rows)[0], 0, keepdims=True)
        offset_row += jnp.sum(d_normed, 0, keepdims=True)
    p_ref[...] = dot(at_ref[...], jnp.concatenate([part[1] for part in parts], 0)).T
    row = lax.broadcasted_iota(jnp.int32, (128, C), 0)
    n_ref[...] = jnp.where(row == 0, gain_row, jnp.where(row == 1, offset_row, 0.0)).T
    for ahead, out in ((0, keep), (1, send)):
        to_core = core if ahead == 0 else 1 - core
        wide_lanes = pl.ds(pl.multiple_of(256 * to_core, 256), 256)
        for to_y in range(4):
            for to_x in range(4):
                member = 4 * to_y + to_x
                for slot in range(3):
                    residue = 12 * to_y + 3 * to_x + slot
                    third_of = lax.rem(residue // 16 - x + 6, 3)
                    start = pl.multiple_of(128 * third_of + 8 * (residue % 16), 8)
                    out[member, 8 * slot : 8 * slot + 8, :] = g_ref[pl.ds(start, 8), wide_lanes]
                for z in range(4):
                    rows = slice(128 * z + 8 * member, 128 * z + 8 * member + 8)
                    lanes = slice(64 * z, 64 * z + 64)
                    piece = p_ref[rows, :]
                    out[member, 24:32, lanes] = jnp.where(
                        to_core == 0, piece[:, :64], piece[:, 64:]
                    )
                    out[member, 32:40, lanes] = n_ref[rows, :64]


def z_parts_kernel(spot, pieces, *outs):
    x, y, z = spot[0], spot[1], spot[3]
    members = [
        (pieces[j] + pieces[4 + j]) + (pieces[8 + j] + pieces[12 + j]) for j in range(4)
    ]
    total = (members[0] + members[1]) + (members[2] + members[3])
    for to_z in range(4):
        block = []
        for slot in range(3):
            rows = slice(8 * slot, 8 * slot + 8)
            owner = lax.rem(48 * to_z + 12 * y + 3 * x + slot, 64) // 16
            picked = members[0][rows]
            for j in range(1, 4):
                picked = jnp.where(owner == j, members[j][rows], picked)
            block.append(picked)
        lanes = slice(64 * to_z, 64 * to_z + 64)
        block.append(jnp.concatenate([part[24:32, lanes] for part in members], 1))
        block.append(jnp.concatenate([total[32:40, lanes], jnp.zeros((8, 192), F32)], 1))
        block = jnp.concatenate(block, 0)
        outs[0][...] = jnp.where(z == to_z, block, outs[0][...]) if to_z else block
        for steps in range(1, 4):
            ahead = lax.rem(to_z - z + 4, 4) == steps
            outs[steps][...] = jnp.where(ahead, block, outs[steps][...]) if to_z else block


def last_kernel(spot, mine, theirs, g_out, p_out, n_out):
    swap = spot[2] == 1
    low = jnp.where(swap, theirs[...], mine[...])
    high = jnp.where(swap, mine[...], theirs[...])
    g_out[:, :256] = low[:24]
    g_out[:, 256:] = high[:24]
    for member in range(4):
        lanes = slice(64 * member, 64 * member + 64)
        p_out[:, 128 * member : 128 * member + 128] = jnp.concatenate(
            [low[24:32, lanes], high[24:32, lanes]], 1
        )
    n_out[...] = low[32:40, :128].T[:2]


def token_kernel(spot, own0, own1, r0, r1, r2, r3, w_qkv, w_proj, norm, out):
    x = spot[0]
    projected = jnp.zeros((SLAB, C), F32)
    d_normed = jnp.zeros((SLAB, C), F32)
    for r_ref, steps in ((r0, 0), (r1, 3), (r2, 1), (r3, 2)):
        member = lax.rem(x + steps, 4)
        start = pl.multiple_of(OWN * member, OWN)
        projected += dot(r_ref[:, 3 * OWN :], w_proj[pl.ds(start, OWN), :])
        for third in range(3):
            lanes = slice(third * OWN, (third + 1) * OWN)
            columns = w_qkv[:, pl.ds(pl.multiple_of(start + C * third, OWN), OWN)]
            d_normed += dot_nt(r_ref[:, lanes], columns)
    out[0] = projected.astype(BF16)
    unit, inv_scale = unit_of(jnp.concatenate([own0[0], own1[0]], 0))
    d_unit = d_normed * norm[0:1, :]
    first_mean = jnp.mean(d_unit, -1, keepdims=True)
    second_mean = jnp.mean(d_unit * unit, -1, keepdims=True)
    out[1] = (inv_scale * (d_unit - first_mean - unit * second_mean)).astype(BF16)


def call(kernel, scalars, arrays, outs, scratch=(), flops=0, moved=0, room=8):
    smem = pl.BlockSpec(memory_space=pltpu.SMEM)
    vmem = pl.BlockSpec(memory_space=pltpu.VMEM)
    return pl.pallas_call(
        kernel,
        out_shape=[jax.ShapeDtypeStruct(shape, dtype) for shape, dtype in outs],
        in_specs=[smem] + [vmem] * len(arrays),
        out_specs=[vmem] * len(outs),
        scratch_shapes=list(scratch),
        compiler_params=pltpu.CompilerParams(vmem_limit_bytes=room * 2**20),
        cost_estimate=pl.CostEstimate(flops=flops, bytes_accessed=moved, transcendentals=0),
        name=kernel.__name__,
    )(scalars, *arrays)


def on_device(inputs, norm_params, w_qkv, w_proj, upstream):
    place = lax.axis_index("wide")
    column = lax.axis_index("narrow")
    x, y, z = place % 4, place // 4 % 4, place // 16
    core = column % 2
    row = 1 - y % 2
    window = (place - 4) % 64 // 8
    spot = jnp.stack([x, y, core, z]).astype(jnp.int32)
    flags = jnp.stack([4 * (window == 7), 2 * (column == 3), row, x]).astype(jnp.int32)

    upper_y = (jnp.arange(8)[:, None] < 4) != (row == 1)
    both = jnp.stack([inputs[0, 0], upstream[0, 0]]).reshape(2, 8, 2, 8, C)
    other = jnp.where(upper_y, both[:, :, 0], both[:, :, 1])
    other_in = move(other[:, 4:], lambda p, n: (partner_of(p), n))
    cross_in = move(other[:, :4], lambda p, n: (partner_of(p), n - 1))
    both, other = lax.optimization_barrier((both, other))
    mine = jnp.where(upper_y, both[:, :, 1], both[:, :, 0])
    lower_in = move(mine[:, :4], lambda p, n: (p, n - 1))

    part0 = jnp.stack([mine[:, 4:], lower_in], 1).reshape(2, SLAB // 2, C)
    parts0 = [part0] + [move(part0, along_x(steps)) for steps in (1, -1, 2)]
    part1 = jnp.stack([other_in, cross_in], 1).reshape(2, SLAB // 2, C)
    parts1 = [part1] + [move(part1, along_x(steps)) for steps in (1, -1, 2)]
    half = TOKENS // 2
    normed0, qkv0, up0 = call(
        first_kernel,
        flags,
        (*parts0, norm_params, w_qkv, w_proj),
        [((half, C), BF16), ((half, 3 * OWN), BF16), ((half, OWN), BF16)],
        flops=10_000_000_000,
        moved=3_000_000,
    )
    r_own, r_left, r_right, r_far, d_t, a_t, normed1 = call(
        attention_kernel,
        flags,
        (*parts1, normed0, qkv0, up0, norm_params, w_qkv, w_proj),
        [((SLAB, C), BF16)] * 4
        + [((3 * OWN, TOKENS), F32), ((OWN, TOKENS), BF16), ((half, C), BF16)],
        flops=1_200_000_000,
        moved=6_000_000,
    )

    from_right = move(r_left, along_x(-1))
    from_left = move(r_right, along_x(1))
    from_far = move(r_far, along_x(2))
    keep, send = call(
        gradient_kernel,
        spot,
        (*parts0, *parts1, d_t, a_t, normed0, normed1, w_qkv),
        [((16, 40, 256), F32)] * 2,
        scratch=[
            pltpu.VMEM((3 * OWN, C), F32),
            pltpu.VMEM((C, OWN), F32),
            pltpu.VMEM((C, 128), F32),
        ],
        flops=20_000_000_000,
        moved=6_000_000,
    )
    send, from_left, from_right = lax.optimization_barrier((send, from_left, from_right))
    halves, from_far = lax.optimization_barrier((keep + move(send, other_core), from_far))
    plane = exchange(halves, plane_groups())
    (back,) = call(
        token_kernel,
        spot,
        (part0, part1, r_own, from_left, from_right, from_far, w_qkv, w_proj, norm_params),
        [((2, SLAB, C), BF16)],
        flops=500_000_000,
        moved=4_000_000,
    )
    back = back.reshape(2, 4, 4, 8, C)
    lower = move(back[:, 1], lambda p, n: (p, n + 1))
    other_upper = move(back[:, 2], lambda p, n: (partner_of(p), n))
    other_lower = move(back[:, 3], lambda p, n: (partner_of(p), n + 1))

    z_parts = call(z_parts_kernel, spot, (plane,), [((40, 256), F32)] * 4)
    line = [z_parts[0]] + [move(z_parts[steps], along_z(steps)) for steps in (1, 2, 3)]
    line = (line[0] + line[1]) + (line[2] + line[3])
    share = line + move(line, other_z)
    grad_qkv, grad_proj, grad_norm = call(
        last_kernel,
        spot,
        (share, move(share, other_core)),
        [((24, C), F32), ((8, C), F32), ((2, 8), F32)],
    )

    own_full = jnp.concatenate([lower, back[:, 0]], 1)
    other_full = jnp.concatenate([other_lower, other_upper], 1)
    first = jnp.where(upper_y, other_full, own_full)
    second = jnp.where(upper_y, own_full, other_full)
    added = jnp.stack([first, second], 2).reshape(2, 8, 16, C).astype(F32)
    output = (inputs.astype(F32) + added[0]).astype(BF16)
    grad_inputs = (upstream.astype(F32) + added[1]).astype(BF16)
    return (output, grad_inputs, grad_qkv.T, grad_proj.T, grad_norm)


def solution(mesh):
    in_specs = (
        P(None, "wide", "narrow", None, None),
        P(),
        P(),
        P(),
        P(None, "wide", "narrow", None, None),
    )
    out_specs = (
        P(None, "wide", "narrow", None, None),
        P(None, "wide", "narrow", None, None),
        P(None, "wide"),
        P(None, "wide"),
        P(None, "wide"),
    )
    return jax.shard_map(
        on_device, mesh=mesh, in_specs=in_specs, out_specs=out_specs, check_vma=False
    )
```

time: 889 us -> 92.2 us (0.10)
  waiting for transfers between devices: 523 us -> 21.1 us
  blocking collectives: 168 us -> 0 us
  matrix products: 57.8 us -> 0 us
  local copies, waits for them, and re-layouts: 53.3 us -> 0.13 us
  Pallas kernels: 0 us -> 14 us
  between operations: 14.9 us -> 0.92 us
  other arithmetic: 17 us -> 4.85 us
    reduce_scatter x2 -> x0, waiting for transfers between devices: 373 us -> none  [the longest x1 301 us: on_device(): lax.psum_scatter(totals[0], 'wide', scatter_dimension=1, tiled=True)]
    unnamed x1 -> x0, blocking collectives: 168 us -> none
    ppermute x14 -> x21, waiting for transfers between devices: 108 us -> 21.1 us  [move(): return lax.ppermute(value, ('wide', 'narrow'), pairs)]
    dot_general x11 -> x0, matrix products: 52.8 us -> none  [the longest x1 18.7 us: attend(): jnp.einsum('...hqk,...qhd->...khd', d_scores, queries, preferred_element_...]
    psum x1 -> x0, waiting for transfers between devices: 42.4 us -> none  [on_device(): totals = lax.psum((grad_qkv, grad_proj, grad_norm), 'narrow')]
    transpose x8 -> x0, local copies, waits for them, and re-layouts: 17.4 us -> none  [the longest x1 7.41 us: attend(): jnp.einsum('...hqk,...qhd->...khd', d_scores, queries, preferred_element_...]
    concatenate x3 -> x0, local copies, waits for them, and re-layouts: 15.5 us -> none  [the longest x2 14.6 us: on_device(): jnp.concatenate([merge_heads(d_key), merge_heads(d_value)], -1)]
    pallas_call x0 -> x6, Pallas kernels: none -> 14 us  [call(): pl.pallas_call(kernel, out_shape=[jax.ShapeDtypeStruct(shape, dtype) for...]
  transfers between devices with their start and end apart: 17 -> 22, of which waited for: 12 -> 11; matrix products, arithmetic and copies ran while one was open for 6% -> 3% of each run, Pallas kernels for 0% -> 6%
where the time goes in v1:
time: 92.2 us; the launch traced here: 92 us
  starting transfers between devices  51 us (55%)
  waiting for transfers between devices  21.1 us (23%)
  Pallas kernels  14 us (15%)
  other arithmetic  4.85 us (5%)
    ppermute x21, starting transfers between devices, move(): return lax.ppermute(value, ('wide', 'narrow'), pairs)  46.6 us
    ppermute x21, waiting for transfers between devices, move(): return lax.ppermute(value, ('wide', 'narrow'), pairs)  21.1 us
    pallas_call x6, Pallas kernels, call(): pl.pallas_call(kernel, out_shape=[jax.ShapeDtypeStruct(shape, dtype) for...  14 us
    all_to_all x1, starting transfers between devices, exchange(): lax.all_to_all(value, ('wide', 'narrow'), 0, 0, axis_index_groups=groups)  4.41 us
  transfers between devices with their start and end apart: 22, of which 11 were waited for; matrix products, arithmetic and copies ran while one was open for 3% of the time, Pallas kernels for 6%

profile of v1, /device:TPU:1, one launch (start us, length us, event | category | flops | bytes accessed | tf_op | source)
XLA Modules:
  0.0 92.0 jit_solution(16065455637406939619)
XLA Ops:
  0.7 0.0 copy-start
  0.7 0.0 copy-start.1
  0.7 0.0 copy-start.2
  0.7 1.1 %pad_maximum_fusion = bf16[2,8,2,8,512]{4,3,2,1,0:T(8,128)(2,1)S(1)} fusion(bf16[1,8,2,8,512]{4,3,2,1,0:T(8,128)(2,1)} %bitcast.71, bf16[1,8,2,8,512]{4,3,2,1,0:T(8,128)(2,1)} %bitcast.73), kind=kLoop, calls=%fused_computation | loop fusion | flops 131072 | bytes 524288 | tf_op jit(solution)/shard_map/stack | solution.py:301
  1.9 1.0 %fusion.2 = bf16[2,8,8,512]{3,2,1,0:T(8,128)(2,1)S(1)} fusion(pred[8]{0:T(512)(128)(4,1)S(1)} %compare_compare_fusion, bf16[1,8,2,8,512]{4,3,2,1,0:T(8,128)(2,1)} %bitcast.72, bf16[1,8,2,8,512]{4,3,2,1,0:T(8,128)(2,1)} %bitcast.74), kind=kLoop, calls=%fused_computation.7 | loop fusion | flops 196608 | bytes 393224 | tf_op jit(solution)/shard_map/jit(_where)/select_n | solution.py:302
  2.9 0.1 bitcast_select_fusion
  3.1 3.3 %collective-permute-start = (bf16[2,4,8,512]{3,2,1,0:T(8,128)(2,1)S(1)}, bf16[2,4,8,512]{3,2,1,0:T(8,128)(2,1)S(1)}, u32[]{:S(2)}, u32[]{:S(2)}) collective-permute-start(bf16[2,4,8,512]{3,2,1,0:T(8,128)(2,1)S(1)} %get-tuple-element.66), channel_id=1, source_target_pairs={{0,3},{1,0},{2,1},{3,2},{4,7},{5,4},{6,5},{7,6},{8,11},{9,8},{10,9... | collective-permute-start | bytes 196616 | tf_op jit(solution)/shard_map/ppermute | solution.py:29
  6.4 6.8 %collective-permute-start.1 = (bf16[2,4,8,512]{3,2,1,0:T(8,128)(2,1)S(1)}, bf16[2,4,8,512]{3,2,1,0:T(8,128)(2,1)S(1)}, u32[]{:S(2)}, u32[]{:S(2)}) collective-permute-start(bf16[2,4,8,512]{3,2,1,0:T(8,128)(2,1)S(1)} %get-tuple-element.63), channel_id=1, source_target_pairs={{0,240},{1,241},{2,242},{3,243},{4,244},{5,245},{6,246},{7,247},{8... | collective-permute-start | bytes 196616 | tf_op jit(solution)/shard_map/ppermute | solution.py:29
  13.2 0.4 collective-permute-start.2
  13.6 0.0 collective-permute-done
  13.7 2.8 %collective-permute-start.8 = (bf16[2,64,512]{2,1,0:T(8,128)(2,1)S(1)}, bf16[2,64,512]{2,1,0:T(8,128)(2,1)S(1)}, u32[]{:S(2)}, u32[]{:S(2)}) collective-permute-start(bf16[2,64,512]{2,1,0:T(8,128)(2,1)S(1)} %bitcast.59), channel_id=1, source_target_pairs={{0,8},{1,9},{2,10},{3,11},{4,12},{5,13},{6,14},{7,15},{8,0},{9,1},... | collective-permute-start | bytes 393224 | tf_op jit(solution)/shard_map/ppermute | solution.py:29
  16.5 0.9 collective-permute-start.7
  17.4 0.6 collective-permute-start.6
  18.0 0.1 pad_add_fusion
  18.1 0.0 collective-permute-done.1
  18.1 2.7 %collective-permute-done.2 = bf16[2,4,8,512]{3,2,1,0:T(8,128)(2,1)S(1)} collective-permute-done((bf16[2,4,8,512]{3,2,1,0:T(8,128)(2,1)S(1)}, bf16[2,4,8,512]{3,2,1,0:T(8,128)(2,1)S(1)}, u32[]{:S(2)}, u32[]{:S(2)}) %collective-permute-start.2) | collective-permute-done | bytes 65568 | tf_op jit(solution)/shard_map/ppermute | solution.py:29
  20.8 2.8 %collective-permute-start.5 = (bf16[2,64,512]{2,1,0:T(8,128)(2,1)S(1)}, bf16[2,64,512]{2,1,0:T(8,128)(2,1)S(1)}, u32[]{:S(2)}, u32[]{:S(2)}) collective-permute-start(bf16[2,64,512]{2,1,0:T(8,128)(2,1)S(1)} %bitcast.65), channel_id=1, source_target_pairs={{0,8},{1,9},{2,10},{3,11},{4,12},{5,13},{6,14},{7,15},{8,0},{9,1},... | collective-permute-start | bytes 393224 | tf_op jit(solution)/shard_map/ppermute | solution.py:29
  23.7 0.9 collective-permute-start.4
  24.5 0.0 collective-permute-done.8.p3
  24.5 0.6 collective-permute-start.3
  25.1 0.0 collective-permute-done.7.p2
  25.1 0.0 collective-permute-done.6.p1
  25.1 0.0 copy-done
  25.1 0.0 copy-done.1
  25.2 1.1 %first_kernel.1 = (bf16[256,512]{1,0:T(8,128)(2,1)S(1)}, bf16[256,384]{1,0:T(8,128)(2,1)S(1)}, bf16[256,128]{1,0:T(8,128)(2,1)S(1)}) custom-call(s32[4]{0:T(128)S(1)} %get-tuple-element.68.flags, bf16[2,64,512]{2,1,0:T(8,128)(2,1)S(1)} %bitcast.62, bf16[2,64,512]{2,1,0:T(8,128)(2,1)S(1)} %collective-permute-done.6.p1, ...), custom_call_target="tpu_custom_call" | custom-call | flops 10000000000 | bytes 3000000 | tf_op jit(solution)/shard_map/first_kernel/pallas_call | solution.py:278
  26.3 0.0 collective-permute-done.5.p3.p7
  26.3 1.4 %collective-permute-done.4.p2.p6 = bf16[2,64,512]{2,1,0:T(8,128)(2,1)S(1)} collective-permute-done((bf16[2,64,512]{2,1,0:T(8,128)(2,1)S(1)}, bf16[2,64,512]{2,1,0:T(8,128)(2,1)S(1)}, u32[]{:S(2)}, u32[]{:S(2)}) %collective-permute-start.4) | collective-permute-done | bytes 131104 | tf_op jit(solution)/shard_map/ppermute | solution.py:29
  27.7 3.0 %collective-permute-done.3.p1.p5 = bf16[2,64,512]{2,1,0:T(8,128)(2,1)S(1)} collective-permute-done((bf16[2,64,512]{2,1,0:T(8,128)(2,1)S(1)}, bf16[2,64,512]{2,1,0:T(8,128)(2,1)S(1)}, u32[]{:S(2)}, u32[]{:S(2)}) %collective-permute-start.3) | collective-permute-done | bytes 131104 | tf_op jit(solution)/shard_map/ppermute | solution.py:29
  30.8 6.8 %attention_kernel.1 = (bf16[128,512]{1,0:T(8,128)(2,1)S(1)}, bf16[128,512]{1,0:T(8,128)(2,1)S(1)}, bf16[128,512]{1,0:T(8,128)(2,1)S(1)}, bf16[128,512]{1,0:T(8,1...) custom-call(s32[4]{0:T(128)S(1)} %get-tuple-element.68.flags, ...), custom_call_target="tpu_custom_call" | custom-call | flops 1200000000 | bytes 6000000 | tf_op jit(solution)/shard_map/attention_kernel/pallas_call | solution.py:278
  37.6 0.1 collective-permute-start.9
  37.7 2.7 %collective-permute-start.10 = (bf16[128,512]{1,0:T(8,128)(2,1)S(1)}, bf16[128,512]{1,0:T(8,128)(2,1)S(1)}, u32[]{:S(2)}, u32[]{:S(2)}) collective-permute-start(bf16[128,512]{1,0:T(8,128)(2,1)S(1)} %get-tuple-element.40), channel_id=1, source_target_pairs={{0,12},{1,13},{2,14},{3,15},{4,0},{5,1},{6,2},{7,3},{8,4},{9,5},{1... | collective-permute-start | bytes 393224 | tf_op jit(solution)/shard_map/ppermute | solution.py:29
  40.3 2.8 %gradient_kernel.1 = (f32[16,40,256]{2,1,0:T(8,128)S(1)}, f32[16,40,256]{2,1,0:T(8,128)S(1)}) custom-call(s32[4]{0:T(128)S(1)} %get-tuple-element.67.spot, bf16[2,64,512]{2,1,0:T(8,128)(2,1)S(1)} %bitcast.63, bf16[2,64,512]{2,1,0:T(8,128)(2,1)S(1)} %collective-permute-done.6.p1, bf16[2,64,512]{2,1,0:T(8,128)(2,1)S(1)} %collective-permute-done.7.p2, ...), custom_call_target="tpu_custom_call" | custom-call | flops 20000000000 | bytes 6000000 | tf_op jit(solution)/shard_map/gradient_kernel/pallas_call | solution.py:278
  43.2 0.0 collective-permute-done.9.r1
  43.2 0.0 collective-permute-done.10.r2
  43.2 3.6 %collective-permute-start.11 = (f32[16,40,256]{2,1,0:T(8,128)S(1)}, f32[16,40,256]{2,1,0:T(8,128)S(1)}, u32[]{:S(2)}, u32[]{:S(2)}) collective-permute-start(f32[16,40,256]{2,1,0:T(8,128)S(1)} %get-tuple-element.44), channel_id=1, source_target_pairs={{0,1},{1,0},{2,3},{3,2},{4,5},{5,4},{6,7},{7,6},{8,9},{9,8},{10,11... | collective-permute-start | bytes 1966088 | tf_op jit(solution)/shard_map/ppermute | solution.py:29
  46.8 1.2 %collective-permute-start.12 = (bf16[128,512]{1,0:T(8,128)(2,1)S(1)}, bf16[128,512]{1,0:T(8,128)(2,1)S(1)}, u32[]{:S(2)}, u32[]{:S(2)}) collective-permute-start(bf16[128,512]{1,0:T(8,128)(2,1)S(1)} %get-tuple-element.45), channel_id=1, source_target_pairs={{0,8},{1,9},{2,10},{3,11},{4,12},{5,13},{6,14},{7,15},{8,0},{9,1},... | collective-permute-start | bytes 393224 | tf_op jit(solution)/shard_map/ppermute | solution.py:29
  48.0 0.5 collective-permute-done.11
  48.5 0.9 %add.46 = f32[16,40,256]{2,1,0:T(8,128)} add(f32[16,40,256]{2,1,0:T(8,128)S(1)} %get-tuple-element.43, f32[16,40,256]{2,1,0:T(8,128)S(1)} %collective-permute-done.11) | non-fusion elementwise | flops 163840 | bytes 1966080 | tf_op jit(solution)/shard_map/add | solution.py:349
  49.5 3.9 %collective-permute-done.12.r3 = bf16[128,512]{1,0:T(8,128)(2,1)S(1)} collective-permute-done((bf16[128,512]{1,0:T(8,128)(2,1)S(1)}, bf16[128,512]{1,0:T(8,128)(2,1)S(1)}, u32[]{:S(2)}, u32[]{:S(2)}) %collective-permute-start.12) | collective-permute-done | bytes 131104 | tf_op jit(solution)/shard_map/ppermute | solution.py:29
  53.4 4.4 %all-to-all-start = ((f32[16,40,256]{2,1,0:T(8,128)}), f32[16,40,256]{2,1,0:T(8,128)S(1)}, u32[]{:S(2)}, u32[]{:S(2)}) async-start(f32[16,40,256]{2,1,0:T(8,128)} %add.46), calls=%async_computation | async-start | bytes 1310720 | tf_op jit(solution)/shard_map/all_to_all | solution.py:61
  57.8 1.4 %token_kernel.1 = bf16[2,128,512]{2,1,0:T(8,128)(2,1)S(1)} custom-call(s32[4]{0:T(128)S(1)} %get-tuple-element.67.spot, bf16[2,64,512]{2,1,0:T(8,128)(2,1)S(1)} %bitcast.64, bf16[2,64,512]{2,1,0:T(8,128)(2,1)S(1)} %bitcast.70, bf16[128,512]{1,0:T(8,128)(2,1)S(1)} %get-tuple-element.34.r0, bf16[128,512]{1,0:T(8,128)(2,1)S(1)} %collective-permute-done.9.r1, ...), custom_call_target="tpu_custom_call" | custom-call | flops 500000000 | bytes 4000000 | tf_op jit(solution)/shard_map/token_kernel/pallas_call | solution.py:278
  59.2 5.6 %collective-permute-start.13 = (bf16[2,4,8,512]{3,2,1,0:T(8,128)(2,1)S(1)}, bf16[2,4,8,512]{3,2,1,0:T(8,128)(2,1)S(1)}, u32[]{:S(2)}, u32[]{:S(2)}) collective-permute-start(bf16[2,4,8,512]{3,2,1,0:T(8,128)(2,1)S(1)} %get-tuple-element.59), channel_id=1, source_target_pairs={{0,241},{1,242},{2,243},{3,240},{4,245},{5,246},{6,247},{7,244},{8... | collective-permute-start | bytes 196616 | tf_op jit(solution)/shard_map/ppermute | solution.py:29
  64.8 2.1 %collective-permute-start.14 = (bf16[2,4,8,512]{3,2,1,0:T(8,128)(2,1)S(1)}, bf16[2,4,8,512]{3,2,1,0:T(8,128)(2,1)S(1)}, u32[]{:S(2)}, u32[]{:S(2)}) collective-permute-start(bf16[2,4,8,512]{3,2,1,0:T(8,128)(2,1)S(1)} %get-tuple-element.60), channel_id=1, source_target_pairs={{0,240},{1,241},{2,242},{3,243},{4,244},{5,245},{6,246},{7,247},{8... | collective-permute-start | bytes 196616 | tf_op jit(solution)/shard_map/ppermute | solution.py:29
  66.8 0.0 collective-permute-start.15
  66.8 2.0 %collective-permute-done.13 = bf16[2,4,8,512]{3,2,1,0:T(8,128)(2,1)S(1)} collective-permute-done((bf16[2,4,8,512]{3,2,1,0:T(8,128)(2,1)S(1)}, bf16[2,4,8,512]{3,2,1,0:T(8,128)(2,1)S(1)}, u32[]{:S(2)}, u32[]{:S(2)}) %collective-permute-start.13) | collective-permute-done | bytes 65568 | tf_op jit(solution)/shard_map/ppermute | solution.py:29
  68.8 5.0 %collective-permute-done.14 = bf16[2,4,8,512]{3,2,1,0:T(8,128)(2,1)S(1)} collective-permute-done((bf16[2,4,8,512]{3,2,1,0:T(8,128)(2,1)S(1)}, bf16[2,4,8,512]{3,2,1,0:T(8,128)(2,1)S(1)}, u32[]{:S(2)}, u32[]{:S(2)}) %collective-permute-start.14) | collective-permute-done | bytes 65568 | tf_op jit(solution)/shard_map/ppermute | solution.py:29
  73.8 0.0 collective-permute-done.15
  73.8 0.1 broadcast_select_fusion.1
  73.9 0.0 copy-start.4
  73.9 0.0 all-to-all-done.pieces
  74.0 0.7 z_parts_kernel.1
  74.7 0.1 collective-permute-start.16
  74.7 2.2 %collective-permute-start.17 = (f32[40,256]{1,0:T(8,128)S(1)}, f32[40,256]{1,0:T(8,128)S(1)}, u32[]{:S(2)}, u32[]{:S(2)}) collective-permute-start(f32[40,256]{1,0:T(8,128)S(1)} %get-tuple-element.50), channel_id=1, source_target_pairs={{0,128},{1,129},{2,130},{3,131},{4,132},{5,133},{6,134},{7,135},{8... | collective-permute-start | bytes 122888 | tf_op jit(solution)/shard_map/ppermute | solution.py:29
  77.0 3.4 %collective-permute-start.18 = (f32[40,256]{1,0:T(8,128)S(1)}, f32[40,256]{1,0:T(8,128)S(1)}, u32[]{:S(2)}, u32[]{:S(2)}) collective-permute-start(f32[40,256]{1,0:T(8,128)S(1)} %get-tuple-element.51), channel_id=1, source_target_pairs={{0,192},{1,193},{2,194},{3,195},{4,196},{5,197},{6,198},{7,199},{8... | collective-permute-start | bytes 122888 | tf_op jit(solution)/shard_map/ppermute | solution.py:29
  80.5 0.0 collective-permute-done.16
  80.5 1.1 %collective-permute-done.17 = f32[40,256]{1,0:T(8,128)S(1)} collective-permute-done((f32[40,256]{1,0:T(8,128)S(1)}, f32[40,256]{1,0:T(8,128)S(1)}, u32[]{:S(2)}, u32[]{:S(2)}) %collective-permute-start.17) | collective-permute-done | bytes 40992 | tf_op jit(solution)/shard_map/ppermute | solution.py:29
  81.6 0.5 collective-permute-done.18
  82.1 3.7 %collective-permute-start.19 = (f32[40,256]{1,0:T(8,128)S(1)}, f32[40,256]{1,0:T(8,128)S(1)}, u32[]{:S(2)}, u32[]{:S(2)}) collective-permute-start(f32[40,256]{1,0:T(8,128)S(1)} %add_add_fusion), channel_id=1, source_target_pairs={{0,2},{1,3},{2,0},{3,1},{4,6},{5,7},{6,4},{7,5},{8,10},{9,11},{10,... | collective-permute-start | bytes 122888 | tf_op jit(solution)/shard_map/ppermute | solution.py:29
  85.7 0.7 fusion
  86.4 0.7 collective-permute-done.19
  87.1 2.8 %collective-permute-start.20 = (f32[40,256]{1,0:T(8,128)S(1)}, f32[40,256]{1,0:T(8,128)S(1)}, u32[]{:S(2)}, u32[]{:S(2)}) collective-permute-start(f32[40,256]{1,0:T(8,128)S(1)} %add.52.mine), channel_id=1, source_target_pairs={{0,1},{1,0},{2,3},{3,2},{4,5},{5,4},{6,7},{7,6},{8,9},{9,8},{10,11... | collective-permute-start | bytes 122888 | tf_op jit(solution)/shard_map/ppermute | solution.py:29
  89.9 0.7 fusion.1
  90.6 0.2 collective-permute-done.20.theirs
  90.8 1.2 %last_kernel.1 = (f32[24,512]{1,0:T(8,128)}, f32[8,512]{1,0:T(8,128)}, f32[2,8]{1,0:T(2,128)}) custom-call(s32[4]{0:T(128)S(1)} %get-tuple-element.67.spot, f32[40,256]{1,0:T(8,128)S(1)} %add.52.mine, f32[40,256]{1,0:T(8,128)S(1)} %collective-permute-done.20.theirs), custom_call_target="tpu_custom_call" | custom-call | tf_op jit(solution)/shard_map/last_kernel/pallas_call | solution.py:278
  (16 shorter events, 0.2 us)
Async XLA Ops:
  0.7 24.4 %copy-start = (bf16[512,1536]{1,0:T(8,128)(2,1)S(1)}, bf16[512,1536]{1,0:T(8,128)(2,1)}, u32[]{:S(2)}) copy-start(bf16[512,1536]{1,0:T(8,128)(2,1)} %w_qkv.7) | copy-start | bytes 4718596
  0.7 24.4 %copy-start.1 = (bf16[512,512]{1,0:T(8,128)(2,1)S(1)}, bf16[512,512]{1,0:T(8,128)(2,1)}, u32[]{:S(2)}) copy-start(bf16[512,512]{1,0:T(8,128)(2,1)} %w_proj.5) | copy-start | bytes 1572868
  0.7 24.4 %copy-start.2 = (f32[2,512]{1,0:T(2,128)S(1)}, f32[2,512]{1,0:T(2,128)}, u32[]{:S(2)}) copy-start(f32[2,512]{1,0:T(2,128)} %norm.5) | copy-start | bytes 12292
  3.1 10.6 %collective-permute-start = (bf16[2,4,8,512]{3,2,1,0:T(8,128)(2,1)S(1)}, bf16[2,4,8,512]{3,2,1,0:T(8,128)(2,1)S(1)}, u32[]{:S(2)}, u32[]{:S(2)}) collective-permute-start(bf16[2,4,8,512]{3,2,1,0:T(8,128)(2,1)S(1)} %get-tuple-element.66), channel_id=1, source_target_pairs={{0,3},{1,0},{2,1},{3,2},{4,7},{5,4},{6,5},{7,6},{8,11},{9,8},{10,9... | collective-permute-start | bytes 196616 | tf_op jit(solution)/shard_map/ppermute | solution.py:29
  6.4 11.7 %collective-permute-start.1 = (bf16[2,4,8,512]{3,2,1,0:T(8,128)(2,1)S(1)}, bf16[2,4,8,512]{3,2,1,0:T(8,128)(2,1)S(1)}, u32[]{:S(2)}, u32[]{:S(2)}) collective-permute-start(bf16[2,4,8,512]{3,2,1,0:T(8,128)(2,1)S(1)} %get-tuple-element.63), channel_id=1, source_target_pairs={{0,240},{1,241},{2,242},{3,243},{4,244},{5,245},{6,246},{7,247},{8... | collective-permute-start | bytes 196616 | tf_op jit(solution)/shard_map/ppermute | solution.py:29
  13.2 7.6 %collective-permute-start.2 = (bf16[2,4,8,512]{3,2,1,0:T(8,128)(2,1)S(1)}, bf16[2,4,8,512]{3,2,1,0:T(8,128)(2,1)S(1)}, u32[]{:S(2)}, u32[]{:S(2)}) collective-permute-start(bf16[2,4,8,512]{3,2,1,0:T(8,128)(2,1)S(1)} %get-tuple-element.64), channel_id=1, source_target_pairs={{0,243},{1,240},{2,241},{3,242},{4,247},{5,244},{6,245},{7,246},{8... | collective-permute-start | bytes 196616 | tf_op jit(solution)/shard_map/ppermute | solution.py:29
  13.7 10.8 %collective-permute-start.8 = (bf16[2,64,512]{2,1,0:T(8,128)(2,1)S(1)}, bf16[2,64,512]{2,1,0:T(8,128)(2,1)S(1)}, u32[]{:S(2)}, u32[]{:S(2)}) collective-permute-start(bf16[2,64,512]{2,1,0:T(8,128)(2,1)S(1)} %bitcast.59), channel_id=1, source_target_pairs={{0,8},{1,9},{2,10},{3,11},{4,12},{5,13},{6,14},{7,15},{8,0},{9,1},... | collective-permute-start | bytes 393224 | tf_op jit(solution)/shard_map/ppermute | solution.py:29
  16.5 8.6 %collective-permute-start.7 = (bf16[2,64,512]{2,1,0:T(8,128)(2,1)S(1)}, bf16[2,64,512]{2,1,0:T(8,128)(2,1)S(1)}, u32[]{:S(2)}, u32[]{:S(2)}) collective-permute-start(bf16[2,64,512]{2,1,0:T(8,128)(2,1)S(1)} %bitcast.60), channel_id=1, source_target_pairs={{0,12},{1,13},{2,14},{3,15},{4,0},{5,1},{6,2},{7,3},{8,4},{9,5},{1... | collective-permute-start | bytes 393224 | tf_op jit(solution)/shard_map/ppermute | solution.py:29
  17.4 7.8 %collective-permute-start.6 = (bf16[2,64,512]{2,1,0:T(8,128)(2,1)S(1)}, bf16[2,64,512]{2,1,0:T(8,128)(2,1)S(1)}, u32[]{:S(2)}, u32[]{:S(2)}) collective-permute-start(bf16[2,64,512]{2,1,0:T(8,128)(2,1)S(1)} %bitcast.61), channel_id=1, source_target_pairs={{0,4},{1,5},{2,6},{3,7},{4,8},{5,9},{6,10},{7,11},{8,12},{9,13},{1... | collective-permute-start | bytes 393224 | tf_op jit(solution)/shard_map/ppermute | solution.py:29
  20.8 5.5 %collective-permute-start.5 = (bf16[2,64,512]{2,1,0:T(8,128)(2,1)S(1)}, bf16[2,64,512]{2,1,0:T(8,128)(2,1)S(1)}, u32[]{:S(2)}, u32[]{:S(2)}) collective-permute-start(bf16[2,64,512]{2,1,0:T(8,128)(2,1)S(1)} %bitcast.65), channel_id=1, source_target_pairs={{0,8},{1,9},{2,10},{3,11},{4,12},{5,13},{6,14},{7,15},{8,0},{9,1},... | collective-permute-start | bytes 393224 | tf_op jit(solution)/shard_map/ppermute | solution.py:29
  23.7 4.1 %collective-permute-start.4 = (bf16[2,64,512]{2,1,0:T(8,128)(2,1)S(1)}, bf16[2,64,512]{2,1,0:T(8,128)(2,1)S(1)}, u32[]{:S(2)}, u32[]{:S(2)}) collective-permute-start(bf16[2,64,512]{2,1,0:T(8,128)(2,1)S(1)} %bitcast.66), channel_id=1, source_target_pairs={{0,12},{1,13},{2,14},{3,15},{4,0},{5,1},{6,2},{7,3},{8,4},{9,5},{1... | collective-permute-start | bytes 393224 | tf_op jit(solution)/shard_map/ppermute | solution.py:29
  24.5 6.3 %collective-permute-start.3 = (bf16[2,64,512]{2,1,0:T(8,128)(2,1)S(1)}, bf16[2,64,512]{2,1,0:T(8,128)(2,1)S(1)}, u32[]{:S(2)}, u32[]{:S(2)}) collective-permute-start(bf16[2,64,512]{2,1,0:T(8,128)(2,1)S(1)} %bitcast.67), channel_id=1, source_target_pairs={{0,4},{1,5},{2,6},{3,7},{4,8},{5,9},{6,10},{7,11},{8,12},{9,13},{1... | collective-permute-start | bytes 393224 | tf_op jit(solution)/shard_map/ppermute | solution.py:29
  37.6 5.6 %collective-permute-start.9 = (bf16[128,512]{1,0:T(8,128)(2,1)S(1)}, bf16[128,512]{1,0:T(8,128)(2,1)S(1)}, u32[]{:S(2)}, u32[]{:S(2)}) collective-permute-start(bf16[128,512]{1,0:T(8,128)(2,1)S(1)} %get-tuple-element.39), channel_id=1, source_target_pairs={{0,4},{1,5},{2,6},{3,7},{4,8},{5,9},{6,10},{7,11},{8,12},{9,13},{1... | collective-permute-start | bytes 393224 | tf_op jit(solution)/shard_map/ppermute | solution.py:29
  37.7 5.5 %collective-permute-start.10 = (bf16[128,512]{1,0:T(8,128)(2,1)S(1)}, bf16[128,512]{1,0:T(8,128)(2,1)S(1)}, u32[]{:S(2)}, u32[]{:S(2)}) collective-permute-start(bf16[128,512]{1,0:T(8,128)(2,1)S(1)} %get-tuple-element.40), channel_id=1, source_target_pairs={{0,12},{1,13},{2,14},{3,15},{4,0},{5,1},{6,2},{7,3},{8,4},{9,5},{1... | collective-permute-start | bytes 393224 | tf_op jit(solution)/shard_map/ppermute | solution.py:29
  43.2 5.3 %collective-permute-start.11 = (f32[16,40,256]{2,1,0:T(8,128)S(1)}, f32[16,40,256]{2,1,0:T(8,128)S(1)}, u32[]{:S(2)}, u32[]{:S(2)}) collective-permute-start(f32[16,40,256]{2,1,0:T(8,128)S(1)} %get-tuple-element.44), channel_id=1, source_target_pairs={{0,1},{1,0},{2,3},{3,2},{4,5},{5,4},{6,7},{7,6},{8,9},{9,8},{10,11... | collective-permute-start | bytes 1966088 | tf_op jit(solution)/shard_map/ppermute | solution.py:29
  46.8 6.6 %collective-permute-start.12 = (bf16[128,512]{1,0:T(8,128)(2,1)S(1)}, bf16[128,512]{1,0:T(8,128)(2,1)S(1)}, u32[]{:S(2)}, u32[]{:S(2)}) collective-permute-start(bf16[128,512]{1,0:T(8,128)(2,1)S(1)} %get-tuple-element.45), channel_id=1, source_target_pairs={{0,8},{1,9},{2,10},{3,11},{4,12},{5,13},{6,14},{7,15},{8,0},{9,1},... | collective-permute-start | bytes 393224 | tf_op jit(solution)/shard_map/ppermute | solution.py:29
  53.4 20.6 %all-to-all-start = ((f32[16,40,256]{2,1,0:T(8,128)}), f32[16,40,256]{2,1,0:T(8,128)S(1)}, u32[]{:S(2)}, u32[]{:S(2)}) async-start(f32[16,40,256]{2,1,0:T(8,128)} %add.46), calls=%async_computation | async-start | bytes 1310720 | tf_op jit(solution)/shard_map/all_to_all | solution.py:61
  59.2 9.6 %collective-permute-start.13 = (bf16[2,4,8,512]{3,2,1,0:T(8,128)(2,1)S(1)}, bf16[2,4,8,512]{3,2,1,0:T(8,128)(2,1)S(1)}, u32[]{:S(2)}, u32[]{:S(2)}) collective-permute-start(bf16[2,4,8,512]{3,2,1,0:T(8,128)(2,1)S(1)} %get-tuple-element.59), channel_id=1, source_target_pairs={{0,241},{1,242},{2,243},{3,240},{4,245},{5,246},{6,247},{7,244},{8... | collective-permute-start | bytes 196616 | tf_op jit(solution)/shard_map/ppermute | solution.py:29
  64.8 9.0 %collective-permute-start.14 = (bf16[2,4,8,512]{3,2,1,0:T(8,128)(2,1)S(1)}, bf16[2,4,8,512]{3,2,1,0:T(8,128)(2,1)S(1)}, u32[]{:S(2)}, u32[]{:S(2)}) collective-permute-start(bf16[2,4,8,512]{3,2,1,0:T(8,128)(2,1)S(1)} %get-tuple-element.60), channel_id=1, source_target_pairs={{0,240},{1,241},{2,242},{3,243},{4,244},{5,245},{6,246},{7,247},{8... | collective-permute-start | bytes 196616 | tf_op jit(solution)/shard_map/ppermute | solution.py:29
  66.8 7.0 %collective-permute-start.15 = (bf16[2,4,8,512]{3,2,1,0:T(8,128)(2,1)S(1)}, bf16[2,4,8,512]{3,2,1,0:T(8,128)(2,1)S(1)}, u32[]{:S(2)}, u32[]{:S(2)}) collective-permute-start(bf16[2,4,8,512]{3,2,1,0:T(8,128)(2,1)S(1)} %get-tuple-element.62), channel_id=1, source_target_pairs={{0,1},{1,2},{2,3},{3,0},{4,5},{5,6},{6,7},{7,4},{8,9},{9,10},{10,1... | collective-permute-start | bytes 196616 | tf_op jit(solution)/shard_map/ppermute | solution.py:29
  73.8 12.0 %copy-start.3 = (bf16[1,1,8,16,512]{4,3,2,1,0:T(8,128)(2,1)S(1)}, bf16[1,1,8,16,512]{4,3,2,1,0:T(8,128)(2,1)}, u32[]{:S(2)}) copy-start(bf16[1,1,8,16,512]{4,3,2,1,0:T(8,128)(2,1)} %param.9) | copy-start | bytes 393220
  73.9 16.0 %copy-start.4 = (bf16[1,1,8,16,512]{4,3,2,1,0:T(8,128)(2,1)S(1)}, bf16[1,1,8,16,512]{4,3,2,1,0:T(8,128)(2,1)}, u32[]{:S(2)}) copy-start(bf16[1,1,8,16,512]{4,3,2,1,0:T(8,128)(2,1)} %param.5) | copy-start | bytes 393220
  74.7 5.8 %collective-permute-start.16 = (f32[40,256]{1,0:T(8,128)S(1)}, f32[40,256]{1,0:T(8,128)S(1)}, u32[]{:S(2)}, u32[]{:S(2)}) collective-permute-start(f32[40,256]{1,0:T(8,128)S(1)} %get-tuple-element.49), channel_id=1, source_target_pairs={{0,64},{1,65},{2,66},{3,67},{4,68},{5,69},{6,70},{7,71},{8,72},{9,... | collective-permute-start | bytes 122888 | tf_op jit(solution)/shard_map/ppermute | solution.py:29
  74.7 6.9 %collective-permute-start.17 = (f32[40,256]{1,0:T(8,128)S(1)}, f32[40,256]{1,0:T(8,128)S(1)}, u32[]{:S(2)}, u32[]{:S(2)}) collective-permute-start(f32[40,256]{1,0:T(8,128)S(1)} %get-tuple-element.50), channel_id=1, source_target_pairs={{0,128},{1,129},{2,130},{3,131},{4,132},{5,133},{6,134},{7,135},{8... | collective-permute-start | bytes 122888 | tf_op jit(solution)/shard_map/ppermute | solution.py:29
  77.0 5.1 %collective-permute-start.18 = (f32[40,256]{1,0:T(8,128)S(1)}, f32[40,256]{1,0:T(8,128)S(1)}, u32[]{:S(2)}, u32[]{:S(2)}) collective-permute-start(f32[40,256]{1,0:T(8,128)S(1)} %get-tuple-element.51), channel_id=1, source_target_pairs={{0,192},{1,193},{2,194},{3,195},{4,196},{5,197},{6,198},{7,199},{8... | collective-permute-start | bytes 122888 | tf_op jit(solution)/shard_map/ppermute | solution.py:29
  82.1 5.0 %collective-permute-start.19 = (f32[40,256]{1,0:T(8,128)S(1)}, f32[40,256]{1,0:T(8,128)S(1)}, u32[]{:S(2)}, u32[]{:S(2)}) collective-permute-start(f32[40,256]{1,0:T(8,128)S(1)} %add_add_fusion), channel_id=1, source_target_pairs={{0,2},{1,3},{2,0},{3,1},{4,6},{5,7},{6,4},{7,5},{8,10},{9,11},{10,... | collective-permute-start | bytes 122888 | tf_op jit(solution)/shard_map/ppermute | solution.py:29
  87.1 3.6 %collective-permute-start.20 = (f32[40,256]{1,0:T(8,128)S(1)}, f32[40,256]{1,0:T(8,128)S(1)}, u32[]{:S(2)}, u32[]{:S(2)}) collective-permute-start(f32[40,256]{1,0:T(8,128)S(1)} %add.52.mine), channel_id=1, source_target_pairs={{0,1},{1,0},{2,3},{3,2},{4,5},{5,4},{6,7},{7,6},{8,9},{9,8},{10,11... | collective-permute-start | bytes 122888 | tf_op jit(solution)/shard_map/ppermute | solution.py:29

commit v2 on v1

--- a/solution.py
+++ b/solution.py
@@ -14,6 +14,7 @@
 SLAB = 128
 TOKENS = RING * SLAB
 BLOCK = 256
+CHUNK = 64
 SCALE = HEAD_DIM**-0.5
 LOG2E = 1.4426950408889634
 F32 = jnp.float32
@@ -55,6 +56,10 @@
 
 def other_z(p, n):
     return (p, n ^ 2)
+
+
+def other_both(p, n):
+    return (p, n ^ 3)
 
 
 def exchange(value, groups):
@@ -143,12 +148,26 @@
             value_head = jnp.where(chosen, values, jnp.zeros_like(values))
             scores = jnp.where(allowed, dot(key_head, queries_t[:, span]), -1e30)
             highest = jnp.max(scores, 0, keepdims=True)
-            weights = jnp.exp2((scores - highest) * (SCALE * LOG2E))
-            probs = weights * (1.0 / jnp.sum(weights, 0, keepdims=True))
-            probs_low = probs.astype(BF16)
             d_probs = dot(value_head, cotangent_t[:, span])
-            inner = jnp.sum(probs * d_probs, 0, keepdims=True)
-            d_scores = (probs * ((d_probs - inner) * SCALE)).astype(BF16)
+            weights = []
+            total = jnp.zeros((8, BLOCK), F32)
+            inner = jnp.zeros((8, BLOCK), F32)
+            for start in range(0, TOKENS, CHUNK):
+                part = slice(start, start + CHUNK)
+                weight = jnp.exp2((scores[part] - highest) * (SCALE * LOG2E))
+                total += jnp.sum(weight.reshape(CHUNK // 8, 8, BLOCK), 0)
+                inner += jnp.sum((weight * d_probs[part]).reshape(CHUNK // 8, 8, BLOCK), 0)
+                weights.append(weight)
+            over = 1.0 / jnp.sum(total, 0, keepdims=True)
+            inner = jnp.sum(inner, 0, keepdims=True) * over
+            over_scaled = over * SCALE
+            probs_low, d_scores = [], []
+            for index, weight in enumerate(weights):
+                part = slice(index * CHUNK, (index + 1) * CHUNK)
+                probs_low.append((weight * over).astype(BF16))
+                d_scores.append(((weight * over_scaled) * (d_probs[part] - inner)).astype(BF16))
+            probs_low = jnp.concatenate(probs_low, 0)
+            d_scores = jnp.concatenate(d_scores, 0)
             at_ref[rows, span] = dot(values_t[rows], probs_low).astype(BF16)
             dt_ref[rows, span] = dot(keys_t[rows], d_scores)
             query_head = jnp.where(chosen[span], queries[span], jnp.zeros_like(queries[span]))
@@ -172,45 +191,58 @@
 
 
 def gradient_kernel(
-    spot, p0, p1, p2, p3, p4, p5, p6, p7, dt_ref, at_ref, normed0, normed1, w_qkv,
-    keep, send, g_ref, p_ref, n_ref,
+    spot, p0, p1, p2, p3, p4, p5, p6, p7, dt_ref, at_ref, normed0, normed1,
+    keep, send, g_ref, p_ref,
 ):
     x, core = spot[0], spot[2]
     parts = (p0, p1, p2, p3, p4, p5, p6, p7)
     d_high, d_low = two_terms(dt_ref[...])
     normed = jnp.concatenate([normed0[...], normed1[...]], 0)
     g_ref[...] = dot(d_high, normed) + dot(d_low, normed)
-    columns = own_columns(w_qkv, x)
+    p_ref[...] = dot(at_ref[...], jnp.concatenate([part[1] for part in parts], 0)).T
+    for ahead, out in ((0, keep), (1, send)):
+        to_core = core if ahead == 0 else 1 - core
+        for member in range(16):
+            for side in range(2):
+                lanes = pl.ds(pl.multiple_of(256 * to_core + 128 * side, 128), 128)
+                for slot in range(3):
+                    residue = 3 * member + slot
+                    third_of = lax.rem(residue // 16 - x + 6, 3)
+                    start = pl.multiple_of(128 * third_of + 8 * (residue % 16), 8)
+                    top = 24 * side + 8 * slot
+                    out[member, top : top + 8, :] = g_ref[pl.ds(start, 8), lanes]
+            for z in range(4):
+                rows = slice(128 * z + 8 * member, 128 * z + 8 * member + 8)
+                piece = p_ref[rows, :]
+                top = 48 + 8 * (z // 2)
+                out[member, top : top + 8, 64 * (z % 2) : 64 * (z % 2) + 64] = jnp.where(
+                    to_core == 0, piece[:, :64], piece[:, 64:]
+                )
+
+
+def norm_kernel(
+    spot, p0, p1, p2, p3, p4, p5, p6, p7, r0, r1, r2, r3, w_qkv, out, n_ref
+):
+    parts = (p0, p1, p2, p3, p4, p5, p6, p7)
+    columns = own_columns(w_qkv, spot[0])
     gain_row = jnp.zeros((1, C), F32)
     offset_row = jnp.zeros((1, C), F32)
-    for piece in range(4):
-        rows = jnp.concatenate([parts[2 * piece][0], parts[2 * piece + 1][0]], 0)
-        high, low = two_terms(dt_ref[:, piece * SLAB : (piece + 1) * SLAB].T)
-        d_normed = dot_nt(high, columns) + dot_nt(low, columns)
+    for member, r_ref in enumerate((r0, r1, r2, r3)):
+        rows = jnp.concatenate([parts[member][0], parts[4 + member][0]], 0)
+        d_normed = dot_nt(r_ref[:, : 3 * OWN], columns)
         gain_row += jnp.sum(d_normed * unit_of(rows)[0], 0, keepdims=True)
         offset_row += jnp.sum(d_normed, 0, keepdims=True)
-    p_ref[...] = dot(at_ref[...], jnp.concatenate([part[1] for part in parts], 0)).T
     row = lax.broadcasted_iota(jnp.int32, (128, C), 0)
     n_ref[...] = jnp.where(row == 0, gain_row, jnp.where(row == 1, offset_row, 0.0)).T
-    for ahead, out in ((0, keep), (1, send)):
-        to_core = core if ahead == 0 else 1 - core
-        wide_lanes = pl.ds(pl.multiple_of(256 * to_core, 256), 256)
-        for to_y in range(4):
-            for to_x in range(4):
-                member = 4 * to_y + to_x
-                for slot in range(3):
-                    residue = 12 * to_y + 3 * to_x + slot
-                    third_of = lax.rem(residue // 16 - x + 6, 3)
-                    start = pl.multiple_of(128 * third_of + 8 * (residue % 16), 8)
-                    out[member, 8 * slot : 8 * slot + 8, :] = g_ref[pl.ds(start, 8), wide_lanes]
-                for z in range(4):
-                    rows = slice(128 * z + 8 * member, 128 * z + 8 * member + 8)
-                    lanes = slice(64 * z, 64 * z + 64)
-                    piece = p_ref[rows, :]
-                    out[member, 24:32, lanes] = jnp.where(
-                        to_core == 0, piece[:, :64], piece[:, 64:]
-                    )
-                    out[member, 32:40, lanes] = n_ref[rows, :64]
+    for member in range(16):
+        for z in range(4):
+            rows = slice(128 * z + 8 * member, 128 * z + 8 * member + 8)
+            out[member, :, 32 * z : 32 * z + 32] = n_ref[rows, :32]
+
+
+def join_kernel(spot, keep, received, norms, out):
+    out[:, :64, :] = keep[...] + received[...]
+    out[:, 64:, :] = norms[...]
 
 
 def z_parts_kernel(spot, pieces, *outs):
@@ -218,38 +250,65 @@
     members = [
         (pieces[j] + pieces[4 + j]) + (pieces[8 + j] + pieces[12 + j]) for j in range(4)
     ]
-    total = (members[0] + members[1]) + (members[2] + members[3])
+    total = (members[0][64:] + members[1][64:]) + (members[2][64:] + members[3][64:])
     for to_z in range(4):
         block = []
-        for slot in range(3):
-            rows = slice(8 * slot, 8 * slot + 8)
-            owner = lax.rem(48 * to_z + 12 * y + 3 * x + slot, 64) // 16
-            picked = members[0][rows]
-            for j in range(1, 4):
-                picked = jnp.where(owner == j, members[j][rows], picked)
-            block.append(picked)
-        lanes = slice(64 * to_z, 64 * to_z + 64)
-        block.append(jnp.concatenate([part[24:32, lanes] for part in members], 1))
-        block.append(jnp.concatenate([total[32:40, lanes], jnp.zeros((8, 192), F32)], 1))
+        for side in range(2):
+            for slot in range(3):
+                rows = slice(24 * side + 8 * slot, 24 * side + 8 * slot + 8)
+                owner = lax.rem(48 * to_z + 12 * y + 3 * x + slot, 64) // 16
+                picked = members[0][rows]
+                for j in range(1, 4):
+                    picked = jnp.where(owner == j, members[j][rows], picked)
+                block.append(picked)
+        rows = slice(48 + 8 * (to_z // 2), 56 + 8 * (to_z // 2))
+        lanes = slice(64 * (to_z % 2), 64 * (to_z % 2) + 64)
+        for pair in range(2):
+            block.append(
+                jnp.concatenate([members[2 * pair + j][rows, lanes] for j in range(2)], 1)
+            )
+        lanes = slice(32 * to_z, 32 * to_z + 32)
+        block.append(jnp.concatenate([total[:, lanes], jnp.zeros((8, 96), F32)], 1))
         block = jnp.concatenate(block, 0)
-        outs[0][...] = jnp.where(z == to_z, block, outs[0][...]) if to_z else block
-        for steps in range(1, 4):
+        for steps in range(4):
             ahead = lax.rem(to_z - z + 4, 4) == steps
             outs[steps][...] = jnp.where(ahead, block, outs[steps][...]) if to_z else block
 
 
-def last_kernel(spot, mine, theirs, g_out, p_out, n_out):
+def last_kernel(spot, near, core_in, z_in, both_in, g_out, p_out, n_out):
+    mine = near[...] + z_in[...]
+    theirs = core_in[...] + both_in[...]
     swap = spot[2] == 1
-    low = jnp.where(swap, theirs[...], mine[...])
-    high = jnp.where(swap, mine[...], theirs[...])
-    g_out[:, :256] = low[:24]
-    g_out[:, 256:] = high[:24]
+    shares = (jnp.where(swap, theirs, mine), jnp.where(swap, mine, theirs))
+    for core in range(2):
+        for side in range(2):
+            lanes = slice(256 * core + 128 * side, 256 * core + 128 * side + 128)
+            g_out[:, lanes] = shares[core][24 * side : 24 * side + 24]
     for member in range(4):
-        lanes = slice(64 * member, 64 * member + 64)
+        rows = slice(48 + 8 * (member // 2), 56 + 8 * (member // 2))
+        lanes = slice(64 * (member % 2), 64 * (member % 2) + 64)
         p_out[:, 128 * member : 128 * member + 128] = jnp.concatenate(
-            [low[24:32, lanes], high[24:32, lanes]], 1
+            [share[rows, lanes] for share in shares], 1
         )
-    n_out[...] = low[32:40, :128].T[:2]
+    n_out[...] = (mine[64:] + theirs[64:]).T[:2]
+
+
+def upper_rows(row):
+    return (lax.broadcasted_iota(jnp.int32, (4, 8, C), 1) < 4) != (row == 1)
+
+
+def merge_kernel(
+    spot, inputs, upstream, mine_high, mine_low, other_high, other_low, output, grad_inputs
+):
+    upper = upper_rows(spot[4])
+    for array, (source, out) in enumerate(((inputs, output), (upstream, grad_inputs))):
+        for start, other, mine in ((4, other_high, mine_high), (0, other_low, mine_low)):
+            rows = source[start : start + 4].astype(F32)
+            from_other = other[array].astype(F32)
+            from_mine = mine[array].astype(F32)
+            first = rows[:, :8] + jnp.where(upper, from_other, from_mine)
+            second = rows[:, 8:] + jnp.where(upper, from_mine, from_other)
+            out[start : start + 4] = jnp.concatenate([first, second], 1).astype(BF16)
 
 
 def token_kernel(spot, own0, own1, r0, r1, r2, r3, w_qkv, w_proj, norm, out):
@@ -272,16 +331,16 @@
     out[1] = (inv_scale * (d_unit - first_mean - unit * second_mean)).astype(BF16)
 
 
-def call(kernel, scalars, arrays, outs, scratch=(), flops=0, moved=0, room=8):
+def call(kernel, scalars, arrays, outs, scratch=(), flops=0, moved=0, fetched=0):
     smem = pl.BlockSpec(memory_space=pltpu.SMEM)
     vmem = pl.BlockSpec(memory_space=pltpu.VMEM)
     return pl.pallas_call(
         kernel,
         out_shape=[jax.ShapeDtypeStruct(shape, dtype) for shape, dtype in outs],
-        in_specs=[smem] + [vmem] * len(arrays),
+        in_specs=[smem] + [pl.BlockSpec()] * fetched + [vmem] * (len(arrays) - fetched),
         out_specs=[vmem] * len(outs),
         scratch_shapes=list(scratch),
-        compiler_params=pltpu.CompilerParams(vmem_limit_bytes=room * 2**20),
+        compiler_params=pltpu.CompilerParams(vmem_limit_bytes=8 * 2**20),
         cost_estimate=pl.CostEstimate(flops=flops, bytes_accessed=moved, transcendentals=0),
         name=kernel.__name__,
     )(scalars, *arrays)
@@ -294,17 +353,17 @@
     core = column % 2
     row = 1 - y % 2
     window = (place - 4) % 64 // 8
-    spot = jnp.stack([x, y, core, z]).astype(jnp.int32)
+    spot = jnp.stack([x, y, core, z, row]).astype(jnp.int32)
     flags = jnp.stack([4 * (window == 7), 2 * (column == 3), row, x]).astype(jnp.int32)
 
+    own_inputs, own_upstream = inputs[0, 0], upstream[0, 0]
     upper_y = (jnp.arange(8)[:, None] < 4) != (row == 1)
-    both = jnp.stack([inputs[0, 0], upstream[0, 0]]).reshape(2, 8, 2, 8, C)
+    both = jnp.stack([own_inputs, own_upstream]).reshape(2, 8, 2, 8, C)
+    mine = jnp.where(upper_y, both[:, :, 1], both[:, :, 0])
     other = jnp.where(upper_y, both[:, :, 0], both[:, :, 1])
+    lower_in = move(mine[:, :4], lambda p, n: (p, n - 1))
     other_in = move(other[:, 4:], lambda p, n: (partner_of(p), n))
     cross_in = move(other[:, :4], lambda p, n: (partner_of(p), n - 1))
-    both, other = lax.optimization_barrier((both, other))
-    mine = jnp.where(upper_y, both[:, :, 1], both[:, :, 0])
-    lower_in = move(mine[:, :4], lambda p, n: (p, n - 1))
 
     part0 = jnp.stack([mine[:, 4:], lower_in], 1).reshape(2, SLAB // 2, C)
     parts0 = [part0] + [move(part0, along_x(steps)) for steps in (1, -1, 2)]
@@ -335,19 +394,16 @@
     keep, send = call(
         gradient_kernel,
         spot,
-        (*parts0, *parts1, d_t, a_t, normed0, normed1, w_qkv),
-        [((16, 40, 256), F32)] * 2,
-        scratch=[
-            pltpu.VMEM((3 * OWN, C), F32),
-            pltpu.VMEM((C, OWN), F32),
-            pltpu.VMEM((C, 128), F32),
-        ],
+        (*parts0, *parts1, d_t, a_t, normed0, normed1),
+        [((16, 64, 128), F32)] * 2,
+        scratch=[pltpu.VMEM((3 * OWN, C), F32), pltpu.VMEM((C, OWN), F32)],
         flops=20_000_000_000,
         moved=6_000_000,
     )
-    send, from_left, from_right = lax.optimization_barrier((send, from_left, from_right))
-    halves, from_far = lax.optimization_barrier((keep + move(send, other_core), from_far))
-    plane = exchange(halves, plane_groups())
+    send, from_left, from_right, from_far = lax.optimization_barrier(
+        (send, from_left, from_right, from_far)
+    )
+    received = move(send, other_core)
     (back,) = call(
         token_kernel,
         spot,
@@ -356,30 +412,46 @@
         flops=500_000_000,
         moved=4_000_000,
     )
+    back, r_far = lax.optimization_barrier((back, r_far))
+    (norms,) = call(
+        norm_kernel,
+        spot,
+        (*parts0, *parts1, r_own, r_left, r_right, r_far, w_qkv),
+        [((16, 8, 128), F32)],
+        scratch=[pltpu.VMEM((C, 128), F32)],
+        flops=1_000_000_000,
+        moved=2_000_000,
+    )
+    (halves,) = call(join_kernel, spot, (keep, received, norms), [((16, 72, 128), F32)])
+    halves, back = lax.optimization_barrier((halves, back))
+    plane = exchange(halves, plane_groups())
     back = back.reshape(2, 4, 4, 8, C)
     lower = move(back[:, 1], lambda p, n: (p, n + 1))
     other_upper = move(back[:, 2], lambda p, n: (partner_of(p), n))
     other_lower = move(back[:, 3], lambda p, n: (partner_of(p), n + 1))
 
-    z_parts = call(z_parts_kernel, spot, (plane,), [((40, 256), F32)] * 4)
+    z_parts = call(z_parts_kernel, spot, (plane,), [((72, 128), F32)] * 4)
+    output, grad_inputs = call(
+        merge_kernel,
+        spot,
+        (own_inputs, own_upstream, back[:, 0], lower, other_upper, other_lower),
+        [((8, 16, C), BF16)] * 2,
+        fetched=2,
+    )
     line = [z_parts[0]] + [move(z_parts[steps], along_z(steps)) for steps in (1, 2, 3)]
+    line[1], line[2], line[3], output, grad_inputs = lax.optimization_barrier(
+        (line[1], line[2], line[3], output, grad_inputs)
+    )
     line = (line[0] + line[1]) + (line[2] + line[3])
-    share = line + move(line, other_z)
     grad_qkv, grad_proj, grad_norm = call(
         last_kernel,
         spot,
-        (share, move(share, other_core)),
+        (line, move(line, other_core), move(line, other_z), move(line, other_both)),
         [((24, C), F32), ((8, C), F32), ((2, 8), F32)],
     )
-
-    own_full = jnp.concatenate([lower, back[:, 0]], 1)
-    other_full = jnp.concatenate([other_lower, other_upper], 1)
-    first = jnp.where(upper_y, other_full, own_full)
-    second = jnp.where(upper_y, own_full, other_full)
-    added = jnp.stack([first, second], 2).reshape(2, 8, 16, C).astype(F32)
-    output = (inputs.astype(F32) + added[0]).astype(BF16)
-    grad_inputs = (upstream.astype(F32) + added[1]).astype(BF16)
-    return (output, grad_inputs, grad_qkv.T, grad_proj.T, grad_norm)
+    return (
+        output[None, None], grad_inputs[None, None], grad_qkv.T, grad_proj.T, grad_norm
+    )
 
 
 def solution(mesh):

time: 92.2 us -> 87.8 us (0.952)
  other arithmetic: 4.85 us -> 1.32 us
  Pallas kernels: 14 us -> 16.8 us
  starting transfers between devices: 51 us -> 48.2 us
  waiting for transfers between devices: 21.1 us -> 19.2 us
  local copies, waits for them, and re-layouts: 0.13 us -> 1.19 us
    ppermute x21 -> x22, waiting for transfers between devices: 21.1 us -> 14.8 us  [move(): return lax.ppermute(value, ('wide', 'narrow'), pairs)]
    all_to_all x1, waiting for transfers between devices: 0.01 us -> 4.41 us  [exchange(): lax.all_to_all(value, ('wide', 'narrow'), 0, 0, axis_index_groups=groups)]
    pallas_call x6 -> x9, Pallas kernels: 14 us -> 16.8 us  [call(): pl.pallas_call(kernel, out_shape=[jax.ShapeDtypeStruct(shape, dtype) for...]
    ppermute x21 -> x22, starting transfers between devices: 46.6 us -> 44.5 us  [move(): return lax.ppermute(value, ('wide', 'narrow'), pairs)]
    convert_element_type x3 -> x0, other arithmetic: 1.41 us -> none  [the longest x1 0.69 us: on_device(): grad_inputs = (upstream.astype(F32) + added[1]).astype(BF16)]
    another operation x2 -> x1, other arithmetic: 1.22 us -> 0.08 us  [on_device(): jnp.stack([4 * (window == 7), 2 * (column == 3), row, x]).astype(jnp.int32)]
    unnamed x10 -> x12, local copies, waits for them, and re-layouts: 0.03 us -> 1.06 us
    add x2 -> x0, other arithmetic: 0.95 us -> none  [the longest x1 0.94 us: on_device(): keep + move(send, other_core)]
  transfers between devices with their start and end apart: 22 -> 23, of which waited for: 11 -> 11; matrix products, arithmetic and copies ran while one was open for 3% -> 0% of each run, Pallas kernels for 6% -> 8%
where the time goes in v2:
time: 87.8 us; the launch traced here: 87.5 us
  starting transfers between devices  48.2 us (55%)
  waiting for transfers between devices  19.2 us (22%)
  Pallas kernels  16.8 us (19%)
  other arithmetic  1.32 us (2%)
  local copies, waits for them, and re-layouts  1.19 us (1%)
    ppermute x22, starting transfers between devices, move(): return lax.ppermute(value, ('wide', 'narrow'), pairs)  44.5 us
    pallas_call x9, Pallas kernels, call(): pl.pallas_call(kernel, out_shape=[jax.ShapeDtypeStruct(shape, dtype) for...  16.8 us
    ppermute x22, waiting for transfers between devices, move(): return lax.ppermute(value, ('wide', 'narrow'), pairs)  14.8 us
    all_to_all x1, waiting for transfers between devices, exchange(): lax.all_to_all(value, ('wide', 'narrow'), 0, 0, axis_index_groups=groups)  4.41 us
    all_to_all x1, starting transfers between devices, exchange(): lax.all_to_all(value, ('wide', 'narrow'), 0, 0, axis_index_groups=groups)  3.71 us
  transfers between devices with their start and end apart: 23, of which 11 were waited for; matrix products, arithmetic and copies ran while one was open for 0% of the time, Pallas kernels for 8%

profile of v2, /device:TPU:1, one launch (start us, length us, event | category | flops | bytes accessed | tf_op | source)
XLA Modules:
  0.0 87.5 jit_solution(17977174516404519888)
XLA Ops:
  0.6 0.0 copy-start
  0.6 0.0 copy-start.5
  0.7 1.2 %broadcast_select_fusion = (bf16[2,8,8,512]{3,2,1,0:T(8,128)(2,1)S(1)}, bf16[2,8,8,512]{3,2,1,0:T(8,128)(2,1)S(1)}) fusion(pred[8]{0:T(512)(128)(4,1)S(1)} %compare_compare_fusion, bf16[1,8,2,8,512]{4,3,2,1,0:T(8,128)(2,1)} %bitcast.60, bf16[1,8,2,8,512]{4,3,2,1,0:T(8,128)(2,1)} %bitcast.58), kind=kLoop, calls=%fused_computation.8 | loop fusion | flops 327680 | bytes 524296 | tf_op jit(solution)/shard_map/jit(_where)/select_n | solution.py:363
  1.9 3.3 %collective-permute-start = (bf16[2,4,8,512]{3,2,1,0:T(8,128)(2,1)S(1)}, bf16[2,4,8,512]{3,2,1,0:T(8,128)(2,1)S(1)}, u32[]{:S(2)}, u32[]{:S(2)}) collective-permute-start(bf16[2,4,8,512]{3,2,1,0:T(8,128)(2,1)S(1)} %get-tuple-element.82), channel_id=1, source_target_pairs={{0,3},{1,0},{2,1},{3,2},{4,7},{5,4},{6,5},{7,6},{8,11},{9,8},{10,9... | collective-permute-start | bytes 196616 | tf_op jit(solution)/shard_map/ppermute | solution.py:30
  5.3 6.8 %collective-permute-start.4 = (bf16[2,4,8,512]{3,2,1,0:T(8,128)(2,1)S(1)}, bf16[2,4,8,512]{3,2,1,0:T(8,128)(2,1)S(1)}, u32[]{:S(2)}, u32[]{:S(2)}) collective-permute-start(bf16[2,4,8,512]{3,2,1,0:T(8,128)(2,1)S(1)} %get-tuple-element.79), channel_id=1, source_target_pairs={{0,240},{1,241},{2,242},{3,243},{4,244},{5,245},{6,246},{7,247},{8... | collective-permute-start | bytes 196616 | tf_op jit(solution)/shard_map/ppermute | solution.py:30
  12.1 0.4 collective-permute-start.5
  12.5 0.0 collective-permute-done
  12.6 2.8 %collective-permute-start.3 = (bf16[2,64,512]{2,1,0:T(8,128)(2,1)S(1)}, bf16[2,64,512]{2,1,0:T(8,128)(2,1)S(1)}, u32[]{:S(2)}, u32[]{:S(2)}) collective-permute-start(bf16[2,64,512]{2,1,0:T(8,128)(2,1)S(1)} %bitcast.62), channel_id=1, source_target_pairs={{0,8},{1,9},{2,10},{3,11},{4,12},{5,13},{6,14},{7,15},{8,0},{9,1},... | collective-permute-start | bytes 393224 | tf_op jit(solution)/shard_map/ppermute | solution.py:30
  15.4 0.9 collective-permute-start.2
  16.3 0.6 collective-permute-start.1
  16.9 0.1 pad_add_fusion.flags
  16.9 0.1 stack.59.spot
  17.0 0.0 collective-permute-done.4
  17.0 2.7 %collective-permute-done.5 = bf16[2,4,8,512]{3,2,1,0:T(8,128)(2,1)S(1)} collective-permute-done((bf16[2,4,8,512]{3,2,1,0:T(8,128)(2,1)S(1)}, bf16[2,4,8,512]{3,2,1,0:T(8,128)(2,1)S(1)}, u32[]{:S(2)}, u32[]{:S(2)}) %collective-permute-start.5) | collective-permute-done | bytes 65568 | tf_op jit(solution)/shard_map/ppermute | solution.py:30
  19.7 2.8 %collective-permute-start.8 = (bf16[2,64,512]{2,1,0:T(8,128)(2,1)S(1)}, bf16[2,64,512]{2,1,0:T(8,128)(2,1)S(1)}, u32[]{:S(2)}, u32[]{:S(2)}) collective-permute-start(bf16[2,64,512]{2,1,0:T(8,128)(2,1)S(1)} %bitcast.69), channel_id=1, source_target_pairs={{0,8},{1,9},{2,10},{3,11},{4,12},{5,13},{6,14},{7,15},{8,0},{9,1},... | collective-permute-start | bytes 393224 | tf_op jit(solution)/shard_map/ppermute | solution.py:30
  22.5 0.9 collective-permute-start.7
  23.4 0.0 collective-permute-done.3.p3
  23.4 0.6 collective-permute-start.6
  24.0 0.0 collective-permute-done.2.p2
  24.0 0.0 collective-permute-done.1.p1
  24.0 0.0 copy-done
  24.0 0.0 copy-done.5
  24.0 0.0 copy-start.3
  24.0 1.0 %copy-done.3 = bf16[512,512]{1,0:T(8,128)(2,1)S(1)} copy-done((bf16[512,512]{1,0:T(8,128)(2,1)S(1)}, bf16[512,512]{1,0:T(8,128)(2,1)}, u32[]{:S(2)}) %copy-start.3) | copy-done | bytes 524312
  25.1 1.1 %first_kernel.1 = (bf16[256,512]{1,0:T(8,128)(2,1)S(1)}, bf16[256,384]{1,0:T(8,128)(2,1)S(1)}, bf16[256,128]{1,0:T(8,128)(2,1)S(1)}) custom-call(s32[4]{0:T(128)S(1)} %pad_add_fusion.flags, bf16[2,64,512]{2,1,0:T(8,128)(2,1)S(1)} %bitcast.65, bf16[2,64,512]{2,1,0:T(8,128)(2,1)S(1)} %collective-permute-done.1.p1, ...), custom_call_target="tpu_custom_call" | custom-call | flops 10000000000 | bytes 3000000 | tf_op jit(solution)/shard_map/first_kernel/pallas_call | solution.py:337
  26.2 0.0 collective-permute-done.8.p3.p7
  26.2 0.4 collective-permute-done.7.p2.p6
  26.6 3.0 %collective-permute-done.6.p1.p5 = bf16[2,64,512]{2,1,0:T(8,128)(2,1)S(1)} collective-permute-done((bf16[2,64,512]{2,1,0:T(8,128)(2,1)S(1)}, bf16[2,64,512]{2,1,0:T(8,128)(2,1)S(1)}, u32[]{:S(2)}, u32[]{:S(2)}) %collective-permute-start.6) | collective-permute-done | bytes 131104 | tf_op jit(solution)/shard_map/ppermute | solution.py:30
  29.7 6.7 %attention_kernel.1 = (bf16[128,512]{1,0:T(8,128)(2,1)S(1)}, bf16[128,512]{1,0:T(8,128)(2,1)S(1)}, bf16[128,512]{1,0:T(8,128)(2,1)S(1)}, bf16[128,512]{1,0:T(8,1...) custom-call(s32[4]{0:T(128)S(1)} %pad_add_fusion.flags, ...), custom_call_target="tpu_custom_call" | custom-call | flops 1200000000 | bytes 6000000 | tf_op jit(solution)/shard_map/attention_kernel/pallas_call | solution.py:337
  36.4 0.3 collective-permute-start.9
  36.6 2.7 %collective-permute-start.10 = (bf16[128,512]{1,0:T(8,128)(2,1)S(1)}, bf16[128,512]{1,0:T(8,128)(2,1)S(1)}, u32[]{:S(2)}, u32[]{:S(2)}) collective-permute-start(bf16[128,512]{1,0:T(8,128)(2,1)S(1)} %get-tuple-element.48.r1), channel_id=1, source_target_pairs={{0,12},{1,13},{2,14},{3,15},{4,0},{5,1},{6,2},{7,3},{8,4},{9,5},{1... | collective-permute-start | bytes 393224 | tf_op jit(solution)/shard_map/ppermute | solution.py:30
  39.3 0.0 collective-permute-start.11
  39.3 1.6 %gradient_kernel.1 = (f32[16,64,128]{2,1,0:T(8,128)S(1)}, f32[16,64,128]{2,1,0:T(8,128)S(1)}) custom-call(s32[5]{0:T(128)S(1)} %stack.59.spot, bf16[2,64,512]{2,1,0:T(8,128)(2,1)S(1)} %bitcast.66, bf16[2,64,512]{2,1,0:T(8,128)(2,1)S(1)} %collective-permute-done.1.p1, bf16[2,64,512]{2,1,0:T(8,128)(2,1)S(1)} %collective-permute-done.2.p2, ...), custom_call_target="tpu_custom_call" | custom-call | flops 20000000000 | bytes 6000000 | tf_op jit(solution)/shard_map/gradient_kernel/pallas_call | solution.py:337
  40.9 0.8 collective-permute-done.9.r1
  41.6 1.0 %collective-permute-done.10.r2 = bf16[128,512]{1,0:T(8,128)(2,1)S(1)} collective-permute-done((bf16[128,512]{1,0:T(8,128)(2,1)S(1)}, bf16[128,512]{1,0:T(8,128)(2,1)S(1)}, u32[]{:S(2)}, u32[]{:S(2)}) %collective-permute-start.10) | collective-permute-done | bytes 131104 | tf_op jit(solution)/shard_map/ppermute | solution.py:30
  42.6 2.5 %collective-permute-done.11.r3 = bf16[128,512]{1,0:T(8,128)(2,1)S(1)} collective-permute-done((bf16[128,512]{1,0:T(8,128)(2,1)S(1)}, bf16[128,512]{1,0:T(8,128)(2,1)S(1)}, u32[]{:S(2)}, u32[]{:S(2)}) %collective-permute-start.11) | collective-permute-done | bytes 131104 | tf_op jit(solution)/shard_map/ppermute | solution.py:30
  45.1 4.2 %collective-permute-start.12 = (f32[16,64,128]{2,1,0:T(8,128)S(1)}, f32[16,64,128]{2,1,0:T(8,128)S(1)}, u32[]{:S(2)}, u32[]{:S(2)}) collective-permute-start(f32[16,64,128]{2,1,0:T(8,128)S(1)} %get-tuple-element.50), channel_id=1, source_target_pairs={{0,1},{1,0},{2,3},{3,2},{4,5},{5,4},{6,7},{7,6},{8,9},{9,8},{10,11... | collective-permute-start | bytes 1572872 | tf_op jit(solution)/shard_map/ppermute | solution.py:30
  49.3 1.4 %token_kernel.1 = bf16[2,128,512]{2,1,0:T(8,128)(2,1)S(1)} custom-call(s32[5]{0:T(128)S(1)} %stack.59.spot, bf16[2,64,512]{2,1,0:T(8,128)(2,1)S(1)} %bitcast.67, bf16[2,64,512]{2,1,0:T(8,128)(2,1)S(1)} %bitcast.74, bf16[128,512]{1,0:T(8,128)(2,1)S(1)} %get-tuple-element.51.r0, bf16[128,512]{1,0:T(8,128)(2,1)S(1)} %collective-permute-done.9.r1, ...), custom_call_target="tpu_custom_call" | custom-call | flops 500000000 | bytes 4000000 | tf_op jit(solution)/shard_map/token_kernel/pallas_call | solution.py:337
  50.7 1.4 %norm_kernel.1.norms = f32[16,8,128]{2,1,0:T(8,128)S(1)} custom-call(s32[5]{0:T(128)S(1)} %stack.59.spot, bf16[2,64,512]{2,1,0:T(8,128)(2,1)S(1)} %bitcast.68, bf16[2,64,512]{2,1,0:T(8,128)(2,1)S(1)} %collective-permute-done.1.p1, bf16[2,64,512]{2,1,0:T(8,128)(2,1)S(1)} %collective-permute-done.2.p2, bf16[2,64,512]{2,1,0:T(8,128)(2,1)S(1)} %collective-permute-done.3.p3, ...), custom_call_target="tpu_custom_call" | custom-call | flops 1000000000 | bytes 2000000 | tf_op jit(solution)/shard_map/norm_kernel/pallas_call | solution.py:337
  52.1 0.0 collective-permute-done.12.received
  52.1 1.4 %join_kernel.1 = f32[16,72,128]{2,1,0:T(8,128)} custom-call(s32[5]{0:T(128)S(1)} %stack.59.spot, f32[16,64,128]{2,1,0:T(8,128)S(1)} %get-tuple-element.45.keep, f32[16,64,128]{2,1,0:T(8,128)S(1)} %collective-permute-done.12.received, f32[16,8,128]{2,1,0:T(8,128)S(1)} %norm_kernel.1.norms), custom_call_target="tpu_custom_call" | custom-call | tf_op jit(solution)/shard_map/join_kernel/pallas_call | solution.py:337
  53.6 3.7 %all-to-all-start = ((f32[16,72,128]{2,1,0:T(8,128)}), f32[16,72,128]{2,1,0:T(8,128)S(1)}, u32[]{:S(2)}, u32[]{:S(2)}) async-start(f32[16,72,128]{2,1,0:T(8,128)} %join_kernel.1), calls=%async_computation | async-start | bytes 1179648 | tf_op jit(solution)/shard_map/all_to_all | solution.py:66
  57.3 4.9 %collective-permute-start.18 = (bf16[2,4,8,512]{3,2,1,0:T(8,128)(2,1)S(1)}, bf16[2,4,8,512]{3,2,1,0:T(8,128)(2,1)S(1)}, u32[]{:S(2)}, u32[]{:S(2)}) collective-permute-start(bf16[2,4,8,512]{3,2,1,0:T(8,128)(2,1)S(1)} %get-tuple-element.75), channel_id=1, source_target_pairs={{0,241},{1,242},{2,243},{3,240},{4,245},{5,246},{6,247},{7,244},{8... | collective-permute-start | bytes 196616 | tf_op jit(solution)/shard_map/ppermute | solution.py:30
  62.2 2.1 %collective-permute-start.17 = (bf16[2,4,8,512]{3,2,1,0:T(8,128)(2,1)S(1)}, bf16[2,4,8,512]{3,2,1,0:T(8,128)(2,1)S(1)}, u32[]{:S(2)}, u32[]{:S(2)}) collective-permute-start(bf16[2,4,8,512]{3,2,1,0:T(8,128)(2,1)S(1)} %get-tuple-element.76), channel_id=1, source_target_pairs={{0,240},{1,241},{2,242},{3,243},{4,244},{5,245},{6,246},{7,247},{8... | collective-permute-start | bytes 196616 | tf_op jit(solution)/shard_map/ppermute | solution.py:30
  64.3 0.7 collective-permute-start.16
  64.9 4.4 %all-to-all-done.pieces = f32[16,72,128]{2,1,0:T(8,128)S(1)} async-done(((f32[16,72,128]{2,1,0:T(8,128)}), f32[16,72,128]{2,1,0:T(8,128)S(1)}, u32[]{:S(2)}, u32[]{:S(2)}) %all-to-all-start) | async-done | bytes 589856 | tf_op jit(solution)/shard_map/all_to_all | solution.py:66
  69.3 0.7 z_parts_kernel.1
  70.0 1.5 %collective-permute-start.13 = (f32[72,128]{1,0:T(8,128)S(1)}, f32[72,128]{1,0:T(8,128)S(1)}, u32[]{:S(2)}, u32[]{:S(2)}) collective-permute-start(f32[72,128]{1,0:T(8,128)S(1)} %get-tuple-element.58), channel_id=1, source_target_pairs={{0,64},{1,65},{2,66},{3,67},{4,68},{5,69},{6,70},{7,71},{8,72},{9,... | collective-permute-start | bytes 110600 | tf_op jit(solution)/shard_map/ppermute | solution.py:30
  71.6 3.2 %collective-permute-start.14 = (f32[72,128]{1,0:T(8,128)S(1)}, f32[72,128]{1,0:T(8,128)S(1)}, u32[]{:S(2)}, u32[]{:S(2)}) collective-permute-start(f32[72,128]{1,0:T(8,128)S(1)} %get-tuple-element.59), channel_id=1, source_target_pairs={{0,128},{1,129},{2,130},{3,131},{4,132},{5,133},{6,134},{7,135},{8... | collective-permute-start | bytes 110600 | tf_op jit(solution)/shard_map/ppermute | solution.py:30
  74.8 0.0 collective-permute-done.18.other_low
  74.8 0.7 collective-permute-start.15
  75.5 0.0 collective-permute-done.17.other_high
  75.5 0.0 collective-permute-done.16.mine_low
  75.5 1.3 %merge_kernel.1 = (bf16[8,16,512]{2,1,0:T(8,128)(2,1)}, bf16[8,16,512]{2,1,0:T(8,128)(2,1)}) custom-call(s32[5]{0:T(128)S(1)} %stack.59.spot, bf16[8,16,512]{2,1,0:T(8,128)(2,1)S(1)} %bitcast.59, bf16[8,16,512]{2,1,0:T(8,128)(2,1)S(1)} %bitcast.61, bf16[2,4,8,512]{3,2,1,0:T(8,128)(2,1)S(1)} %get-tuple-element.78.mine_high, ...), custom_call_target="tpu_custom_call" | custom-call | tf_op jit(solution)/shard_map/merge_kernel/pallas_call | solution.py:337
  76.8 0.0 collective-permute-done.13
  76.8 2.0 %collective-permute-done.14 = f32[72,128]{1,0:T(8,128)S(1)} collective-permute-done((f32[72,128]{1,0:T(8,128)S(1)}, f32[72,128]{1,0:T(8,128)S(1)}, u32[]{:S(2)}, u32[]{:S(2)}) %collective-permute-start.14) | collective-permute-done | bytes 36896 | tf_op jit(solution)/shard_map/ppermute | solution.py:30
  78.8 0.2 collective-permute-done.15
  79.0 3.9 %collective-permute-start.21 = (f32[72,128]{1,0:T(8,128)S(1)}, f32[72,128]{1,0:T(8,128)S(1)}, u32[]{:S(2)}, u32[]{:S(2)}) collective-permute-start(f32[72,128]{1,0:T(8,128)S(1)} %add_add_fusion.near), channel_id=1, source_target_pairs={{0,3},{1,2},{2,1},{3,0},{4,7},{5,6},{6,5},{7,4},{8,11},{9,10},{10,... | collective-permute-start | bytes 110600 | tf_op jit(solution)/shard_map/ppermute | solution.py:30
  82.9 1.3 %collective-permute-start.20 = (f32[72,128]{1,0:T(8,128)S(1)}, f32[72,128]{1,0:T(8,128)S(1)}, u32[]{:S(2)}, u32[]{:S(2)}) collective-permute-start(f32[72,128]{1,0:T(8,128)S(1)} %add_add_fusion.near), channel_id=1, source_target_pairs={{0,2},{1,3},{2,0},{3,1},{4,6},{5,7},{6,4},{7,5},{8,10},{9,11},{10,... | collective-permute-start | bytes 110600 | tf_op jit(solution)/shard_map/ppermute | solution.py:30
  84.1 0.0 collective-permute-start.19
  84.1 0.4 collective-permute-done.21.both_in
  84.5 1.8 %collective-permute-done.20.z_in = f32[72,128]{1,0:T(8,128)S(1)} collective-permute-done((f32[72,128]{1,0:T(8,128)S(1)}, f32[72,128]{1,0:T(8,128)S(1)}, u32[]{:S(2)}, u32[]{:S(2)}) %collective-permute-start.20) | collective-permute-done | bytes 36896 | tf_op jit(solution)/shard_map/ppermute | solution.py:30
  86.3 0.0 collective-permute-done.19.core_in
  86.3 1.2 %last_kernel.1 = (f32[24,512]{1,0:T(8,128)}, f32[8,512]{1,0:T(8,128)}, f32[2,8]{1,0:T(2,128)}) custom-call(s32[5]{0:T(128)S(1)} %stack.59.spot, f32[72,128]{1,0:T(8,128)S(1)} %add_add_fusion.near, f32[72,128]{1,0:T(8,128)S(1)} %collective-permute-done.19.core_in, f32[72,128]{1,0:T(8,128)S(1)} %collective-permute-done.20.z_in, ...), custom_call_target="tpu_custom_call" | custom-call | tf_op jit(solution)/shard_map/last_kernel/pallas_call | solution.py:337
  (14 shorter events, 0.1 us)
Async XLA Ops:
  0.6 23.4 %copy-start = (bf16[512,1536]{1,0:T(8,128)(2,1)S(1)}, bf16[512,1536]{1,0:T(8,128)(2,1)}, u32[]{:S(2)}) copy-start(bf16[512,1536]{1,0:T(8,128)(2,1)} %w_qkv.7) | copy-start | bytes 4718596
  0.6 23.4 %copy-start.5 = (f32[2,512]{1,0:T(2,128)S(1)}, f32[2,512]{1,0:T(2,128)}, u32[]{:S(2)}) copy-start(f32[2,512]{1,0:T(2,128)} %norm.5) | copy-start | bytes 12292
  1.9 10.6 %collective-permute-start = (bf16[2,4,8,512]{3,2,1,0:T(8,128)(2,1)S(1)}, bf16[2,4,8,512]{3,2,1,0:T(8,128)(2,1)S(1)}, u32[]{:S(2)}, u32[]{:S(2)}) collective-permute-start(bf16[2,4,8,512]{3,2,1,0:T(8,128)(2,1)S(1)} %get-tuple-element.82), channel_id=1, source_target_pairs={{0,3},{1,0},{2,1},{3,2},{4,7},{5,4},{6,5},{7,6},{8,11},{9,8},{10,9... | collective-permute-start | bytes 196616 | tf_op jit(solution)/shard_map/ppermute | solution.py:30
  5.3 11.8 %collective-permute-start.4 = (bf16[2,4,8,512]{3,2,1,0:T(8,128)(2,1)S(1)}, bf16[2,4,8,512]{3,2,1,0:T(8,128)(2,1)S(1)}, u32[]{:S(2)}, u32[]{:S(2)}) collective-permute-start(bf16[2,4,8,512]{3,2,1,0:T(8,128)(2,1)S(1)} %get-tuple-element.79), channel_id=1, source_target_pairs={{0,240},{1,241},{2,242},{3,243},{4,244},{5,245},{6,246},{7,247},{8... | collective-permute-start | bytes 196616 | tf_op jit(solution)/shard_map/ppermute | solution.py:30
  12.1 7.6 %collective-permute-start.5 = (bf16[2,4,8,512]{3,2,1,0:T(8,128)(2,1)S(1)}, bf16[2,4,8,512]{3,2,1,0:T(8,128)(2,1)S(1)}, u32[]{:S(2)}, u32[]{:S(2)}) collective-permute-start(bf16[2,4,8,512]{3,2,1,0:T(8,128)(2,1)S(1)} %get-tuple-element.80), channel_id=1, source_target_pairs={{0,243},{1,240},{2,241},{3,242},{4,247},{5,244},{6,245},{7,246},{8... | collective-permute-start | bytes 196616 | tf_op jit(solution)/shard_map/ppermute | solution.py:30
  12.6 10.8 %collective-permute-start.3 = (bf16[2,64,512]{2,1,0:T(8,128)(2,1)S(1)}, bf16[2,64,512]{2,1,0:T(8,128)(2,1)S(1)}, u32[]{:S(2)}, u32[]{:S(2)}) collective-permute-start(bf16[2,64,512]{2,1,0:T(8,128)(2,1)S(1)} %bitcast.62), channel_id=1, source_target_pairs={{0,8},{1,9},{2,10},{3,11},{4,12},{5,13},{6,14},{7,15},{8,0},{9,1},... | collective-permute-start | bytes 393224 | tf_op jit(solution)/shard_map/ppermute | solution.py:30
  15.4 8.6 %collective-permute-start.2 = (bf16[2,64,512]{2,1,0:T(8,128)(2,1)S(1)}, bf16[2,64,512]{2,1,0:T(8,128)(2,1)S(1)}, u32[]{:S(2)}, u32[]{:S(2)}) collective-permute-start(bf16[2,64,512]{2,1,0:T(8,128)(2,1)S(1)} %bitcast.63), channel_id=1, source_target_pairs={{0,12},{1,13},{2,14},{3,15},{4,0},{5,1},{6,2},{7,3},{8,4},{9,5},{1... | collective-permute-start | bytes 393224 | tf_op jit(solution)/shard_map/ppermute | solution.py:30
  16.3 7.8 %collective-permute-start.1 = (bf16[2,64,512]{2,1,0:T(8,128)(2,1)S(1)}, bf16[2,64,512]{2,1,0:T(8,128)(2,1)S(1)}, u32[]{:S(2)}, u32[]{:S(2)}) collective-permute-start(bf16[2,64,512]{2,1,0:T(8,128)(2,1)S(1)} %bitcast.64), channel_id=1, source_target_pairs={{0,4},{1,5},{2,6},{3,7},{4,8},{5,9},{6,10},{7,11},{8,12},{9,13},{1... | collective-permute-start | bytes 393224 | tf_op jit(solution)/shard_map/ppermute | solution.py:30
  19.7 6.5 %collective-permute-start.8 = (bf16[2,64,512]{2,1,0:T(8,128)(2,1)S(1)}, bf16[2,64,512]{2,1,0:T(8,128)(2,1)S(1)}, u32[]{:S(2)}, u32[]{:S(2)}) collective-permute-start(bf16[2,64,512]{2,1,0:T(8,128)(2,1)S(1)} %bitcast.69), channel_id=1, source_target_pairs={{0,8},{1,9},{2,10},{3,11},{4,12},{5,13},{6,14},{7,15},{8,0},{9,1},... | collective-permute-start | bytes 393224 | tf_op jit(solution)/shard_map/ppermute | solution.py:30
  22.5 4.1 %collective-permute-start.7 = (bf16[2,64,512]{2,1,0:T(8,128)(2,1)S(1)}, bf16[2,64,512]{2,1,0:T(8,128)(2,1)S(1)}, u32[]{:S(2)}, u32[]{:S(2)}) collective-permute-start(bf16[2,64,512]{2,1,0:T(8,128)(2,1)S(1)} %bitcast.70), channel_id=1, source_target_pairs={{0,12},{1,13},{2,14},{3,15},{4,0},{5,1},{6,2},{7,3},{8,4},{9,5},{1... | collective-permute-start | bytes 393224 | tf_op jit(solution)/shard_map/ppermute | solution.py:30
  23.4 6.3 %collective-permute-start.6 = (bf16[2,64,512]{2,1,0:T(8,128)(2,1)S(1)}, bf16[2,64,512]{2,1,0:T(8,128)(2,1)S(1)}, u32[]{:S(2)}, u32[]{:S(2)}) collective-permute-start(bf16[2,64,512]{2,1,0:T(8,128)(2,1)S(1)} %bitcast.71), channel_id=1, source_target_pairs={{0,4},{1,5},{2,6},{3,7},{4,8},{5,9},{6,10},{7,11},{8,12},{9,13},{1... | collective-permute-start | bytes 393224 | tf_op jit(solution)/shard_map/ppermute | solution.py:30
  24.0 1.0 %copy-start.3 = (bf16[512,512]{1,0:T(8,128)(2,1)S(1)}, bf16[512,512]{1,0:T(8,128)(2,1)}, u32[]{:S(2)}) copy-start(bf16[512,512]{1,0:T(8,128)(2,1)} %w_proj.5) | copy-start | bytes 1572868
  36.4 5.3 %collective-permute-start.9 = (bf16[128,512]{1,0:T(8,128)(2,1)S(1)}, bf16[128,512]{1,0:T(8,128)(2,1)S(1)}, u32[]{:S(2)}, u32[]{:S(2)}) collective-permute-start(bf16[128,512]{1,0:T(8,128)(2,1)S(1)} %get-tuple-element.47.r2), channel_id=1, source_target_pairs={{0,4},{1,5},{2,6},{3,7},{4,8},{5,9},{6,10},{7,11},{8,12},{9,13},{1... | collective-permute-start | bytes 393224 | tf_op jit(solution)/shard_map/ppermute | solution.py:30
  36.6 6.0 %collective-permute-start.10 = (bf16[128,512]{1,0:T(8,128)(2,1)S(1)}, bf16[128,512]{1,0:T(8,128)(2,1)S(1)}, u32[]{:S(2)}, u32[]{:S(2)}) collective-permute-start(bf16[128,512]{1,0:T(8,128)(2,1)S(1)} %get-tuple-element.48.r1), channel_id=1, source_target_pairs={{0,12},{1,13},{2,14},{3,15},{4,0},{5,1},{6,2},{7,3},{8,4},{9,5},{1... | collective-permute-start | bytes 393224 | tf_op jit(solution)/shard_map/ppermute | solution.py:30
  39.3 5.8 %collective-permute-start.11 = (bf16[128,512]{1,0:T(8,128)(2,1)S(1)}, bf16[128,512]{1,0:T(8,128)(2,1)S(1)}, u32[]{:S(2)}, u32[]{:S(2)}) collective-permute-start(bf16[128,512]{1,0:T(8,128)(2,1)S(1)} %get-tuple-element.55.r3), channel_id=1, source_target_pairs={{0,8},{1,9},{2,10},{3,11},{4,12},{5,13},{6,14},{7,15},{8,0},{9,1},... | collective-permute-start | bytes 393224 | tf_op jit(solution)/shard_map/ppermute | solution.py:30
  39.3 10.0 %copy-start.4 = (bf16[512,512]{1,0:T(8,128)(2,1)S(1)}, bf16[512,512]{1,0:T(8,128)(2,1)}, u32[]{:S(2)}) copy-start(bf16[512,512]{1,0:T(8,128)(2,1)} %w_proj.5) | copy-start | bytes 1572868
  45.1 7.0 %collective-permute-start.12 = (f32[16,64,128]{2,1,0:T(8,128)S(1)}, f32[16,64,128]{2,1,0:T(8,128)S(1)}, u32[]{:S(2)}, u32[]{:S(2)}) collective-permute-start(f32[16,64,128]{2,1,0:T(8,128)S(1)} %get-tuple-element.50), channel_id=1, source_target_pairs={{0,1},{1,0},{2,3},{3,2},{4,5},{5,4},{6,7},{7,6},{8,9},{9,8},{10,11... | collective-permute-start | bytes 1572872 | tf_op jit(solution)/shard_map/ppermute | solution.py:30
  53.6 21.9 %copy-start.1 = (bf16[1,1,8,16,512]{4,3,2,1,0:T(8,128)(2,1)S(1)}, bf16[1,1,8,16,512]{4,3,2,1,0:T(8,128)(2,1)}, u32[]{:S(2)}) copy-start(bf16[1,1,8,16,512]{4,3,2,1,0:T(8,128)(2,1)} %param.5) | copy-start | bytes 393220
  53.6 21.9 %copy-start.2 = (bf16[1,1,8,16,512]{4,3,2,1,0:T(8,128)(2,1)S(1)}, bf16[1,1,8,16,512]{4,3,2,1,0:T(8,128)(2,1)}, u32[]{:S(2)}) copy-start(bf16[1,1,8,16,512]{4,3,2,1,0:T(8,128)(2,1)} %param.9) | copy-start | bytes 393220
  53.6 15.8 %all-to-all-start = ((f32[16,72,128]{2,1,0:T(8,128)}), f32[16,72,128]{2,1,0:T(8,128)S(1)}, u32[]{:S(2)}, u32[]{:S(2)}) async-start(f32[16,72,128]{2,1,0:T(8,128)} %join_kernel.1), calls=%async_computation | async-start | bytes 1179648 | tf_op jit(solution)/shard_map/all_to_all | solution.py:66
  57.3 17.5 %collective-permute-start.18 = (bf16[2,4,8,512]{3,2,1,0:T(8,128)(2,1)S(1)}, bf16[2,4,8,512]{3,2,1,0:T(8,128)(2,1)S(1)}, u32[]{:S(2)}, u32[]{:S(2)}) collective-permute-start(bf16[2,4,8,512]{3,2,1,0:T(8,128)(2,1)S(1)} %get-tuple-element.75), channel_id=1, source_target_pairs={{0,241},{1,242},{2,243},{3,240},{4,245},{5,246},{6,247},{7,244},{8... | collective-permute-start | bytes 196616 | tf_op jit(solution)/shard_map/ppermute | solution.py:30
  62.2 13.3 %collective-permute-start.17 = (bf16[2,4,8,512]{3,2,1,0:T(8,128)(2,1)S(1)}, bf16[2,4,8,512]{3,2,1,0:T(8,128)(2,1)S(1)}, u32[]{:S(2)}, u32[]{:S(2)}) collective-permute-start(bf16[2,4,8,512]{3,2,1,0:T(8,128)(2,1)S(1)} %get-tuple-element.76), channel_id=1, source_target_pairs={{0,240},{1,241},{2,242},{3,243},{4,244},{5,245},{6,246},{7,247},{8... | collective-permute-start | bytes 196616 | tf_op jit(solution)/shard_map/ppermute | solution.py:30
  64.3 11.2 %collective-permute-start.16 = (bf16[2,4,8,512]{3,2,1,0:T(8,128)(2,1)S(1)}, bf16[2,4,8,512]{3,2,1,0:T(8,128)(2,1)S(1)}, u32[]{:S(2)}, u32[]{:S(2)}) collective-permute-start(bf16[2,4,8,512]{3,2,1,0:T(8,128)(2,1)S(1)} %get-tuple-element.77), channel_id=1, source_target_pairs={{0,1},{1,2},{2,3},{3,0},{4,5},{5,6},{6,7},{7,4},{8,9},{9,10},{10,1... | collective-permute-start | bytes 196616 | tf_op jit(solution)/shard_map/ppermute | solution.py:30
  70.0 6.7 %collective-permute-start.13 = (f32[72,128]{1,0:T(8,128)S(1)}, f32[72,128]{1,0:T(8,128)S(1)}, u32[]{:S(2)}, u32[]{:S(2)}) collective-permute-start(f32[72,128]{1,0:T(8,128)S(1)} %get-tuple-element.58), channel_id=1, source_target_pairs={{0,64},{1,65},{2,66},{3,67},{4,68},{5,69},{6,70},{7,71},{8,72},{9,... | collective-permute-start | bytes 110600 | tf_op jit(solution)/shard_map/ppermute | solution.py:30
  71.6 7.2 %collective-permute-start.14 = (f32[72,128]{1,0:T(8,128)S(1)}, f32[72,128]{1,0:T(8,128)S(1)}, u32[]{:S(2)}, u32[]{:S(2)}) collective-permute-start(f32[72,128]{1,0:T(8,128)S(1)} %get-tuple-element.59), channel_id=1, source_target_pairs={{0,128},{1,129},{2,130},{3,131},{4,132},{5,133},{6,134},{7,135},{8... | collective-permute-start | bytes 110600 | tf_op jit(solution)/shard_map/ppermute | solution.py:30
  74.8 4.2 %collective-permute-start.15 = (f32[72,128]{1,0:T(8,128)S(1)}, f32[72,128]{1,0:T(8,128)S(1)}, u32[]{:S(2)}, u32[]{:S(2)}) collective-permute-start(f32[72,128]{1,0:T(8,128)S(1)} %get-tuple-element.60), channel_id=1, source_target_pairs={{0,192},{1,193},{2,194},{3,195},{4,196},{5,197},{6,198},{7,199},{8... | collective-permute-start | bytes 110600 | tf_op jit(solution)/shard_map/ppermute | solution.py:30
  79.0 5.5 %collective-permute-start.21 = (f32[72,128]{1,0:T(8,128)S(1)}, f32[72,128]{1,0:T(8,128)S(1)}, u32[]{:S(2)}, u32[]{:S(2)}) collective-permute-start(f32[72,128]{1,0:T(8,128)S(1)} %add_add_fusion.near), channel_id=1, source_target_pairs={{0,3},{1,2},{2,1},{3,0},{4,7},{5,6},{6,5},{7,4},{8,11},{9,10},{10,... | collective-permute-start | bytes 110600 | tf_op jit(solution)/shard_map/ppermute | solution.py:30
  82.9 3.5 %collective-permute-start.20 = (f32[72,128]{1,0:T(8,128)S(1)}, f32[72,128]{1,0:T(8,128)S(1)}, u32[]{:S(2)}, u32[]{:S(2)}) collective-permute-start(f32[72,128]{1,0:T(8,128)S(1)} %add_add_fusion.near), channel_id=1, source_target_pairs={{0,2},{1,3},{2,0},{3,1},{4,6},{5,7},{6,4},{7,5},{8,10},{9,11},{10,... | collective-permute-start | bytes 110600 | tf_op jit(solution)/shard_map/ppermute | solution.py:30
  84.1 2.2 %collective-permute-start.19 = (f32[72,128]{1,0:T(8,128)S(1)}, f32[72,128]{1,0:T(8,128)S(1)}, u32[]{:S(2)}, u32[]{:S(2)}) collective-permute-start(f32[72,128]{1,0:T(8,128)S(1)} %add_add_fusion.near), channel_id=1, source_target_pairs={{0,1},{1,0},{2,3},{3,2},{4,5},{5,4},{6,7},{7,6},{8,9},{9,8},{10,11... | collective-permute-start | bytes 110600 | tf_op jit(solution)/shard_map/ppermute | solution.py:30

commit v3 on v2

--- a/solution.py
+++ b/solution.py
@@ -191,8 +191,8 @@
 
 
 def gradient_kernel(
-    spot, p0, p1, p2, p3, p4, p5, p6, p7, dt_ref, at_ref, normed0, normed1,
-    keep, send, g_ref, p_ref,
+    spot, p0, p1, p2, p3, p4, p5, p6, p7, r0, r1, r2, r3, dt_ref, at_ref, normed0, normed1, w_qkv,
+    keep, send, g_ref, p_ref, n_ref,
 ):
     x, core = spot[0], spot[2]
     parts = (p0, p1, p2, p3, p4, p5, p6, p7)
@@ -200,6 +200,16 @@
     normed = jnp.concatenate([normed0[...], normed1[...]], 0)
     g_ref[...] = dot(d_high, normed) + dot(d_low, normed)
     p_ref[...] = dot(at_ref[...], jnp.concatenate([part[1] for part in parts], 0)).T
+    columns = own_columns(w_qkv, x)
+    gain_row = jnp.zeros((1, C), F32)
+    offset_row = jnp.zeros((1, C), F32)
+    for member, r_ref in enumerate((r0, r1, r2, r3)):
+        rows = jnp.concatenate([parts[member][0], parts[4 + member][0]], 0)
+        d_normed = dot_nt(r_ref[:, : 3 * OWN], columns)
+        gain_row += jnp.sum(d_normed * unit_of(rows)[0], 0, keepdims=True)
+        offset_row += jnp.sum(d_normed, 0, keepdims=True)
+    row = lax.broadcasted_iota(jnp.int32, (128, C), 0)
+    n_ref[...] = jnp.where(row == 0, gain_row, jnp.where(row == 1, offset_row, 0.0)).T
     for ahead, out in ((0, keep), (1, send)):
         to_core = core if ahead == 0 else 1 - core
         for member in range(16):
@@ -218,31 +228,10 @@
                 out[member, top : top + 8, 64 * (z % 2) : 64 * (z % 2) + 64] = jnp.where(
                     to_core == 0, piece[:, :64], piece[:, 64:]
                 )
-
-
-def norm_kernel(
-    spot, p0, p1, p2, p3, p4, p5, p6, p7, r0, r1, r2, r3, w_qkv, out, n_ref
-):
-    parts = (p0, p1, p2, p3, p4, p5, p6, p7)
-    columns = own_columns(w_qkv, spot[0])
-    gain_row = jnp.zeros((1, C), F32)
-    offset_row = jnp.zeros((1, C), F32)
-    for member, r_ref in enumerate((r0, r1, r2, r3)):
-        rows = jnp.concatenate([parts[member][0], parts[4 + member][0]], 0)
-        d_normed = dot_nt(r_ref[:, : 3 * OWN], columns)
-        gain_row += jnp.sum(d_normed * unit_of(rows)[0], 0, keepdims=True)
-        offset_row += jnp.sum(d_normed, 0, keepdims=True)
-    row = lax.broadcasted_iota(jnp.int32, (128, C), 0)
-    n_ref[...] = jnp.where(row == 0, gain_row, jnp.where(row == 1, offset_row, 0.0)).T
-    for member in range(16):
-        for z in range(4):
-            rows = slice(128 * z + 8 * member, 128 * z + 8 * member + 8)
-            out[member, :, 32 * z : 32 * z + 32] = n_ref[rows, :32]
-
-
-def join_kernel(spot, keep, received, norms, out):
-    out[:, :64, :] = keep[...] + received[...]
-    out[:, 64:, :] = norms[...]
+                if ahead == 0:
+                    out[member, 64:, 32 * z : 32 * z + 32] = n_ref[rows, :32]
+            if ahead == 1:
+                out[member, 64:, :] = jnp.zeros((8, 128), F32)
 
 
 def z_parts_kernel(spot, pieces, *outs):
@@ -311,18 +300,21 @@
             out[start : start + 4] = jnp.concatenate([first, second], 1).astype(BF16)
 
 
-def token_kernel(spot, own0, own1, r0, r1, r2, r3, w_qkv, w_proj, norm, out):
+def token_kernel(
+    spot, r0, r1, r2, r3, own0, own1, w_qkv, w_proj, norm, out
+):
     x = spot[0]
     projected = jnp.zeros((SLAB, C), F32)
     d_normed = jnp.zeros((SLAB, C), F32)
     for r_ref, steps in ((r0, 0), (r1, 3), (r2, 1), (r3, 2)):
+        rows = r_ref[...]
         member = lax.rem(x + steps, 4)
         start = pl.multiple_of(OWN * member, OWN)
-        projected += dot(r_ref[:, 3 * OWN :], w_proj[pl.ds(start, OWN), :])
+        projected += dot(rows[:, 3 * OWN :], w_proj[pl.ds(start, OWN), :])
         for third in range(3):
             lanes = slice(third * OWN, (third + 1) * OWN)
             columns = w_qkv[:, pl.ds(pl.multiple_of(start + C * third, OWN), OWN)]
-            d_normed += dot_nt(r_ref[:, lanes], columns)
+            d_normed += dot_nt(rows[:, lanes], columns)
     out[0] = projected.astype(BF16)
     unit, inv_scale = unit_of(jnp.concatenate([own0[0], own1[0]], 0))
     d_unit = d_normed * norm[0:1, :]
@@ -331,13 +323,13 @@
     out[1] = (inv_scale * (d_unit - first_mean - unit * second_mean)).astype(BF16)
 
 
-def call(kernel, scalars, arrays, outs, scratch=(), flops=0, moved=0, fetched=0):
+def call(kernel, scalars, arrays, outs, scratch=(), flops=0, moved=0):
     smem = pl.BlockSpec(memory_space=pltpu.SMEM)
     vmem = pl.BlockSpec(memory_space=pltpu.VMEM)
     return pl.pallas_call(
         kernel,
         out_shape=[jax.ShapeDtypeStruct(shape, dtype) for shape, dtype in outs],
-        in_specs=[smem] + [pl.BlockSpec()] * fetched + [vmem] * (len(arrays) - fetched),
+        in_specs=[smem] + [vmem] * len(arrays),
         out_specs=[vmem] * len(outs),
         scratch_shapes=list(scratch),
         compiler_params=pltpu.CompilerParams(vmem_limit_bytes=8 * 2**20),
@@ -394,37 +386,29 @@
     keep, send = call(
         gradient_kernel,
         spot,
-        (*parts0, *parts1, d_t, a_t, normed0, normed1),
-        [((16, 64, 128), F32)] * 2,
-        scratch=[pltpu.VMEM((3 * OWN, C), F32), pltpu.VMEM((C, OWN), F32)],
+        (*parts0, *parts1, r_own, r_left, r_right, r_far, d_t, a_t, normed0, normed1, w_qkv),
+        [((16, 72, 128), F32)] * 2,
+        scratch=[
+            pltpu.VMEM((3 * OWN, C), F32),
+            pltpu.VMEM((C, OWN), F32),
+            pltpu.VMEM((C, 128), F32),
+        ],
         flops=20_000_000_000,
         moved=6_000_000,
     )
-    send, from_left, from_right, from_far = lax.optimization_barrier(
-        (send, from_left, from_right, from_far)
-    )
-    received = move(send, other_core)
+    halves = keep + move(send, other_core)
+    halves, from_left, from_right, from_far = lax.optimization_barrier(
+        (halves, from_left, from_right, from_far)
+    )
+    plane = exchange(halves, plane_groups())
     (back,) = call(
         token_kernel,
         spot,
-        (part0, part1, r_own, from_left, from_right, from_far, w_qkv, w_proj, norm_params),
+        (r_own, from_left, from_right, from_far, part0, part1, w_qkv, w_proj, norm_params),
         [((2, SLAB, C), BF16)],
         flops=500_000_000,
         moved=4_000_000,
     )
-    back, r_far = lax.optimization_barrier((back, r_far))
-    (norms,) = call(
-        norm_kernel,
-        spot,
-        (*parts0, *parts1, r_own, r_left, r_right, r_far, w_qkv),
-        [((16, 8, 128), F32)],
-        scratch=[pltpu.VMEM((C, 128), F32)],
-        flops=1_000_000_000,
-        moved=2_000_000,
-    )
-    (halves,) = call(join_kernel, spot, (keep, received, norms), [((16, 72, 128), F32)])
-    halves, back = lax.optimization_barrier((halves, back))
-    plane = exchange(halves, plane_groups())
     back = back.reshape(2, 4, 4, 8, C)
     lower = move(back[:, 1], lambda p, n: (p, n + 1))
     other_upper = move(back[:, 2], lambda p, n: (partner_of(p), n))
@@ -436,7 +420,6 @@
         spot,
         (own_inputs, own_upstream, back[:, 0], lower, other_upper, other_lower),
         [((8, 16, C), BF16)] * 2,
-        fetched=2,
     )
     line = [z_parts[0]] + [move(z_parts[steps], along_z(steps)) for steps in (1, 2, 3)]
     line[1], line[2], line[3], output, grad_inputs = lax.optimization_barrier(

time: 87.8 us -> 85.1 us (0.969)
  local copies, waits for them, and re-layouts: 1.19 us -> 3.69 us
  Pallas kernels: 16.8 us -> 14.5 us
  waiting for transfers between devices: 19.2 us -> 17.2 us
  starting transfers between devices: 48.2 us -> 46.4 us
  other arithmetic: 1.32 us -> 2.2 us
    all_to_all x1, waiting for transfers between devices: 4.41 us -> 0.01 us  [exchange(): lax.all_to_all(value, ('wide', 'narrow'), 0, 0, axis_index_groups=groups)]
    unnamed x12 -> x20, local copies, waits for them, and re-layouts: 1.06 us -> 3.56 us
    ppermute x22, waiting for transfers between devices: 14.8 us -> 17.2 us  [move(): return lax.ppermute(value, ('wide', 'narrow'), pairs)]
    pallas_call x9 -> x7, Pallas kernels: 16.8 us -> 14.5 us  [call(): pl.pallas_call(kernel, out_shape=[jax.ShapeDtypeStruct(shape, dtype) for...]
    ppermute x22, starting transfers between devices: 44.5 us -> 42.8 us  [move(): return lax.ppermute(value, ('wide', 'narrow'), pairs)]
    add x0 -> x1, other arithmetic: none -> 0.88 us  [on_device(): halves = keep + move(send, other_core)]
  transfers between devices with their start and end apart: 23 -> 23, of which waited for: 11 -> 9; matrix products, arithmetic and copies ran while one was open for 0% -> 1% of each run, Pallas kernels for 8% -> 5%
where the time goes in v3:
time: 85.1 us; the launch traced here: 84.8 us
  starting transfers between devices  46.4 us (55%)
  waiting for transfers between devices  17.2 us (20%)
  Pallas kernels  14.5 us (17%)
  local copies, waits for them, and re-layouts  3.69 us (4%)
  other arithmetic  2.2 us (3%)
  between operations  0.88 us (1%)
    ppermute x22, starting transfers between devices, move(): return lax.ppermute(value, ('wide', 'narrow'), pairs)  42.8 us
    ppermute x22, waiting for transfers between devices, move(): return lax.ppermute(value, ('wide', 'narrow'), pairs)  17.2 us
    pallas_call x7, Pallas kernels, call(): pl.pallas_call(kernel, out_shape=[jax.ShapeDtypeStruct(shape, dtype) for...  14.5 us
    all_to_all x1, starting transfers between devices, exchange(): lax.all_to_all(value, ('wide', 'narrow'), 0, 0, axis_index_groups=groups)  3.58 us
    unnamed x20, local copies, waits for them, and re-layouts  3.56 us
  transfers between devices with their start and end apart: 23, of which 9 were waited for; matrix products, arithmetic and copies ran while one was open for 1% of the time, Pallas kernels for 5%

profile of v3, /device:TPU:1, one launch (start us, length us, event | category | flops | bytes accessed | tf_op | source)
XLA Modules:
  0.0 84.8 jit_solution(2509085371896370987)
XLA Ops:
  0.7 1.2 %broadcast_select_fusion = (bf16[2,8,8,512]{3,2,1,0:T(8,128)(2,1)S(1)}, bf16[2,8,8,512]{3,2,1,0:T(8,128)(2,1)S(1)}) fusion(pred[8]{0:T(512)(128)(4,1)S(1)} %compare_compare_fusion, bf16[1,8,2,8,512]{4,3,2,1,0:T(8,128)(2,1)} %bitcast.60, bf16[1,8,2,8,512]{4,3,2,1,0:T(8,128)(2,1)} %bitcast.58), kind=kLoop, calls=%fused_computation.8 | loop fusion | flops 327680 | bytes 524296 | tf_op jit(solution)/shard_map/jit(_where)/select_n | solution.py:355
  1.9 3.3 %collective-permute-start = (bf16[2,4,8,512]{3,2,1,0:T(8,128)(2,1)S(1)}, bf16[2,4,8,512]{3,2,1,0:T(8,128)(2,1)S(1)}, u32[]{:S(2)}, u32[]{:S(2)}) collective-permute-start(bf16[2,4,8,512]{3,2,1,0:T(8,128)(2,1)S(1)} %get-tuple-element.74), channel_id=1, source_target_pairs={{0,3},{1,0},{2,1},{3,2},{4,7},{5,4},{6,5},{7,6},{8,11},{9,8},{10,9... | collective-permute-start | bytes 196616 | tf_op jit(solution)/shard_map/ppermute | solution.py:30
  5.3 6.8 %collective-permute-start.4 = (bf16[2,4,8,512]{3,2,1,0:T(8,128)(2,1)S(1)}, bf16[2,4,8,512]{3,2,1,0:T(8,128)(2,1)S(1)}, u32[]{:S(2)}, u32[]{:S(2)}) collective-permute-start(bf16[2,4,8,512]{3,2,1,0:T(8,128)(2,1)S(1)} %get-tuple-element.71), channel_id=1, source_target_pairs={{0,240},{1,241},{2,242},{3,243},{4,244},{5,245},{6,246},{7,247},{8... | collective-permute-start | bytes 196616 | tf_op jit(solution)/shard_map/ppermute | solution.py:30
  12.1 0.4 collective-permute-start.5
  12.5 0.0 collective-permute-done
  12.6 2.8 %collective-permute-start.3 = (bf16[2,64,512]{2,1,0:T(8,128)(2,1)S(1)}, bf16[2,64,512]{2,1,0:T(8,128)(2,1)S(1)}, u32[]{:S(2)}, u32[]{:S(2)}) collective-permute-start(bf16[2,64,512]{2,1,0:T(8,128)(2,1)S(1)} %bitcast.62), channel_id=1, source_target_pairs={{0,8},{1,9},{2,10},{3,11},{4,12},{5,13},{6,14},{7,15},{8,0},{9,1},... | collective-permute-start | bytes 393224 | tf_op jit(solution)/shard_map/ppermute | solution.py:30
  15.4 0.9 %collective-permute-start.2 = (bf16[2,64,512]{2,1,0:T(8,128)(2,1)S(1)}, bf16[2,64,512]{2,1,0:T(8,128)(2,1)S(1)}, u32[]{:S(2)}, u32[]{:S(2)}) collective-permute-start(bf16[2,64,512]{2,1,0:T(8,128)(2,1)S(1)} %bitcast.63), channel_id=1, source_target_pairs={{0,12},{1,13},{2,14},{3,15},{4,0},{5,1},{6,2},{7,3},{8,4},{9,5},{1... | collective-permute-start | bytes 393224 | tf_op jit(solution)/shard_map/ppermute | solution.py:30
  16.3 0.6 collective-permute-start.1
  16.9 0.1 pad_add_fusion.flags
  16.9 0.1 stack.59.spot
  17.0 0.0 collective-permute-done.4
  17.0 2.7 %collective-permute-done.5 = bf16[2,4,8,512]{3,2,1,0:T(8,128)(2,1)S(1)} collective-permute-done((bf16[2,4,8,512]{3,2,1,0:T(8,128)(2,1)S(1)}, bf16[2,4,8,512]{3,2,1,0:T(8,128)(2,1)S(1)}, u32[]{:S(2)}, u32[]{:S(2)}) %collective-permute-start.5) | collective-permute-done | bytes 65568 | tf_op jit(solution)/shard_map/ppermute | solution.py:30
  19.7 2.8 %collective-permute-start.8 = (bf16[2,64,512]{2,1,0:T(8,128)(2,1)S(1)}, bf16[2,64,512]{2,1,0:T(8,128)(2,1)S(1)}, u32[]{:S(2)}, u32[]{:S(2)}) collective-permute-start(bf16[2,64,512]{2,1,0:T(8,128)(2,1)S(1)} %bitcast.68), channel_id=1, source_target_pairs={{0,8},{1,9},{2,10},{3,11},{4,12},{5,13},{6,14},{7,15},{8,0},{9,1},... | collective-permute-start | bytes 393224 | tf_op jit(solution)/shard_map/ppermute | solution.py:30
  22.5 0.9 %collective-permute-start.7 = (bf16[2,64,512]{2,1,0:T(8,128)(2,1)S(1)}, bf16[2,64,512]{2,1,0:T(8,128)(2,1)S(1)}, u32[]{:S(2)}, u32[]{:S(2)}) collective-permute-start(bf16[2,64,512]{2,1,0:T(8,128)(2,1)S(1)} %bitcast.69), channel_id=1, source_target_pairs={{0,12},{1,13},{2,14},{3,15},{4,0},{5,1},{6,2},{7,3},{8,4},{9,5},{1... | collective-permute-start | bytes 393224 | tf_op jit(solution)/shard_map/ppermute | solution.py:30
  23.4 0.0 collective-permute-done.3.p3
  23.4 0.6 collective-permute-start.6
  24.0 0.0 collective-permute-done.2.p2
  24.0 0.0 collective-permute-done.1.p1
  24.0 0.0 copy-start.3
  24.0 1.0 %copy-done.3 = bf16[512,512]{1,0:T(8,128)(2,1)S(1)} copy-done((bf16[512,512]{1,0:T(8,128)(2,1)S(1)}, bf16[512,512]{1,0:T(8,128)(2,1)}, u32[]{:S(2)}) %copy-start.3) | copy-done | bytes 524312
  25.1 1.1 %first_kernel.1 = (bf16[256,512]{1,0:T(8,128)(2,1)S(1)}, bf16[256,384]{1,0:T(8,128)(2,1)S(1)}, bf16[256,128]{1,0:T(8,128)(2,1)S(1)}) custom-call(s32[4]{0:T(128)S(1)} %pad_add_fusion.flags, bf16[2,64,512]{2,1,0:T(8,128)(2,1)S(1)} %bitcast.65, bf16[2,64,512]{2,1,0:T(8,128)(2,1)S(1)} %collective-permute-done.1.p1, ...), custom_call_target="tpu_custom_call" | custom-call | flops 10000000000 | bytes 3000000 | tf_op jit(solution)/shard_map/first_kernel/pallas_call | solution.py:329
  26.2 0.0 collective-permute-done.8.p3.p7
  26.2 0.4 collective-permute-done.7.p2.p6
  26.6 3.0 %collective-permute-done.6.p1.p5 = bf16[2,64,512]{2,1,0:T(8,128)(2,1)S(1)} collective-permute-done((bf16[2,64,512]{2,1,0:T(8,128)(2,1)S(1)}, bf16[2,64,512]{2,1,0:T(8,128)(2,1)S(1)}, u32[]{:S(2)}, u32[]{:S(2)}) %collective-permute-start.6) | collective-permute-done | bytes 131104 | tf_op jit(solution)/shard_map/ppermute | solution.py:30
  29.7 6.7 %attention_kernel.1 = (bf16[128,512]{1,0:T(8,128)(2,1)S(1)}, bf16[128,512]{1,0:T(8,128)(2,1)S(1)}, bf16[128,512]{1,0:T(8,128)(2,1)S(1)}, bf16[128,512]{1,0:T(8,1...) custom-call(s32[4]{0:T(128)S(1)} %pad_add_fusion.flags, ...), custom_call_target="tpu_custom_call" | custom-call | flops 1200000000 | bytes 6000000 | tf_op jit(solution)/shard_map/attention_kernel/pallas_call | solution.py:329
  36.4 2.1 %gradient_kernel.1 = (f32[16,72,128]{2,1,0:T(8,128)S(1)}, f32[16,72,128]{2,1,0:T(8,128)S(1)}) custom-call(s32[5]{0:T(128)S(1)} %stack.59.spot, bf16[2,64,512]{2,1,0:T(8,128)(2,1)S(1)} %bitcast.66, bf16[2,64,512]{2,1,0:T(8,128)(2,1)S(1)} %collective-permute-done.1.p1, bf16[2,64,512]{2,1,0:T(8,128)(2,1)S(1)} %collective-permute-done.2.p2, ...), custom_call_target="tpu_custom_call" | custom-call | flops 20000000000 | bytes 6000000 | tf_op jit(solution)/shard_map/gradient_kernel/pallas_call | solution.py:329
  38.5 0.0 copy-start.4
  38.5 3.1 %collective-permute-start.9 = (f32[16,72,128]{2,1,0:T(8,128)S(1)}, f32[16,72,128]{2,1,0:T(8,128)S(1)}, u32[]{:S(2)}, u32[]{:S(2)}) collective-permute-start(f32[16,72,128]{2,1,0:T(8,128)S(1)} %get-tuple-element.46), channel_id=1, source_target_pairs={{0,1},{1,0},{2,3},{3,2},{4,5},{5,4},{6,7},{7,6},{8,9},{9,8},{10,11... | collective-permute-start | bytes 1769480 | tf_op jit(solution)/shard_map/ppermute | solution.py:30
  41.5 0.1 collective-permute-start.11
  41.6 1.4 %collective-permute-start.10 = (bf16[128,512]{1,0:T(8,128)(2,1)S(1)}, bf16[128,512]{1,0:T(8,128)(2,1)S(1)}, u32[]{:S(2)}, u32[]{:S(2)}) collective-permute-start(bf16[128,512]{1,0:T(8,128)(2,1)S(1)} %get-tuple-element.40.r2), channel_id=1, source_target_pairs={{0,4},{1,5},{2,6},{3,7},{4,8},{5,9},{6,10},{7,11},{8,12},{9,13},{1... | collective-permute-start | bytes 393224 | tf_op jit(solution)/shard_map/ppermute | solution.py:30
  43.0 0.3 collective-permute-start.12
  43.3 0.0 collective-permute-done.9
  43.3 0.9 %add.37 = f32[16,72,128]{2,1,0:T(8,128)} add(f32[16,72,128]{2,1,0:T(8,128)S(1)} %get-tuple-element.45, f32[16,72,128]{2,1,0:T(8,128)S(1)} %collective-permute-done.9) | non-fusion elementwise | flops 147456 | bytes 1769472 | tf_op jit(solution)/shard_map/add | solution.py:399
  44.2 2.4 %collective-permute-done.11.r2 = bf16[128,512]{1,0:T(8,128)(2,1)S(1)} collective-permute-done((bf16[128,512]{1,0:T(8,128)(2,1)S(1)}, bf16[128,512]{1,0:T(8,128)(2,1)S(1)}, u32[]{:S(2)}, u32[]{:S(2)}) %collective-permute-start.11) | collective-permute-done | bytes 131104 | tf_op jit(solution)/shard_map/ppermute | solution.py:30
  46.6 3.8 %collective-permute-done.10.r1 = bf16[128,512]{1,0:T(8,128)(2,1)S(1)} collective-permute-done((bf16[128,512]{1,0:T(8,128)(2,1)S(1)}, bf16[128,512]{1,0:T(8,128)(2,1)S(1)}, u32[]{:S(2)}, u32[]{:S(2)}) %collective-permute-start.10) | collective-permute-done | bytes 131104 | tf_op jit(solution)/shard_map/ppermute | solution.py:30
  50.4 0.0 collective-permute-done.12.r3
  50.4 0.6 copy-done.5
  51.0 0.0 copy-done.7
  51.1 3.6 %all-to-all-start = ((f32[16,72,128]{2,1,0:T(8,128)}), f32[16,72,128]{2,1,0:T(8,128)S(1)}, u32[]{:S(2)}, u32[]{:S(2)}) async-start(f32[16,72,128]{2,1,0:T(8,128)} %add.37), calls=%async_computation | async-start | bytes 1179648 | tf_op jit(solution)/shard_map/all_to_all | solution.py:66
  54.7 0.0 copy-start.6
  54.7 0.9 %copy-done.6 = bf16[128,512]{1,0:T(8,128)(2,1)S(1)} copy-done((bf16[128,512]{1,0:T(8,128)(2,1)S(1)}, bf16[128,512]{1,0:T(8,128)(2,1)}, u32[]{:S(2)}) %copy-start.6) | copy-done | bytes 131096
  55.6 0.9 %copy-done.8 = bf16[128,512]{1,0:T(8,128)(2,1)S(1)} copy-done((bf16[128,512]{1,0:T(8,128)(2,1)S(1)}, bf16[128,512]{1,0:T(8,128)(2,1)}, u32[]{:S(2)}) %copy-start.8) | copy-done | bytes 131096
  56.5 1.4 %token_kernel.1 = bf16[2,128,512]{2,1,0:T(8,128)(2,1)S(1)} custom-call(s32[5]{0:T(128)S(1)} %stack.59.spot, bf16[128,512]{1,0:T(8,128)(2,1)S(1)} %get-tuple-element.38.r0, bf16[128,512]{1,0:T(8,128)(2,1)S(1)} %copy-done.6, bf16[128,512]{1,0:T(8,128)(2,1)S(1)} %collective-permute-done.11.r2, bf16[128,512]{1,0:T(8,128)(2,1)S(1)} %copy-done.8, ...), custom_call_target="tpu_custom_call" | custom-call | flops 500000000 | bytes 4000000 | tf_op jit(solution)/shard_map/token_kernel/pallas_call | solution.py:329
  57.9 5.6 %collective-permute-start.18 = (bf16[2,4,8,512]{3,2,1,0:T(8,128)(2,1)S(1)}, bf16[2,4,8,512]{3,2,1,0:T(8,128)(2,1)S(1)}, u32[]{:S(2)}, u32[]{:S(2)}) collective-permute-start(bf16[2,4,8,512]{3,2,1,0:T(8,128)(2,1)S(1)} %get-tuple-element.67), channel_id=1, source_target_pairs={{0,241},{1,242},{2,243},{3,240},{4,245},{5,246},{6,247},{7,244},{8... | collective-permute-start | bytes 196616 | tf_op jit(solution)/shard_map/ppermute | solution.py:30
  63.5 3.6 %collective-permute-start.17 = (bf16[2,4,8,512]{3,2,1,0:T(8,128)(2,1)S(1)}, bf16[2,4,8,512]{3,2,1,0:T(8,128)(2,1)S(1)}, u32[]{:S(2)}, u32[]{:S(2)}) collective-permute-start(bf16[2,4,8,512]{3,2,1,0:T(8,128)(2,1)S(1)} %get-tuple-element.68), channel_id=1, source_target_pairs={{0,240},{1,241},{2,242},{3,243},{4,244},{5,245},{6,246},{7,247},{8... | collective-permute-start | bytes 196616 | tf_op jit(solution)/shard_map/ppermute | solution.py:30
  67.1 0.0 collective-permute-start.16
  67.1 0.0 all-to-all-done.pieces
  67.1 0.7 z_parts_kernel.1
  67.8 0.1 collective-permute-start.13
  67.9 4.0 %collective-permute-start.14 = (f32[72,128]{1,0:T(8,128)S(1)}, f32[72,128]{1,0:T(8,128)S(1)}, u32[]{:S(2)}, u32[]{:S(2)}) collective-permute-start(f32[72,128]{1,0:T(8,128)S(1)} %get-tuple-element.49), channel_id=1, source_target_pairs={{0,128},{1,129},{2,130},{3,131},{4,132},{5,133},{6,134},{7,135},{8... | collective-permute-start | bytes 110600 | tf_op jit(solution)/shard_map/ppermute | solution.py:30
  71.8 0.0 collective-permute-done.18.other_low
  71.8 1.0 %collective-permute-start.15 = (f32[72,128]{1,0:T(8,128)S(1)}, f32[72,128]{1,0:T(8,128)S(1)}, u32[]{:S(2)}, u32[]{:S(2)}) collective-permute-start(f32[72,128]{1,0:T(8,128)S(1)} %get-tuple-element.50), channel_id=1, source_target_pairs={{0,192},{1,193},{2,194},{3,195},{4,196},{5,197},{6,198},{7,199},{8... | collective-permute-start | bytes 110600 | tf_op jit(solution)/shard_map/ppermute | solution.py:30
  72.8 0.0 collective-permute-done.17.other_high
  72.8 0.0 collective-permute-done.16.mine_low
  72.8 1.3 %merge_kernel.1 = (bf16[8,16,512]{2,1,0:T(8,128)(2,1)}, bf16[8,16,512]{2,1,0:T(8,128)(2,1)}) custom-call(s32[5]{0:T(128)S(1)} %stack.59.spot, bf16[8,16,512]{2,1,0:T(8,128)(2,1)S(1)} %bitcast.59, bf16[8,16,512]{2,1,0:T(8,128)(2,1)S(1)} %bitcast.61, bf16[2,4,8,512]{3,2,1,0:T(8,128)(2,1)S(1)} %get-tuple-element.70.mine_high, ...), custom_call_target="tpu_custom_call" | custom-call | tf_op jit(solution)/shard_map/merge_kernel/pallas_call | solution.py:329
  74.1 0.0 collective-permute-done.13
  74.1 0.8 collective-permute-done.14
  74.9 1.8 %collective-permute-done.15 = f32[72,128]{1,0:T(8,128)S(1)} collective-permute-done((f32[72,128]{1,0:T(8,128)S(1)}, f32[72,128]{1,0:T(8,128)S(1)}, u32[]{:S(2)}, u32[]{:S(2)}) %collective-permute-start.15) | collective-permute-done | bytes 36896 | tf_op jit(solution)/shard_map/ppermute | solution.py:30
  76.8 4.0 %collective-permute-start.21 = (f32[72,128]{1,0:T(8,128)S(1)}, f32[72,128]{1,0:T(8,128)S(1)}, u32[]{:S(2)}, u32[]{:S(2)}) collective-permute-start(f32[72,128]{1,0:T(8,128)S(1)} %add_add_fusion.near), channel_id=1, source_target_pairs={{0,3},{1,2},{2,1},{3,0},{4,7},{5,6},{6,5},{7,4},{8,11},{9,10},{10,... | collective-permute-start | bytes 110600 | tf_op jit(solution)/shard_map/ppermute | solution.py:30
  80.8 0.0 collective-permute-start.20
  80.8 0.5 collective-permute-start.19
  81.3 1.1 %collective-permute-done.21.both_in = f32[72,128]{1,0:T(8,128)S(1)} collective-permute-done((f32[72,128]{1,0:T(8,128)S(1)}, f32[72,128]{1,0:T(8,128)S(1)}, u32[]{:S(2)}, u32[]{:S(2)}) %collective-permute-start.21) | collective-permute-done | bytes 36896 | tf_op jit(solution)/shard_map/ppermute | solution.py:30
  82.4 1.2 %collective-permute-done.20.z_in = f32[72,128]{1,0:T(8,128)S(1)} collective-permute-done((f32[72,128]{1,0:T(8,128)S(1)}, f32[72,128]{1,0:T(8,128)S(1)}, u32[]{:S(2)}, u32[]{:S(2)}) %collective-permute-start.20) | collective-permute-done | bytes 36896 | tf_op jit(solution)/shard_map/ppermute | solution.py:30
  83.6 1.2 %last_kernel.1 = (f32[24,512]{1,0:T(8,128)}, f32[8,512]{1,0:T(8,128)}, f32[2,8]{1,0:T(2,128)}) custom-call(s32[5]{0:T(128)S(1)} %stack.59.spot, f32[72,128]{1,0:T(8,128)S(1)} %add_add_fusion.near, f32[72,128]{1,0:T(8,128)S(1)} %collective-permute-done.19.core_in, f32[72,128]{1,0:T(8,128)S(1)} %collective-permute-done.20.z_in, ...), custom_call_target="tpu_custom_call" | custom-call | tf_op jit(solution)/shard_map/last_kernel/pallas_call | solution.py:329
  (21 shorter events, 0.1 us)
Async XLA Ops:
  0.6 23.4 %copy-start = (bf16[512,1536]{1,0:T(8,128)(2,1)S(1)}, bf16[512,1536]{1,0:T(8,128)(2,1)}, u32[]{:S(2)}) copy-start(bf16[512,1536]{1,0:T(8,128)(2,1)} %w_qkv.7) | copy-start | bytes 4718596
  0.6 23.4 %copy-start.9 = (f32[2,512]{1,0:T(2,128)S(1)}, f32[2,512]{1,0:T(2,128)}, u32[]{:S(2)}) copy-start(f32[2,512]{1,0:T(2,128)} %norm.5) | copy-start | bytes 12292
  1.9 10.6 %collective-permute-start = (bf16[2,4,8,512]{3,2,1,0:T(8,128)(2,1)S(1)}, bf16[2,4,8,512]{3,2,1,0:T(8,128)(2,1)S(1)}, u32[]{:S(2)}, u32[]{:S(2)}) collective-permute-start(bf16[2,4,8,512]{3,2,1,0:T(8,128)(2,1)S(1)} %get-tuple-element.74), channel_id=1, source_target_pairs={{0,3},{1,0},{2,1},{3,2},{4,7},{5,4},{6,5},{7,6},{8,11},{9,8},{10,9... | collective-permute-start | bytes 196616 | tf_op jit(solution)/shard_map/ppermute | solution.py:30
  5.3 11.8 %collective-permute-start.4 = (bf16[2,4,8,512]{3,2,1,0:T(8,128)(2,1)S(1)}, bf16[2,4,8,512]{3,2,1,0:T(8,128)(2,1)S(1)}, u32[]{:S(2)}, u32[]{:S(2)}) collective-permute-start(bf16[2,4,8,512]{3,2,1,0:T(8,128)(2,1)S(1)} %get-tuple-element.71), channel_id=1, source_target_pairs={{0,240},{1,241},{2,242},{3,243},{4,244},{5,245},{6,246},{7,247},{8... | collective-permute-start | bytes 196616 | tf_op jit(solution)/shard_map/ppermute | solution.py:30
  12.1 7.6 %collective-permute-start.5 = (bf16[2,4,8,512]{3,2,1,0:T(8,128)(2,1)S(1)}, bf16[2,4,8,512]{3,2,1,0:T(8,128)(2,1)S(1)}, u32[]{:S(2)}, u32[]{:S(2)}) collective-permute-start(bf16[2,4,8,512]{3,2,1,0:T(8,128)(2,1)S(1)} %get-tuple-element.72), channel_id=1, source_target_pairs={{0,243},{1,240},{2,241},{3,242},{4,247},{5,244},{6,245},{7,246},{8... | collective-permute-start | bytes 196616 | tf_op jit(solution)/shard_map/ppermute | solution.py:30
  12.6 10.8 %collective-permute-start.3 = (bf16[2,64,512]{2,1,0:T(8,128)(2,1)S(1)}, bf16[2,64,512]{2,1,0:T(8,128)(2,1)S(1)}, u32[]{:S(2)}, u32[]{:S(2)}) collective-permute-start(bf16[2,64,512]{2,1,0:T(8,128)(2,1)S(1)} %bitcast.62), channel_id=1, source_target_pairs={{0,8},{1,9},{2,10},{3,11},{4,12},{5,13},{6,14},{7,15},{8,0},{9,1},... | collective-permute-start | bytes 393224 | tf_op jit(solution)/shard_map/ppermute | solution.py:30
  15.4 8.6 %collective-permute-start.2 = (bf16[2,64,512]{2,1,0:T(8,128)(2,1)S(1)}, bf16[2,64,512]{2,1,0:T(8,128)(2,1)S(1)}, u32[]{:S(2)}, u32[]{:S(2)}) collective-permute-start(bf16[2,64,512]{2,1,0:T(8,128)(2,1)S(1)} %bitcast.63), channel_id=1, source_target_pairs={{0,12},{1,13},{2,14},{3,15},{4,0},{5,1},{6,2},{7,3},{8,4},{9,5},{1... | collective-permute-start | bytes 393224 | tf_op jit(solution)/shard_map/ppermute | solution.py:30
  16.3 7.8 %collective-permute-start.1 = (bf16[2,64,512]{2,1,0:T(8,128)(2,1)S(1)}, bf16[2,64,512]{2,1,0:T(8,128)(2,1)S(1)}, u32[]{:S(2)}, u32[]{:S(2)}) collective-permute-start(bf16[2,64,512]{2,1,0:T(8,128)(2,1)S(1)} %bitcast.64), channel_id=1, source_target_pairs={{0,4},{1,5},{2,6},{3,7},{4,8},{5,9},{6,10},{7,11},{8,12},{9,13},{1... | collective-permute-start | bytes 393224 | tf_op jit(solution)/shard_map/ppermute | solution.py:30
  19.7 6.5 %collective-permute-start.8 = (bf16[2,64,512]{2,1,0:T(8,128)(2,1)S(1)}, bf16[2,64,512]{2,1,0:T(8,128)(2,1)S(1)}, u32[]{:S(2)}, u32[]{:S(2)}) collective-permute-start(bf16[2,64,512]{2,1,0:T(8,128)(2,1)S(1)} %bitcast.68), channel_id=1, source_target_pairs={{0,8},{1,9},{2,10},{3,11},{4,12},{5,13},{6,14},{7,15},{8,0},{9,1},... | collective-permute-start | bytes 393224 | tf_op jit(solution)/shard_map/ppermute | solution.py:30
  22.5 4.1 %collective-permute-start.7 = (bf16[2,64,512]{2,1,0:T(8,128)(2,1)S(1)}, bf16[2,64,512]{2,1,0:T(8,128)(2,1)S(1)}, u32[]{:S(2)}, u32[]{:S(2)}) collective-permute-start(bf16[2,64,512]{2,1,0:T(8,128)(2,1)S(1)} %bitcast.69), channel_id=1, source_target_pairs={{0,12},{1,13},{2,14},{3,15},{4,0},{5,1},{6,2},{7,3},{8,4},{9,5},{1... | collective-permute-start | bytes 393224 | tf_op jit(solution)/shard_map/ppermute | solution.py:30
  23.4 6.3 %collective-permute-start.6 = (bf16[2,64,512]{2,1,0:T(8,128)(2,1)S(1)}, bf16[2,64,512]{2,1,0:T(8,128)(2,1)S(1)}, u32[]{:S(2)}, u32[]{:S(2)}) collective-permute-start(bf16[2,64,512]{2,1,0:T(8,128)(2,1)S(1)} %bitcast.70), channel_id=1, source_target_pairs={{0,4},{1,5},{2,6},{3,7},{4,8},{5,9},{6,10},{7,11},{8,12},{9,13},{1... | collective-permute-start | bytes 393224 | tf_op jit(solution)/shard_map/ppermute | solution.py:30
  24.0 1.0 %copy-start.3 = (bf16[512,512]{1,0:T(8,128)(2,1)S(1)}, bf16[512,512]{1,0:T(8,128)(2,1)}, u32[]{:S(2)}) copy-start(bf16[512,512]{1,0:T(8,128)(2,1)} %w_proj.5) | copy-start | bytes 1572868
  38.5 16.2 %copy-start.4 = (bf16[512,512]{1,0:T(8,128)(2,1)S(1)}, bf16[512,512]{1,0:T(8,128)(2,1)}, u32[]{:S(2)}) copy-start(bf16[512,512]{1,0:T(8,128)(2,1)} %w_proj.5) | copy-start | bytes 1572868
  38.5 4.9 %collective-permute-start.9 = (f32[16,72,128]{2,1,0:T(8,128)S(1)}, f32[16,72,128]{2,1,0:T(8,128)S(1)}, u32[]{:S(2)}, u32[]{:S(2)}) collective-permute-start(f32[16,72,128]{2,1,0:T(8,128)S(1)} %get-tuple-element.46), channel_id=1, source_target_pairs={{0,1},{1,0},{2,3},{3,2},{4,5},{5,4},{6,7},{7,6},{8,9},{9,8},{10,11... | collective-permute-start | bytes 1769480 | tf_op jit(solution)/shard_map/ppermute | solution.py:30
  41.5 5.1 %collective-permute-start.11 = (bf16[128,512]{1,0:T(8,128)(2,1)S(1)}, bf16[128,512]{1,0:T(8,128)(2,1)S(1)}, u32[]{:S(2)}, u32[]{:S(2)}) collective-permute-start(bf16[128,512]{1,0:T(8,128)(2,1)S(1)} %get-tuple-element.39.r1), channel_id=1, source_target_pairs={{0,12},{1,13},{2,14},{3,15},{4,0},{5,1},{6,2},{7,3},{8,4},{9,5},{1... | collective-permute-start | bytes 393224 | tf_op jit(solution)/shard_map/ppermute | solution.py:30
  41.6 8.7 %collective-permute-start.10 = (bf16[128,512]{1,0:T(8,128)(2,1)S(1)}, bf16[128,512]{1,0:T(8,128)(2,1)S(1)}, u32[]{:S(2)}, u32[]{:S(2)}) collective-permute-start(bf16[128,512]{1,0:T(8,128)(2,1)S(1)} %get-tuple-element.40.r2), channel_id=1, source_target_pairs={{0,4},{1,5},{2,6},{3,7},{4,8},{5,9},{6,10},{7,11},{8,12},{9,13},{1... | collective-permute-start | bytes 393224 | tf_op jit(solution)/shard_map/ppermute | solution.py:30
  43.0 7.3 %collective-permute-start.12 = (bf16[128,512]{1,0:T(8,128)(2,1)S(1)}, bf16[128,512]{1,0:T(8,128)(2,1)S(1)}, u32[]{:S(2)}, u32[]{:S(2)}) collective-permute-start(bf16[128,512]{1,0:T(8,128)(2,1)S(1)} %get-tuple-element.41.r3), channel_id=1, source_target_pairs={{0,8},{1,9},{2,10},{3,11},{4,12},{5,13},{6,14},{7,15},{8,0},{9,1},... | collective-permute-start | bytes 393224 | tf_op jit(solution)/shard_map/ppermute | solution.py:30
  50.4 0.7 copy-start.5
  50.4 0.7 copy-start.7
  51.1 16.0 %all-to-all-start = ((f32[16,72,128]{2,1,0:T(8,128)}), f32[16,72,128]{2,1,0:T(8,128)S(1)}, u32[]{:S(2)}, u32[]{:S(2)}) async-start(f32[16,72,128]{2,1,0:T(8,128)} %add.37), calls=%async_computation | async-start | bytes 1179648 | tf_op jit(solution)/shard_map/all_to_all | solution.py:66
  54.7 0.9 %copy-start.6 = (bf16[128,512]{1,0:T(8,128)(2,1)S(1)}, bf16[128,512]{1,0:T(8,128)(2,1)}, u32[]{:S(2)}) copy-start(bf16[128,512]{1,0:T(8,128)(2,1)} %copy-done.5) | copy-start | bytes 393220
  55.6 0.9 %copy-start.8 = (bf16[128,512]{1,0:T(8,128)(2,1)S(1)}, bf16[128,512]{1,0:T(8,128)(2,1)}, u32[]{:S(2)}) copy-start(bf16[128,512]{1,0:T(8,128)(2,1)} %copy-done.7) | copy-start | bytes 393220
  56.5 16.4 %copy-start.1 = (bf16[1,1,8,16,512]{4,3,2,1,0:T(8,128)(2,1)S(1)}, bf16[1,1,8,16,512]{4,3,2,1,0:T(8,128)(2,1)}, u32[]{:S(2)}) copy-start(bf16[1,1,8,16,512]{4,3,2,1,0:T(8,128)(2,1)} %param.5) | copy-start | bytes 393220
  56.5 16.4 %copy-start.2 = (bf16[1,1,8,16,512]{4,3,2,1,0:T(8,128)(2,1)S(1)}, bf16[1,1,8,16,512]{4,3,2,1,0:T(8,128)(2,1)}, u32[]{:S(2)}) copy-start(bf16[1,1,8,16,512]{4,3,2,1,0:T(8,128)(2,1)} %param.9) | copy-start | bytes 393220
  57.9 14.0 %collective-permute-start.18 = (bf16[2,4,8,512]{3,2,1,0:T(8,128)(2,1)S(1)}, bf16[2,4,8,512]{3,2,1,0:T(8,128)(2,1)S(1)}, u32[]{:S(2)}, u32[]{:S(2)}) collective-permute-start(bf16[2,4,8,512]{3,2,1,0:T(8,128)(2,1)S(1)} %get-tuple-element.67), channel_id=1, source_target_pairs={{0,241},{1,242},{2,243},{3,240},{4,245},{5,246},{6,247},{7,244},{8... | collective-permute-start | bytes 196616 | tf_op jit(solution)/shard_map/ppermute | solution.py:30
  63.5 9.3 %collective-permute-start.17 = (bf16[2,4,8,512]{3,2,1,0:T(8,128)(2,1)S(1)}, bf16[2,4,8,512]{3,2,1,0:T(8,128)(2,1)S(1)}, u32[]{:S(2)}, u32[]{:S(2)}) collective-permute-start(bf16[2,4,8,512]{3,2,1,0:T(8,128)(2,1)S(1)} %get-tuple-element.68), channel_id=1, source_target_pairs={{0,240},{1,241},{2,242},{3,243},{4,244},{5,245},{6,246},{7,247},{8... | collective-permute-start | bytes 196616 | tf_op jit(solution)/shard_map/ppermute | solution.py:30
  67.1 5.7 %collective-permute-start.16 = (bf16[2,4,8,512]{3,2,1,0:T(8,128)(2,1)S(1)}, bf16[2,4,8,512]{3,2,1,0:T(8,128)(2,1)S(1)}, u32[]{:S(2)}, u32[]{:S(2)}) collective-permute-start(bf16[2,4,8,512]{3,2,1,0:T(8,128)(2,1)S(1)} %get-tuple-element.69), channel_id=1, source_target_pairs={{0,1},{1,2},{2,3},{3,0},{4,5},{5,6},{6,7},{7,4},{8,9},{9,10},{10,1... | collective-permute-start | bytes 196616 | tf_op jit(solution)/shard_map/ppermute | solution.py:30
  67.8 6.3 %collective-permute-start.13 = (f32[72,128]{1,0:T(8,128)S(1)}, f32[72,128]{1,0:T(8,128)S(1)}, u32[]{:S(2)}, u32[]{:S(2)}) collective-permute-start(f32[72,128]{1,0:T(8,128)S(1)} %get-tuple-element.48), channel_id=1, source_target_pairs={{0,64},{1,65},{2,66},{3,67},{4,68},{5,69},{6,70},{7,71},{8,72},{9,... | collective-permute-start | bytes 110600 | tf_op jit(solution)/shard_map/ppermute | solution.py:30
  67.9 7.0 %collective-permute-start.14 = (f32[72,128]{1,0:T(8,128)S(1)}, f32[72,128]{1,0:T(8,128)S(1)}, u32[]{:S(2)}, u32[]{:S(2)}) collective-permute-start(f32[72,128]{1,0:T(8,128)S(1)} %get-tuple-element.49), channel_id=1, source_target_pairs={{0,128},{1,129},{2,130},{3,131},{4,132},{5,133},{6,134},{7,135},{8... | collective-permute-start | bytes 110600 | tf_op jit(solution)/shard_map/ppermute | solution.py:30
  71.8 4.9 %collective-permute-start.15 = (f32[72,128]{1,0:T(8,128)S(1)}, f32[72,128]{1,0:T(8,128)S(1)}, u32[]{:S(2)}, u32[]{:S(2)}) collective-permute-start(f32[72,128]{1,0:T(8,128)S(1)} %get-tuple-element.50), channel_id=1, source_target_pairs={{0,192},{1,193},{2,194},{3,195},{4,196},{5,197},{6,198},{7,199},{8... | collective-permute-start | bytes 110600 | tf_op jit(solution)/shard_map/ppermute | solution.py:30
  76.8 5.6 %collective-permute-start.21 = (f32[72,128]{1,0:T(8,128)S(1)}, f32[72,128]{1,0:T(8,128)S(1)}, u32[]{:S(2)}, u32[]{:S(2)}) collective-permute-start(f32[72,128]{1,0:T(8,128)S(1)} %add_add_fusion.near), channel_id=1, source_target_pairs={{0,3},{1,2},{2,1},{3,0},{4,7},{5,6},{6,5},{7,4},{8,11},{9,10},{10,... | collective-permute-start | bytes 110600 | tf_op jit(solution)/shard_map/ppermute | solution.py:30
  80.8 2.8 %collective-permute-start.20 = (f32[72,128]{1,0:T(8,128)S(1)}, f32[72,128]{1,0:T(8,128)S(1)}, u32[]{:S(2)}, u32[]{:S(2)}) collective-permute-start(f32[72,128]{1,0:T(8,128)S(1)} %add_add_fusion.near), channel_id=1, source_target_pairs={{0,2},{1,3},{2,0},{3,1},{4,6},{5,7},{6,4},{7,5},{8,10},{9,11},{10,... | collective-permute-start | bytes 110600 | tf_op jit(solution)/shard_map/ppermute | solution.py:30
  80.8 2.8 %collective-permute-start.19 = (f32[72,128]{1,0:T(8,128)S(1)}, f32[72,128]{1,0:T(8,128)S(1)}, u32[]{:S(2)}, u32[]{:S(2)}) collective-permute-start(f32[72,128]{1,0:T(8,128)S(1)} %add_add_fusion.near), channel_id=1, source_target_pairs={{0,1},{1,0},{2,3},{3,2},{4,5},{5,4},{6,7},{7,6},{8,9},{9,8},{10,11... | collective-permute-start | bytes 110600 | tf_op jit(solution)/shard_map/ppermute | solution.py:30

commit v4 on v3

--- a/solution.py
+++ b/solution.py
@@ -34,36 +34,20 @@
     return place + 4 if (place // 4) % 2 else place - 4
 
 
-def along_x(steps):
-    return lambda p, n: (p // 4 * 4 + (p + steps) % 4, n)
-
-
-def other_core(p, n):
-    return (p, n ^ 1)
-
-
-def plane_groups():
-    return [
-        [(16 * z + member) * 4 + column for member in range(16)]
-        for z in range(4)
-        for column in range(4)
-    ]
-
-
-def along_z(steps):
-    return lambda p, n: (p + 16 * steps, n)
-
-
-def other_z(p, n):
-    return (p, n ^ 2)
-
-
-def other_both(p, n):
-    return (p, n ^ 3)
-
-
-def exchange(value, groups):
-    return lax.all_to_all(value, ("wide", "narrow"), 0, 0, axis_index_groups=groups)
+def across_x(mask):
+    return lambda p, n: (p ^ mask, n)
+
+
+def across_y(mask):
+    return lambda p, n: (p ^ (4 * mask), n)
+
+
+def across_z(mask):
+    return lambda p, n: (p ^ (16 * mask), n)
+
+
+def across_narrow(mask):
+    return lambda p, n: (p, n ^ mask)
 
 
 def dot(a, b):
@@ -194,7 +178,7 @@
     spot, p0, p1, p2, p3, p4, p5, p6, p7, r0, r1, r2, r3, dt_ref, at_ref, normed0, normed1, w_qkv,
     keep, send, g_ref, p_ref, n_ref,
 ):
-    x, core = spot[0], spot[2]
+    x, y, core = spot[0], spot[1], spot[2]
     parts = (p0, p1, p2, p3, p4, p5, p6, p7)
     d_high, d_low = two_terms(dt_ref[...])
     normed = jnp.concatenate([normed0[...], normed1[...]], 0)
@@ -212,56 +196,70 @@
     n_ref[...] = jnp.where(row == 0, gain_row, jnp.where(row == 1, offset_row, 0.0)).T
     for ahead, out in ((0, keep), (1, send)):
         to_core = core if ahead == 0 else 1 - core
-        for member in range(16):
-            for side in range(2):
-                lanes = pl.ds(pl.multiple_of(256 * to_core + 128 * side, 128), 128)
-                for slot in range(3):
-                    residue = 3 * member + slot
-                    third_of = lax.rem(residue // 16 - x + 6, 3)
-                    start = pl.multiple_of(128 * third_of + 8 * (residue % 16), 8)
-                    top = 24 * side + 8 * slot
-                    out[member, top : top + 8, :] = g_ref[pl.ds(start, 8), lanes]
-            for z in range(4):
-                rows = slice(128 * z + 8 * member, 128 * z + 8 * member + 8)
-                piece = p_ref[rows, :]
-                top = 48 + 8 * (z // 2)
-                out[member, top : top + 8, 64 * (z % 2) : 64 * (z % 2) + 64] = jnp.where(
-                    to_core == 0, piece[:, :64], piece[:, 64:]
-                )
-                if ahead == 0:
-                    out[member, 64:, 32 * z : 32 * z + 32] = n_ref[rows, :32]
-            if ahead == 1:
-                out[member, 64:, :] = jnp.zeros((8, 128), F32)
-
-
-def z_parts_kernel(spot, pieces, *outs):
+        for across in range(4):
+            to_y = y ^ across
+            for to_x in range(4):
+                block = 4 * across + to_x
+                for side in range(2):
+                    lanes = pl.ds(pl.multiple_of(256 * to_core + 128 * side, 128), 128)
+                    for slot in range(3):
+                        residue = 12 * to_y + 3 * to_x + slot
+                        third_of = lax.rem(residue // 16 - x + 6, 3)
+                        start = pl.multiple_of(128 * third_of + 8 * lax.rem(residue, 16), 8)
+                        top = 24 * side + 8 * slot
+                        out[block, top : top + 8, :] = g_ref[pl.ds(start, 8), lanes]
+                for z in range(4):
+                    rows = pl.ds(pl.multiple_of(128 * z + 32 * to_y + 8 * to_x, 8), 8)
+                    piece = p_ref[rows, :]
+                    top = 48 + 8 * (z // 2)
+                    out[block, top : top + 8, 64 * (z % 2) : 64 * (z % 2) + 64] = jnp.where(
+                        to_core == 0, piece[:, :64], piece[:, 64:]
+                    )
+                    if ahead == 0:
+                        out[block, 64:, 32 * z : 32 * z + 32] = n_ref[rows, :32]
+                if ahead == 1:
+                    out[block, 64:, :] = jnp.zeros((8, 128), F32)
+
+
+def x_parts_kernel(spot, s0, s1, s2, s3, *outs):
+    x = spot[0]
+    for across, out in enumerate(outs):
+        to_x = x ^ across
+        out[...] = (s0[to_x] + s1[to_x]) + (s2[to_x] + s3[to_x])
+
+
+def z_parts_kernel(spot, m0, m1, m2, m3, *outs):
     x, y, z = spot[0], spot[1], spot[3]
-    members = [
-        (pieces[j] + pieces[4 + j]) + (pieces[8 + j] + pieces[12 + j]) for j in range(4)
-    ]
-    total = (members[0][64:] + members[1][64:]) + (members[2][64:] + members[3][64:])
+    pieces = (m0, m1, m2, m3)
+
+    def from_member(member, rows):
+        across = member ^ x
+        picked = pieces[0][rows, :]
+        for index in range(1, 4):
+            picked = jnp.where(across == index, pieces[index][rows, :], picked)
+        return picked
+
+    total = (m0[64:, :] + m1[64:, :]) + (m2[64:, :] + m3[64:, :])
+    proj = [from_member(member, slice(48, 64)) for member in range(4)]
     for to_z in range(4):
         block = []
         for side in range(2):
             for slot in range(3):
-                rows = slice(24 * side + 8 * slot, 24 * side + 8 * slot + 8)
                 owner = lax.rem(48 * to_z + 12 * y + 3 * x + slot, 64) // 16
-                picked = members[0][rows]
-                for j in range(1, 4):
-                    picked = jnp.where(owner == j, members[j][rows], picked)
-                block.append(picked)
-        rows = slice(48 + 8 * (to_z // 2), 56 + 8 * (to_z // 2))
+                top = 24 * side + 8 * slot
+                block.append(from_member(owner, slice(top, top + 8)))
+        rows = slice(8 * (to_z // 2), 8 * (to_z // 2) + 8)
         lanes = slice(64 * (to_z % 2), 64 * (to_z % 2) + 64)
         for pair in range(2):
             block.append(
-                jnp.concatenate([members[2 * pair + j][rows, lanes] for j in range(2)], 1)
+                jnp.concatenate([proj[2 * pair][rows, lanes], proj[2 * pair + 1][rows, lanes]], 1)
             )
         lanes = slice(32 * to_z, 32 * to_z + 32)
         block.append(jnp.concatenate([total[:, lanes], jnp.zeros((8, 96), F32)], 1))
         block = jnp.concatenate(block, 0)
-        for steps in range(4):
-            ahead = lax.rem(to_z - z + 4, 4) == steps
-            outs[steps][...] = jnp.where(ahead, block, outs[steps][...]) if to_z else block
+        for across in range(4):
+            ahead = (to_z ^ z) == across
+            outs[across][...] = jnp.where(ahead, block, outs[across][...]) if to_z else block
 
 
 def last_kernel(spot, near, core_in, z_in, both_in, g_out, p_out, n_out):
@@ -306,9 +304,9 @@
     x = spot[0]
     projected = jnp.zeros((SLAB, C), F32)
     d_normed = jnp.zeros((SLAB, C), F32)
-    for r_ref, steps in ((r0, 0), (r1, 3), (r2, 1), (r3, 2)):
+    for across, r_ref in enumerate((r0, r1, r2, r3)):
         rows = r_ref[...]
-        member = lax.rem(x + steps, 4)
+        member = x ^ across
         start = pl.multiple_of(OWN * member, OWN)
         projected += dot(rows[:, 3 * OWN :], w_proj[pl.ds(start, OWN), :])
         for third in range(3):
@@ -358,9 +356,9 @@
     cross_in = move(other[:, :4], lambda p, n: (partner_of(p), n - 1))
 
     part0 = jnp.stack([mine[:, 4:], lower_in], 1).reshape(2, SLAB // 2, C)
-    parts0 = [part0] + [move(part0, along_x(steps)) for steps in (1, -1, 2)]
+    parts0 = [part0] + [move(part0, across_x(mask)) for mask in (1, 2, 3)]
     part1 = jnp.stack([other_in, cross_in], 1).reshape(2, SLAB // 2, C)
-    parts1 = [part1] + [move(part1, along_x(steps)) for steps in (1, -1, 2)]
+    parts1 = [part1] + [move(part1, across_x(mask)) for mask in (1, 2, 3)]
     half = TOKENS // 2
     normed0, qkv0, up0 = call(
         first_kernel,
@@ -370,7 +368,7 @@
         flops=10_000_000_000,
         moved=3_000_000,
     )
-    r_own, r_left, r_right, r_far, d_t, a_t, normed1 = call(
+    r0, r1, r2, r3, d_t, a_t, normed1 = call(
         attention_kernel,
         flags,
         (*parts1, normed0, qkv0, up0, norm_params, w_qkv, w_proj),
@@ -380,13 +378,11 @@
         moved=6_000_000,
     )
 
-    from_right = move(r_left, along_x(-1))
-    from_left = move(r_right, along_x(1))
-    from_far = move(r_far, along_x(2))
+    returned = [r0] + [move(rows, across_x(mask)) for mask, rows in ((1, r1), (2, r2), (3, r3))]
     keep, send = call(
         gradient_kernel,
         spot,
-        (*parts0, *parts1, r_own, r_left, r_right, r_far, d_t, a_t, normed0, normed1, w_qkv),
+        (*parts0, *parts1, r0, r1, r2, r3, d_t, a_t, normed0, normed1, w_qkv),
         [((16, 72, 128), F32)] * 2,
         scratch=[
             pltpu.VMEM((3 * OWN, C), F32),
@@ -396,32 +392,37 @@
         flops=20_000_000_000,
         moved=6_000_000,
     )
-    halves = keep + move(send, other_core)
-    halves, from_left, from_right, from_far = lax.optimization_barrier(
-        (halves, from_left, from_right, from_far)
-    )
-    plane = exchange(halves, plane_groups())
+    received = move(send, across_narrow(1))
+    blocks = [slice(4 * mask, 4 * mask + 4) for mask in range(4)]
+    halves = [keep[block] + received[block] for block in blocks]
+    from_y = [halves[0]] + [move(halves[mask], across_y(mask)) for mask in (1, 2, 3)]
     (back,) = call(
         token_kernel,
         spot,
-        (r_own, from_left, from_right, from_far, part0, part1, w_qkv, w_proj, norm_params),
+        (*returned, part0, part1, w_qkv, w_proj, norm_params),
         [((2, SLAB, C), BF16)],
         flops=500_000_000,
         moved=4_000_000,
+    )
+    from_y[1], from_y[2], from_y[3], back = lax.optimization_barrier(
+        (from_y[1], from_y[2], from_y[3], back)
     )
     back = back.reshape(2, 4, 4, 8, C)
     lower = move(back[:, 1], lambda p, n: (p, n + 1))
     other_upper = move(back[:, 2], lambda p, n: (partner_of(p), n))
     other_lower = move(back[:, 3], lambda p, n: (partner_of(p), n + 1))
 
-    z_parts = call(z_parts_kernel, spot, (plane,), [((72, 128), F32)] * 4)
+    share = ((72, 128), F32)
+    x_parts = call(x_parts_kernel, spot, from_y, [share] * 4)
+    from_x = [x_parts[0]] + [move(x_parts[mask], across_x(mask)) for mask in (1, 2, 3)]
+    z_parts = call(z_parts_kernel, spot, from_x, [share] * 4)
     output, grad_inputs = call(
         merge_kernel,
         spot,
         (own_inputs, own_upstream, back[:, 0], lower, other_upper, other_lower),
         [((8, 16, C), BF16)] * 2,
     )
-    line = [z_parts[0]] + [move(z_parts[steps], along_z(steps)) for steps in (1, 2, 3)]
+    line = [z_parts[0]] + [move(z_parts[mask], across_z(mask)) for mask in (1, 2, 3)]
     line[1], line[2], line[3], output, grad_inputs = lax.optimization_barrier(
         (line[1], line[2], line[3], output, grad_inputs)
     )
@@ -429,7 +430,7 @@
     grad_qkv, grad_proj, grad_norm = call(
         last_kernel,
         spot,
-        (line, move(line, other_core), move(line, other_z), move(line, other_both)),
+        (line, *[move(line, across_narrow(mask)) for mask in (1, 2, 3)]),
         [((24, C), F32), ((8, C), F32), ((2, 8), F32)],
     )
     return (

time: 85.1 us -> 85.2 us (level)
  starting transfers between devices: 46.4 us -> 49.7 us
  local copies, waits for them, and re-layouts: 3.69 us -> 1.19 us
  Pallas kernels: 14.5 us -> 15.4 us
    ppermute x22 -> x28, starting transfers between devices: 42.8 us -> 49.7 us  [move(): return lax.ppermute(value, ('wide', 'narrow'), pairs)]
    all_to_all x1 -> x0, starting transfers between devices: 3.58 us -> none  [exchange(): lax.all_to_all(value, ('wide', 'narrow'), 0, 0, axis_index_groups=groups)]
    unnamed x20 -> x12, local copies, waits for them, and re-layouts: 3.56 us -> 1.06 us
    pallas_call x7 -> x8, Pallas kernels: 14.5 us -> 15.4 us  [call(): pl.pallas_call(kernel, out_shape=[jax.ShapeDtypeStruct(shape, dtype) for...]
    ppermute x22 -> x28, waiting for transfers between devices: 17.2 us -> 16.5 us  [move(): return lax.ppermute(value, ('wide', 'narrow'), pairs)]
  transfers between devices with their start and end apart: 23 -> 28, of which waited for: 9 -> 11; matrix products, arithmetic and copies ran while one was open for 1% -> 0% of each run, Pallas kernels for 5% -> 5%
where the time goes in v4:
time: 85.2 us; the launch traced here: 85 us
  starting transfers between devices  49.7 us (58%)
  waiting for transfers between devices  16.5 us (19%)
  Pallas kernels  15.4 us (18%)
  other arithmetic  1.38 us (2%)
  local copies, waits for them, and re-layouts  1.19 us (1%)
  between operations  0.88 us (1%)
    ppermute x28, starting transfers between devices, move(): return lax.ppermute(value, ('wide', 'narrow'), pairs)  49.7 us
    ppermute x28, waiting for transfers between devices, move(): return lax.ppermute(value, ('wide', 'narrow'), pairs)  16.5 us
    pallas_call x8, Pallas kernels, call(): pl.pallas_call(kernel, out_shape=[jax.ShapeDtypeStruct(shape, dtype) for...  15.4 us
  transfers between devices with their start and end apart: 28, of which 11 were waited for; matrix products, arithmetic and copies ran while one was open for 0% of the time, Pallas kernels for 5%

profile of v4, /device:TPU:1, one launch (start us, length us, event | category | flops | bytes accessed | tf_op | source)
XLA Modules:
  0.0 85.0 jit_solution(9437408132902588935)
XLA Ops:
  0.7 1.2 %broadcast_select_fusion = (bf16[2,8,8,512]{3,2,1,0:T(8,128)(2,1)S(1)}, bf16[2,8,8,512]{3,2,1,0:T(8,128)(2,1)S(1)}) fusion(pred[8]{0:T(512)(128)(4,1)S(1)} %compare_compare_fusion, bf16[1,8,2,8,512]{4,3,2,1,0:T(8,128)(2,1)} %bitcast.60, bf16[1,8,2,8,512]{4,3,2,1,0:T(8,128)(2,1)} %bitcast.58), kind=kLoop, calls=%fused_computation.12 | loop fusion | flops 327680 | bytes 524296 | tf_op jit(solution)/shard_map/jit(_where)/select_n | solution.py:353
  1.9 3.3 %collective-permute-start = (bf16[2,4,8,512]{3,2,1,0:T(8,128)(2,1)S(1)}, bf16[2,4,8,512]{3,2,1,0:T(8,128)(2,1)S(1)}, u32[]{:S(2)}, u32[]{:S(2)}) collective-permute-start(bf16[2,4,8,512]{3,2,1,0:T(8,128)(2,1)S(1)} %get-tuple-element.86), channel_id=1, source_target_pairs={{0,3},{1,0},{2,1},{3,2},{4,7},{5,4},{6,5},{7,6},{8,11},{9,8},{10,9... | collective-permute-start | bytes 196616 | tf_op jit(solution)/shard_map/ppermute | solution.py:30
  5.3 6.8 %collective-permute-start.4 = (bf16[2,4,8,512]{3,2,1,0:T(8,128)(2,1)S(1)}, bf16[2,4,8,512]{3,2,1,0:T(8,128)(2,1)S(1)}, u32[]{:S(2)}, u32[]{:S(2)}) collective-permute-start(bf16[2,4,8,512]{3,2,1,0:T(8,128)(2,1)S(1)} %get-tuple-element.83), channel_id=1, source_target_pairs={{0,240},{1,241},{2,242},{3,243},{4,244},{5,245},{6,246},{7,247},{8... | collective-permute-start | bytes 196616 | tf_op jit(solution)/shard_map/ppermute | solution.py:30
  12.1 0.4 collective-permute-start.5
  12.6 2.6 %collective-permute-start.3 = (bf16[2,64,512]{2,1,0:T(8,128)(2,1)S(1)}, bf16[2,64,512]{2,1,0:T(8,128)(2,1)S(1)}, u32[]{:S(2)}, u32[]{:S(2)}) collective-permute-start(bf16[2,64,512]{2,1,0:T(8,128)(2,1)S(1)} %bitcast.62), channel_id=1, source_target_pairs={{0,12},{1,13},{2,14},{3,15},{4,8},{5,9},{6,10},{7,11},{8,4},{9,5},... | collective-permute-start | bytes 393224 | tf_op jit(solution)/shard_map/ppermute | solution.py:30
  15.1 0.5 collective-permute-start.2
  15.7 0.3 collective-permute-start.1
  15.9 0.1 pad_add_fusion.flags
  16.0 0.1 stack.59.spot
  16.1 0.0 collective-permute-done.4
  16.1 3.6 %collective-permute-done.5 = bf16[2,4,8,512]{3,2,1,0:T(8,128)(2,1)S(1)} collective-permute-done((bf16[2,4,8,512]{3,2,1,0:T(8,128)(2,1)S(1)}, bf16[2,4,8,512]{3,2,1,0:T(8,128)(2,1)S(1)}, u32[]{:S(2)}, u32[]{:S(2)}) %collective-permute-start.5) | collective-permute-done | bytes 65568 | tf_op jit(solution)/shard_map/ppermute | solution.py:30
  19.7 2.6 %collective-permute-start.8 = (bf16[2,64,512]{2,1,0:T(8,128)(2,1)S(1)}, bf16[2,64,512]{2,1,0:T(8,128)(2,1)S(1)}, u32[]{:S(2)}, u32[]{:S(2)}) collective-permute-start(bf16[2,64,512]{2,1,0:T(8,128)(2,1)S(1)} %bitcast.68), channel_id=1, source_target_pairs={{0,12},{1,13},{2,14},{3,15},{4,8},{5,9},{6,10},{7,11},{8,4},{9,5},... | collective-permute-start | bytes 393224 | tf_op jit(solution)/shard_map/ppermute | solution.py:30
  22.3 0.5 collective-permute-start.7
  22.8 0.0 collective-permute-done.3.p3
  22.8 0.3 collective-permute-start.6
  23.1 0.0 collective-permute-done.2.p2
  23.1 0.0 collective-permute-done.1.p1
  23.1 0.0 copy-start.3
  23.1 1.0 %copy-done.3 = bf16[512,512]{1,0:T(8,128)(2,1)S(1)} copy-done((bf16[512,512]{1,0:T(8,128)(2,1)S(1)}, bf16[512,512]{1,0:T(8,128)(2,1)}, u32[]{:S(2)}) %copy-start.3) | copy-done | bytes 524312
  24.1 1.1 %first_kernel.1 = (bf16[256,512]{1,0:T(8,128)(2,1)S(1)}, bf16[256,384]{1,0:T(8,128)(2,1)S(1)}, bf16[256,128]{1,0:T(8,128)(2,1)S(1)}) custom-call(s32[4]{0:T(128)S(1)} %pad_add_fusion.flags, bf16[2,64,512]{2,1,0:T(8,128)(2,1)S(1)} %bitcast.65, bf16[2,64,512]{2,1,0:T(8,128)(2,1)S(1)} %collective-permute-done.1.p1, ...), custom_call_target="tpu_custom_call" | custom-call | flops 10000000000 | bytes 3000000 | tf_op jit(solution)/shard_map/first_kernel/pallas_call | solution.py:327
  25.2 0.4 collective-permute-done.8.p3.p7
  25.6 2.1 %collective-permute-done.7.p2.p6 = bf16[2,64,512]{2,1,0:T(8,128)(2,1)S(1)} collective-permute-done((bf16[2,64,512]{2,1,0:T(8,128)(2,1)S(1)}, bf16[2,64,512]{2,1,0:T(8,128)(2,1)S(1)}, u32[]{:S(2)}, u32[]{:S(2)}) %collective-permute-start.7) | collective-permute-done | bytes 131104 | tf_op jit(solution)/shard_map/ppermute | solution.py:30
  27.7 0.0 collective-permute-done.6.p1.p5
  27.7 6.7 %attention_kernel.1 = (bf16[128,512]{1,0:T(8,128)(2,1)S(1)}, bf16[128,512]{1,0:T(8,128)(2,1)S(1)}, bf16[128,512]{1,0:T(8,128)(2,1)S(1)}, bf16[128,512]{1,0:T(8,1...) custom-call(s32[4]{0:T(128)S(1)} %pad_add_fusion.flags, ...), custom_call_target="tpu_custom_call" | custom-call | flops 1200000000 | bytes 6000000 | tf_op jit(solution)/shard_map/attention_kernel/pallas_call | solution.py:327
  34.4 2.4 %gradient_kernel.1 = (f32[16,72,128]{2,1,0:T(8,128)S(1)}, f32[16,72,128]{2,1,0:T(8,128)S(1)}) custom-call(s32[5]{0:T(128)S(1)} %stack.59.spot, bf16[2,64,512]{2,1,0:T(8,128)(2,1)S(1)} %bitcast.66, bf16[2,64,512]{2,1,0:T(8,128)(2,1)S(1)} %collective-permute-done.1.p1, bf16[2,64,512]{2,1,0:T(8,128)(2,1)S(1)} %collective-permute-done.2.p2, ...), custom_call_target="tpu_custom_call" | custom-call | flops 20000000000 | bytes 6000000 | tf_op jit(solution)/shard_map/gradient_kernel/pallas_call | solution.py:327
  36.9 0.0 copy-start.4
  36.9 3.9 %collective-permute-start.9 = (f32[16,72,128]{2,1,0:T(8,128)S(1)}, f32[16,72,128]{2,1,0:T(8,128)S(1)}, u32[]{:S(2)}, u32[]{:S(2)}) collective-permute-start(f32[16,72,128]{2,1,0:T(8,128)S(1)} %get-tuple-element.50), channel_id=1, source_target_pairs={{0,1},{1,0},{2,3},{3,2},{4,5},{5,4},{6,7},{7,6},{8,9},{9,8},{10,11... | collective-permute-start | bytes 1769480 | tf_op jit(solution)/shard_map/ppermute | solution.py:30
  40.8 0.4 collective-permute-start.13
  41.2 2.5 %collective-permute-start.14 = (bf16[128,512]{1,0:T(8,128)(2,1)S(1)}, bf16[128,512]{1,0:T(8,128)(2,1)S(1)}, u32[]{:S(2)}, u32[]{:S(2)}) collective-permute-start(bf16[128,512]{1,0:T(8,128)(2,1)S(1)} %get-tuple-element.44.r2), channel_id=1, source_target_pairs={{0,8},{1,9},{2,10},{3,11},{4,12},{5,13},{6,14},{7,15},{8,0},{9,1},... | collective-permute-start | bytes 393224 | tf_op jit(solution)/shard_map/ppermute | solution.py:30
  43.7 1.0 %collective-permute-start.15 = (bf16[128,512]{1,0:T(8,128)(2,1)S(1)}, bf16[128,512]{1,0:T(8,128)(2,1)S(1)}, u32[]{:S(2)}, u32[]{:S(2)}) collective-permute-start(bf16[128,512]{1,0:T(8,128)(2,1)S(1)} %get-tuple-element.45.r3), channel_id=1, source_target_pairs={{0,12},{1,13},{2,14},{3,15},{4,8},{5,9},{6,10},{7,11},{8,4},{9,5},... | collective-permute-start | bytes 393224 | tf_op jit(solution)/shard_map/ppermute | solution.py:30
  44.7 0.0 collective-permute-done.9
  44.7 0.1 slice_add_fusion
  44.7 0.1 collective-permute-start.12
  44.8 0.1 collective-permute-start.11
  44.9 0.9 %collective-permute-done.13.r1 = bf16[128,512]{1,0:T(8,128)(2,1)S(1)} collective-permute-done((bf16[128,512]{1,0:T(8,128)(2,1)S(1)}, bf16[128,512]{1,0:T(8,128)(2,1)S(1)}, u32[]{:S(2)}, u32[]{:S(2)}) %collective-permute-start.13) | collective-permute-done | bytes 131104 | tf_op jit(solution)/shard_map/ppermute | solution.py:30
  45.8 2.2 %collective-permute-start.10 = (f32[4,72,128]{2,1,0:T(8,128)S(1)}, f32[4,72,128]{2,1,0:T(8,128)S(1)}, u32[]{:S(2)}, u32[]{:S(2)}) collective-permute-start(f32[4,72,128]{2,1,0:T(8,128)S(1)} %get-tuple-element.75), channel_id=1, source_target_pairs={{0,16},{1,17},{2,18},{3,19},{4,20},{5,21},{6,22},{7,23},{8,24},{9,... | collective-permute-start | bytes 442376 | tf_op jit(solution)/shard_map/ppermute | solution.py:30
  48.1 2.0 %collective-permute-done.14.r2 = bf16[128,512]{1,0:T(8,128)(2,1)S(1)} collective-permute-done((bf16[128,512]{1,0:T(8,128)(2,1)S(1)}, bf16[128,512]{1,0:T(8,128)(2,1)S(1)}, u32[]{:S(2)}, u32[]{:S(2)}) %collective-permute-start.14) | collective-permute-done | bytes 131104 | tf_op jit(solution)/shard_map/ppermute | solution.py:30
  50.1 2.5 %collective-permute-done.15.r3 = bf16[128,512]{1,0:T(8,128)(2,1)S(1)} collective-permute-done((bf16[128,512]{1,0:T(8,128)(2,1)S(1)}, bf16[128,512]{1,0:T(8,128)(2,1)S(1)}, u32[]{:S(2)}, u32[]{:S(2)}) %collective-permute-start.15) | collective-permute-done | bytes 131104 | tf_op jit(solution)/shard_map/ppermute | solution.py:30
  52.7 1.3 %token_kernel.1 = bf16[2,128,512]{2,1,0:T(8,128)(2,1)S(1)} custom-call(s32[5]{0:T(128)S(1)} %stack.59.spot, bf16[128,512]{1,0:T(8,128)(2,1)S(1)} %get-tuple-element.42.r0, bf16[128,512]{1,0:T(8,128)(2,1)S(1)} %collective-permute-done.13.r1, bf16[128,512]{1,0:T(8,128)(2,1)S(1)} %collective-permute-done.14.r2, ...), custom_call_target="tpu_custom_call" | custom-call | flops 500000000 | bytes 4000000 | tf_op jit(solution)/shard_map/token_kernel/pallas_call | solution.py:327
  54.0 0.5 collective-permute-done.12.s3
  54.5 0.0 collective-permute-done.11.s2
  54.5 0.0 collective-permute-done.10.s1
  54.5 0.6 x_parts_kernel.1
  55.1 0.3 collective-permute-start.16
  55.5 4.6 %collective-permute-start.24 = (bf16[2,4,8,512]{3,2,1,0:T(8,128)(2,1)S(1)}, bf16[2,4,8,512]{3,2,1,0:T(8,128)(2,1)S(1)}, u32[]{:S(2)}, u32[]{:S(2)}) collective-permute-start(bf16[2,4,8,512]{3,2,1,0:T(8,128)(2,1)S(1)} %get-tuple-element.79), channel_id=1, source_target_pairs={{0,241},{1,242},{2,243},{3,240},{4,245},{5,246},{6,247},{7,244},{8... | collective-permute-start | bytes 196616 | tf_op jit(solution)/shard_map/ppermute | solution.py:30
  60.0 3.6 %collective-permute-start.17 = (f32[72,128]{1,0:T(8,128)S(1)}, f32[72,128]{1,0:T(8,128)S(1)}, u32[]{:S(2)}, u32[]{:S(2)}) collective-permute-start(f32[72,128]{1,0:T(8,128)S(1)} %get-tuple-element.56), channel_id=1, source_target_pairs={{0,8},{1,9},{2,10},{3,11},{4,12},{5,13},{6,14},{7,15},{8,0},{9,1},... | collective-permute-start | bytes 110600 | tf_op jit(solution)/shard_map/ppermute | solution.py:30
  63.6 0.3 collective-permute-start.18
  63.9 4.4 %collective-permute-start.23 = (bf16[2,4,8,512]{3,2,1,0:T(8,128)(2,1)S(1)}, bf16[2,4,8,512]{3,2,1,0:T(8,128)(2,1)S(1)}, u32[]{:S(2)}, u32[]{:S(2)}) collective-permute-start(bf16[2,4,8,512]{3,2,1,0:T(8,128)(2,1)S(1)} %get-tuple-element.80), channel_id=1, source_target_pairs={{0,240},{1,241},{2,242},{3,243},{4,244},{5,245},{6,246},{7,247},{8... | collective-permute-start | bytes 196616 | tf_op jit(solution)/shard_map/ppermute | solution.py:30
  68.3 0.0 collective-permute-done.16.m1
  68.3 0.0 collective-permute-start.22
  68.3 0.0 collective-permute-done.17.m2
  68.3 0.0 collective-permute-done.18.m3
  68.3 0.7 z_parts_kernel.1
  69.0 0.5 collective-permute-start.19
  69.5 1.4 %collective-permute-start.20 = (f32[72,128]{1,0:T(8,128)S(1)}, f32[72,128]{1,0:T(8,128)S(1)}, u32[]{:S(2)}, u32[]{:S(2)}) collective-permute-start(f32[72,128]{1,0:T(8,128)S(1)} %get-tuple-element.59), channel_id=1, source_target_pairs={{0,128},{1,129},{2,130},{3,131},{4,132},{5,133},{6,134},{7,135},{8... | collective-permute-start | bytes 110600 | tf_op jit(solution)/shard_map/ppermute | solution.py:30
  70.9 3.8 %collective-permute-start.21 = (f32[72,128]{1,0:T(8,128)S(1)}, f32[72,128]{1,0:T(8,128)S(1)}, u32[]{:S(2)}, u32[]{:S(2)}) collective-permute-start(f32[72,128]{1,0:T(8,128)S(1)} %get-tuple-element.60), channel_id=1, source_target_pairs={{0,192},{1,193},{2,194},{3,195},{4,196},{5,197},{6,198},{7,199},{8... | collective-permute-start | bytes 110600 | tf_op jit(solution)/shard_map/ppermute | solution.py:30
  74.8 1.3 %merge_kernel.1 = (bf16[8,16,512]{2,1,0:T(8,128)(2,1)}, bf16[8,16,512]{2,1,0:T(8,128)(2,1)}) custom-call(s32[5]{0:T(128)S(1)} %stack.59.spot, bf16[8,16,512]{2,1,0:T(8,128)(2,1)S(1)} %bitcast.59, bf16[8,16,512]{2,1,0:T(8,128)(2,1)S(1)} %bitcast.61, bf16[2,4,8,512]{3,2,1,0:T(8,128)(2,1)S(1)} %get-tuple-element.82.mine_high, ...), custom_call_target="tpu_custom_call" | custom-call | tf_op jit(solution)/shard_map/merge_kernel/pallas_call | solution.py:327
  76.0 0.4 collective-permute-done.20
  76.4 1.3 %collective-permute-done.21 = f32[72,128]{1,0:T(8,128)S(1)} collective-permute-done((f32[72,128]{1,0:T(8,128)S(1)}, f32[72,128]{1,0:T(8,128)S(1)}, u32[]{:S(2)}, u32[]{:S(2)}) %collective-permute-start.21) | collective-permute-done | bytes 36896 | tf_op jit(solution)/shard_map/ppermute | solution.py:30
  77.7 2.9 %collective-permute-start.27 = (f32[72,128]{1,0:T(8,128)S(1)}, f32[72,128]{1,0:T(8,128)S(1)}, u32[]{:S(2)}, u32[]{:S(2)}) collective-permute-start(f32[72,128]{1,0:T(8,128)S(1)} %add_add_fusion.near), channel_id=1, source_target_pairs={{0,3},{1,2},{2,1},{3,0},{4,7},{5,6},{6,5},{7,4},{8,11},{9,10},{10,... | collective-permute-start | bytes 110600 | tf_op jit(solution)/shard_map/ppermute | solution.py:30
  80.6 0.5 collective-permute-start.25
  81.1 1.1 %collective-permute-done.27.both_in = f32[72,128]{1,0:T(8,128)S(1)} collective-permute-done((f32[72,128]{1,0:T(8,128)S(1)}, f32[72,128]{1,0:T(8,128)S(1)}, u32[]{:S(2)}, u32[]{:S(2)}) %collective-permute-start.27) | collective-permute-done | bytes 36896 | tf_op jit(solution)/shard_map/ppermute | solution.py:30
  82.2 1.6 %collective-permute-done.26.z_in = f32[72,128]{1,0:T(8,128)S(1)} collective-permute-done((f32[72,128]{1,0:T(8,128)S(1)}, f32[72,128]{1,0:T(8,128)S(1)}, u32[]{:S(2)}, u32[]{:S(2)}) %collective-permute-start.26) | collective-permute-done | bytes 36896 | tf_op jit(solution)/shard_map/ppermute | solution.py:30
  83.8 1.2 %last_kernel.1 = (f32[24,512]{1,0:T(8,128)}, f32[8,512]{1,0:T(8,128)}, f32[2,8]{1,0:T(2,128)}) custom-call(s32[5]{0:T(128)S(1)} %stack.59.spot, f32[72,128]{1,0:T(8,128)S(1)} %add_add_fusion.near, f32[72,128]{1,0:T(8,128)S(1)} %collective-permute-done.25.core_in, f32[72,128]{1,0:T(8,128)S(1)} %collective-permute-done.26.z_in, ...), custom_call_target="tpu_custom_call" | custom-call | tf_op jit(solution)/shard_map/last_kernel/pallas_call | solution.py:327
  (24 shorter events, 0.1 us)
Async XLA Ops:
  0.6 22.4 %copy-start = (bf16[512,1536]{1,0:T(8,128)(2,1)S(1)}, bf16[512,1536]{1,0:T(8,128)(2,1)}, u32[]{:S(2)}) copy-start(bf16[512,1536]{1,0:T(8,128)(2,1)} %w_qkv.7) | copy-start | bytes 4718596
  0.6 22.4 %copy-start.5 = (f32[2,512]{1,0:T(2,128)S(1)}, f32[2,512]{1,0:T(2,128)}, u32[]{:S(2)}) copy-start(f32[2,512]{1,0:T(2,128)} %norm.5) | copy-start | bytes 12292
  1.9 10.6 %collective-permute-start = (bf16[2,4,8,512]{3,2,1,0:T(8,128)(2,1)S(1)}, bf16[2,4,8,512]{3,2,1,0:T(8,128)(2,1)S(1)}, u32[]{:S(2)}, u32[]{:S(2)}) collective-permute-start(bf16[2,4,8,512]{3,2,1,0:T(8,128)(2,1)S(1)} %get-tuple-element.86), channel_id=1, source_target_pairs={{0,3},{1,0},{2,1},{3,2},{4,7},{5,4},{6,5},{7,6},{8,11},{9,8},{10,9... | collective-permute-start | bytes 196616 | tf_op jit(solution)/shard_map/ppermute | solution.py:30
  5.3 10.8 %collective-permute-start.4 = (bf16[2,4,8,512]{3,2,1,0:T(8,128)(2,1)S(1)}, bf16[2,4,8,512]{3,2,1,0:T(8,128)(2,1)S(1)}, u32[]{:S(2)}, u32[]{:S(2)}) collective-permute-start(bf16[2,4,8,512]{3,2,1,0:T(8,128)(2,1)S(1)} %get-tuple-element.83), channel_id=1, source_target_pairs={{0,240},{1,241},{2,242},{3,243},{4,244},{5,245},{6,246},{7,247},{8... | collective-permute-start | bytes 196616 | tf_op jit(solution)/shard_map/ppermute | solution.py:30
  12.1 7.6 %collective-permute-start.5 = (bf16[2,4,8,512]{3,2,1,0:T(8,128)(2,1)S(1)}, bf16[2,4,8,512]{3,2,1,0:T(8,128)(2,1)S(1)}, u32[]{:S(2)}, u32[]{:S(2)}) collective-permute-start(bf16[2,4,8,512]{3,2,1,0:T(8,128)(2,1)S(1)} %get-tuple-element.84), channel_id=1, source_target_pairs={{0,243},{1,240},{2,241},{3,242},{4,247},{5,244},{6,245},{7,246},{8... | collective-permute-start | bytes 196616 | tf_op jit(solution)/shard_map/ppermute | solution.py:30
  12.6 10.2 %collective-permute-start.3 = (bf16[2,64,512]{2,1,0:T(8,128)(2,1)S(1)}, bf16[2,64,512]{2,1,0:T(8,128)(2,1)S(1)}, u32[]{:S(2)}, u32[]{:S(2)}) collective-permute-start(bf16[2,64,512]{2,1,0:T(8,128)(2,1)S(1)} %bitcast.62), channel_id=1, source_target_pairs={{0,12},{1,13},{2,14},{3,15},{4,8},{5,9},{6,10},{7,11},{8,4},{9,5},... | collective-permute-start | bytes 393224 | tf_op jit(solution)/shard_map/ppermute | solution.py:30
  15.1 7.9 %collective-permute-start.2 = (bf16[2,64,512]{2,1,0:T(8,128)(2,1)S(1)}, bf16[2,64,512]{2,1,0:T(8,128)(2,1)S(1)}, u32[]{:S(2)}, u32[]{:S(2)}) collective-permute-start(bf16[2,64,512]{2,1,0:T(8,128)(2,1)S(1)} %bitcast.63), channel_id=1, source_target_pairs={{0,8},{1,9},{2,10},{3,11},{4,12},{5,13},{6,14},{7,15},{8,0},{9,1},... | collective-permute-start | bytes 393224 | tf_op jit(solution)/shard_map/ppermute | solution.py:30
  15.7 7.4 %collective-permute-start.1 = (bf16[2,64,512]{2,1,0:T(8,128)(2,1)S(1)}, bf16[2,64,512]{2,1,0:T(8,128)(2,1)S(1)}, u32[]{:S(2)}, u32[]{:S(2)}) collective-permute-start(bf16[2,64,512]{2,1,0:T(8,128)(2,1)S(1)} %bitcast.64), channel_id=1, source_target_pairs={{0,4},{1,5},{2,6},{3,7},{4,0},{5,1},{6,2},{7,3},{8,12},{9,13},{10,... | collective-permute-start | bytes 393224 | tf_op jit(solution)/shard_map/ppermute | solution.py:30
  19.7 5.9 %collective-permute-start.8 = (bf16[2,64,512]{2,1,0:T(8,128)(2,1)S(1)}, bf16[2,64,512]{2,1,0:T(8,128)(2,1)S(1)}, u32[]{:S(2)}, u32[]{:S(2)}) collective-permute-start(bf16[2,64,512]{2,1,0:T(8,128)(2,1)S(1)} %bitcast.68), channel_id=1, source_target_pairs={{0,12},{1,13},{2,14},{3,15},{4,8},{5,9},{6,10},{7,11},{8,4},{9,5},... | collective-permute-start | bytes 393224 | tf_op jit(solution)/shard_map/ppermute | solution.py:30
  22.3 5.4 %collective-permute-start.7 = (bf16[2,64,512]{2,1,0:T(8,128)(2,1)S(1)}, bf16[2,64,512]{2,1,0:T(8,128)(2,1)S(1)}, u32[]{:S(2)}, u32[]{:S(2)}) collective-permute-start(bf16[2,64,512]{2,1,0:T(8,128)(2,1)S(1)} %bitcast.69), channel_id=1, source_target_pairs={{0,8},{1,9},{2,10},{3,11},{4,12},{5,13},{6,14},{7,15},{8,0},{9,1},... | collective-permute-start | bytes 393224 | tf_op jit(solution)/shard_map/ppermute | solution.py:30
  22.8 4.9 %collective-permute-start.6 = (bf16[2,64,512]{2,1,0:T(8,128)(2,1)S(1)}, bf16[2,64,512]{2,1,0:T(8,128)(2,1)S(1)}, u32[]{:S(2)}, u32[]{:S(2)}) collective-permute-start(bf16[2,64,512]{2,1,0:T(8,128)(2,1)S(1)} %bitcast.70), channel_id=1, source_target_pairs={{0,4},{1,5},{2,6},{3,7},{4,0},{5,1},{6,2},{7,3},{8,12},{9,13},{10,... | collective-permute-start | bytes 393224 | tf_op jit(solution)/shard_map/ppermute | solution.py:30
  23.1 1.0 %copy-start.3 = (bf16[512,512]{1,0:T(8,128)(2,1)S(1)}, bf16[512,512]{1,0:T(8,128)(2,1)}, u32[]{:S(2)}) copy-start(bf16[512,512]{1,0:T(8,128)(2,1)} %w_proj.5) | copy-start | bytes 1572868
  36.9 15.8 %copy-start.4 = (bf16[512,512]{1,0:T(8,128)(2,1)S(1)}, bf16[512,512]{1,0:T(8,128)(2,1)}, u32[]{:S(2)}) copy-start(bf16[512,512]{1,0:T(8,128)(2,1)} %w_proj.5) | copy-start | bytes 1572868
  36.9 7.8 %collective-permute-start.9 = (f32[16,72,128]{2,1,0:T(8,128)S(1)}, f32[16,72,128]{2,1,0:T(8,128)S(1)}, u32[]{:S(2)}, u32[]{:S(2)}) collective-permute-start(f32[16,72,128]{2,1,0:T(8,128)S(1)} %get-tuple-element.50), channel_id=1, source_target_pairs={{0,1},{1,0},{2,3},{3,2},{4,5},{5,4},{6,7},{7,6},{8,9},{9,8},{10,11... | collective-permute-start | bytes 1769480 | tf_op jit(solution)/shard_map/ppermute | solution.py:30
  40.8 5.1 %collective-permute-start.13 = (bf16[128,512]{1,0:T(8,128)(2,1)S(1)}, bf16[128,512]{1,0:T(8,128)(2,1)S(1)}, u32[]{:S(2)}, u32[]{:S(2)}) collective-permute-start(bf16[128,512]{1,0:T(8,128)(2,1)S(1)} %get-tuple-element.43.r1), channel_id=1, source_target_pairs={{0,4},{1,5},{2,6},{3,7},{4,0},{5,1},{6,2},{7,3},{8,12},{9,13},{10,... | collective-permute-start | bytes 393224 | tf_op jit(solution)/shard_map/ppermute | solution.py:30
  41.2 8.9 %collective-permute-start.14 = (bf16[128,512]{1,0:T(8,128)(2,1)S(1)}, bf16[128,512]{1,0:T(8,128)(2,1)S(1)}, u32[]{:S(2)}, u32[]{:S(2)}) collective-permute-start(bf16[128,512]{1,0:T(8,128)(2,1)S(1)} %get-tuple-element.44.r2), channel_id=1, source_target_pairs={{0,8},{1,9},{2,10},{3,11},{4,12},{5,13},{6,14},{7,15},{8,0},{9,1},... | collective-permute-start | bytes 393224 | tf_op jit(solution)/shard_map/ppermute | solution.py:30
  43.7 9.0 %collective-permute-start.15 = (bf16[128,512]{1,0:T(8,128)(2,1)S(1)}, bf16[128,512]{1,0:T(8,128)(2,1)S(1)}, u32[]{:S(2)}, u32[]{:S(2)}) collective-permute-start(bf16[128,512]{1,0:T(8,128)(2,1)S(1)} %get-tuple-element.45.r3), channel_id=1, source_target_pairs={{0,12},{1,13},{2,14},{3,15},{4,8},{5,9},{6,10},{7,11},{8,4},{9,5},... | collective-permute-start | bytes 393224 | tf_op jit(solution)/shard_map/ppermute | solution.py:30
  44.7 9.8 %collective-permute-start.12 = (f32[4,72,128]{2,1,0:T(8,128)S(1)}, f32[4,72,128]{2,1,0:T(8,128)S(1)}, u32[]{:S(2)}, u32[]{:S(2)}) collective-permute-start(f32[4,72,128]{2,1,0:T(8,128)S(1)} %get-tuple-element.73), channel_id=1, source_target_pairs={{0,48},{1,49},{2,50},{3,51},{4,52},{5,53},{6,54},{7,55},{8,56},{9,... | collective-permute-start | bytes 442376 | tf_op jit(solution)/shard_map/ppermute | solution.py:30
  44.8 9.7 %collective-permute-start.11 = (f32[4,72,128]{2,1,0:T(8,128)S(1)}, f32[4,72,128]{2,1,0:T(8,128)S(1)}, u32[]{:S(2)}, u32[]{:S(2)}) collective-permute-start(f32[4,72,128]{2,1,0:T(8,128)S(1)} %get-tuple-element.74), channel_id=1, source_target_pairs={{0,32},{1,33},{2,34},{3,35},{4,36},{5,37},{6,38},{7,39},{8,40},{9,... | collective-permute-start | bytes 442376 | tf_op jit(solution)/shard_map/ppermute | solution.py:30
  45.8 28.9 %copy-start.1 = (bf16[1,1,8,16,512]{4,3,2,1,0:T(8,128)(2,1)S(1)}, bf16[1,1,8,16,512]{4,3,2,1,0:T(8,128)(2,1)}, u32[]{:S(2)}) copy-start(bf16[1,1,8,16,512]{4,3,2,1,0:T(8,128)(2,1)} %param.5) | copy-start | bytes 393220
  45.8 28.9 %copy-start.2 = (bf16[1,1,8,16,512]{4,3,2,1,0:T(8,128)(2,1)S(1)}, bf16[1,1,8,16,512]{4,3,2,1,0:T(8,128)(2,1)}, u32[]{:S(2)}) copy-start(bf16[1,1,8,16,512]{4,3,2,1,0:T(8,128)(2,1)} %param.9) | copy-start | bytes 393220
  45.8 8.7 %collective-permute-start.10 = (f32[4,72,128]{2,1,0:T(8,128)S(1)}, f32[4,72,128]{2,1,0:T(8,128)S(1)}, u32[]{:S(2)}, u32[]{:S(2)}) collective-permute-start(f32[4,72,128]{2,1,0:T(8,128)S(1)} %get-tuple-element.75), channel_id=1, source_target_pairs={{0,16},{1,17},{2,18},{3,19},{4,20},{5,21},{6,22},{7,23},{8,24},{9,... | collective-permute-start | bytes 442376 | tf_op jit(solution)/shard_map/ppermute | solution.py:30
  55.1 13.2 %collective-permute-start.16 = (f32[72,128]{1,0:T(8,128)S(1)}, f32[72,128]{1,0:T(8,128)S(1)}, u32[]{:S(2)}, u32[]{:S(2)}) collective-permute-start(f32[72,128]{1,0:T(8,128)S(1)} %get-tuple-element.55), channel_id=1, source_target_pairs={{0,4},{1,5},{2,6},{3,7},{4,0},{5,1},{6,2},{7,3},{8,12},{9,13},{10,... | collective-permute-start | bytes 110600 | tf_op jit(solution)/shard_map/ppermute | solution.py:30
  55.5 15.5 %collective-permute-start.24 = (bf16[2,4,8,512]{3,2,1,0:T(8,128)(2,1)S(1)}, bf16[2,4,8,512]{3,2,1,0:T(8,128)(2,1)S(1)}, u32[]{:S(2)}, u32[]{:S(2)}) collective-permute-start(bf16[2,4,8,512]{3,2,1,0:T(8,128)(2,1)S(1)} %get-tuple-element.79), channel_id=1, source_target_pairs={{0,241},{1,242},{2,243},{3,240},{4,245},{5,246},{6,247},{7,244},{8... | collective-permute-start | bytes 196616 | tf_op jit(solution)/shard_map/ppermute | solution.py:30
  60.0 8.3 %collective-permute-start.17 = (f32[72,128]{1,0:T(8,128)S(1)}, f32[72,128]{1,0:T(8,128)S(1)}, u32[]{:S(2)}, u32[]{:S(2)}) collective-permute-start(f32[72,128]{1,0:T(8,128)S(1)} %get-tuple-element.56), channel_id=1, source_target_pairs={{0,8},{1,9},{2,10},{3,11},{4,12},{5,13},{6,14},{7,15},{8,0},{9,1},... | collective-permute-start | bytes 110600 | tf_op jit(solution)/shard_map/ppermute | solution.py:30
  63.6 4.7 %collective-permute-start.18 = (f32[72,128]{1,0:T(8,128)S(1)}, f32[72,128]{1,0:T(8,128)S(1)}, u32[]{:S(2)}, u32[]{:S(2)}) collective-permute-start(f32[72,128]{1,0:T(8,128)S(1)} %get-tuple-element.57), channel_id=1, source_target_pairs={{0,12},{1,13},{2,14},{3,15},{4,8},{5,9},{6,10},{7,11},{8,4},{9,5},... | collective-permute-start | bytes 110600 | tf_op jit(solution)/shard_map/ppermute | solution.py:30
  63.9 10.9 %collective-permute-start.23 = (bf16[2,4,8,512]{3,2,1,0:T(8,128)(2,1)S(1)}, bf16[2,4,8,512]{3,2,1,0:T(8,128)(2,1)S(1)}, u32[]{:S(2)}, u32[]{:S(2)}) collective-permute-start(bf16[2,4,8,512]{3,2,1,0:T(8,128)(2,1)S(1)} %get-tuple-element.80), channel_id=1, source_target_pairs={{0,240},{1,241},{2,242},{3,243},{4,244},{5,245},{6,246},{7,247},{8... | collective-permute-start | bytes 196616 | tf_op jit(solution)/shard_map/ppermute | solution.py:30
  68.3 6.5 %collective-permute-start.22 = (bf16[2,4,8,512]{3,2,1,0:T(8,128)(2,1)S(1)}, bf16[2,4,8,512]{3,2,1,0:T(8,128)(2,1)S(1)}, u32[]{:S(2)}, u32[]{:S(2)}) collective-permute-start(bf16[2,4,8,512]{3,2,1,0:T(8,128)(2,1)S(1)} %get-tuple-element.81), channel_id=1, source_target_pairs={{0,1},{1,2},{2,3},{3,0},{4,5},{5,6},{6,7},{7,4},{8,9},{9,10},{10,1... | collective-permute-start | bytes 196616 | tf_op jit(solution)/shard_map/ppermute | solution.py:30
  69.0 7.1 %collective-permute-start.19 = (f32[72,128]{1,0:T(8,128)S(1)}, f32[72,128]{1,0:T(8,128)S(1)}, u32[]{:S(2)}, u32[]{:S(2)}) collective-permute-start(f32[72,128]{1,0:T(8,128)S(1)} %get-tuple-element.58), channel_id=1, source_target_pairs={{0,64},{1,65},{2,66},{3,67},{4,68},{5,69},{6,70},{7,71},{8,72},{9,... | collective-permute-start | bytes 110600 | tf_op jit(solution)/shard_map/ppermute | solution.py:30
  69.5 6.9 %collective-permute-start.20 = (f32[72,128]{1,0:T(8,128)S(1)}, f32[72,128]{1,0:T(8,128)S(1)}, u32[]{:S(2)}, u32[]{:S(2)}) collective-permute-start(f32[72,128]{1,0:T(8,128)S(1)} %get-tuple-element.59), channel_id=1, source_target_pairs={{0,128},{1,129},{2,130},{3,131},{4,132},{5,133},{6,134},{7,135},{8... | collective-permute-start | bytes 110600 | tf_op jit(solution)/shard_map/ppermute | solution.py:30
  70.9 6.8 %collective-permute-start.21 = (f32[72,128]{1,0:T(8,128)S(1)}, f32[72,128]{1,0:T(8,128)S(1)}, u32[]{:S(2)}, u32[]{:S(2)}) collective-permute-start(f32[72,128]{1,0:T(8,128)S(1)} %get-tuple-element.60), channel_id=1, source_target_pairs={{0,192},{1,193},{2,194},{3,195},{4,196},{5,197},{6,198},{7,199},{8... | collective-permute-start | bytes 110600 | tf_op jit(solution)/shard_map/ppermute | solution.py:30
  77.7 4.5 %collective-permute-start.27 = (f32[72,128]{1,0:T(8,128)S(1)}, f32[72,128]{1,0:T(8,128)S(1)}, u32[]{:S(2)}, u32[]{:S(2)}) collective-permute-start(f32[72,128]{1,0:T(8,128)S(1)} %add_add_fusion.near), channel_id=1, source_target_pairs={{0,3},{1,2},{2,1},{3,0},{4,7},{5,6},{6,5},{7,4},{8,11},{9,10},{10,... | collective-permute-start | bytes 110600 | tf_op jit(solution)/shard_map/ppermute | solution.py:30
  80.6 3.2 %collective-permute-start.26 = (f32[72,128]{1,0:T(8,128)S(1)}, f32[72,128]{1,0:T(8,128)S(1)}, u32[]{:S(2)}, u32[]{:S(2)}) collective-permute-start(f32[72,128]{1,0:T(8,128)S(1)} %add_add_fusion.near), channel_id=1, source_target_pairs={{0,2},{1,3},{2,0},{3,1},{4,6},{5,7},{6,4},{7,5},{8,10},{9,11},{10,... | collective-permute-start | bytes 110600 | tf_op jit(solution)/shard_map/ppermute | solution.py:30
  80.6 3.2 %collective-permute-start.25 = (f32[72,128]{1,0:T(8,128)S(1)}, f32[72,128]{1,0:T(8,128)S(1)}, u32[]{:S(2)}, u32[]{:S(2)}) collective-permute-start(f32[72,128]{1,0:T(8,128)S(1)} %add_add_fusion.near), channel_id=1, source_target_pairs={{0,1},{1,0},{2,3},{3,2},{4,5},{5,4},{6,7},{7,6},{8,9},{9,8},{10,11... | collective-permute-start | bytes 110600 | tf_op jit(solution)/shard_map/ppermute | solution.py:30

commit v5 on v4

--- a/solution.py
+++ b/solution.py
@@ -95,13 +95,19 @@
     )
 
 
+def keeper_kernel(flags, own, norm, w_qkv, w_proj, *outs):
+    for across, out in enumerate(outs):
+        _, out[:, : 3 * OWN], out[:, 3 * OWN :] = project(
+            (own,), norm, w_qkv, w_proj, flags[3] ^ across
+        )
+
+
 def attention_kernel(
-    flags, p0, p1, p2, p3, normed0, qkv0, up0, norm, w_qkv, w_proj,
-    r0, r1, r2, r3, dt_ref, at_ref, normed1,
+    flags, s0, s1, s2, s3, qkv0, up0, r0, r1, r2, r3, dt_ref, at_ref
 ):
-    normed1[...], qkv1, up1 = project((p0, p1, p2, p3), norm, w_qkv, w_proj, flags[3])
-    qkv = jnp.concatenate([qkv0[...], qkv1], 0)
-    cotangent = jnp.concatenate([up0[...], up1], 0)
+    shares = jnp.concatenate([s0[...], s1[...], s2[...], s3[...]], 0)
+    qkv = jnp.concatenate([qkv0[...], shares[:, : 3 * OWN]], 0)
+    cotangent = jnp.concatenate([up0[...], shares[:, 3 * OWN :]], 0)
     queries = qkv[:, :OWN]
     keys = qkv[:, OWN : 2 * OWN]
     values = qkv[:, 2 * OWN :]
@@ -175,22 +181,24 @@
 
 
 def gradient_kernel(
-    spot, p0, p1, p2, p3, p4, p5, p6, p7, r0, r1, r2, r3, dt_ref, at_ref, normed0, normed1, w_qkv,
+    spot, p0, p1, p2, p3, p4, p5, p6, p7, r0, r1, r2, r3, dt_ref, at_ref, normed0, norm, w_qkv,
     keep, send, g_ref, p_ref, n_ref,
 ):
     x, y, core = spot[0], spot[1], spot[2]
     parts = (p0, p1, p2, p3, p4, p5, p6, p7)
     d_high, d_low = two_terms(dt_ref[...])
-    normed = jnp.concatenate([normed0[...], normed1[...]], 0)
+    units = [unit_of(part[0])[0] for part in parts]
+    normed1 = [(unit * norm[0:1, :] + norm[1:2, :]).astype(BF16) for unit in units[4:]]
+    normed = jnp.concatenate([normed0[...]] + normed1, 0)
     g_ref[...] = dot(d_high, normed) + dot(d_low, normed)
     p_ref[...] = dot(at_ref[...], jnp.concatenate([part[1] for part in parts], 0)).T
     columns = own_columns(w_qkv, x)
     gain_row = jnp.zeros((1, C), F32)
     offset_row = jnp.zeros((1, C), F32)
     for member, r_ref in enumerate((r0, r1, r2, r3)):
-        rows = jnp.concatenate([parts[member][0], parts[4 + member][0]], 0)
+        unit = jnp.concatenate([units[member], units[4 + member]], 0)
         d_normed = dot_nt(r_ref[:, : 3 * OWN], columns)
-        gain_row += jnp.sum(d_normed * unit_of(rows)[0], 0, keepdims=True)
+        gain_row += jnp.sum(d_normed * unit, 0, keepdims=True)
         offset_row += jnp.sum(d_normed, 0, keepdims=True)
     row = lax.broadcasted_iota(jnp.int32, (128, C), 0)
     n_ref[...] = jnp.where(row == 0, gain_row, jnp.where(row == 1, offset_row, 0.0)).T
@@ -358,7 +366,6 @@
     part0 = jnp.stack([mine[:, 4:], lower_in], 1).reshape(2, SLAB // 2, C)
     parts0 = [part0] + [move(part0, across_x(mask)) for mask in (1, 2, 3)]
     part1 = jnp.stack([other_in, cross_in], 1).reshape(2, SLAB // 2, C)
-    parts1 = [part1] + [move(part1, across_x(mask)) for mask in (1, 2, 3)]
     half = TOKENS // 2
     normed0, qkv0, up0 = call(
         first_kernel,
@@ -368,12 +375,22 @@
         flops=10_000_000_000,
         moved=3_000_000,
     )
-    r0, r1, r2, r3, d_t, a_t, normed1 = call(
+    shares = call(
+        keeper_kernel,
+        flags,
+        (part1, norm_params, w_qkv, w_proj),
+        [((SLAB // 2, C), BF16)] * 4,
+        flops=300_000_000,
+        moved=3_000_000,
+    )
+    shares = [shares[0]] + [move(shares[mask], across_x(mask)) for mask in (1, 2, 3)]
+    part1, normed0 = lax.optimization_barrier((part1, normed0))
+    parts1 = [part1] + [move(part1, across_x(mask)) for mask in (1, 2, 3)]
+    r0, r1, r2, r3, d_t, a_t = call(
         attention_kernel,
         flags,
-        (*parts1, normed0, qkv0, up0, norm_params, w_qkv, w_proj),
-        [((SLAB, C), BF16)] * 4
-        + [((3 * OWN, TOKENS), F32), ((OWN, TOKENS), BF16), ((half, C), BF16)],
+        (*shares, qkv0, up0),
+        [((SLAB, C), BF16)] * 4 + [((3 * OWN, TOKENS), F32), ((OWN, TOKENS), BF16)],
         flops=1_200_000_000,
         moved=6_000_000,
     )
@@ -382,7 +399,7 @@
     keep, send = call(
         gradient_kernel,
         spot,
-        (*parts0, *parts1, r0, r1, r2, r3, d_t, a_t, normed0, normed1, w_qkv),
+        (*parts0, *parts1, r0, r1, r2, r3, d_t, a_t, normed0, norm_params, w_qkv),
         [((16, 72, 128), F32)] * 2,
         scratch=[
             pltpu.VMEM((3 * OWN, C), F32),
@@ -408,30 +425,30 @@
         (from_y[1], from_y[2], from_y[3], back)
     )
     back = back.reshape(2, 4, 4, 8, C)
-    lower = move(back[:, 1], lambda p, n: (p, n + 1))
-    other_upper = move(back[:, 2], lambda p, n: (partner_of(p), n))
-    other_lower = move(back[:, 3], lambda p, n: (partner_of(p), n + 1))
+    crossed = move(back[:, 2:], lambda p, n: (partner_of(p), n))
 
     share = ((72, 128), F32)
     x_parts = call(x_parts_kernel, spot, from_y, [share] * 4)
     from_x = [x_parts[0]] + [move(x_parts[mask], across_x(mask)) for mask in (1, 2, 3)]
     z_parts = call(z_parts_kernel, spot, from_x, [share] * 4)
+    line = [z_parts[0]] + [move(z_parts[mask], across_z(mask)) for mask in (1, 2, 3)]
+    line[1], line[2], line[3], crossed = lax.optimization_barrier(
+        (line[1], line[2], line[3], crossed)
+    )
+    low = move(jnp.stack([back[:, 1], crossed[:, 1]], 1), lambda p, n: (p, n + 1))
+    line = (line[0] + line[1]) + (line[2] + line[3])
+    last = [line] + [move(line, across_narrow(mask)) for mask in (1, 2, 3)]
     output, grad_inputs = call(
         merge_kernel,
         spot,
-        (own_inputs, own_upstream, back[:, 0], lower, other_upper, other_lower),
+        (own_inputs, own_upstream, back[:, 0], low[:, 0], crossed[:, 0], low[:, 1]),
         [((8, 16, C), BF16)] * 2,
     )
-    line = [z_parts[0]] + [move(z_parts[mask], across_z(mask)) for mask in (1, 2, 3)]
-    line[1], line[2], line[3], output, grad_inputs = lax.optimization_barrier(
-        (line[1], line[2], line[3], output, grad_inputs)
-    )
-    line = (line[0] + line[1]) + (line[2] + line[3])
+    last[1], last[2], last[3], output, grad_inputs = lax.optimization_barrier(
+        (last[1], last[2], last[3], output, grad_inputs)
+    )
     grad_qkv, grad_proj, grad_norm = call(
-        last_kernel,
-        spot,
-        (line, *[move(line, across_narrow(mask)) for mask in (1, 2, 3)]),
-        [((24, C), F32), ((8, C), F32), ((2, 8), F32)],
+        last_kernel, spot, last, [((24, C), F32), ((8, C), F32), ((2, 8), F32)]
     )
     return (
         output[None, None], grad_inputs[None, None], grad_qkv.T, grad_proj.T, grad_norm

time: 85.2 us -> 87.4 us (1.026)
  starting transfers between devices: 49.7 us -> 52.8 us
  waiting for transfers between devices: 16.5 us -> 14.4 us
  Pallas kernels: 15.4 us -> 16.4 us
    ppermute x28 -> x30, starting transfers between devices: 49.7 us -> 52.8 us  [move(): return lax.ppermute(value, ('wide', 'narrow'), pairs)]
    ppermute x28 -> x30, waiting for transfers between devices: 16.5 us -> 14.4 us  [move(): return lax.ppermute(value, ('wide', 'narrow'), pairs)]
    pallas_call x8 -> x9, Pallas kernels: 15.4 us -> 16.4 us  [call(): pl.pallas_call(kernel, out_shape=[jax.ShapeDtypeStruct(shape, dtype) for...]
  transfers between devices with their start and end apart: 28 -> 30, of which waited for: 11 -> 8; matrix products, arithmetic and copies ran while one was open for 0% -> 0% of each run, Pallas kernels for 5% -> 14%
where the time goes in v5:
time: 87.4 us; the launch traced here: 87.2 us
  starting transfers between devices  52.8 us (60%)
  Pallas kernels  16.4 us (19%)
  waiting for transfers between devices  14.4 us (16%)
  other arithmetic  1.4 us (2%)
  local copies, waits for them, and re-layouts  1.23 us (1%)
  between operations  0.99 us (1%)
    ppermute x30, starting transfers between devices, move(): return lax.ppermute(value, ('wide', 'narrow'), pairs)  52.8 us
    pallas_call x9, Pallas kernels, call(): pl.pallas_call(kernel, out_shape=[jax.ShapeDtypeStruct(shape, dtype) for...  16.4 us
    ppermute x30, waiting for transfers between devices, move(): return lax.ppermute(value, ('wide', 'narrow'), pairs)  14.4 us
  transfers between devices with their start and end apart: 30, of which 8 were waited for; matrix products, arithmetic and copies ran while one was open for 0% of the time, Pallas kernels for 14%

profile of v5, /device:TPU:1, one launch (start us, length us, event | category | flops | bytes accessed | tf_op | source)
XLA Modules:
  0.0 87.2 jit_solution(14609619641607430256)
XLA Ops:
  0.7 1.2 %broadcast_select_fusion = (bf16[2,8,8,512]{3,2,1,0:T(8,128)(2,1)S(1)}, bf16[2,8,8,512]{3,2,1,0:T(8,128)(2,1)S(1)}) fusion(pred[8]{0:T(512)(128)(4,1)S(1)} %compare_compare_fusion, bf16[1,8,2,8,512]{4,3,2,1,0:T(8,128)(2,1)} %bitcast.63, bf16[1,8,2,8,512]{4,3,2,1,0:T(8,128)(2,1)} %bitcast.61), kind=kLoop, calls=%fused_computation.13 | loop fusion | flops 327680 | bytes 524296 | tf_op jit(solution)/shard_map/jit(_where)/select_n | solution.py:361
  1.9 9.4 %collective-permute-start.4 = (bf16[2,4,8,512]{3,2,1,0:T(8,128)(2,1)S(1)}, bf16[2,4,8,512]{3,2,1,0:T(8,128)(2,1)S(1)}, u32[]{:S(2)}, u32[]{:S(2)}) collective-permute-start(bf16[2,4,8,512]{3,2,1,0:T(8,128)(2,1)S(1)} %get-tuple-element.103), channel_id=1, source_target_pairs={{0,240},{1,241},{2,242},{3,243},{4,244},{5,245},{6,246},{7,247},{8... | collective-permute-start | bytes 196616 | tf_op jit(solution)/shard_map/ppermute | solution.py:30
  11.3 0.7 collective-permute-start.5
  12.0 0.4 collective-permute-start
  12.4 0.1 pad_add_fusion.flags
  12.5 4.9 %collective-permute-done = bf16[2,4,8,512]{3,2,1,0:T(8,128)(2,1)S(1)} collective-permute-done((bf16[2,4,8,512]{3,2,1,0:T(8,128)(2,1)S(1)}, bf16[2,4,8,512]{3,2,1,0:T(8,128)(2,1)S(1)}, u32[]{:S(2)}, u32[]{:S(2)}) %collective-permute-start) | collective-permute-done | bytes 65568 | tf_op jit(solution)/shard_map/ppermute | solution.py:30
  17.4 2.6 %collective-permute-start.3 = (bf16[2,64,512]{2,1,0:T(8,128)(2,1)S(1)}, bf16[2,64,512]{2,1,0:T(8,128)(2,1)S(1)}, u32[]{:S(2)}, u32[]{:S(2)}) collective-permute-start(bf16[2,64,512]{2,1,0:T(8,128)(2,1)S(1)} %bitcast.65), channel_id=1, source_target_pairs={{0,12},{1,13},{2,14},{3,15},{4,8},{5,9},{6,10},{7,11},{8,4},{9,5},... | collective-permute-start | bytes 393224 | tf_op jit(solution)/shard_map/ppermute | solution.py:30
  20.0 0.5 collective-permute-start.2
  20.5 0.3 collective-permute-start.1
  20.8 0.0 collective-permute-done.4
  20.8 0.0 collective-permute-done.5
  20.8 0.0 copy-start.1
  20.8 1.0 %copy-done.1 = bf16[512,512]{1,0:T(8,128)(2,1)S(1)} copy-done((bf16[512,512]{1,0:T(8,128)(2,1)S(1)}, bf16[512,512]{1,0:T(8,128)(2,1)}, u32[]{:S(2)}) %copy-start.1) | copy-done | bytes 524312
  21.8 1.3 %keeper_kernel.1 = (bf16[64,512]{1,0:T(8,128)(2,1)S(1)}, bf16[64,512]{1,0:T(8,128)(2,1)S(1)}, bf16[64,512]{1,0:T(8,128)(2,1)S(1)}, bf16[64,512]{1,0:T(8,128)(2,1)S(1)}) custom-call(s32[4]{0:T(128)S(1)} %pad_add_fusion.flags, bf16[2,64,512]{2,1,0:T(8,128)(2,1)S(1)} %bitcast.53, f32[2,512]{1,0:T(2,128)S(1)} %copy-done.5, bf16[512,1536]{1,0:T(8,128)(2,1)S(1)} %copy-done, ...), custom_call_target="tpu_custom_call" | custom-call | flops 300000000 | bytes 3000000 | tf_op jit(solution)/shard_map/keeper_kernel/pallas_call | solution.py:335
  23.1 1.3 %collective-permute-start.9 = (bf16[64,512]{1,0:T(8,128)(2,1)S(1)}, bf16[64,512]{1,0:T(8,128)(2,1)S(1)}, u32[]{:S(2)}, u32[]{:S(2)}) collective-permute-start(bf16[64,512]{1,0:T(8,128)(2,1)S(1)} %get-tuple-element.51), channel_id=1, source_target_pairs={{0,4},{1,5},{2,6},{3,7},{4,0},{5,1},{6,2},{7,3},{8,12},{9,13},{10,... | collective-permute-start | bytes 196616 | tf_op jit(solution)/shard_map/ppermute | solution.py:30
  24.4 2.4 %collective-permute-start.10 = (bf16[64,512]{1,0:T(8,128)(2,1)S(1)}, bf16[64,512]{1,0:T(8,128)(2,1)S(1)}, u32[]{:S(2)}, u32[]{:S(2)}) collective-permute-start(bf16[64,512]{1,0:T(8,128)(2,1)S(1)} %get-tuple-element.52), channel_id=1, source_target_pairs={{0,8},{1,9},{2,10},{3,11},{4,12},{5,13},{6,14},{7,15},{8,0},{9,1},... | collective-permute-start | bytes 196616 | tf_op jit(solution)/shard_map/ppermute | solution.py:30
  26.9 0.0 collective-permute-done.3.p3
  26.9 0.5 collective-permute-start.11
  27.4 1.1 %first_kernel.1 = (bf16[256,512]{1,0:T(8,128)(2,1)S(1)}, bf16[256,384]{1,0:T(8,128)(2,1)S(1)}, bf16[256,128]{1,0:T(8,128)(2,1)S(1)}) custom-call(s32[4]{0:T(128)S(1)} %pad_add_fusion.flags, bf16[2,64,512]{2,1,0:T(8,128)(2,1)S(1)} %bitcast.68, bf16[2,64,512]{2,1,0:T(8,128)(2,1)S(1)} %collective-permute-done.1.p1, ...), custom_call_target="tpu_custom_call" | custom-call | flops 10000000000 | bytes 3000000 | tf_op jit(solution)/shard_map/first_kernel/pallas_call | solution.py:335
  28.5 2.2 %collective-permute-start.8 = (bf16[2,64,512]{2,1,0:T(8,128)(2,1)S(1)}, bf16[2,64,512]{2,1,0:T(8,128)(2,1)S(1)}, u32[]{:S(2)}, u32[]{:S(2)}) collective-permute-start(bf16[2,64,512]{2,1,0:T(8,128)(2,1)S(1)} %bitcast.54), channel_id=1, source_target_pairs={{0,12},{1,13},{2,14},{3,15},{4,8},{5,9},{6,10},{7,11},{8,4},{9,5},... | collective-permute-start | bytes 393224 | tf_op jit(solution)/shard_map/ppermute | solution.py:30
  30.8 0.0 collective-permute-start.7
  30.8 1.1 %collective-permute-start.6 = (bf16[2,64,512]{2,1,0:T(8,128)(2,1)S(1)}, bf16[2,64,512]{2,1,0:T(8,128)(2,1)S(1)}, u32[]{:S(2)}, u32[]{:S(2)}) collective-permute-start(bf16[2,64,512]{2,1,0:T(8,128)(2,1)S(1)} %bitcast.56), channel_id=1, source_target_pairs={{0,4},{1,5},{2,6},{3,7},{4,0},{5,1},{6,2},{7,3},{8,12},{9,13},{10,... | collective-permute-start | bytes 393224 | tf_op jit(solution)/shard_map/ppermute | solution.py:30
  31.9 0.1 stack.62.spot
  32.0 0.0 collective-permute-done.10.s2
  32.0 0.0 collective-permute-done.11.s3
  32.0 6.3 %attention_kernel.1 = (bf16[128,512]{1,0:T(8,128)(2,1)S(1)}, bf16[128,512]{1,0:T(8,128)(2,1)S(1)}, bf16[128,512]{1,0:T(8,128)(2,1)S(1)}, bf16[128,512]{1,0:T(8,1...) custom-call(s32[4]{0:T(128)S(1)} %pad_add_fusion.flags, bf16[64,512]{1,0:T(8,128)(2,1)S(1)} %get-tuple-element.50.s0, ...), custom_call_target="tpu_custom_call" | custom-call | flops 1200000000 | bytes 6000000 | tf_op jit(solution)/shard_map/attention_kernel/pallas_call | solution.py:335
  38.2 0.0 collective-permute-done.7.p6
  38.3 2.6 %gradient_kernel.1 = (f32[16,72,128]{2,1,0:T(8,128)S(1)}, f32[16,72,128]{2,1,0:T(8,128)S(1)}) custom-call(s32[5]{0:T(128)S(1)} %stack.62.spot, bf16[2,64,512]{2,1,0:T(8,128)(2,1)S(1)} %bitcast.69, bf16[2,64,512]{2,1,0:T(8,128)(2,1)S(1)} %collective-permute-done.1.p1, bf16[2,64,512]{2,1,0:T(8,128)(2,1)S(1)} %collective-permute-done.2.p2, ...), custom_call_target="tpu_custom_call" | custom-call | flops 20000000000 | bytes 6000000 | tf_op jit(solution)/shard_map/gradient_kernel/pallas_call | solution.py:335
  40.8 0.0 copy-start.2
  40.9 2.5 %collective-permute-start.12 = (f32[16,72,128]{2,1,0:T(8,128)S(1)}, f32[16,72,128]{2,1,0:T(8,128)S(1)}, u32[]{:S(2)}, u32[]{:S(2)}) collective-permute-start(f32[16,72,128]{2,1,0:T(8,128)S(1)} %get-tuple-element.64), channel_id=1, source_target_pairs={{0,1},{1,0},{2,3},{3,2},{4,5},{5,4},{6,7},{7,6},{8,9},{9,8},{10,11... | collective-permute-start | bytes 1769480 | tf_op jit(solution)/shard_map/ppermute | solution.py:30
  43.3 0.1 collective-permute-start.16
  43.5 3.3 %collective-permute-start.17 = (bf16[128,512]{1,0:T(8,128)(2,1)S(1)}, bf16[128,512]{1,0:T(8,128)(2,1)S(1)}, u32[]{:S(2)}, u32[]{:S(2)}) collective-permute-start(bf16[128,512]{1,0:T(8,128)(2,1)S(1)} %get-tuple-element.58.r2), channel_id=1, source_target_pairs={{0,8},{1,9},{2,10},{3,11},{4,12},{5,13},{6,14},{7,15},{8,0},{9,1},... | collective-permute-start | bytes 393224 | tf_op jit(solution)/shard_map/ppermute | solution.py:30
  46.7 0.5 collective-permute-start.18
  47.2 0.1 slice_add_fusion
  47.3 0.1 collective-permute-start.15
  47.4 0.1 collective-permute-start.14
  47.5 0.9 %collective-permute-done.16.r1 = bf16[128,512]{1,0:T(8,128)(2,1)S(1)} collective-permute-done((bf16[128,512]{1,0:T(8,128)(2,1)S(1)}, bf16[128,512]{1,0:T(8,128)(2,1)S(1)}, u32[]{:S(2)}, u32[]{:S(2)}) %collective-permute-start.16) | collective-permute-done | bytes 131104 | tf_op jit(solution)/shard_map/ppermute | solution.py:30
  48.4 2.2 %collective-permute-start.13 = (f32[4,72,128]{2,1,0:T(8,128)S(1)}, f32[4,72,128]{2,1,0:T(8,128)S(1)}, u32[]{:S(2)}, u32[]{:S(2)}) collective-permute-start(f32[4,72,128]{2,1,0:T(8,128)S(1)} %get-tuple-element.93), channel_id=1, source_target_pairs={{0,16},{1,17},{2,18},{3,19},{4,20},{5,21},{6,22},{7,23},{8,24},{9,... | collective-permute-start | bytes 442376 | tf_op jit(solution)/shard_map/ppermute | solution.py:30
  50.6 2.5 %collective-permute-done.17.r2 = bf16[128,512]{1,0:T(8,128)(2,1)S(1)} collective-permute-done((bf16[128,512]{1,0:T(8,128)(2,1)S(1)}, bf16[128,512]{1,0:T(8,128)(2,1)S(1)}, u32[]{:S(2)}, u32[]{:S(2)}) %collective-permute-start.17) | collective-permute-done | bytes 131104 | tf_op jit(solution)/shard_map/ppermute | solution.py:30
  53.2 2.5 %collective-permute-done.18.r3 = bf16[128,512]{1,0:T(8,128)(2,1)S(1)} collective-permute-done((bf16[128,512]{1,0:T(8,128)(2,1)S(1)}, bf16[128,512]{1,0:T(8,128)(2,1)S(1)}, u32[]{:S(2)}, u32[]{:S(2)}) %collective-permute-start.18) | collective-permute-done | bytes 131104 | tf_op jit(solution)/shard_map/ppermute | solution.py:30
  55.7 1.3 %token_kernel.1 = bf16[2,128,512]{2,1,0:T(8,128)(2,1)S(1)} custom-call(s32[5]{0:T(128)S(1)} %stack.62.spot, bf16[128,512]{1,0:T(8,128)(2,1)S(1)} %get-tuple-element.56.r0, bf16[128,512]{1,0:T(8,128)(2,1)S(1)} %collective-permute-done.16.r1, bf16[128,512]{1,0:T(8,128)(2,1)S(1)} %collective-permute-done.17.r2, ...), custom_call_target="tpu_custom_call" | custom-call | flops 500000000 | bytes 4000000 | tf_op jit(solution)/shard_map/token_kernel/pallas_call | solution.py:335
  57.0 0.0 copy-start.3
  57.1 0.0 copy-start.4
  57.1 0.0 collective-permute-done.14.s2
  57.1 0.0 collective-permute-done.13.s1
  57.1 0.6 x_parts_kernel.1
  57.7 0.1 collective-permute-start.19
  57.8 3.3 %collective-permute-start.20 = (f32[72,128]{1,0:T(8,128)S(1)}, f32[72,128]{1,0:T(8,128)S(1)}, u32[]{:S(2)}, u32[]{:S(2)}) collective-permute-start(f32[72,128]{1,0:T(8,128)S(1)} %get-tuple-element.70), channel_id=1, source_target_pairs={{0,8},{1,9},{2,10},{3,11},{4,12},{5,13},{6,14},{7,15},{8,0},{9,1},... | collective-permute-start | bytes 110600 | tf_op jit(solution)/shard_map/ppermute | solution.py:30
  61.1 0.5 collective-permute-start.21
  61.7 5.8 %collective-permute-start.25 = (bf16[2,2,4,8,512]{4,3,2,0,1:T(8,128)(2,1)S(1)}, bf16[2,2,4,8,512]{4,3,2,0,1:T(8,128)(2,1)S(1)}, u32[]{:S(2)}, u32[]{:S(2)}) collective-permute-start(bf16[2,2,4,8,512]{4,3,2,0,1:T(8,128)(2,1)S(1)} %copy.24), channel_id=1, source_target_pairs={{0,240},{1,241},{2,242},{3,243},{4,244},{5,245},{6,246},{7,247},{8... | collective-permute-start | bytes 393224 | tf_op jit(solution)/shard_map/ppermute | solution.py:30
  67.5 0.7 z_parts_kernel.1
  68.2 0.1 collective-permute-start.22
  68.3 2.0 %collective-permute-start.23 = (f32[72,128]{1,0:T(8,128)S(1)}, f32[72,128]{1,0:T(8,128)S(1)}, u32[]{:S(2)}, u32[]{:S(2)}) collective-permute-start(f32[72,128]{1,0:T(8,128)S(1)} %get-tuple-element.74), channel_id=1, source_target_pairs={{0,128},{1,129},{2,130},{3,131},{4,132},{5,133},{6,134},{7,135},{8... | collective-permute-start | bytes 110600 | tf_op jit(solution)/shard_map/ppermute | solution.py:30
  70.3 3.6 %collective-permute-start.24 = (f32[72,128]{1,0:T(8,128)S(1)}, f32[72,128]{1,0:T(8,128)S(1)}, u32[]{:S(2)}, u32[]{:S(2)}) collective-permute-start(f32[72,128]{1,0:T(8,128)S(1)} %get-tuple-element.75), channel_id=1, source_target_pairs={{0,192},{1,193},{2,194},{3,195},{4,196},{5,197},{6,198},{7,199},{8... | collective-permute-start | bytes 110600 | tf_op jit(solution)/shard_map/ppermute | solution.py:30
  74.0 1.8 %collective-permute-done.23 = f32[72,128]{1,0:T(8,128)S(1)} collective-permute-done((f32[72,128]{1,0:T(8,128)S(1)}, f32[72,128]{1,0:T(8,128)S(1)}, u32[]{:S(2)}, u32[]{:S(2)}) %collective-permute-start.23) | collective-permute-done | bytes 36896 | tf_op jit(solution)/shard_map/ppermute | solution.py:30
  75.8 0.3 collective-permute-done.24
  76.1 4.9 %collective-permute-start.29 = (bf16[2,2,4,8,512]{4,3,2,0,1:T(8,128)(2,1)S(1)}, bf16[2,2,4,8,512]{4,3,2,0,1:T(8,128)(2,1)S(1)}, u32[]{:S(2)}, u32[]{:S(2)}) collective-permute-start(bf16[2,2,4,8,512]{4,3,2,0,1:T(8,128)(2,1)S(1)} %pad_maximum_fusion.3), channel_id=1, source_target_pairs={{0,1},{1,2},{2,3},{3,0},{4,5},{5,6},{6,7},{7,4},{8,9},{9,10},{10,1... | collective-permute-start | bytes 393224 | tf_op jit(solution)/shard_map/ppermute | solution.py:30
  81.0 0.1 collective-permute-start.28
  81.1 1.2 %collective-permute-start.27 = (f32[72,128]{1,0:T(8,128)S(1)}, f32[72,128]{1,0:T(8,128)S(1)}, u32[]{:S(2)}, u32[]{:S(2)}) collective-permute-start(f32[72,128]{1,0:T(8,128)S(1)} %add_add_fusion.near), channel_id=1, source_target_pairs={{0,2},{1,3},{2,0},{3,1},{4,6},{5,7},{6,4},{7,5},{8,10},{9,11},{10,... | collective-permute-start | bytes 110600 | tf_op jit(solution)/shard_map/ppermute | solution.py:30
  82.3 1.0 %collective-permute-start.26 = (f32[72,128]{1,0:T(8,128)S(1)}, f32[72,128]{1,0:T(8,128)S(1)}, u32[]{:S(2)}, u32[]{:S(2)}) collective-permute-start(f32[72,128]{1,0:T(8,128)S(1)} %add_add_fusion.near), channel_id=1, source_target_pairs={{0,1},{1,0},{2,3},{3,2},{4,5},{5,4},{6,7},{7,6},{8,9},{9,8},{10,11... | collective-permute-start | bytes 110600 | tf_op jit(solution)/shard_map/ppermute | solution.py:30
  83.3 1.3 %merge_kernel.1 = (bf16[8,16,512]{2,1,0:T(8,128)(2,1)}, bf16[8,16,512]{2,1,0:T(8,128)(2,1)}) custom-call(s32[5]{0:T(128)S(1)} %stack.62.spot, bf16[8,16,512]{2,1,0:T(8,128)(2,1)S(1)} %bitcast.62, bf16[8,16,512]{2,1,0:T(8,128)(2,1)S(1)} %bitcast.64, bf16[2,4,8,512]{3,2,1,0:T(8,128)(2,1)S(1)} %get-tuple-element.98.mine_high, ...), custom_call_target="tpu_custom_call" | custom-call | tf_op jit(solution)/shard_map/merge_kernel/pallas_call | solution.py:335
  84.6 0.6 collective-permute-done.28.both_in
  85.2 0.8 collective-permute-done.27.z_in
  86.0 1.2 %last_kernel.1 = (f32[24,512]{1,0:T(8,128)}, f32[8,512]{1,0:T(8,128)}, f32[2,8]{1,0:T(2,128)}) custom-call(s32[5]{0:T(128)S(1)} %stack.62.spot, f32[72,128]{1,0:T(8,128)S(1)} %add_add_fusion.near, f32[72,128]{1,0:T(8,128)S(1)} %collective-permute-done.26.core_in, f32[72,128]{1,0:T(8,128)S(1)} %collective-permute-done.27.z_in, ...), custom_call_target="tpu_custom_call" | custom-call | tf_op jit(solution)/shard_map/last_kernel/pallas_call | solution.py:335
  (34 shorter events, 0.2 us)
Async XLA Ops:
  0.6 20.1 %copy-start = (bf16[512,1536]{1,0:T(8,128)(2,1)S(1)}, bf16[512,1536]{1,0:T(8,128)(2,1)}, u32[]{:S(2)}) copy-start(bf16[512,1536]{1,0:T(8,128)(2,1)} %w_qkv.7) | copy-start | bytes 4718596
  0.6 20.1 %copy-start.5 = (f32[2,512]{1,0:T(2,128)S(1)}, f32[2,512]{1,0:T(2,128)}, u32[]{:S(2)}) copy-start(f32[2,512]{1,0:T(2,128)} %norm.7) | copy-start | bytes 12292
  1.9 18.8 %collective-permute-start.4 = (bf16[2,4,8,512]{3,2,1,0:T(8,128)(2,1)S(1)}, bf16[2,4,8,512]{3,2,1,0:T(8,128)(2,1)S(1)}, u32[]{:S(2)}, u32[]{:S(2)}) collective-permute-start(bf16[2,4,8,512]{3,2,1,0:T(8,128)(2,1)S(1)} %get-tuple-element.103), channel_id=1, source_target_pairs={{0,240},{1,241},{2,242},{3,243},{4,244},{5,245},{6,246},{7,247},{8... | collective-permute-start | bytes 196616 | tf_op jit(solution)/shard_map/ppermute | solution.py:30
  11.3 9.4 %collective-permute-start.5 = (bf16[2,4,8,512]{3,2,1,0:T(8,128)(2,1)S(1)}, bf16[2,4,8,512]{3,2,1,0:T(8,128)(2,1)S(1)}, u32[]{:S(2)}, u32[]{:S(2)}) collective-permute-start(bf16[2,4,8,512]{3,2,1,0:T(8,128)(2,1)S(1)} %get-tuple-element.104), channel_id=1, source_target_pairs={{0,243},{1,240},{2,241},{3,242},{4,247},{5,244},{6,245},{7,246},{8... | collective-permute-start | bytes 196616 | tf_op jit(solution)/shard_map/ppermute | solution.py:30
  12.0 5.4 %collective-permute-start = (bf16[2,4,8,512]{3,2,1,0:T(8,128)(2,1)S(1)}, bf16[2,4,8,512]{3,2,1,0:T(8,128)(2,1)S(1)}, u32[]{:S(2)}, u32[]{:S(2)}) collective-permute-start(bf16[2,4,8,512]{3,2,1,0:T(8,128)(2,1)S(1)} %get-tuple-element.106), channel_id=1, source_target_pairs={{0,3},{1,0},{2,1},{3,2},{4,7},{5,4},{6,5},{7,6},{8,11},{9,8},{10,9... | collective-permute-start | bytes 196616 | tf_op jit(solution)/shard_map/ppermute | solution.py:30
  17.4 9.5 %collective-permute-start.3 = (bf16[2,64,512]{2,1,0:T(8,128)(2,1)S(1)}, bf16[2,64,512]{2,1,0:T(8,128)(2,1)S(1)}, u32[]{:S(2)}, u32[]{:S(2)}) collective-permute-start(bf16[2,64,512]{2,1,0:T(8,128)(2,1)S(1)} %bitcast.65), channel_id=1, source_target_pairs={{0,12},{1,13},{2,14},{3,15},{4,8},{5,9},{6,10},{7,11},{8,4},{9,5},... | collective-permute-start | bytes 393224 | tf_op jit(solution)/shard_map/ppermute | solution.py:30
  20.0 7.4 %collective-permute-start.2 = (bf16[2,64,512]{2,1,0:T(8,128)(2,1)S(1)}, bf16[2,64,512]{2,1,0:T(8,128)(2,1)S(1)}, u32[]{:S(2)}, u32[]{:S(2)}) collective-permute-start(bf16[2,64,512]{2,1,0:T(8,128)(2,1)S(1)} %bitcast.66), channel_id=1, source_target_pairs={{0,8},{1,9},{2,10},{3,11},{4,12},{5,13},{6,14},{7,15},{8,0},{9,1},... | collective-permute-start | bytes 393224 | tf_op jit(solution)/shard_map/ppermute | solution.py:30
  20.5 6.9 %collective-permute-start.1 = (bf16[2,64,512]{2,1,0:T(8,128)(2,1)S(1)}, bf16[2,64,512]{2,1,0:T(8,128)(2,1)S(1)}, u32[]{:S(2)}, u32[]{:S(2)}) collective-permute-start(bf16[2,64,512]{2,1,0:T(8,128)(2,1)S(1)} %bitcast.67), channel_id=1, source_target_pairs={{0,4},{1,5},{2,6},{3,7},{4,0},{5,1},{6,2},{7,3},{8,12},{9,13},{10,... | collective-permute-start | bytes 393224 | tf_op jit(solution)/shard_map/ppermute | solution.py:30
  20.8 1.0 %copy-start.1 = (bf16[512,512]{1,0:T(8,128)(2,1)S(1)}, bf16[512,512]{1,0:T(8,128)(2,1)}, u32[]{:S(2)}) copy-start(bf16[512,512]{1,0:T(8,128)(2,1)} %w_proj.5) | copy-start | bytes 1572868
  23.1 7.6 %collective-permute-start.9 = (bf16[64,512]{1,0:T(8,128)(2,1)S(1)}, bf16[64,512]{1,0:T(8,128)(2,1)S(1)}, u32[]{:S(2)}, u32[]{:S(2)}) collective-permute-start(bf16[64,512]{1,0:T(8,128)(2,1)S(1)} %get-tuple-element.51), channel_id=1, source_target_pairs={{0,4},{1,5},{2,6},{3,7},{4,0},{5,1},{6,2},{7,3},{8,12},{9,13},{10,... | collective-permute-start | bytes 196616 | tf_op jit(solution)/shard_map/ppermute | solution.py:30
  24.4 7.5 %collective-permute-start.10 = (bf16[64,512]{1,0:T(8,128)(2,1)S(1)}, bf16[64,512]{1,0:T(8,128)(2,1)S(1)}, u32[]{:S(2)}, u32[]{:S(2)}) collective-permute-start(bf16[64,512]{1,0:T(8,128)(2,1)S(1)} %get-tuple-element.52), channel_id=1, source_target_pairs={{0,8},{1,9},{2,10},{3,11},{4,12},{5,13},{6,14},{7,15},{8,0},{9,1},... | collective-permute-start | bytes 196616 | tf_op jit(solution)/shard_map/ppermute | solution.py:30
  26.9 5.1 %collective-permute-start.11 = (bf16[64,512]{1,0:T(8,128)(2,1)S(1)}, bf16[64,512]{1,0:T(8,128)(2,1)S(1)}, u32[]{:S(2)}, u32[]{:S(2)}) collective-permute-start(bf16[64,512]{1,0:T(8,128)(2,1)S(1)} %get-tuple-element.53), channel_id=1, source_target_pairs={{0,12},{1,13},{2,14},{3,15},{4,8},{5,9},{6,10},{7,11},{8,4},{9,5},... | collective-permute-start | bytes 196616 | tf_op jit(solution)/shard_map/ppermute | solution.py:30
  28.5 9.7 %collective-permute-start.8 = (bf16[2,64,512]{2,1,0:T(8,128)(2,1)S(1)}, bf16[2,64,512]{2,1,0:T(8,128)(2,1)S(1)}, u32[]{:S(2)}, u32[]{:S(2)}) collective-permute-start(bf16[2,64,512]{2,1,0:T(8,128)(2,1)S(1)} %bitcast.54), channel_id=1, source_target_pairs={{0,12},{1,13},{2,14},{3,15},{4,8},{5,9},{6,10},{7,11},{8,4},{9,5},... | collective-permute-start | bytes 393224 | tf_op jit(solution)/shard_map/ppermute | solution.py:30
  30.8 7.5 %collective-permute-start.7 = (bf16[2,64,512]{2,1,0:T(8,128)(2,1)S(1)}, bf16[2,64,512]{2,1,0:T(8,128)(2,1)S(1)}, u32[]{:S(2)}, u32[]{:S(2)}) collective-permute-start(bf16[2,64,512]{2,1,0:T(8,128)(2,1)S(1)} %bitcast.55), channel_id=1, source_target_pairs={{0,8},{1,9},{2,10},{3,11},{4,12},{5,13},{6,14},{7,15},{8,0},{9,1},... | collective-permute-start | bytes 393224 | tf_op jit(solution)/shard_map/ppermute | solution.py:30
  30.8 7.5 %collective-permute-start.6 = (bf16[2,64,512]{2,1,0:T(8,128)(2,1)S(1)}, bf16[2,64,512]{2,1,0:T(8,128)(2,1)S(1)}, u32[]{:S(2)}, u32[]{:S(2)}) collective-permute-start(bf16[2,64,512]{2,1,0:T(8,128)(2,1)S(1)} %bitcast.56), channel_id=1, source_target_pairs={{0,4},{1,5},{2,6},{3,7},{4,0},{5,1},{6,2},{7,3},{8,12},{9,13},{10,... | collective-permute-start | bytes 393224 | tf_op jit(solution)/shard_map/ppermute | solution.py:30
  40.8 14.8 %copy-start.2 = (bf16[512,512]{1,0:T(8,128)(2,1)S(1)}, bf16[512,512]{1,0:T(8,128)(2,1)}, u32[]{:S(2)}) copy-start(bf16[512,512]{1,0:T(8,128)(2,1)} %w_proj.5) | copy-start | bytes 1572868
  40.9 6.3 %collective-permute-start.12 = (f32[16,72,128]{2,1,0:T(8,128)S(1)}, f32[16,72,128]{2,1,0:T(8,128)S(1)}, u32[]{:S(2)}, u32[]{:S(2)}) collective-permute-start(f32[16,72,128]{2,1,0:T(8,128)S(1)} %get-tuple-element.64), channel_id=1, source_target_pairs={{0,1},{1,0},{2,3},{3,2},{4,5},{5,4},{6,7},{7,6},{8,9},{9,8},{10,11... | collective-permute-start | bytes 1769480 | tf_op jit(solution)/shard_map/ppermute | solution.py:30
  43.3 5.1 %collective-permute-start.16 = (bf16[128,512]{1,0:T(8,128)(2,1)S(1)}, bf16[128,512]{1,0:T(8,128)(2,1)S(1)}, u32[]{:S(2)}, u32[]{:S(2)}) collective-permute-start(bf16[128,512]{1,0:T(8,128)(2,1)S(1)} %get-tuple-element.57.r1), channel_id=1, source_target_pairs={{0,4},{1,5},{2,6},{3,7},{4,0},{5,1},{6,2},{7,3},{8,12},{9,13},{10,... | collective-permute-start | bytes 393224 | tf_op jit(solution)/shard_map/ppermute | solution.py:30
  43.5 9.7 %collective-permute-start.17 = (bf16[128,512]{1,0:T(8,128)(2,1)S(1)}, bf16[128,512]{1,0:T(8,128)(2,1)S(1)}, u32[]{:S(2)}, u32[]{:S(2)}) collective-permute-start(bf16[128,512]{1,0:T(8,128)(2,1)S(1)} %get-tuple-element.58.r2), channel_id=1, source_target_pairs={{0,8},{1,9},{2,10},{3,11},{4,12},{5,13},{6,14},{7,15},{8,0},{9,1},... | collective-permute-start | bytes 393224 | tf_op jit(solution)/shard_map/ppermute | solution.py:30
  46.7 9.0 %collective-permute-start.18 = (bf16[128,512]{1,0:T(8,128)(2,1)S(1)}, bf16[128,512]{1,0:T(8,128)(2,1)S(1)}, u32[]{:S(2)}, u32[]{:S(2)}) collective-permute-start(bf16[128,512]{1,0:T(8,128)(2,1)S(1)} %get-tuple-element.59.r3), channel_id=1, source_target_pairs={{0,12},{1,13},{2,14},{3,15},{4,8},{5,9},{6,10},{7,11},{8,4},{9,5},... | collective-permute-start | bytes 393224 | tf_op jit(solution)/shard_map/ppermute | solution.py:30
  47.3 9.8 %collective-permute-start.15 = (f32[4,72,128]{2,1,0:T(8,128)S(1)}, f32[4,72,128]{2,1,0:T(8,128)S(1)}, u32[]{:S(2)}, u32[]{:S(2)}) collective-permute-start(f32[4,72,128]{2,1,0:T(8,128)S(1)} %get-tuple-element.91), channel_id=1, source_target_pairs={{0,48},{1,49},{2,50},{3,51},{4,52},{5,53},{6,54},{7,55},{8,56},{9,... | collective-permute-start | bytes 442376 | tf_op jit(solution)/shard_map/ppermute | solution.py:30
  47.4 9.7 %collective-permute-start.14 = (f32[4,72,128]{2,1,0:T(8,128)S(1)}, f32[4,72,128]{2,1,0:T(8,128)S(1)}, u32[]{:S(2)}, u32[]{:S(2)}) collective-permute-start(f32[4,72,128]{2,1,0:T(8,128)S(1)} %get-tuple-element.92), channel_id=1, source_target_pairs={{0,32},{1,33},{2,34},{3,35},{4,36},{5,37},{6,38},{7,39},{8,40},{9,... | collective-permute-start | bytes 442376 | tf_op jit(solution)/shard_map/ppermute | solution.py:30
  48.4 8.7 %collective-permute-start.13 = (f32[4,72,128]{2,1,0:T(8,128)S(1)}, f32[4,72,128]{2,1,0:T(8,128)S(1)}, u32[]{:S(2)}, u32[]{:S(2)}) collective-permute-start(f32[4,72,128]{2,1,0:T(8,128)S(1)} %get-tuple-element.93), channel_id=1, source_target_pairs={{0,16},{1,17},{2,18},{3,19},{4,20},{5,21},{6,22},{7,23},{8,24},{9,... | collective-permute-start | bytes 442376 | tf_op jit(solution)/shard_map/ppermute | solution.py:30
  57.0 26.2 %copy-start.3 = (bf16[1,1,8,16,512]{4,3,2,1,0:T(8,128)(2,1)S(1)}, bf16[1,1,8,16,512]{4,3,2,1,0:T(8,128)(2,1)}, u32[]{:S(2)}) copy-start(bf16[1,1,8,16,512]{4,3,2,1,0:T(8,128)(2,1)} %param.5) | copy-start | bytes 393220
  57.1 26.2 %copy-start.4 = (bf16[1,1,8,16,512]{4,3,2,1,0:T(8,128)(2,1)S(1)}, bf16[1,1,8,16,512]{4,3,2,1,0:T(8,128)(2,1)}, u32[]{:S(2)}) copy-start(bf16[1,1,8,16,512]{4,3,2,1,0:T(8,128)(2,1)} %param.9) | copy-start | bytes 393220
  57.7 9.8 %collective-permute-start.19 = (f32[72,128]{1,0:T(8,128)S(1)}, f32[72,128]{1,0:T(8,128)S(1)}, u32[]{:S(2)}, u32[]{:S(2)}) collective-permute-start(f32[72,128]{1,0:T(8,128)S(1)} %get-tuple-element.69), channel_id=1, source_target_pairs={{0,4},{1,5},{2,6},{3,7},{4,0},{5,1},{6,2},{7,3},{8,12},{9,13},{10,... | collective-permute-start | bytes 110600 | tf_op jit(solution)/shard_map/ppermute | solution.py:30
  57.8 9.7 %collective-permute-start.20 = (f32[72,128]{1,0:T(8,128)S(1)}, f32[72,128]{1,0:T(8,128)S(1)}, u32[]{:S(2)}, u32[]{:S(2)}) collective-permute-start(f32[72,128]{1,0:T(8,128)S(1)} %get-tuple-element.70), channel_id=1, source_target_pairs={{0,8},{1,9},{2,10},{3,11},{4,12},{5,13},{6,14},{7,15},{8,0},{9,1},... | collective-permute-start | bytes 110600 | tf_op jit(solution)/shard_map/ppermute | solution.py:30
  61.1 6.4 %collective-permute-start.21 = (f32[72,128]{1,0:T(8,128)S(1)}, f32[72,128]{1,0:T(8,128)S(1)}, u32[]{:S(2)}, u32[]{:S(2)}) collective-permute-start(f32[72,128]{1,0:T(8,128)S(1)} %get-tuple-element.71), channel_id=1, source_target_pairs={{0,12},{1,13},{2,14},{3,15},{4,8},{5,9},{6,10},{7,11},{8,4},{9,5},... | collective-permute-start | bytes 110600 | tf_op jit(solution)/shard_map/ppermute | solution.py:30
  61.7 14.4 %collective-permute-start.25 = (bf16[2,2,4,8,512]{4,3,2,0,1:T(8,128)(2,1)S(1)}, bf16[2,2,4,8,512]{4,3,2,0,1:T(8,128)(2,1)S(1)}, u32[]{:S(2)}, u32[]{:S(2)}) collective-permute-start(bf16[2,2,4,8,512]{4,3,2,0,1:T(8,128)(2,1)S(1)} %copy.24), channel_id=1, source_target_pairs={{0,240},{1,241},{2,242},{3,243},{4,244},{5,245},{6,246},{7,247},{8... | collective-permute-start | bytes 393224 | tf_op jit(solution)/shard_map/ppermute | solution.py:30
  68.2 5.8 %collective-permute-start.22 = (f32[72,128]{1,0:T(8,128)S(1)}, f32[72,128]{1,0:T(8,128)S(1)}, u32[]{:S(2)}, u32[]{:S(2)}) collective-permute-start(f32[72,128]{1,0:T(8,128)S(1)} %get-tuple-element.73), channel_id=1, source_target_pairs={{0,64},{1,65},{2,66},{3,67},{4,68},{5,69},{6,70},{7,71},{8,72},{9,... | collective-permute-start | bytes 110600 | tf_op jit(solution)/shard_map/ppermute | solution.py:30
  68.3 7.4 %collective-permute-start.23 = (f32[72,128]{1,0:T(8,128)S(1)}, f32[72,128]{1,0:T(8,128)S(1)}, u32[]{:S(2)}, u32[]{:S(2)}) collective-permute-start(f32[72,128]{1,0:T(8,128)S(1)} %get-tuple-element.74), channel_id=1, source_target_pairs={{0,128},{1,129},{2,130},{3,131},{4,132},{5,133},{6,134},{7,135},{8... | collective-permute-start | bytes 110600 | tf_op jit(solution)/shard_map/ppermute | solution.py:30
  70.3 5.7 %collective-permute-start.24 = (f32[72,128]{1,0:T(8,128)S(1)}, f32[72,128]{1,0:T(8,128)S(1)}, u32[]{:S(2)}, u32[]{:S(2)}) collective-permute-start(f32[72,128]{1,0:T(8,128)S(1)} %get-tuple-element.75), channel_id=1, source_target_pairs={{0,192},{1,193},{2,194},{3,195},{4,196},{5,197},{6,198},{7,199},{8... | collective-permute-start | bytes 110600 | tf_op jit(solution)/shard_map/ppermute | solution.py:30
  76.1 7.2 %collective-permute-start.29 = (bf16[2,2,4,8,512]{4,3,2,0,1:T(8,128)(2,1)S(1)}, bf16[2,2,4,8,512]{4,3,2,0,1:T(8,128)(2,1)S(1)}, u32[]{:S(2)}, u32[]{:S(2)}) collective-permute-start(bf16[2,2,4,8,512]{4,3,2,0,1:T(8,128)(2,1)S(1)} %pad_maximum_fusion.3), channel_id=1, source_target_pairs={{0,1},{1,2},{2,3},{3,0},{4,5},{5,6},{6,7},{7,4},{8,9},{9,10},{10,1... | collective-permute-start | bytes 393224 | tf_op jit(solution)/shard_map/ppermute | solution.py:30
  81.0 4.2 %collective-permute-start.28 = (f32[72,128]{1,0:T(8,128)S(1)}, f32[72,128]{1,0:T(8,128)S(1)}, u32[]{:S(2)}, u32[]{:S(2)}) collective-permute-start(f32[72,128]{1,0:T(8,128)S(1)} %add_add_fusion.near), channel_id=1, source_target_pairs={{0,3},{1,2},{2,1},{3,0},{4,7},{5,6},{6,5},{7,4},{8,11},{9,10},{10,... | collective-permute-start | bytes 110600 | tf_op jit(solution)/shard_map/ppermute | solution.py:30
  81.1 4.9 %collective-permute-start.27 = (f32[72,128]{1,0:T(8,128)S(1)}, f32[72,128]{1,0:T(8,128)S(1)}, u32[]{:S(2)}, u32[]{:S(2)}) collective-permute-start(f32[72,128]{1,0:T(8,128)S(1)} %add_add_fusion.near), channel_id=1, source_target_pairs={{0,2},{1,3},{2,0},{3,1},{4,6},{5,7},{6,4},{7,5},{8,10},{9,11},{10,... | collective-permute-start | bytes 110600 | tf_op jit(solution)/shard_map/ppermute | solution.py:30
  82.3 3.7 %collective-permute-start.26 = (f32[72,128]{1,0:T(8,128)S(1)}, f32[72,128]{1,0:T(8,128)S(1)}, u32[]{:S(2)}, u32[]{:S(2)}) collective-permute-start(f32[72,128]{1,0:T(8,128)S(1)} %add_add_fusion.near), channel_id=1, source_target_pairs={{0,1},{1,0},{2,3},{3,2},{4,5},{5,4},{6,7},{7,6},{8,9},{9,8},{10,11... | collective-permute-start | bytes 110600 | tf_op jit(solution)/shard_map/ppermute | solution.py:30

commit v6 on v4

--- a/solution.py
+++ b/solution.py
@@ -378,7 +378,6 @@
         moved=6_000_000,
     )
 
-    returned = [r0] + [move(rows, across_x(mask)) for mask, rows in ((1, r1), (2, r2), (3, r3))]
     keep, send = call(
         gradient_kernel,
         spot,
@@ -395,7 +394,11 @@
     received = move(send, across_narrow(1))
     blocks = [slice(4 * mask, 4 * mask + 4) for mask in range(4)]
     halves = [keep[block] + received[block] for block in blocks]
+    *halves, late2, late3 = lax.optimization_barrier((*halves, r2, r3))
     from_y = [halves[0]] + [move(halves[mask], across_y(mask)) for mask in (1, 2, 3)]
+    returned = [r0] + [
+        move(rows, across_x(mask)) for mask, rows in ((1, r1), (2, late2), (3, late3))
+    ]
     (back,) = call(
         token_kernel,
         spot,
@@ -404,34 +407,34 @@
         flops=500_000_000,
         moved=4_000_000,
     )
-    from_y[1], from_y[2], from_y[3], back = lax.optimization_barrier(
-        (from_y[1], from_y[2], from_y[3], back)
-    )
-    back = back.reshape(2, 4, 4, 8, C)
-    lower = move(back[:, 1], lambda p, n: (p, n + 1))
-    other_upper = move(back[:, 2], lambda p, n: (partner_of(p), n))
-    other_lower = move(back[:, 3], lambda p, n: (partner_of(p), n + 1))
-
     share = ((72, 128), F32)
     x_parts = call(x_parts_kernel, spot, from_y, [share] * 4)
     from_x = [x_parts[0]] + [move(x_parts[mask], across_x(mask)) for mask in (1, 2, 3)]
+    from_x[1], from_x[2], from_x[3], back = lax.optimization_barrier(
+        (from_x[1], from_x[2], from_x[3], back)
+    )
+    back = back.reshape(2, 2, 2, 4, 8, C)
+    low = move(back[:, :, 1], lambda p, n: (p, n + 1))
     z_parts = call(z_parts_kernel, spot, from_x, [share] * 4)
+    *z_parts, low = lax.optimization_barrier((*z_parts, low))
+    crossed = move(jnp.stack([back[:, 1, 0], low[:, 1]], 1), lambda p, n: (partner_of(p), n))
+    line = [z_parts[0]] + [move(z_parts[mask], across_z(mask)) for mask in (1, 2, 3)]
+    line[1], line[2], line[3], crossed = lax.optimization_barrier(
+        (line[1], line[2], line[3], crossed)
+    )
+    line = (line[0] + line[1]) + (line[2] + line[3])
+    last = [line] + [move(line, across_narrow(mask)) for mask in (1, 2, 3)]
     output, grad_inputs = call(
         merge_kernel,
         spot,
-        (own_inputs, own_upstream, back[:, 0], lower, other_upper, other_lower),
+        (own_inputs, own_upstream, back[:, 0, 0], low[:, 0], crossed[:, 0], crossed[:, 1]),
         [((8, 16, C), BF16)] * 2,
     )
-    line = [z_parts[0]] + [move(z_parts[mask], across_z(mask)) for mask in (1, 2, 3)]
-    line[1], line[2], line[3], output, grad_inputs = lax.optimization_barrier(
-        (line[1], line[2], line[3], output, grad_inputs)
-    )
-    line = (line[0] + line[1]) + (line[2] + line[3])
+    last[1], last[2], last[3], output, grad_inputs = lax.optimization_barrier(
+        (last[1], last[2], last[3], output, grad_inputs)
+    )
     grad_qkv, grad_proj, grad_norm = call(
-        last_kernel,
-        spot,
-        (line, *[move(line, across_narrow(mask)) for mask in (1, 2, 3)]),
-        [((24, C), F32), ((8, C), F32), ((2, 8), F32)],
+        last_kernel, spot, last, [((24, C), F32), ((8, C), F32), ((2, 8), F32)]
     )
     return (
         output[None, None], grad_inputs[None, None], grad_qkv.T, grad_proj.T, grad_norm

time: 85.2 us -> 88.3 us (1.036)
  waiting for transfers between devices: 16.5 us -> 19.4 us
    ppermute x28 -> x27, waiting for transfers between devices: 16.5 us -> 19.4 us  [move(): return lax.ppermute(value, ('wide', 'narrow'), pairs)]
    ppermute x28 -> x27, starting transfers between devices: 49.7 us -> 49.8 us  [move(): return lax.ppermute(value, ('wide', 'narrow'), pairs)]
  transfers between devices with their start and end apart: 28 -> 27, of which waited for: 11 -> 9; matrix products, arithmetic and copies ran while one was open for 0% -> 0% of each run, Pallas kernels for 5% -> 6%
where the time goes in v6:
time: 88.3 us; the launch traced here: 88.1 us
  starting transfers between devices  49.8 us (56%)
  waiting for transfers between devices  19.4 us (22%)
  Pallas kernels  15.4 us (17%)
  other arithmetic  1.4 us (2%)
  local copies, waits for them, and re-layouts  1.22 us (1%)
  between operations  0.93 us (1%)
    ppermute x27, starting transfers between devices, move(): return lax.ppermute(value, ('wide', 'narrow'), pairs)  49.8 us
    ppermute x27, waiting for transfers between devices, move(): return lax.ppermute(value, ('wide', 'narrow'), pairs)  19.4 us
    pallas_call x8, Pallas kernels, call(): pl.pallas_call(kernel, out_shape=[jax.ShapeDtypeStruct(shape, dtype) for...  15.4 us
  transfers between devices with their start and end apart: 27, of which 9 were waited for; matrix products, arithmetic and copies ran while one was open for 0% of the time, Pallas kernels for 6%

profile of v6, /device:TPU:1, one launch (start us, length us, event | category | flops | bytes accessed | tf_op | source)
XLA Modules:
  0.0 88.1 jit_solution(15587667124927999787)
XLA Ops:
  0.7 1.2 %broadcast_select_fusion = (bf16[2,8,8,512]{3,2,1,0:T(8,128)(2,1)S(1)}, bf16[2,8,8,512]{3,2,1,0:T(8,128)(2,1)S(1)}) fusion(pred[8]{0:T(512)(128)(4,1)S(1)} %compare_compare_fusion, bf16[1,8,2,8,512]{4,3,2,1,0:T(8,128)(2,1)} %bitcast.61, bf16[1,8,2,8,512]{4,3,2,1,0:T(8,128)(2,1)} %bitcast.59), kind=kLoop, calls=%fused_computation.14 | loop fusion | flops 327680 | bytes 524296 | tf_op jit(solution)/shard_map/jit(_where)/select_n | solution.py:353
  1.9 3.3 %collective-permute-start = (bf16[2,4,8,512]{3,2,1,0:T(8,128)(2,1)S(1)}, bf16[2,4,8,512]{3,2,1,0:T(8,128)(2,1)S(1)}, u32[]{:S(2)}, u32[]{:S(2)}) collective-permute-start(bf16[2,4,8,512]{3,2,1,0:T(8,128)(2,1)S(1)} %get-tuple-element.118), channel_id=1, source_target_pairs={{0,3},{1,0},{2,1},{3,2},{4,7},{5,4},{6,5},{7,6},{8,11},{9,8},{10,9... | collective-permute-start | bytes 196616 | tf_op jit(solution)/shard_map/ppermute | solution.py:30
  5.3 6.8 %collective-permute-start.4 = (bf16[2,4,8,512]{3,2,1,0:T(8,128)(2,1)S(1)}, bf16[2,4,8,512]{3,2,1,0:T(8,128)(2,1)S(1)}, u32[]{:S(2)}, u32[]{:S(2)}) collective-permute-start(bf16[2,4,8,512]{3,2,1,0:T(8,128)(2,1)S(1)} %get-tuple-element.115), channel_id=1, source_target_pairs={{0,240},{1,241},{2,242},{3,243},{4,244},{5,245},{6,246},{7,247},{8... | collective-permute-start | bytes 196616 | tf_op jit(solution)/shard_map/ppermute | solution.py:30
  12.1 0.4 collective-permute-start.5
  12.5 0.0 collective-permute-done
  12.6 2.6 %collective-permute-start.3 = (bf16[2,64,512]{2,1,0:T(8,128)(2,1)S(1)}, bf16[2,64,512]{2,1,0:T(8,128)(2,1)S(1)}, u32[]{:S(2)}, u32[]{:S(2)}) collective-permute-start(bf16[2,64,512]{2,1,0:T(8,128)(2,1)S(1)} %bitcast.63), channel_id=1, source_target_pairs={{0,12},{1,13},{2,14},{3,15},{4,8},{5,9},{6,10},{7,11},{8,4},{9,5},... | collective-permute-start | bytes 393224 | tf_op jit(solution)/shard_map/ppermute | solution.py:30
  15.1 0.5 collective-permute-start.2
  15.7 0.3 collective-permute-start.1
  15.9 0.1 pad_add_fusion.flags
  16.0 0.1 stack.62.spot
  16.1 0.0 collective-permute-done.4
  16.1 3.6 %collective-permute-done.5 = bf16[2,4,8,512]{3,2,1,0:T(8,128)(2,1)S(1)} collective-permute-done((bf16[2,4,8,512]{3,2,1,0:T(8,128)(2,1)S(1)}, bf16[2,4,8,512]{3,2,1,0:T(8,128)(2,1)S(1)}, u32[]{:S(2)}, u32[]{:S(2)}) %collective-permute-start.5) | collective-permute-done | bytes 65568 | tf_op jit(solution)/shard_map/ppermute | solution.py:30
  19.7 2.6 %collective-permute-start.8 = (bf16[2,64,512]{2,1,0:T(8,128)(2,1)S(1)}, bf16[2,64,512]{2,1,0:T(8,128)(2,1)S(1)}, u32[]{:S(2)}, u32[]{:S(2)}) collective-permute-start(bf16[2,64,512]{2,1,0:T(8,128)(2,1)S(1)} %bitcast.69), channel_id=1, source_target_pairs={{0,12},{1,13},{2,14},{3,15},{4,8},{5,9},{6,10},{7,11},{8,4},{9,5},... | collective-permute-start | bytes 393224 | tf_op jit(solution)/shard_map/ppermute | solution.py:30
  22.3 0.5 collective-permute-start.7
  22.8 0.3 collective-permute-start.6
  23.1 0.0 copy-start.3
  23.1 1.0 %copy-done.3 = bf16[512,512]{1,0:T(8,128)(2,1)S(1)} copy-done((bf16[512,512]{1,0:T(8,128)(2,1)S(1)}, bf16[512,512]{1,0:T(8,128)(2,1)}, u32[]{:S(2)}) %copy-start.3) | copy-done | bytes 524312
  24.1 1.1 %first_kernel.1 = (bf16[256,512]{1,0:T(8,128)(2,1)S(1)}, bf16[256,384]{1,0:T(8,128)(2,1)S(1)}, bf16[256,128]{1,0:T(8,128)(2,1)S(1)}) custom-call(s32[4]{0:T(128)S(1)} %pad_add_fusion.flags, bf16[2,64,512]{2,1,0:T(8,128)(2,1)S(1)} %bitcast.66, bf16[2,64,512]{2,1,0:T(8,128)(2,1)S(1)} %collective-permute-done.1.p1, ...), custom_call_target="tpu_custom_call" | custom-call | flops 10000000000 | bytes 3000000 | tf_op jit(solution)/shard_map/first_kernel/pallas_call | solution.py:327
  25.2 0.4 collective-permute-done.8.p3.p7
  25.6 2.1 %collective-permute-done.7.p2.p6 = bf16[2,64,512]{2,1,0:T(8,128)(2,1)S(1)} collective-permute-done((bf16[2,64,512]{2,1,0:T(8,128)(2,1)S(1)}, bf16[2,64,512]{2,1,0:T(8,128)(2,1)S(1)}, u32[]{:S(2)}, u32[]{:S(2)}) %collective-permute-start.7) | collective-permute-done | bytes 131104 | tf_op jit(solution)/shard_map/ppermute | solution.py:30
  27.7 6.7 %attention_kernel.1 = (bf16[128,512]{1,0:T(8,128)(2,1)S(1)}, bf16[128,512]{1,0:T(8,128)(2,1)S(1)}, bf16[128,512]{1,0:T(8,128)(2,1)S(1)}, bf16[128,512]{1,0:T(8,1...) custom-call(s32[4]{0:T(128)S(1)} %pad_add_fusion.flags, ...), custom_call_target="tpu_custom_call" | custom-call | flops 1200000000 | bytes 6000000 | tf_op jit(solution)/shard_map/attention_kernel/pallas_call | solution.py:327
  34.4 2.4 %gradient_kernel.1 = (f32[16,72,128]{2,1,0:T(8,128)S(1)}, f32[16,72,128]{2,1,0:T(8,128)S(1)}) custom-call(s32[5]{0:T(128)S(1)} %stack.62.spot, bf16[2,64,512]{2,1,0:T(8,128)(2,1)S(1)} %bitcast.67, bf16[2,64,512]{2,1,0:T(8,128)(2,1)S(1)} %collective-permute-done.1.p1, bf16[2,64,512]{2,1,0:T(8,128)(2,1)S(1)} %collective-permute-done.2.p2, ...), custom_call_target="tpu_custom_call" | custom-call | flops 20000000000 | bytes 6000000 | tf_op jit(solution)/shard_map/gradient_kernel/pallas_call | solution.py:327
  36.9 0.0 copy-start.4
  36.9 3.9 %collective-permute-start.9 = (f32[16,72,128]{2,1,0:T(8,128)S(1)}, f32[16,72,128]{2,1,0:T(8,128)S(1)}, u32[]{:S(2)}, u32[]{:S(2)}) collective-permute-start(f32[16,72,128]{2,1,0:T(8,128)S(1)} %get-tuple-element.65), channel_id=1, source_target_pairs={{0,1},{1,0},{2,3},{3,2},{4,5},{5,4},{6,7},{7,6},{8,9},{9,8},{10,11... | collective-permute-start | bytes 1769480 | tf_op jit(solution)/shard_map/ppermute | solution.py:30
  40.8 1.6 %collective-permute-done.9 = f32[16,72,128]{2,1,0:T(8,128)S(1)} collective-permute-done((f32[16,72,128]{2,1,0:T(8,128)S(1)}, f32[16,72,128]{2,1,0:T(8,128)S(1)}, u32[]{:S(2)}, u32[]{:S(2)}) %collective-permute-start.9) | collective-permute-done | bytes 589856 | tf_op jit(solution)/shard_map/ppermute | solution.py:30
  42.4 0.1 slice_add_fusion
  42.5 0.1 collective-permute-start.10
  42.6 0.1 collective-permute-start.11
  42.7 3.7 %collective-permute-start.12 = (f32[4,72,128]{2,1,0:T(8,128)S(1)}, f32[4,72,128]{2,1,0:T(8,128)S(1)}, u32[]{:S(2)}, u32[]{:S(2)}) collective-permute-start(f32[4,72,128]{2,1,0:T(8,128)S(1)} %get-tuple-element.69), channel_id=1, source_target_pairs={{0,48},{1,49},{2,50},{3,51},{4,52},{5,53},{6,54},{7,55},{8,56},{9,... | collective-permute-start | bytes 442376 | tf_op jit(solution)/shard_map/ppermute | solution.py:30
  46.4 0.4 collective-permute-start.16
  46.8 2.5 %collective-permute-start.17 = (bf16[128,512]{1,0:T(8,128)(2,1)S(1)}, bf16[128,512]{1,0:T(8,128)(2,1)S(1)}, u32[]{:S(2)}, u32[]{:S(2)}) collective-permute-start(bf16[128,512]{1,0:T(8,128)(2,1)S(1)} %get-tuple-element.74.r2), channel_id=1, source_target_pairs={{0,8},{1,9},{2,10},{3,11},{4,12},{5,13},{6,14},{7,15},{8,0},{9,1},... | collective-permute-start | bytes 393224 | tf_op jit(solution)/shard_map/ppermute | solution.py:30
  49.3 0.0 collective-permute-done.10.s1
  49.3 1.0 %collective-permute-start.18 = (bf16[128,512]{1,0:T(8,128)(2,1)S(1)}, bf16[128,512]{1,0:T(8,128)(2,1)S(1)}, u32[]{:S(2)}, u32[]{:S(2)}) collective-permute-start(bf16[128,512]{1,0:T(8,128)(2,1)S(1)} %get-tuple-element.75.r3), channel_id=1, source_target_pairs={{0,12},{1,13},{2,14},{3,15},{4,8},{5,9},{6,10},{7,11},{8,4},{9,5},... | collective-permute-start | bytes 393224 | tf_op jit(solution)/shard_map/ppermute | solution.py:30
  50.3 0.0 collective-permute-done.11.s2
  50.3 2.8 %collective-permute-done.12.s3 = f32[4,72,128]{2,1,0:T(8,128)S(1)} collective-permute-done((f32[4,72,128]{2,1,0:T(8,128)S(1)}, f32[4,72,128]{2,1,0:T(8,128)S(1)}, u32[]{:S(2)}, u32[]{:S(2)}) %collective-permute-start.12) | collective-permute-done | bytes 147488 | tf_op jit(solution)/shard_map/ppermute | solution.py:30
  53.1 0.6 x_parts_kernel.1
  53.7 0.5 collective-permute-start.13
  54.2 2.5 %collective-permute-start.14 = (f32[72,128]{1,0:T(8,128)S(1)}, f32[72,128]{1,0:T(8,128)S(1)}, u32[]{:S(2)}, u32[]{:S(2)}) collective-permute-start(f32[72,128]{1,0:T(8,128)S(1)} %get-tuple-element.72), channel_id=1, source_target_pairs={{0,8},{1,9},{2,10},{3,11},{4,12},{5,13},{6,14},{7,15},{8,0},{9,1},... | collective-permute-start | bytes 110600 | tf_op jit(solution)/shard_map/ppermute | solution.py:30
  56.7 0.0 collective-permute-done.16.r1
  56.7 1.0 %collective-permute-start.15 = (f32[72,128]{1,0:T(8,128)S(1)}, f32[72,128]{1,0:T(8,128)S(1)}, u32[]{:S(2)}, u32[]{:S(2)}) collective-permute-start(f32[72,128]{1,0:T(8,128)S(1)} %get-tuple-element.73), channel_id=1, source_target_pairs={{0,12},{1,13},{2,14},{3,15},{4,8},{5,9},{6,10},{7,11},{8,4},{9,5},... | collective-permute-start | bytes 110600 | tf_op jit(solution)/shard_map/ppermute | solution.py:30
  57.6 0.0 collective-permute-done.17.r2
  57.6 0.0 collective-permute-done.18.r3
  57.6 1.3 %token_kernel.1 = bf16[2,128,512]{2,1,0:T(8,128)(2,1)S(1)} custom-call(s32[5]{0:T(128)S(1)} %stack.62.spot, bf16[128,512]{1,0:T(8,128)(2,1)S(1)} %get-tuple-element.57.r0, bf16[128,512]{1,0:T(8,128)(2,1)S(1)} %collective-permute-done.16.r1, bf16[128,512]{1,0:T(8,128)(2,1)S(1)} %collective-permute-done.17.r2, ...), custom_call_target="tpu_custom_call" | custom-call | flops 500000000 | bytes 4000000 | tf_op jit(solution)/shard_map/token_kernel/pallas_call | solution.py:327
  59.0 0.0 copy-start.1
  59.0 0.0 copy-start.2
  59.0 0.0 collective-permute-done.14.m2
  59.0 1.6 %collective-permute-done.15.m3 = f32[72,128]{1,0:T(8,128)S(1)} collective-permute-done((f32[72,128]{1,0:T(8,128)S(1)}, f32[72,128]{1,0:T(8,128)S(1)}, u32[]{:S(2)}, u32[]{:S(2)}) %collective-permute-start.15) | collective-permute-done | bytes 36896 | tf_op jit(solution)/shard_map/ppermute | solution.py:30
  60.7 4.7 %collective-permute-start.19 = (bf16[2,2,4,8,512]{4,3,2,0,1:T(8,128)(2,1)S(1)}, bf16[2,2,4,8,512]{4,3,2,0,1:T(8,128)(2,1)S(1)}, u32[]{:S(2)}, u32[]{:S(2)}) collective-permute-start(bf16[2,2,4,8,512]{4,3,2,0,1:T(8,128)(2,1)S(1)} %copy_bitcast_fusion), channel_id=1, source_target_pairs={{0,1},{1,2},{2,3},{3,0},{4,5},{5,6},{6,7},{7,4},{8,9},{9,10},{10,1... | collective-permute-start | bytes 393224 | tf_op jit(solution)/shard_map/ppermute | solution.py:30
  65.4 0.7 z_parts_kernel.1
  66.1 1.2 %collective-permute-done.19 = bf16[2,2,4,8,512]{4,3,2,0,1:T(8,128)(2,1)S(1)} collective-permute-done((bf16[2,2,4,8,512]{4,3,2,0,1:T(8,128)(2,1)S(1)}, bf16[2,2,4,8,512]{4,3,2,0,1:T(8,128)(2,1)S(1)}, u32[]{:S(2)}, u32[]{:S(2)}) %collective-permute-start.19) | collective-permute-done | bytes 131104 | tf_op jit(solution)/shard_map/ppermute | solution.py:30
  67.4 3.4 %collective-permute-start.23 = (bf16[2,2,4,8,512]{4,3,2,0,1:T(8,128)(2,1)S(1)}, bf16[2,2,4,8,512]{4,3,2,0,1:T(8,128)(2,1)S(1)}, u32[]{:S(2)}, u32[]{:S(2)}) collective-permute-start(bf16[2,2,4,8,512]{4,3,2,0,1:T(8,128)(2,1)S(1)} %pad_maximum_fusion.3), channel_id=1, source_target_pairs={{0,240},{1,241},{2,242},{3,243},{4,244},{5,245},{6,246},{7,247},{8... | collective-permute-start | bytes 393224 | tf_op jit(solution)/shard_map/ppermute | solution.py:30
  70.8 2.1 %collective-permute-start.20 = (f32[72,128]{1,0:T(8,128)S(1)}, f32[72,128]{1,0:T(8,128)S(1)}, u32[]{:S(2)}, u32[]{:S(2)}) collective-permute-start(f32[72,128]{1,0:T(8,128)S(1)} %get-tuple-element.85), channel_id=1, source_target_pairs={{0,64},{1,65},{2,66},{3,67},{4,68},{5,69},{6,70},{7,71},{8,72},{9,... | collective-permute-start | bytes 110600 | tf_op jit(solution)/shard_map/ppermute | solution.py:30
  72.9 0.7 collective-permute-start.21
  73.6 2.8 %collective-permute-start.22 = (f32[72,128]{1,0:T(8,128)S(1)}, f32[72,128]{1,0:T(8,128)S(1)}, u32[]{:S(2)}, u32[]{:S(2)}) collective-permute-start(f32[72,128]{1,0:T(8,128)S(1)} %get-tuple-element.87), channel_id=1, source_target_pairs={{0,192},{1,193},{2,194},{3,195},{4,196},{5,197},{6,198},{7,199},{8... | collective-permute-start | bytes 110600 | tf_op jit(solution)/shard_map/ppermute | solution.py:30
  76.4 5.0 %collective-permute-done.20 = f32[72,128]{1,0:T(8,128)S(1)} collective-permute-done((f32[72,128]{1,0:T(8,128)S(1)}, f32[72,128]{1,0:T(8,128)S(1)}, u32[]{:S(2)}, u32[]{:S(2)}) %collective-permute-start.20) | collective-permute-done | bytes 36896 | tf_op jit(solution)/shard_map/ppermute | solution.py:30
  81.4 0.0 collective-permute-done.22
  81.4 0.0 collective-permute-done.23
  81.5 2.6 %collective-permute-start.26 = (f32[72,128]{1,0:T(8,128)S(1)}, f32[72,128]{1,0:T(8,128)S(1)}, u32[]{:S(2)}, u32[]{:S(2)}) collective-permute-start(f32[72,128]{1,0:T(8,128)S(1)} %add_add_fusion.near), channel_id=1, source_target_pairs={{0,3},{1,2},{2,1},{3,0},{4,7},{5,6},{6,5},{7,4},{8,11},{9,10},{10,... | collective-permute-start | bytes 110600 | tf_op jit(solution)/shard_map/ppermute | solution.py:30
  84.1 0.5 collective-permute-start.24
  84.6 1.3 %merge_kernel.1 = (bf16[8,16,512]{2,1,0:T(8,128)(2,1)}, bf16[8,16,512]{2,1,0:T(8,128)(2,1)}) custom-call(s32[5]{0:T(128)S(1)} %stack.62.spot, bf16[8,16,512]{2,1,0:T(8,128)(2,1)S(1)} %bitcast.60, bf16[8,16,512]{2,1,0:T(8,128)(2,1)S(1)} %bitcast.62, bf16[2,4,8,512]{3,2,1,0:T(8,128)(2,1)S(1)} %get-tuple-element.109.mine_high, ...), custom_call_target="tpu_custom_call" | custom-call | tf_op jit(solution)/shard_map/merge_kernel/pallas_call | solution.py:327
  85.9 0.0 collective-permute-done.26.both_in
  85.9 1.0 %collective-permute-done.25.z_in = f32[72,128]{1,0:T(8,128)S(1)} collective-permute-done((f32[72,128]{1,0:T(8,128)S(1)}, f32[72,128]{1,0:T(8,128)S(1)}, u32[]{:S(2)}, u32[]{:S(2)}) %collective-permute-start.25) | collective-permute-done | bytes 36896 | tf_op jit(solution)/shard_map/ppermute | solution.py:30
  86.9 0.0 collective-permute-done.24.core_in
  86.9 1.2 %last_kernel.1 = (f32[24,512]{1,0:T(8,128)}, f32[8,512]{1,0:T(8,128)}, f32[2,8]{1,0:T(2,128)}) custom-call(s32[5]{0:T(128)S(1)} %stack.62.spot, f32[72,128]{1,0:T(8,128)S(1)} %add_add_fusion.near, f32[72,128]{1,0:T(8,128)S(1)} %collective-permute-done.24.core_in, f32[72,128]{1,0:T(8,128)S(1)} %collective-permute-done.25.z_in, ...), custom_call_target="tpu_custom_call" | custom-call | tf_op jit(solution)/shard_map/last_kernel/pallas_call | solution.py:327
  (26 shorter events, 0.2 us)
Async XLA Ops:
  0.6 22.4 %copy-start = (bf16[512,1536]{1,0:T(8,128)(2,1)S(1)}, bf16[512,1536]{1,0:T(8,128)(2,1)}, u32[]{:S(2)}) copy-start(bf16[512,1536]{1,0:T(8,128)(2,1)} %w_qkv.7) | copy-start | bytes 4718596
  0.6 22.4 %copy-start.5 = (f32[2,512]{1,0:T(2,128)S(1)}, f32[2,512]{1,0:T(2,128)}, u32[]{:S(2)}) copy-start(f32[2,512]{1,0:T(2,128)} %norm.5) | copy-start | bytes 12292
  1.9 10.6 %collective-permute-start = (bf16[2,4,8,512]{3,2,1,0:T(8,128)(2,1)S(1)}, bf16[2,4,8,512]{3,2,1,0:T(8,128)(2,1)S(1)}, u32[]{:S(2)}, u32[]{:S(2)}) collective-permute-start(bf16[2,4,8,512]{3,2,1,0:T(8,128)(2,1)S(1)} %get-tuple-element.118), channel_id=1, source_target_pairs={{0,3},{1,0},{2,1},{3,2},{4,7},{5,4},{6,5},{7,6},{8,11},{9,8},{10,9... | collective-permute-start | bytes 196616 | tf_op jit(solution)/shard_map/ppermute | solution.py:30
  5.3 10.8 %collective-permute-start.4 = (bf16[2,4,8,512]{3,2,1,0:T(8,128)(2,1)S(1)}, bf16[2,4,8,512]{3,2,1,0:T(8,128)(2,1)S(1)}, u32[]{:S(2)}, u32[]{:S(2)}) collective-permute-start(bf16[2,4,8,512]{3,2,1,0:T(8,128)(2,1)S(1)} %get-tuple-element.115), channel_id=1, source_target_pairs={{0,240},{1,241},{2,242},{3,243},{4,244},{5,245},{6,246},{7,247},{8... | collective-permute-start | bytes 196616 | tf_op jit(solution)/shard_map/ppermute | solution.py:30
  12.1 7.6 %collective-permute-start.5 = (bf16[2,4,8,512]{3,2,1,0:T(8,128)(2,1)S(1)}, bf16[2,4,8,512]{3,2,1,0:T(8,128)(2,1)S(1)}, u32[]{:S(2)}, u32[]{:S(2)}) collective-permute-start(bf16[2,4,8,512]{3,2,1,0:T(8,128)(2,1)S(1)} %get-tuple-element.116), channel_id=1, source_target_pairs={{0,243},{1,240},{2,241},{3,242},{4,247},{5,244},{6,245},{7,246},{8... | collective-permute-start | bytes 196616 | tf_op jit(solution)/shard_map/ppermute | solution.py:30
  12.6 10.2 %collective-permute-start.3 = (bf16[2,64,512]{2,1,0:T(8,128)(2,1)S(1)}, bf16[2,64,512]{2,1,0:T(8,128)(2,1)S(1)}, u32[]{:S(2)}, u32[]{:S(2)}) collective-permute-start(bf16[2,64,512]{2,1,0:T(8,128)(2,1)S(1)} %bitcast.63), channel_id=1, source_target_pairs={{0,12},{1,13},{2,14},{3,15},{4,8},{5,9},{6,10},{7,11},{8,4},{9,5},... | collective-permute-start | bytes 393224 | tf_op jit(solution)/shard_map/ppermute | solution.py:30
  15.1 7.9 %collective-permute-start.2 = (bf16[2,64,512]{2,1,0:T(8,128)(2,1)S(1)}, bf16[2,64,512]{2,1,0:T(8,128)(2,1)S(1)}, u32[]{:S(2)}, u32[]{:S(2)}) collective-permute-start(bf16[2,64,512]{2,1,0:T(8,128)(2,1)S(1)} %bitcast.64), channel_id=1, source_target_pairs={{0,8},{1,9},{2,10},{3,11},{4,12},{5,13},{6,14},{7,15},{8,0},{9,1},... | collective-permute-start | bytes 393224 | tf_op jit(solution)/shard_map/ppermute | solution.py:30
  15.7 7.4 %collective-permute-start.1 = (bf16[2,64,512]{2,1,0:T(8,128)(2,1)S(1)}, bf16[2,64,512]{2,1,0:T(8,128)(2,1)S(1)}, u32[]{:S(2)}, u32[]{:S(2)}) collective-permute-start(bf16[2,64,512]{2,1,0:T(8,128)(2,1)S(1)} %bitcast.65), channel_id=1, source_target_pairs={{0,4},{1,5},{2,6},{3,7},{4,0},{5,1},{6,2},{7,3},{8,12},{9,13},{10,... | collective-permute-start | bytes 393224 | tf_op jit(solution)/shard_map/ppermute | solution.py:30
  19.7 5.9 %collective-permute-start.8 = (bf16[2,64,512]{2,1,0:T(8,128)(2,1)S(1)}, bf16[2,64,512]{2,1,0:T(8,128)(2,1)S(1)}, u32[]{:S(2)}, u32[]{:S(2)}) collective-permute-start(bf16[2,64,512]{2,1,0:T(8,128)(2,1)S(1)} %bitcast.69), channel_id=1, source_target_pairs={{0,12},{1,13},{2,14},{3,15},{4,8},{5,9},{6,10},{7,11},{8,4},{9,5},... | collective-permute-start | bytes 393224 | tf_op jit(solution)/shard_map/ppermute | solution.py:30
  22.3 5.4 %collective-permute-start.7 = (bf16[2,64,512]{2,1,0:T(8,128)(2,1)S(1)}, bf16[2,64,512]{2,1,0:T(8,128)(2,1)S(1)}, u32[]{:S(2)}, u32[]{:S(2)}) collective-permute-start(bf16[2,64,512]{2,1,0:T(8,128)(2,1)S(1)} %bitcast.70), channel_id=1, source_target_pairs={{0,8},{1,9},{2,10},{3,11},{4,12},{5,13},{6,14},{7,15},{8,0},{9,1},... | collective-permute-start | bytes 393224 | tf_op jit(solution)/shard_map/ppermute | solution.py:30
  22.8 4.9 %collective-permute-start.6 = (bf16[2,64,512]{2,1,0:T(8,128)(2,1)S(1)}, bf16[2,64,512]{2,1,0:T(8,128)(2,1)S(1)}, u32[]{:S(2)}, u32[]{:S(2)}) collective-permute-start(bf16[2,64,512]{2,1,0:T(8,128)(2,1)S(1)} %bitcast.71), channel_id=1, source_target_pairs={{0,4},{1,5},{2,6},{3,7},{4,0},{5,1},{6,2},{7,3},{8,12},{9,13},{10,... | collective-permute-start | bytes 393224 | tf_op jit(solution)/shard_map/ppermute | solution.py:30
  23.1 1.0 %copy-start.3 = (bf16[512,512]{1,0:T(8,128)(2,1)S(1)}, bf16[512,512]{1,0:T(8,128)(2,1)}, u32[]{:S(2)}) copy-start(bf16[512,512]{1,0:T(8,128)(2,1)} %w_proj.5) | copy-start | bytes 1572868
  36.9 20.8 %copy-start.4 = (bf16[512,512]{1,0:T(8,128)(2,1)S(1)}, bf16[512,512]{1,0:T(8,128)(2,1)}, u32[]{:S(2)}) copy-start(bf16[512,512]{1,0:T(8,128)(2,1)} %w_proj.5) | copy-start | bytes 1572868
  36.9 5.6 %collective-permute-start.9 = (f32[16,72,128]{2,1,0:T(8,128)S(1)}, f32[16,72,128]{2,1,0:T(8,128)S(1)}, u32[]{:S(2)}, u32[]{:S(2)}) collective-permute-start(f32[16,72,128]{2,1,0:T(8,128)S(1)} %get-tuple-element.65), channel_id=1, source_target_pairs={{0,1},{1,0},{2,3},{3,2},{4,5},{5,4},{6,7},{7,6},{8,9},{9,8},{10,11... | collective-permute-start | bytes 1769480 | tf_op jit(solution)/shard_map/ppermute | solution.py:30
  42.5 6.8 %collective-permute-start.10 = (f32[4,72,128]{2,1,0:T(8,128)S(1)}, f32[4,72,128]{2,1,0:T(8,128)S(1)}, u32[]{:S(2)}, u32[]{:S(2)}) collective-permute-start(f32[4,72,128]{2,1,0:T(8,128)S(1)} %get-tuple-element.67), channel_id=1, source_target_pairs={{0,16},{1,17},{2,18},{3,19},{4,20},{5,21},{6,22},{7,23},{8,24},{9,... | collective-permute-start | bytes 442376 | tf_op jit(solution)/shard_map/ppermute | solution.py:30
  42.6 7.7 %collective-permute-start.11 = (f32[4,72,128]{2,1,0:T(8,128)S(1)}, f32[4,72,128]{2,1,0:T(8,128)S(1)}, u32[]{:S(2)}, u32[]{:S(2)}) collective-permute-start(f32[4,72,128]{2,1,0:T(8,128)S(1)} %get-tuple-element.68), channel_id=1, source_target_pairs={{0,32},{1,33},{2,34},{3,35},{4,36},{5,37},{6,38},{7,39},{8,40},{9,... | collective-permute-start | bytes 442376 | tf_op jit(solution)/shard_map/ppermute | solution.py:30
  42.7 10.4 %collective-permute-start.12 = (f32[4,72,128]{2,1,0:T(8,128)S(1)}, f32[4,72,128]{2,1,0:T(8,128)S(1)}, u32[]{:S(2)}, u32[]{:S(2)}) collective-permute-start(f32[4,72,128]{2,1,0:T(8,128)S(1)} %get-tuple-element.69), channel_id=1, source_target_pairs={{0,48},{1,49},{2,50},{3,51},{4,52},{5,53},{6,54},{7,55},{8,56},{9,... | collective-permute-start | bytes 442376 | tf_op jit(solution)/shard_map/ppermute | solution.py:30
  46.4 10.2 %collective-permute-start.16 = (bf16[128,512]{1,0:T(8,128)(2,1)S(1)}, bf16[128,512]{1,0:T(8,128)(2,1)S(1)}, u32[]{:S(2)}, u32[]{:S(2)}) collective-permute-start(bf16[128,512]{1,0:T(8,128)(2,1)S(1)} %get-tuple-element.58.r1), channel_id=1, source_target_pairs={{0,4},{1,5},{2,6},{3,7},{4,0},{5,1},{6,2},{7,3},{8,12},{9,13},{10,... | collective-permute-start | bytes 393224 | tf_op jit(solution)/shard_map/ppermute | solution.py:30
  46.8 10.8 %collective-permute-start.17 = (bf16[128,512]{1,0:T(8,128)(2,1)S(1)}, bf16[128,512]{1,0:T(8,128)(2,1)S(1)}, u32[]{:S(2)}, u32[]{:S(2)}) collective-permute-start(bf16[128,512]{1,0:T(8,128)(2,1)S(1)} %get-tuple-element.74.r2), channel_id=1, source_target_pairs={{0,8},{1,9},{2,10},{3,11},{4,12},{5,13},{6,14},{7,15},{8,0},{9,1},... | collective-permute-start | bytes 393224 | tf_op jit(solution)/shard_map/ppermute | solution.py:30
  49.3 8.3 %collective-permute-start.18 = (bf16[128,512]{1,0:T(8,128)(2,1)S(1)}, bf16[128,512]{1,0:T(8,128)(2,1)S(1)}, u32[]{:S(2)}, u32[]{:S(2)}) collective-permute-start(bf16[128,512]{1,0:T(8,128)(2,1)S(1)} %get-tuple-element.75.r3), channel_id=1, source_target_pairs={{0,12},{1,13},{2,14},{3,15},{4,8},{5,9},{6,10},{7,11},{8,4},{9,5},... | collective-permute-start | bytes 393224 | tf_op jit(solution)/shard_map/ppermute | solution.py:30
  53.7 5.3 %collective-permute-start.13 = (f32[72,128]{1,0:T(8,128)S(1)}, f32[72,128]{1,0:T(8,128)S(1)}, u32[]{:S(2)}, u32[]{:S(2)}) collective-permute-start(f32[72,128]{1,0:T(8,128)S(1)} %get-tuple-element.71), channel_id=1, source_target_pairs={{0,4},{1,5},{2,6},{3,7},{4,0},{5,1},{6,2},{7,3},{8,12},{9,13},{10,... | collective-permute-start | bytes 110600 | tf_op jit(solution)/shard_map/ppermute | solution.py:30
  54.2 4.9 %collective-permute-start.14 = (f32[72,128]{1,0:T(8,128)S(1)}, f32[72,128]{1,0:T(8,128)S(1)}, u32[]{:S(2)}, u32[]{:S(2)}) collective-permute-start(f32[72,128]{1,0:T(8,128)S(1)} %get-tuple-element.72), channel_id=1, source_target_pairs={{0,8},{1,9},{2,10},{3,11},{4,12},{5,13},{6,14},{7,15},{8,0},{9,1},... | collective-permute-start | bytes 110600 | tf_op jit(solution)/shard_map/ppermute | solution.py:30
  56.7 4.0 %collective-permute-start.15 = (f32[72,128]{1,0:T(8,128)S(1)}, f32[72,128]{1,0:T(8,128)S(1)}, u32[]{:S(2)}, u32[]{:S(2)}) collective-permute-start(f32[72,128]{1,0:T(8,128)S(1)} %get-tuple-element.73), channel_id=1, source_target_pairs={{0,12},{1,13},{2,14},{3,15},{4,8},{5,9},{6,10},{7,11},{8,4},{9,5},... | collective-permute-start | bytes 110600 | tf_op jit(solution)/shard_map/ppermute | solution.py:30
  59.0 25.6 %copy-start.1 = (bf16[1,1,8,16,512]{4,3,2,1,0:T(8,128)(2,1)S(1)}, bf16[1,1,8,16,512]{4,3,2,1,0:T(8,128)(2,1)}, u32[]{:S(2)}) copy-start(bf16[1,1,8,16,512]{4,3,2,1,0:T(8,128)(2,1)} %param.5) | copy-start | bytes 393220
  59.0 25.6 %copy-start.2 = (bf16[1,1,8,16,512]{4,3,2,1,0:T(8,128)(2,1)S(1)}, bf16[1,1,8,16,512]{4,3,2,1,0:T(8,128)(2,1)}, u32[]{:S(2)}) copy-start(bf16[1,1,8,16,512]{4,3,2,1,0:T(8,128)(2,1)} %param.9) | copy-start | bytes 393220
  60.7 6.7 %collective-permute-start.19 = (bf16[2,2,4,8,512]{4,3,2,0,1:T(8,128)(2,1)S(1)}, bf16[2,2,4,8,512]{4,3,2,0,1:T(8,128)(2,1)S(1)}, u32[]{:S(2)}, u32[]{:S(2)}) collective-permute-start(bf16[2,2,4,8,512]{4,3,2,0,1:T(8,128)(2,1)S(1)} %copy_bitcast_fusion), channel_id=1, source_target_pairs={{0,1},{1,2},{2,3},{3,0},{4,5},{5,6},{6,7},{7,4},{8,9},{9,10},{10,1... | collective-permute-start | bytes 393224 | tf_op jit(solution)/shard_map/ppermute | solution.py:30
  67.4 14.1 %collective-permute-start.23 = (bf16[2,2,4,8,512]{4,3,2,0,1:T(8,128)(2,1)S(1)}, bf16[2,2,4,8,512]{4,3,2,0,1:T(8,128)(2,1)S(1)}, u32[]{:S(2)}, u32[]{:S(2)}) collective-permute-start(bf16[2,2,4,8,512]{4,3,2,0,1:T(8,128)(2,1)S(1)} %pad_maximum_fusion.3), channel_id=1, source_target_pairs={{0,240},{1,241},{2,242},{3,243},{4,244},{5,245},{6,246},{7,247},{8... | collective-permute-start | bytes 393224 | tf_op jit(solution)/shard_map/ppermute | solution.py:30
  70.8 10.7 %collective-permute-start.20 = (f32[72,128]{1,0:T(8,128)S(1)}, f32[72,128]{1,0:T(8,128)S(1)}, u32[]{:S(2)}, u32[]{:S(2)}) collective-permute-start(f32[72,128]{1,0:T(8,128)S(1)} %get-tuple-element.85), channel_id=1, source_target_pairs={{0,64},{1,65},{2,66},{3,67},{4,68},{5,69},{6,70},{7,71},{8,72},{9,... | collective-permute-start | bytes 110600 | tf_op jit(solution)/shard_map/ppermute | solution.py:30
  72.9 8.6 %collective-permute-start.21 = (f32[72,128]{1,0:T(8,128)S(1)}, f32[72,128]{1,0:T(8,128)S(1)}, u32[]{:S(2)}, u32[]{:S(2)}) collective-permute-start(f32[72,128]{1,0:T(8,128)S(1)} %get-tuple-element.86), channel_id=1, source_target_pairs={{0,128},{1,129},{2,130},{3,131},{4,132},{5,133},{6,134},{7,135},{8... | collective-permute-start | bytes 110600 | tf_op jit(solution)/shard_map/ppermute | solution.py:30
  73.6 7.8 %collective-permute-start.22 = (f32[72,128]{1,0:T(8,128)S(1)}, f32[72,128]{1,0:T(8,128)S(1)}, u32[]{:S(2)}, u32[]{:S(2)}) collective-permute-start(f32[72,128]{1,0:T(8,128)S(1)} %get-tuple-element.87), channel_id=1, source_target_pairs={{0,192},{1,193},{2,194},{3,195},{4,196},{5,197},{6,198},{7,199},{8... | collective-permute-start | bytes 110600 | tf_op jit(solution)/shard_map/ppermute | solution.py:30
  81.5 4.4 %collective-permute-start.26 = (f32[72,128]{1,0:T(8,128)S(1)}, f32[72,128]{1,0:T(8,128)S(1)}, u32[]{:S(2)}, u32[]{:S(2)}) collective-permute-start(f32[72,128]{1,0:T(8,128)S(1)} %add_add_fusion.near), channel_id=1, source_target_pairs={{0,3},{1,2},{2,1},{3,0},{4,7},{5,6},{6,5},{7,4},{8,11},{9,10},{10,... | collective-permute-start | bytes 110600 | tf_op jit(solution)/shard_map/ppermute | solution.py:30
  84.1 2.8 %collective-permute-start.25 = (f32[72,128]{1,0:T(8,128)S(1)}, f32[72,128]{1,0:T(8,128)S(1)}, u32[]{:S(2)}, u32[]{:S(2)}) collective-permute-start(f32[72,128]{1,0:T(8,128)S(1)} %add_add_fusion.near), channel_id=1, source_target_pairs={{0,2},{1,3},{2,0},{3,1},{4,6},{5,7},{6,4},{7,5},{8,10},{9,11},{10,... | collective-permute-start | bytes 110600 | tf_op jit(solution)/shard_map/ppermute | solution.py:30
  84.1 2.8 %collective-permute-start.24 = (f32[72,128]{1,0:T(8,128)S(1)}, f32[72,128]{1,0:T(8,128)S(1)}, u32[]{:S(2)}, u32[]{:S(2)}) collective-permute-start(f32[72,128]{1,0:T(8,128)S(1)} %add_add_fusion.near), channel_id=1, source_target_pairs={{0,1},{1,0},{2,3},{3,2},{4,5},{5,4},{6,7},{7,6},{8,9},{9,8},{10,11... | collective-permute-start | bytes 110600 | tf_op jit(solution)/shard_map/ppermute | solution.py:30

commit v7 on v4

--- a/solution.py
+++ b/solution.py
@@ -48,6 +48,22 @@
 
 def across_narrow(mask):
     return lambda p, n: (p, n ^ mask)
+
+
+def index_of(z, y, x, column):
+    return (16 * z + 4 * y + x) * 4 + column
+
+
+X_GROUPS = [
+    [index_of(z, y, x, n) for x in range(4)] for z in range(4) for y in range(4) for n in range(4)
+]
+Z_GROUPS = [
+    [index_of(z, y, x, n) for z in range(4)] for y in range(4) for x in range(4) for n in range(4)
+]
+
+
+def exchange(value, groups):
+    return lax.all_to_all(value, ("wide", "narrow"), 0, 0, axis_index_groups=groups)
 
 
 def dot(a, b):
@@ -221,45 +237,27 @@
                     out[block, 64:, :] = jnp.zeros((8, 128), F32)
 
 
-def x_parts_kernel(spot, s0, s1, s2, s3, *outs):
-    x = spot[0]
-    for across, out in enumerate(outs):
-        to_x = x ^ across
-        out[...] = (s0[to_x] + s1[to_x]) + (s2[to_x] + s3[to_x])
-
-
-def z_parts_kernel(spot, m0, m1, m2, m3, *outs):
-    x, y, z = spot[0], spot[1], spot[3]
-    pieces = (m0, m1, m2, m3)
-
-    def from_member(member, rows):
-        across = member ^ x
-        picked = pieces[0][rows, :]
-        for index in range(1, 4):
-            picked = jnp.where(across == index, pieces[index][rows, :], picked)
-        return picked
-
-    total = (m0[64:, :] + m1[64:, :]) + (m2[64:, :] + m3[64:, :])
-    proj = [from_member(member, slice(48, 64)) for member in range(4)]
+def x_parts_kernel(spot, s0, s1, s2, s3, out):
+    out[...] = (s0[...] + s1[...]) + (s2[...] + s3[...])
+
+
+def z_parts_kernel(spot, pieces, out):
+    x, y = spot[0], spot[1]
+    total = (pieces[0, 64:] + pieces[1, 64:]) + (pieces[2, 64:] + pieces[3, 64:])
     for to_z in range(4):
-        block = []
         for side in range(2):
             for slot in range(3):
                 owner = lax.rem(48 * to_z + 12 * y + 3 * x + slot, 64) // 16
-                top = 24 * side + 8 * slot
-                block.append(from_member(owner, slice(top, top + 8)))
-        rows = slice(8 * (to_z // 2), 8 * (to_z // 2) + 8)
+                rows = slice(24 * side + 8 * slot, 24 * side + 8 * slot + 8)
+                out[to_z, rows, :] = pieces[owner, rows, :]
+        rows = slice(48 + 8 * (to_z // 2), 56 + 8 * (to_z // 2))
         lanes = slice(64 * (to_z % 2), 64 * (to_z % 2) + 64)
         for pair in range(2):
-            block.append(
-                jnp.concatenate([proj[2 * pair][rows, lanes], proj[2 * pair + 1][rows, lanes]], 1)
+            out[to_z, 48 + 8 * pair : 56 + 8 * pair, :] = jnp.concatenate(
+                [pieces[2 * pair, rows, lanes], pieces[2 * pair + 1, rows, lanes]], 1
             )
         lanes = slice(32 * to_z, 32 * to_z + 32)
-        block.append(jnp.concatenate([total[:, lanes], jnp.zeros((8, 96), F32)], 1))
-        block = jnp.concatenate(block, 0)
-        for across in range(4):
-            ahead = (to_z ^ z) == across
-            outs[across][...] = jnp.where(ahead, block, outs[across][...]) if to_z else block
+        out[to_z, 64:, :] = jnp.concatenate([total[:, lanes], jnp.zeros((8, 96), F32)], 1)
 
 
 def last_kernel(spot, near, core_in, z_in, both_in, g_out, p_out, n_out):
@@ -412,21 +410,19 @@
     other_upper = move(back[:, 2], lambda p, n: (partner_of(p), n))
     other_lower = move(back[:, 3], lambda p, n: (partner_of(p), n + 1))
 
-    share = ((72, 128), F32)
-    x_parts = call(x_parts_kernel, spot, from_y, [share] * 4)
-    from_x = [x_parts[0]] + [move(x_parts[mask], across_x(mask)) for mask in (1, 2, 3)]
-    z_parts = call(z_parts_kernel, spot, from_x, [share] * 4)
+    shares = ((4, 72, 128), F32)
+    (x_parts,) = call(x_parts_kernel, spot, from_y, [shares])
+    (z_parts,) = call(z_parts_kernel, spot, (exchange(x_parts, X_GROUPS),), [shares])
     output, grad_inputs = call(
         merge_kernel,
         spot,
         (own_inputs, own_upstream, back[:, 0], lower, other_upper, other_lower),
         [((8, 16, C), BF16)] * 2,
     )
-    line = [z_parts[0]] + [move(z_parts[mask], across_z(mask)) for mask in (1, 2, 3)]
-    line[1], line[2], line[3], output, grad_inputs = lax.optimization_barrier(
-        (line[1], line[2], line[3], output, grad_inputs)
-    )
-    line = (line[0] + line[1]) + (line[2] + line[3])
+    line, output, grad_inputs = lax.optimization_barrier(
+        (exchange(z_parts, Z_GROUPS), output, grad_inputs)
+    )
+    line = jnp.sum(line, 0)
     grad_qkv, grad_proj, grad_norm = call(
         last_kernel,
         spot,

time: 85.2 us -> 90.8 us (1.066)
  blocking collectives: 0 us -> 7.7 us
  starting transfers between devices: 49.7 us -> 44.1 us
  waiting for transfers between devices: 16.5 us -> 19.2 us
    ppermute x28 -> x22, starting transfers between devices: 49.7 us -> 40.8 us  [move(): return lax.ppermute(value, ('wide', 'narrow'), pairs)]
    all_to_all x0 -> x1, blocking collectives: none -> 7.7 us  [exchange(): lax.all_to_all(value, ('wide', 'narrow'), 0, 0, axis_index_groups=groups)]
    all_to_all x0 -> x1, starting transfers between devices: none -> 3.33 us  [exchange(): lax.all_to_all(value, ('wide', 'narrow'), 0, 0, axis_index_groups=groups)]
    ppermute x28 -> x22, waiting for transfers between devices: 16.5 us -> 19.2 us  [move(): return lax.ppermute(value, ('wide', 'narrow'), pairs)]
  transfers between devices with their start and end apart: 28 -> 23, of which waited for: 11 -> 11; matrix products, arithmetic and copies ran while one was open for 0% -> 0% of each run, Pallas kernels for 5% -> 4%
where the time goes in v7:
time: 90.8 us; the launch traced here: 90.5 us
  starting transfers between devices  44.1 us (49%)
  waiting for transfers between devices  19.2 us (21%)
  Pallas kernels  16 us (18%)
  blocking collectives  7.7 us (8%)
  other arithmetic  1.38 us (2%)
  local copies, waits for them, and re-layouts  1.2 us (1%)
    ppermute x22, starting transfers between devices, move(): return lax.ppermute(value, ('wide', 'narrow'), pairs)  40.8 us
    ppermute x22, waiting for transfers between devices, move(): return lax.ppermute(value, ('wide', 'narrow'), pairs)  19.2 us
    pallas_call x8, Pallas kernels, call(): pl.pallas_call(kernel, out_shape=[jax.ShapeDtypeStruct(shape, dtype) for...  16 us
    all_to_all x1, blocking collectives, exchange(): lax.all_to_all(value, ('wide', 'narrow'), 0, 0, axis_index_groups=groups)  7.7 us
    all_to_all x1, starting transfers between devices, exchange(): lax.all_to_all(value, ('wide', 'narrow'), 0, 0, axis_index_groups=groups)  3.33 us
  transfers between devices with their start and end apart: 23, of which 11 were waited for; matrix products, arithmetic and copies ran while one was open for 0% of the time, Pallas kernels for 4%

profile of v7, /device:TPU:1, one launch (start us, length us, event | category | flops | bytes accessed | tf_op | source)
XLA Modules:
  0.0 90.5 jit_solution(8176411405478299386)
XLA Ops:
  0.7 1.2 %broadcast_select_fusion = (bf16[2,8,8,512]{3,2,1,0:T(8,128)(2,1)S(1)}, bf16[2,8,8,512]{3,2,1,0:T(8,128)(2,1)S(1)}) fusion(pred[8]{0:T(512)(128)(4,1)S(1)} %compare_compare_fusion, bf16[1,8,2,8,512]{4,3,2,1,0:T(8,128)(2,1)} %bitcast.60, bf16[1,8,2,8,512]{4,3,2,1,0:T(8,128)(2,1)} %bitcast.58), kind=kLoop, calls=%fused_computation.12 | loop fusion | flops 327680 | bytes 524296 | tf_op jit(solution)/shard_map/jit(_where)/select_n | solution.py:351
  1.9 3.3 %collective-permute-start = (bf16[2,4,8,512]{3,2,1,0:T(8,128)(2,1)S(1)}, bf16[2,4,8,512]{3,2,1,0:T(8,128)(2,1)S(1)}, u32[]{:S(2)}, u32[]{:S(2)}) collective-permute-start(bf16[2,4,8,512]{3,2,1,0:T(8,128)(2,1)S(1)} %get-tuple-element.66), channel_id=1, source_target_pairs={{0,3},{1,0},{2,1},{3,2},{4,7},{5,4},{6,5},{7,6},{8,11},{9,8},{10,9... | collective-permute-start | bytes 196616 | tf_op jit(solution)/shard_map/ppermute | solution.py:30
  5.3 6.8 %collective-permute-start.4 = (bf16[2,4,8,512]{3,2,1,0:T(8,128)(2,1)S(1)}, bf16[2,4,8,512]{3,2,1,0:T(8,128)(2,1)S(1)}, u32[]{:S(2)}, u32[]{:S(2)}) collective-permute-start(bf16[2,4,8,512]{3,2,1,0:T(8,128)(2,1)S(1)} %get-tuple-element.63), channel_id=1, source_target_pairs={{0,240},{1,241},{2,242},{3,243},{4,244},{5,245},{6,246},{7,247},{8... | collective-permute-start | bytes 196616 | tf_op jit(solution)/shard_map/ppermute | solution.py:30
  12.1 0.4 collective-permute-start.5
  12.5 0.0 collective-permute-done
  12.6 2.6 %collective-permute-start.3 = (bf16[2,64,512]{2,1,0:T(8,128)(2,1)S(1)}, bf16[2,64,512]{2,1,0:T(8,128)(2,1)S(1)}, u32[]{:S(2)}, u32[]{:S(2)}) collective-permute-start(bf16[2,64,512]{2,1,0:T(8,128)(2,1)S(1)} %bitcast.62), channel_id=1, source_target_pairs={{0,12},{1,13},{2,14},{3,15},{4,8},{5,9},{6,10},{7,11},{8,4},{9,5},... | collective-permute-start | bytes 393224 | tf_op jit(solution)/shard_map/ppermute | solution.py:30
  15.1 0.5 collective-permute-start.2
  15.7 0.3 collective-permute-start.1
  15.9 0.1 pad_add_fusion.flags
  16.0 0.1 stack.59.spot
  16.1 0.0 collective-permute-done.4
  16.1 3.6 %collective-permute-done.5 = bf16[2,4,8,512]{3,2,1,0:T(8,128)(2,1)S(1)} collective-permute-done((bf16[2,4,8,512]{3,2,1,0:T(8,128)(2,1)S(1)}, bf16[2,4,8,512]{3,2,1,0:T(8,128)(2,1)S(1)}, u32[]{:S(2)}, u32[]{:S(2)}) %collective-permute-start.5) | collective-permute-done | bytes 65568 | tf_op jit(solution)/shard_map/ppermute | solution.py:30
  19.7 2.6 %collective-permute-start.8 = (bf16[2,64,512]{2,1,0:T(8,128)(2,1)S(1)}, bf16[2,64,512]{2,1,0:T(8,128)(2,1)S(1)}, u32[]{:S(2)}, u32[]{:S(2)}) collective-permute-start(bf16[2,64,512]{2,1,0:T(8,128)(2,1)S(1)} %bitcast.68), channel_id=1, source_target_pairs={{0,12},{1,13},{2,14},{3,15},{4,8},{5,9},{6,10},{7,11},{8,4},{9,5},... | collective-permute-start | bytes 393224 | tf_op jit(solution)/shard_map/ppermute | solution.py:30
  22.3 0.5 collective-permute-start.7
  22.8 0.0 collective-permute-done.3.p3
  22.8 0.3 collective-permute-start.6
  23.1 0.0 collective-permute-done.2.p2
  23.1 0.0 collective-permute-done.1.p1
  23.1 0.0 copy-start.3
  23.1 1.0 %copy-done.3 = bf16[512,512]{1,0:T(8,128)(2,1)S(1)} copy-done((bf16[512,512]{1,0:T(8,128)(2,1)S(1)}, bf16[512,512]{1,0:T(8,128)(2,1)}, u32[]{:S(2)}) %copy-start.3) | copy-done | bytes 524312
  24.1 1.1 %first_kernel.1 = (bf16[256,512]{1,0:T(8,128)(2,1)S(1)}, bf16[256,384]{1,0:T(8,128)(2,1)S(1)}, bf16[256,128]{1,0:T(8,128)(2,1)S(1)}) custom-call(s32[4]{0:T(128)S(1)} %pad_add_fusion.flags, bf16[2,64,512]{2,1,0:T(8,128)(2,1)S(1)} %bitcast.65, bf16[2,64,512]{2,1,0:T(8,128)(2,1)S(1)} %collective-permute-done.1.p1, ...), custom_call_target="tpu_custom_call" | custom-call | flops 10000000000 | bytes 3000000 | tf_op jit(solution)/shard_map/first_kernel/pallas_call | solution.py:325
  25.2 0.4 collective-permute-done.8.p3.p7
  25.6 2.1 %collective-permute-done.7.p2.p6 = bf16[2,64,512]{2,1,0:T(8,128)(2,1)S(1)} collective-permute-done((bf16[2,64,512]{2,1,0:T(8,128)(2,1)S(1)}, bf16[2,64,512]{2,1,0:T(8,128)(2,1)S(1)}, u32[]{:S(2)}, u32[]{:S(2)}) %collective-permute-start.7) | collective-permute-done | bytes 131104 | tf_op jit(solution)/shard_map/ppermute | solution.py:30
  27.7 0.0 collective-permute-done.6.p1.p5
  27.7 6.7 %attention_kernel.1 = (bf16[128,512]{1,0:T(8,128)(2,1)S(1)}, bf16[128,512]{1,0:T(8,128)(2,1)S(1)}, bf16[128,512]{1,0:T(8,128)(2,1)S(1)}, bf16[128,512]{1,0:T(8,1...) custom-call(s32[4]{0:T(128)S(1)} %pad_add_fusion.flags, ...), custom_call_target="tpu_custom_call" | custom-call | flops 1200000000 | bytes 6000000 | tf_op jit(solution)/shard_map/attention_kernel/pallas_call | solution.py:325
  34.4 2.4 %gradient_kernel.1 = (f32[16,72,128]{2,1,0:T(8,128)S(1)}, f32[16,72,128]{2,1,0:T(8,128)S(1)}) custom-call(s32[5]{0:T(128)S(1)} %stack.59.spot, bf16[2,64,512]{2,1,0:T(8,128)(2,1)S(1)} %bitcast.66, bf16[2,64,512]{2,1,0:T(8,128)(2,1)S(1)} %collective-permute-done.1.p1, bf16[2,64,512]{2,1,0:T(8,128)(2,1)S(1)} %collective-permute-done.2.p2, ...), custom_call_target="tpu_custom_call" | custom-call | flops 20000000000 | bytes 6000000 | tf_op jit(solution)/shard_map/gradient_kernel/pallas_call | solution.py:325
  36.9 0.0 copy-start.4
  36.9 3.9 %collective-permute-start.9 = (f32[16,72,128]{2,1,0:T(8,128)S(1)}, f32[16,72,128]{2,1,0:T(8,128)S(1)}, u32[]{:S(2)}, u32[]{:S(2)}) collective-permute-start(f32[16,72,128]{2,1,0:T(8,128)S(1)} %get-tuple-element.40), channel_id=1, source_target_pairs={{0,1},{1,0},{2,3},{3,2},{4,5},{5,4},{6,7},{7,6},{8,9},{9,8},{10,11... | collective-permute-start | bytes 1769480 | tf_op jit(solution)/shard_map/ppermute | solution.py:30
  40.8 0.4 collective-permute-start.13
  41.2 2.5 %collective-permute-start.14 = (bf16[128,512]{1,0:T(8,128)(2,1)S(1)}, bf16[128,512]{1,0:T(8,128)(2,1)S(1)}, u32[]{:S(2)}, u32[]{:S(2)}) collective-permute-start(bf16[128,512]{1,0:T(8,128)(2,1)S(1)} %get-tuple-element.34.r2), channel_id=1, source_target_pairs={{0,8},{1,9},{2,10},{3,11},{4,12},{5,13},{6,14},{7,15},{8,0},{9,1},... | collective-permute-start | bytes 393224 | tf_op jit(solution)/shard_map/ppermute | solution.py:30
  43.7 1.0 %collective-permute-start.15 = (bf16[128,512]{1,0:T(8,128)(2,1)S(1)}, bf16[128,512]{1,0:T(8,128)(2,1)S(1)}, u32[]{:S(2)}, u32[]{:S(2)}) collective-permute-start(bf16[128,512]{1,0:T(8,128)(2,1)S(1)} %get-tuple-element.35.r3), channel_id=1, source_target_pairs={{0,12},{1,13},{2,14},{3,15},{4,8},{5,9},{6,10},{7,11},{8,4},{9,5},... | collective-permute-start | bytes 393224 | tf_op jit(solution)/shard_map/ppermute | solution.py:30
  44.6 0.0 collective-permute-done.9
  44.7 0.1 slice_add_fusion
  44.7 0.1 collective-permute-start.12
  44.8 0.1 collective-permute-start.11
  44.9 0.9 %collective-permute-done.13.r1 = bf16[128,512]{1,0:T(8,128)(2,1)S(1)} collective-permute-done((bf16[128,512]{1,0:T(8,128)(2,1)S(1)}, bf16[128,512]{1,0:T(8,128)(2,1)S(1)}, u32[]{:S(2)}, u32[]{:S(2)}) %collective-permute-start.13) | collective-permute-done | bytes 131104 | tf_op jit(solution)/shard_map/ppermute | solution.py:30
  45.8 2.2 %collective-permute-start.10 = (f32[4,72,128]{2,1,0:T(8,128)S(1)}, f32[4,72,128]{2,1,0:T(8,128)S(1)}, u32[]{:S(2)}, u32[]{:S(2)}) collective-permute-start(f32[4,72,128]{2,1,0:T(8,128)S(1)} %get-tuple-element.55), channel_id=1, source_target_pairs={{0,16},{1,17},{2,18},{3,19},{4,20},{5,21},{6,22},{7,23},{8,24},{9,... | collective-permute-start | bytes 442376 | tf_op jit(solution)/shard_map/ppermute | solution.py:30
  48.1 2.0 %collective-permute-done.14.r2 = bf16[128,512]{1,0:T(8,128)(2,1)S(1)} collective-permute-done((bf16[128,512]{1,0:T(8,128)(2,1)S(1)}, bf16[128,512]{1,0:T(8,128)(2,1)S(1)}, u32[]{:S(2)}, u32[]{:S(2)}) %collective-permute-start.14) | collective-permute-done | bytes 131104 | tf_op jit(solution)/shard_map/ppermute | solution.py:30
  50.1 2.5 %collective-permute-done.15.r3 = bf16[128,512]{1,0:T(8,128)(2,1)S(1)} collective-permute-done((bf16[128,512]{1,0:T(8,128)(2,1)S(1)}, bf16[128,512]{1,0:T(8,128)(2,1)S(1)}, u32[]{:S(2)}, u32[]{:S(2)}) %collective-permute-start.15) | collective-permute-done | bytes 131104 | tf_op jit(solution)/shard_map/ppermute | solution.py:30
  52.6 1.3 %token_kernel.1 = bf16[2,128,512]{2,1,0:T(8,128)(2,1)S(1)} custom-call(s32[5]{0:T(128)S(1)} %stack.59.spot, bf16[128,512]{1,0:T(8,128)(2,1)S(1)} %get-tuple-element.32.r0, bf16[128,512]{1,0:T(8,128)(2,1)S(1)} %collective-permute-done.13.r1, bf16[128,512]{1,0:T(8,128)(2,1)S(1)} %collective-permute-done.14.r2, ...), custom_call_target="tpu_custom_call" | custom-call | flops 500000000 | bytes 4000000 | tf_op jit(solution)/shard_map/token_kernel/pallas_call | solution.py:325
  54.0 0.0 copy-start.1
  54.0 0.0 copy-start.2
  54.0 0.5 collective-permute-done.12.s3
  54.5 0.0 collective-permute-done.11.s2
  54.5 0.0 collective-permute-done.10.s1
  54.5 0.6 x_parts_kernel.1
  55.1 7.7 %all_to_all.10.pieces = f32[4,72,128]{2,1,0:T(8,128)S(1)} all-to-all(f32[4,72,128]{2,1,0:T(8,128)S(1)} %x_parts_kernel.1), channel_id=1, replica_groups={{0,4,8,12},{1,5,9,13},{2,6,10,14},{3,7,11,15},{16,20,24,28},{17,21,25,2..., dimensions={0} | all-to-all | bytes 294912 | tf_op jit(solution)/shard_map/all_to_all | solution.py:66
  62.8 1.3 %z_parts_kernel.1 = f32[4,72,128]{2,1,0:T(8,128)} custom-call(s32[5]{0:T(128)S(1)} %stack.59.spot, f32[4,72,128]{2,1,0:T(8,128)S(1)} %all_to_all.10.pieces), custom_call_target="tpu_custom_call" | custom-call | tf_op jit(solution)/shard_map/z_parts_kernel/pallas_call | solution.py:325
  64.1 3.3 %all-to-all-start.1 = ((f32[4,72,128]{2,1,0:T(8,128)}), f32[4,72,128]{2,1,0:T(8,128)S(1)}, u32[]{:S(2)}, u32[]{:S(2)}) async-start(f32[4,72,128]{2,1,0:T(8,128)} %z_parts_kernel.1), calls=%async_computation.1 | async-start | bytes 294912 | tf_op jit(solution)/shard_map/all_to_all | solution.py:66
  67.4 8.9 %collective-permute-start.18 = (bf16[2,4,8,512]{3,2,1,0:T(8,128)(2,1)S(1)}, bf16[2,4,8,512]{3,2,1,0:T(8,128)(2,1)S(1)}, u32[]{:S(2)}, u32[]{:S(2)}) collective-permute-start(bf16[2,4,8,512]{3,2,1,0:T(8,128)(2,1)S(1)} %get-tuple-element.59), channel_id=1, source_target_pairs={{0,241},{1,242},{2,243},{3,240},{4,245},{5,246},{6,247},{7,244},{8... | collective-permute-start | bytes 196616 | tf_op jit(solution)/shard_map/ppermute | solution.py:30
  76.3 2.2 %collective-permute-start.17 = (bf16[2,4,8,512]{3,2,1,0:T(8,128)(2,1)S(1)}, bf16[2,4,8,512]{3,2,1,0:T(8,128)(2,1)S(1)}, u32[]{:S(2)}, u32[]{:S(2)}) collective-permute-start(bf16[2,4,8,512]{3,2,1,0:T(8,128)(2,1)S(1)} %get-tuple-element.60), channel_id=1, source_target_pairs={{0,240},{1,241},{2,242},{3,243},{4,244},{5,245},{6,246},{7,247},{8... | collective-permute-start | bytes 196616 | tf_op jit(solution)/shard_map/ppermute | solution.py:30
  78.6 0.0 collective-permute-start.16
  78.6 0.8 collective-permute-done.18.other_low
  79.4 4.7 %collective-permute-done.17.other_high = bf16[2,4,8,512]{3,2,1,0:T(8,128)(2,1)S(1)} collective-permute-done((bf16[2,4,8,512]{3,2,1,0:T(8,128)(2,1)S(1)}, bf16[2,4,8,512]{3,2,1,0:T(8,128)(2,1)S(1)}, u32[]{:S(2)}, u32[]{:S(2)}) %collective-permute-start.17) | collective-permute-done | bytes 65568 | tf_op jit(solution)/shard_map/ppermute | solution.py:30
  84.1 0.0 collective-permute-done.16.mine_low
  84.1 1.3 %merge_kernel.1 = (bf16[8,16,512]{2,1,0:T(8,128)(2,1)}, bf16[8,16,512]{2,1,0:T(8,128)(2,1)}) custom-call(s32[5]{0:T(128)S(1)} %stack.59.spot, bf16[8,16,512]{2,1,0:T(8,128)(2,1)S(1)} %bitcast.59, bf16[8,16,512]{2,1,0:T(8,128)(2,1)S(1)} %bitcast.61, bf16[2,4,8,512]{3,2,1,0:T(8,128)(2,1)S(1)} %get-tuple-element.62.mine_high, ...), custom_call_target="tpu_custom_call" | custom-call | tf_op jit(solution)/shard_map/merge_kernel/pallas_call | solution.py:325
  85.4 0.0 all-to-all-done.1
  85.4 0.7 collective-permute-start.21
  86.0 1.2 %collective-permute-start.20 = (f32[72,128]{1,0:T(8,128)S(1)}, f32[72,128]{1,0:T(8,128)S(1)}, u32[]{:S(2)}, u32[]{:S(2)}) collective-permute-start(f32[72,128]{1,0:T(8,128)S(1)} %reduce_sum.9.near), channel_id=1, source_target_pairs={{0,2},{1,3},{2,0},{3,1},{4,6},{5,7},{6,4},{7,5},{8,10},{9,11},{10,... | collective-permute-start | bytes 110600 | tf_op jit(solution)/shard_map/ppermute | solution.py:30
  87.3 0.4 collective-permute-start.19
  87.6 1.5 %collective-permute-done.21.both_in = f32[72,128]{1,0:T(8,128)S(1)} collective-permute-done((f32[72,128]{1,0:T(8,128)S(1)}, f32[72,128]{1,0:T(8,128)S(1)}, u32[]{:S(2)}, u32[]{:S(2)}) %collective-permute-start.21) | collective-permute-done | bytes 36896 | tf_op jit(solution)/shard_map/ppermute | solution.py:30
  89.2 0.1 collective-permute-done.20.z_in
  89.3 0.0 collective-permute-done.19.core_in
  89.3 1.2 %last_kernel.1 = (f32[24,512]{1,0:T(8,128)}, f32[8,512]{1,0:T(8,128)}, f32[2,8]{1,0:T(2,128)}) custom-call(s32[5]{0:T(128)S(1)} %stack.59.spot, f32[72,128]{1,0:T(8,128)S(1)} %reduce_sum.9.near, f32[72,128]{1,0:T(8,128)S(1)} %collective-permute-done.19.core_in, f32[72,128]{1,0:T(8,128)S(1)} %collective-permute-done.20.z_in, ...), custom_call_target="tpu_custom_call" | custom-call | tf_op jit(solution)/shard_map/last_kernel/pallas_call | solution.py:325
  (15 shorter events, 0.1 us)
Async XLA Ops:
  0.6 22.4 %copy-start = (bf16[512,1536]{1,0:T(8,128)(2,1)S(1)}, bf16[512,1536]{1,0:T(8,128)(2,1)}, u32[]{:S(2)}) copy-start(bf16[512,1536]{1,0:T(8,128)(2,1)} %w_qkv.7) | copy-start | bytes 4718596
  0.6 22.4 %copy-start.5 = (f32[2,512]{1,0:T(2,128)S(1)}, f32[2,512]{1,0:T(2,128)}, u32[]{:S(2)}) copy-start(f32[2,512]{1,0:T(2,128)} %norm.5) | copy-start | bytes 12292
  1.9 10.6 %collective-permute-start = (bf16[2,4,8,512]{3,2,1,0:T(8,128)(2,1)S(1)}, bf16[2,4,8,512]{3,2,1,0:T(8,128)(2,1)S(1)}, u32[]{:S(2)}, u32[]{:S(2)}) collective-permute-start(bf16[2,4,8,512]{3,2,1,0:T(8,128)(2,1)S(1)} %get-tuple-element.66), channel_id=1, source_target_pairs={{0,3},{1,0},{2,1},{3,2},{4,7},{5,4},{6,5},{7,6},{8,11},{9,8},{10,9... | collective-permute-start | bytes 196616 | tf_op jit(solution)/shard_map/ppermute | solution.py:30
  5.3 10.8 %collective-permute-start.4 = (bf16[2,4,8,512]{3,2,1,0:T(8,128)(2,1)S(1)}, bf16[2,4,8,512]{3,2,1,0:T(8,128)(2,1)S(1)}, u32[]{:S(2)}, u32[]{:S(2)}) collective-permute-start(bf16[2,4,8,512]{3,2,1,0:T(8,128)(2,1)S(1)} %get-tuple-element.63), channel_id=1, source_target_pairs={{0,240},{1,241},{2,242},{3,243},{4,244},{5,245},{6,246},{7,247},{8... | collective-permute-start | bytes 196616 | tf_op jit(solution)/shard_map/ppermute | solution.py:30
  12.1 7.6 %collective-permute-start.5 = (bf16[2,4,8,512]{3,2,1,0:T(8,128)(2,1)S(1)}, bf16[2,4,8,512]{3,2,1,0:T(8,128)(2,1)S(1)}, u32[]{:S(2)}, u32[]{:S(2)}) collective-permute-start(bf16[2,4,8,512]{3,2,1,0:T(8,128)(2,1)S(1)} %get-tuple-element.64), channel_id=1, source_target_pairs={{0,243},{1,240},{2,241},{3,242},{4,247},{5,244},{6,245},{7,246},{8... | collective-permute-start | bytes 196616 | tf_op jit(solution)/shard_map/ppermute | solution.py:30
  12.6 10.2 %collective-permute-start.3 = (bf16[2,64,512]{2,1,0:T(8,128)(2,1)S(1)}, bf16[2,64,512]{2,1,0:T(8,128)(2,1)S(1)}, u32[]{:S(2)}, u32[]{:S(2)}) collective-permute-start(bf16[2,64,512]{2,1,0:T(8,128)(2,1)S(1)} %bitcast.62), channel_id=1, source_target_pairs={{0,12},{1,13},{2,14},{3,15},{4,8},{5,9},{6,10},{7,11},{8,4},{9,5},... | collective-permute-start | bytes 393224 | tf_op jit(solution)/shard_map/ppermute | solution.py:30
  15.1 7.9 %collective-permute-start.2 = (bf16[2,64,512]{2,1,0:T(8,128)(2,1)S(1)}, bf16[2,64,512]{2,1,0:T(8,128)(2,1)S(1)}, u32[]{:S(2)}, u32[]{:S(2)}) collective-permute-start(bf16[2,64,512]{2,1,0:T(8,128)(2,1)S(1)} %bitcast.63), channel_id=1, source_target_pairs={{0,8},{1,9},{2,10},{3,11},{4,12},{5,13},{6,14},{7,15},{8,0},{9,1},... | collective-permute-start | bytes 393224 | tf_op jit(solution)/shard_map/ppermute | solution.py:30
  15.7 7.4 %collective-permute-start.1 = (bf16[2,64,512]{2,1,0:T(8,128)(2,1)S(1)}, bf16[2,64,512]{2,1,0:T(8,128)(2,1)S(1)}, u32[]{:S(2)}, u32[]{:S(2)}) collective-permute-start(bf16[2,64,512]{2,1,0:T(8,128)(2,1)S(1)} %bitcast.64), channel_id=1, source_target_pairs={{0,4},{1,5},{2,6},{3,7},{4,0},{5,1},{6,2},{7,3},{8,12},{9,13},{10,... | collective-permute-start | bytes 393224 | tf_op jit(solution)/shard_map/ppermute | solution.py:30
  19.7 5.9 %collective-permute-start.8 = (bf16[2,64,512]{2,1,0:T(8,128)(2,1)S(1)}, bf16[2,64,512]{2,1,0:T(8,128)(2,1)S(1)}, u32[]{:S(2)}, u32[]{:S(2)}) collective-permute-start(bf16[2,64,512]{2,1,0:T(8,128)(2,1)S(1)} %bitcast.68), channel_id=1, source_target_pairs={{0,12},{1,13},{2,14},{3,15},{4,8},{5,9},{6,10},{7,11},{8,4},{9,5},... | collective-permute-start | bytes 393224 | tf_op jit(solution)/shard_map/ppermute | solution.py:30
  22.3 5.4 %collective-permute-start.7 = (bf16[2,64,512]{2,1,0:T(8,128)(2,1)S(1)}, bf16[2,64,512]{2,1,0:T(8,128)(2,1)S(1)}, u32[]{:S(2)}, u32[]{:S(2)}) collective-permute-start(bf16[2,64,512]{2,1,0:T(8,128)(2,1)S(1)} %bitcast.69), channel_id=1, source_target_pairs={{0,8},{1,9},{2,10},{3,11},{4,12},{5,13},{6,14},{7,15},{8,0},{9,1},... | collective-permute-start | bytes 393224 | tf_op jit(solution)/shard_map/ppermute | solution.py:30
  22.8 4.9 %collective-permute-start.6 = (bf16[2,64,512]{2,1,0:T(8,128)(2,1)S(1)}, bf16[2,64,512]{2,1,0:T(8,128)(2,1)S(1)}, u32[]{:S(2)}, u32[]{:S(2)}) collective-permute-start(bf16[2,64,512]{2,1,0:T(8,128)(2,1)S(1)} %bitcast.70), channel_id=1, source_target_pairs={{0,4},{1,5},{2,6},{3,7},{4,0},{5,1},{6,2},{7,3},{8,12},{9,13},{10,... | collective-permute-start | bytes 393224 | tf_op jit(solution)/shard_map/ppermute | solution.py:30
  23.1 1.0 %copy-start.3 = (bf16[512,512]{1,0:T(8,128)(2,1)S(1)}, bf16[512,512]{1,0:T(8,128)(2,1)}, u32[]{:S(2)}) copy-start(bf16[512,512]{1,0:T(8,128)(2,1)} %w_proj.5) | copy-start | bytes 1572868
  36.9 15.8 %copy-start.4 = (bf16[512,512]{1,0:T(8,128)(2,1)S(1)}, bf16[512,512]{1,0:T(8,128)(2,1)}, u32[]{:S(2)}) copy-start(bf16[512,512]{1,0:T(8,128)(2,1)} %w_proj.5) | copy-start | bytes 1572868
  36.9 7.8 %collective-permute-start.9 = (f32[16,72,128]{2,1,0:T(8,128)S(1)}, f32[16,72,128]{2,1,0:T(8,128)S(1)}, u32[]{:S(2)}, u32[]{:S(2)}) collective-permute-start(f32[16,72,128]{2,1,0:T(8,128)S(1)} %get-tuple-element.40), channel_id=1, source_target_pairs={{0,1},{1,0},{2,3},{3,2},{4,5},{5,4},{6,7},{7,6},{8,9},{9,8},{10,11... | collective-permute-start | bytes 1769480 | tf_op jit(solution)/shard_map/ppermute | solution.py:30
  40.8 5.1 %collective-permute-start.13 = (bf16[128,512]{1,0:T(8,128)(2,1)S(1)}, bf16[128,512]{1,0:T(8,128)(2,1)S(1)}, u32[]{:S(2)}, u32[]{:S(2)}) collective-permute-start(bf16[128,512]{1,0:T(8,128)(2,1)S(1)} %get-tuple-element.33.r1), channel_id=1, source_target_pairs={{0,4},{1,5},{2,6},{3,7},{4,0},{5,1},{6,2},{7,3},{8,12},{9,13},{10,... | collective-permute-start | bytes 393224 | tf_op jit(solution)/shard_map/ppermute | solution.py:30
  41.2 8.9 %collective-permute-start.14 = (bf16[128,512]{1,0:T(8,128)(2,1)S(1)}, bf16[128,512]{1,0:T(8,128)(2,1)S(1)}, u32[]{:S(2)}, u32[]{:S(2)}) collective-permute-start(bf16[128,512]{1,0:T(8,128)(2,1)S(1)} %get-tuple-element.34.r2), channel_id=1, source_target_pairs={{0,8},{1,9},{2,10},{3,11},{4,12},{5,13},{6,14},{7,15},{8,0},{9,1},... | collective-permute-start | bytes 393224 | tf_op jit(solution)/shard_map/ppermute | solution.py:30
  43.7 9.0 %collective-permute-start.15 = (bf16[128,512]{1,0:T(8,128)(2,1)S(1)}, bf16[128,512]{1,0:T(8,128)(2,1)S(1)}, u32[]{:S(2)}, u32[]{:S(2)}) collective-permute-start(bf16[128,512]{1,0:T(8,128)(2,1)S(1)} %get-tuple-element.35.r3), channel_id=1, source_target_pairs={{0,12},{1,13},{2,14},{3,15},{4,8},{5,9},{6,10},{7,11},{8,4},{9,5},... | collective-permute-start | bytes 393224 | tf_op jit(solution)/shard_map/ppermute | solution.py:30
  44.7 9.8 %collective-permute-start.12 = (f32[4,72,128]{2,1,0:T(8,128)S(1)}, f32[4,72,128]{2,1,0:T(8,128)S(1)}, u32[]{:S(2)}, u32[]{:S(2)}) collective-permute-start(f32[4,72,128]{2,1,0:T(8,128)S(1)} %get-tuple-element.53), channel_id=1, source_target_pairs={{0,48},{1,49},{2,50},{3,51},{4,52},{5,53},{6,54},{7,55},{8,56},{9,... | collective-permute-start | bytes 442376 | tf_op jit(solution)/shard_map/ppermute | solution.py:30
  44.8 9.7 %collective-permute-start.11 = (f32[4,72,128]{2,1,0:T(8,128)S(1)}, f32[4,72,128]{2,1,0:T(8,128)S(1)}, u32[]{:S(2)}, u32[]{:S(2)}) collective-permute-start(f32[4,72,128]{2,1,0:T(8,128)S(1)} %get-tuple-element.54), channel_id=1, source_target_pairs={{0,32},{1,33},{2,34},{3,35},{4,36},{5,37},{6,38},{7,39},{8,40},{9,... | collective-permute-start | bytes 442376 | tf_op jit(solution)/shard_map/ppermute | solution.py:30
  45.8 8.7 %collective-permute-start.10 = (f32[4,72,128]{2,1,0:T(8,128)S(1)}, f32[4,72,128]{2,1,0:T(8,128)S(1)}, u32[]{:S(2)}, u32[]{:S(2)}) collective-permute-start(f32[4,72,128]{2,1,0:T(8,128)S(1)} %get-tuple-element.55), channel_id=1, source_target_pairs={{0,16},{1,17},{2,18},{3,19},{4,20},{5,21},{6,22},{7,23},{8,24},{9,... | collective-permute-start | bytes 442376 | tf_op jit(solution)/shard_map/ppermute | solution.py:30
  54.0 30.1 %copy-start.1 = (bf16[1,1,8,16,512]{4,3,2,1,0:T(8,128)(2,1)S(1)}, bf16[1,1,8,16,512]{4,3,2,1,0:T(8,128)(2,1)}, u32[]{:S(2)}) copy-start(bf16[1,1,8,16,512]{4,3,2,1,0:T(8,128)(2,1)} %param.5) | copy-start | bytes 393220
  54.0 30.1 %copy-start.2 = (bf16[1,1,8,16,512]{4,3,2,1,0:T(8,128)(2,1)S(1)}, bf16[1,1,8,16,512]{4,3,2,1,0:T(8,128)(2,1)}, u32[]{:S(2)}) copy-start(bf16[1,1,8,16,512]{4,3,2,1,0:T(8,128)(2,1)} %param.9) | copy-start | bytes 393220
  64.1 21.3 %all-to-all-start.1 = ((f32[4,72,128]{2,1,0:T(8,128)}), f32[4,72,128]{2,1,0:T(8,128)S(1)}, u32[]{:S(2)}, u32[]{:S(2)}) async-start(f32[4,72,128]{2,1,0:T(8,128)} %z_parts_kernel.1), calls=%async_computation.1 | async-start | bytes 294912 | tf_op jit(solution)/shard_map/all_to_all | solution.py:66
  67.4 12.0 %collective-permute-start.18 = (bf16[2,4,8,512]{3,2,1,0:T(8,128)(2,1)S(1)}, bf16[2,4,8,512]{3,2,1,0:T(8,128)(2,1)S(1)}, u32[]{:S(2)}, u32[]{:S(2)}) collective-permute-start(bf16[2,4,8,512]{3,2,1,0:T(8,128)(2,1)S(1)} %get-tuple-element.59), channel_id=1, source_target_pairs={{0,241},{1,242},{2,243},{3,240},{4,245},{5,246},{6,247},{7,244},{8... | collective-permute-start | bytes 196616 | tf_op jit(solution)/shard_map/ppermute | solution.py:30
  76.3 7.7 %collective-permute-start.17 = (bf16[2,4,8,512]{3,2,1,0:T(8,128)(2,1)S(1)}, bf16[2,4,8,512]{3,2,1,0:T(8,128)(2,1)S(1)}, u32[]{:S(2)}, u32[]{:S(2)}) collective-permute-start(bf16[2,4,8,512]{3,2,1,0:T(8,128)(2,1)S(1)} %get-tuple-element.60), channel_id=1, source_target_pairs={{0,240},{1,241},{2,242},{3,243},{4,244},{5,245},{6,246},{7,247},{8... | collective-permute-start | bytes 196616 | tf_op jit(solution)/shard_map/ppermute | solution.py:30
  78.6 5.5 %collective-permute-start.16 = (bf16[2,4,8,512]{3,2,1,0:T(8,128)(2,1)S(1)}, bf16[2,4,8,512]{3,2,1,0:T(8,128)(2,1)S(1)}, u32[]{:S(2)}, u32[]{:S(2)}) collective-permute-start(bf16[2,4,8,512]{3,2,1,0:T(8,128)(2,1)S(1)} %get-tuple-element.61), channel_id=1, source_target_pairs={{0,1},{1,2},{2,3},{3,0},{4,5},{5,6},{6,7},{7,4},{8,9},{9,10},{10,1... | collective-permute-start | bytes 196616 | tf_op jit(solution)/shard_map/ppermute | solution.py:30
  85.4 3.8 %collective-permute-start.21 = (f32[72,128]{1,0:T(8,128)S(1)}, f32[72,128]{1,0:T(8,128)S(1)}, u32[]{:S(2)}, u32[]{:S(2)}) collective-permute-start(f32[72,128]{1,0:T(8,128)S(1)} %reduce_sum.9.near), channel_id=1, source_target_pairs={{0,3},{1,2},{2,1},{3,0},{4,7},{5,6},{6,5},{7,4},{8,11},{9,10},{10,... | collective-permute-start | bytes 110600 | tf_op jit(solution)/shard_map/ppermute | solution.py:30
  86.0 3.2 %collective-permute-start.20 = (f32[72,128]{1,0:T(8,128)S(1)}, f32[72,128]{1,0:T(8,128)S(1)}, u32[]{:S(2)}, u32[]{:S(2)}) collective-permute-start(f32[72,128]{1,0:T(8,128)S(1)} %reduce_sum.9.near), channel_id=1, source_target_pairs={{0,2},{1,3},{2,0},{3,1},{4,6},{5,7},{6,4},{7,5},{8,10},{9,11},{10,... | collective-permute-start | bytes 110600 | tf_op jit(solution)/shard_map/ppermute | solution.py:30
  87.3 2.0 %collective-permute-start.19 = (f32[72,128]{1,0:T(8,128)S(1)}, f32[72,128]{1,0:T(8,128)S(1)}, u32[]{:S(2)}, u32[]{:S(2)}) collective-permute-start(f32[72,128]{1,0:T(8,128)S(1)} %reduce_sum.9.near), channel_id=1, source_target_pairs={{0,1},{1,0},{2,3},{3,2},{4,5},{5,4},{6,7},{7,6},{8,9},{9,8},{10,11... | collective-permute-start | bytes 110600 | tf_op jit(solution)/shard_map/ppermute | solution.py:30

commit v8 on v4

--- a/solution.py
+++ b/solution.py
@@ -34,19 +34,19 @@
     return place + 4 if (place // 4) % 2 else place - 4
 
 
-def across_x(mask):
+def over_x(mask):
     return lambda p, n: (p ^ mask, n)
 
 
-def across_y(mask):
+def over_y(mask):
     return lambda p, n: (p ^ (4 * mask), n)
 
 
-def across_z(mask):
+def over_z(mask):
     return lambda p, n: (p ^ (16 * mask), n)
 
 
-def across_narrow(mask):
+def over_narrow(mask):
     return lambda p, n: (p, n ^ mask)
 
 
@@ -198,8 +198,9 @@
         to_core = core if ahead == 0 else 1 - core
         for across in range(4):
             to_y = y ^ across
-            for to_x in range(4):
-                block = 4 * across + to_x
+            for across_x in range(4):
+                to_x = x ^ across_x
+                block = 4 * across + across_x
                 for side in range(2):
                     lanes = pl.ds(pl.multiple_of(256 * to_core + 128 * side, 128), 128)
                     for slot in range(3):
@@ -219,13 +220,6 @@
                         out[block, 64:, 32 * z : 32 * z + 32] = n_ref[rows, :32]
                 if ahead == 1:
                     out[block, 64:, :] = jnp.zeros((8, 128), F32)
-
-
-def x_parts_kernel(spot, s0, s1, s2, s3, *outs):
-    x = spot[0]
-    for across, out in enumerate(outs):
-        to_x = x ^ across
-        out[...] = (s0[to_x] + s1[to_x]) + (s2[to_x] + s3[to_x])
 
 
 def z_parts_kernel(spot, m0, m1, m2, m3, *outs):
@@ -356,9 +350,9 @@
     cross_in = move(other[:, :4], lambda p, n: (partner_of(p), n - 1))
 
     part0 = jnp.stack([mine[:, 4:], lower_in], 1).reshape(2, SLAB // 2, C)
-    parts0 = [part0] + [move(part0, across_x(mask)) for mask in (1, 2, 3)]
+    parts0 = [part0] + [move(part0, over_x(mask)) for mask in (1, 2, 3)]
     part1 = jnp.stack([other_in, cross_in], 1).reshape(2, SLAB // 2, C)
-    parts1 = [part1] + [move(part1, across_x(mask)) for mask in (1, 2, 3)]
+    parts1 = [part1] + [move(part1, over_x(mask)) for mask in (1, 2, 3)]
     half = TOKENS // 2
     normed0, qkv0, up0 = call(
         first_kernel,
@@ -378,7 +372,6 @@
         moved=6_000_000,
     )
 
-    returned = [r0] + [move(rows, across_x(mask)) for mask, rows in ((1, r1), (2, r2), (3, r3))]
     keep, send = call(
         gradient_kernel,
         spot,
@@ -392,10 +385,17 @@
         flops=20_000_000_000,
         moved=6_000_000,
     )
-    received = move(send, across_narrow(1))
+    received = move(send, over_narrow(1))
     blocks = [slice(4 * mask, 4 * mask + 4) for mask in range(4)]
     halves = [keep[block] + received[block] for block in blocks]
-    from_y = [halves[0]] + [move(halves[mask], across_y(mask)) for mask in (1, 2, 3)]
+    halves[1:] = [half.astype(BF16) for half in halves[1:]]
+    from_y = [halves[0]] + [move(halves[mask], over_y(mask)) for mask in (1, 2, 3)]
+    returned = [r0] + [
+        move(rows, over_x(mask)) for mask, rows in ((1, r1), (2, r2), (3, r3))
+    ]
+    *from_y, returned[1], returned[2] = lax.optimization_barrier(
+        (*from_y, returned[1], returned[2])
+    )
     (back,) = call(
         token_kernel,
         spot,
@@ -404,17 +404,17 @@
         flops=500_000_000,
         moved=4_000_000,
     )
-    from_y[1], from_y[2], from_y[3], back = lax.optimization_barrier(
-        (from_y[1], from_y[2], from_y[3], back)
+    share = ((72, 128), F32)
+    sums = [piece.astype(F32) for piece in from_y]
+    x_parts = [(sums[0][k] + sums[1][k]) + (sums[2][k] + sums[3][k]) for k in range(4)]
+    from_x = [x_parts[0]] + [move(x_parts[mask], over_x(mask)) for mask in (1, 2, 3)]
+    from_x[1], from_x[2], from_x[3], back = lax.optimization_barrier(
+        (from_x[1], from_x[2], from_x[3], back)
     )
     back = back.reshape(2, 4, 4, 8, C)
     lower = move(back[:, 1], lambda p, n: (p, n + 1))
     other_upper = move(back[:, 2], lambda p, n: (partner_of(p), n))
     other_lower = move(back[:, 3], lambda p, n: (partner_of(p), n + 1))
-
-    share = ((72, 128), F32)
-    x_parts = call(x_parts_kernel, spot, from_y, [share] * 4)
-    from_x = [x_parts[0]] + [move(x_parts[mask], across_x(mask)) for mask in (1, 2, 3)]
     z_parts = call(z_parts_kernel, spot, from_x, [share] * 4)
     output, grad_inputs = call(
         merge_kernel,
@@ -422,16 +422,14 @@
         (own_inputs, own_upstream, back[:, 0], lower, other_upper, other_lower),
         [((8, 16, C), BF16)] * 2,
     )
-    line = [z_parts[0]] + [move(z_parts[mask], across_z(mask)) for mask in (1, 2, 3)]
+    line = [z_parts[0]] + [move(z_parts[mask], over_z(mask)) for mask in (1, 2, 3)]
     line[1], line[2], line[3], output, grad_inputs = lax.optimization_barrier(
         (line[1], line[2], line[3], output, grad_inputs)
     )
     line = (line[0] + line[1]) + (line[2] + line[3])
+    last = [line] + [move(line, over_narrow(mask)) for mask in (1, 2, 3)]
     grad_qkv, grad_proj, grad_norm = call(
-        last_kernel,
-        spot,
-        (line, *[move(line, across_narrow(mask)) for mask in (1, 2, 3)]),
-        [((24, C), F32), ((8, C), F32), ((2, 8), F32)],
+        last_kernel, spot, last, [((24, C), F32), ((8, C), F32), ((2, 8), F32)]
     )
     return (
         output[None, None], grad_inputs[None, None], grad_qkv.T, grad_proj.T, grad_norm

time: 85.2 us -> 82.6 us (0.969)
  waiting for transfers between devices: 16.5 us -> 12.2 us
  starting transfers between devices: 49.7 us -> 51.8 us
    ppermute x28, waiting for transfers between devices: 16.5 us -> 12.2 us  [move(): return lax.ppermute(value, ('wide', 'narrow'), pairs)]
    ppermute x28, starting transfers between devices: 49.7 us -> 51.8 us  [move(): return lax.ppermute(value, ('wide', 'narrow'), pairs)]
    pallas_call x8 -> x7, Pallas kernels: 15.4 us -> 14.9 us  [call(): pl.pallas_call(kernel, out_shape=[jax.ShapeDtypeStruct(shape, dtype) for...]
  transfers between devices with their start and end apart: 28 -> 28, of which waited for: 11 -> 8; matrix products, arithmetic and copies ran while one was open for 0% -> 0% of each run, Pallas kernels for 5% -> 5%
where the time goes in v8:
time: 82.6 us; the launch traced here: 82.4 us
  starting transfers between devices  51.8 us (63%)
  Pallas kernels  14.9 us (18%)
  waiting for transfers between devices  12.2 us (15%)
  other arithmetic  1.46 us (2%)
  local copies, waits for them, and re-layouts  1.19 us (1%)
  between operations  0.91 us (1%)
    ppermute x28, starting transfers between devices, move(): return lax.ppermute(value, ('wide', 'narrow'), pairs)  51.8 us
    pallas_call x7, Pallas kernels, call(): pl.pallas_call(kernel, out_shape=[jax.ShapeDtypeStruct(shape, dtype) for...  14.9 us
    ppermute x28, waiting for transfers between devices, move(): return lax.ppermute(value, ('wide', 'narrow'), pairs)  12.2 us
  transfers between devices with their start and end apart: 28, of which 8 were waited for; matrix products, arithmetic and copies ran while one was open for 0% of the time, Pallas kernels for 5%

profile of v8, /device:TPU:1, one launch (start us, length us, event | category | flops | bytes accessed | tf_op | source)
XLA Modules:
  0.0 82.4 jit_solution(18104233513670413788)
XLA Ops:
  0.7 1.2 %broadcast_select_fusion = (bf16[2,8,8,512]{3,2,1,0:T(8,128)(2,1)S(1)}, bf16[2,8,8,512]{3,2,1,0:T(8,128)(2,1)S(1)}) fusion(pred[8]{0:T(512)(128)(4,1)S(1)} %compare_compare_fusion, bf16[1,8,2,8,512]{4,3,2,1,0:T(8,128)(2,1)} %bitcast.68, bf16[1,8,2,8,512]{4,3,2,1,0:T(8,128)(2,1)} %bitcast.66), kind=kLoop, calls=%fused_computation.15 | loop fusion | flops 327680 | bytes 524296 | tf_op jit(solution)/shard_map/jit(_where)/select_n | solution.py:347
  1.9 3.3 %collective-permute-start = (bf16[2,4,8,512]{3,2,1,0:T(8,128)(2,1)S(1)}, bf16[2,4,8,512]{3,2,1,0:T(8,128)(2,1)S(1)}, u32[]{:S(2)}, u32[]{:S(2)}) collective-permute-start(bf16[2,4,8,512]{3,2,1,0:T(8,128)(2,1)S(1)} %get-tuple-element.94), channel_id=1, source_target_pairs={{0,3},{1,0},{2,1},{3,2},{4,7},{5,4},{6,5},{7,6},{8,11},{9,8},{10,9... | collective-permute-start | bytes 196616 | tf_op jit(solution)/shard_map/ppermute | solution.py:30
  5.3 6.8 %collective-permute-start.4 = (bf16[2,4,8,512]{3,2,1,0:T(8,128)(2,1)S(1)}, bf16[2,4,8,512]{3,2,1,0:T(8,128)(2,1)S(1)}, u32[]{:S(2)}, u32[]{:S(2)}) collective-permute-start(bf16[2,4,8,512]{3,2,1,0:T(8,128)(2,1)S(1)} %get-tuple-element.91), channel_id=1, source_target_pairs={{0,240},{1,241},{2,242},{3,243},{4,244},{5,245},{6,246},{7,247},{8... | collective-permute-start | bytes 196616 | tf_op jit(solution)/shard_map/ppermute | solution.py:30
  12.1 0.4 collective-permute-start.5
  12.6 2.6 %collective-permute-start.3 = (bf16[2,64,512]{2,1,0:T(8,128)(2,1)S(1)}, bf16[2,64,512]{2,1,0:T(8,128)(2,1)S(1)}, u32[]{:S(2)}, u32[]{:S(2)}) collective-permute-start(bf16[2,64,512]{2,1,0:T(8,128)(2,1)S(1)} %bitcast.70), channel_id=1, source_target_pairs={{0,12},{1,13},{2,14},{3,15},{4,8},{5,9},{6,10},{7,11},{8,4},{9,5},... | collective-permute-start | bytes 393224 | tf_op jit(solution)/shard_map/ppermute | solution.py:30
  15.1 0.5 collective-permute-start.2
  15.7 0.3 collective-permute-start.1
  15.9 0.1 pad_add_fusion.flags
  16.0 0.1 stack.59.spot
  16.1 0.0 collective-permute-done.4
  16.1 3.6 %collective-permute-done.5 = bf16[2,4,8,512]{3,2,1,0:T(8,128)(2,1)S(1)} collective-permute-done((bf16[2,4,8,512]{3,2,1,0:T(8,128)(2,1)S(1)}, bf16[2,4,8,512]{3,2,1,0:T(8,128)(2,1)S(1)}, u32[]{:S(2)}, u32[]{:S(2)}) %collective-permute-start.5) | collective-permute-done | bytes 65568 | tf_op jit(solution)/shard_map/ppermute | solution.py:30
  19.7 2.6 %collective-permute-start.8 = (bf16[2,64,512]{2,1,0:T(8,128)(2,1)S(1)}, bf16[2,64,512]{2,1,0:T(8,128)(2,1)S(1)}, u32[]{:S(2)}, u32[]{:S(2)}) collective-permute-start(bf16[2,64,512]{2,1,0:T(8,128)(2,1)S(1)} %bitcast.76), channel_id=1, source_target_pairs={{0,12},{1,13},{2,14},{3,15},{4,8},{5,9},{6,10},{7,11},{8,4},{9,5},... | collective-permute-start | bytes 393224 | tf_op jit(solution)/shard_map/ppermute | solution.py:30
  22.3 0.5 collective-permute-start.7
  22.8 0.0 collective-permute-done.3.p3
  22.8 0.3 collective-permute-start.6
  23.1 0.0 collective-permute-done.2.p2
  23.1 0.0 collective-permute-done.1.p1
  23.1 0.0 copy-start.3
  23.1 1.0 %copy-done.3 = bf16[512,512]{1,0:T(8,128)(2,1)S(1)} copy-done((bf16[512,512]{1,0:T(8,128)(2,1)S(1)}, bf16[512,512]{1,0:T(8,128)(2,1)}, u32[]{:S(2)}) %copy-start.3) | copy-done | bytes 524312
  24.1 1.1 %first_kernel.1 = (bf16[256,512]{1,0:T(8,128)(2,1)S(1)}, bf16[256,384]{1,0:T(8,128)(2,1)S(1)}, bf16[256,128]{1,0:T(8,128)(2,1)S(1)}) custom-call(s32[4]{0:T(128)S(1)} %pad_add_fusion.flags, bf16[2,64,512]{2,1,0:T(8,128)(2,1)S(1)} %bitcast.73, bf16[2,64,512]{2,1,0:T(8,128)(2,1)S(1)} %collective-permute-done.1.p1, ...), custom_call_target="tpu_custom_call" | custom-call | flops 10000000000 | bytes 3000000 | tf_op jit(solution)/shard_map/first_kernel/pallas_call | solution.py:321
  25.2 0.4 collective-permute-done.8.p3.p7
  25.6 2.1 %collective-permute-done.7.p2.p6 = bf16[2,64,512]{2,1,0:T(8,128)(2,1)S(1)} collective-permute-done((bf16[2,64,512]{2,1,0:T(8,128)(2,1)S(1)}, bf16[2,64,512]{2,1,0:T(8,128)(2,1)S(1)}, u32[]{:S(2)}, u32[]{:S(2)}) %collective-permute-start.7) | collective-permute-done | bytes 131104 | tf_op jit(solution)/shard_map/ppermute | solution.py:30
  27.7 0.0 collective-permute-done.6.p1.p5
  27.7 6.7 %attention_kernel.1 = (bf16[128,512]{1,0:T(8,128)(2,1)S(1)}, bf16[128,512]{1,0:T(8,128)(2,1)S(1)}, bf16[128,512]{1,0:T(8,128)(2,1)S(1)}, bf16[128,512]{1,0:T(8,1...) custom-call(s32[4]{0:T(128)S(1)} %pad_add_fusion.flags, ...), custom_call_target="tpu_custom_call" | custom-call | flops 1200000000 | bytes 6000000 | tf_op jit(solution)/shard_map/attention_kernel/pallas_call | solution.py:321
  34.4 2.5 %gradient_kernel.1 = (f32[16,72,128]{2,1,0:T(8,128)S(1)}, f32[16,72,128]{2,1,0:T(8,128)S(1)}) custom-call(s32[5]{0:T(128)S(1)} %stack.59.spot, bf16[2,64,512]{2,1,0:T(8,128)(2,1)S(1)} %bitcast.74, bf16[2,64,512]{2,1,0:T(8,128)(2,1)S(1)} %collective-permute-done.1.p1, bf16[2,64,512]{2,1,0:T(8,128)(2,1)S(1)} %collective-permute-done.2.p2, ...), custom_call_target="tpu_custom_call" | custom-call | flops 20000000000 | bytes 6000000 | tf_op jit(solution)/shard_map/gradient_kernel/pallas_call | solution.py:321
  36.9 0.0 copy-start.4
  36.9 3.9 %collective-permute-start.9 = (f32[16,72,128]{2,1,0:T(8,128)S(1)}, f32[16,72,128]{2,1,0:T(8,128)S(1)}, u32[]{:S(2)}, u32[]{:S(2)}) collective-permute-start(f32[16,72,128]{2,1,0:T(8,128)S(1)} %get-tuple-element.52), channel_id=1, source_target_pairs={{0,1},{1,0},{2,3},{3,2},{4,5},{5,4},{6,7},{7,6},{8,9},{9,8},{10,11... | collective-permute-start | bytes 1769480 | tf_op jit(solution)/shard_map/ppermute | solution.py:30
  40.8 0.4 collective-permute-start.13
  41.3 2.5 %collective-permute-start.14 = (bf16[128,512]{1,0:T(8,128)(2,1)S(1)}, bf16[128,512]{1,0:T(8,128)(2,1)S(1)}, u32[]{:S(2)}, u32[]{:S(2)}) collective-permute-start(bf16[128,512]{1,0:T(8,128)(2,1)S(1)} %get-tuple-element.46.r2), channel_id=1, source_target_pairs={{0,8},{1,9},{2,10},{3,11},{4,12},{5,13},{6,14},{7,15},{8,0},{9,1},... | collective-permute-start | bytes 393224 | tf_op jit(solution)/shard_map/ppermute | solution.py:30
  43.8 0.0 collective-permute-done.9
  43.8 0.1 fusion
  43.8 0.1 collective-permute-start.12
  43.9 0.1 collective-permute-start.11
  44.0 3.1 %collective-permute-start.10 = (bf16[4,72,128]{2,1,0:T(8,128)(2,1)S(1)}, bf16[4,72,128]{2,1,0:T(8,128)(2,1)S(1)}, u32[]{:S(2)}, u32[]{:S(2)}) collective-permute-start(bf16[4,72,128]{2,1,0:T(8,128)(2,1)S(1)} %get-tuple-element.79), channel_id=1, source_target_pairs={{0,16},{1,17},{2,18},{3,19},{4,20},{5,21},{6,22},{7,23},{8,24},{9,... | collective-permute-start | bytes 221192 | tf_op jit(solution)/shard_map/ppermute | solution.py:30
  47.2 1.0 %collective-permute-start.18 = (bf16[128,512]{1,0:T(8,128)(2,1)S(1)}, bf16[128,512]{1,0:T(8,128)(2,1)S(1)}, u32[]{:S(2)}, u32[]{:S(2)}) collective-permute-start(bf16[128,512]{1,0:T(8,128)(2,1)S(1)} %get-tuple-element.47.r3), channel_id=1, source_target_pairs={{0,12},{1,13},{2,14},{3,15},{4,8},{5,9},{6,10},{7,11},{8,4},{9,5},... | collective-permute-start | bytes 393224 | tf_op jit(solution)/shard_map/ppermute | solution.py:30
  48.1 2.0 %collective-permute-done.14.r2 = bf16[128,512]{1,0:T(8,128)(2,1)S(1)} collective-permute-done((bf16[128,512]{1,0:T(8,128)(2,1)S(1)}, bf16[128,512]{1,0:T(8,128)(2,1)S(1)}, u32[]{:S(2)}, u32[]{:S(2)}) %collective-permute-start.14) | collective-permute-done | bytes 131104 | tf_op jit(solution)/shard_map/ppermute | solution.py:30
  50.1 0.0 collective-permute-done.11
  50.1 0.0 collective-permute-done.10
  50.3 1.0 %collective-permute-start.17 = (f32[72,128]{1,0:T(8,128)S(1)}, f32[72,128]{1,0:T(8,128)S(1)}, u32[]{:S(2)}, u32[]{:S(2)}) collective-permute-start(f32[72,128]{1,0:T(8,128)S(1)} %get-tuple-element.81), channel_id=1, source_target_pairs={{0,12},{1,13},{2,14},{3,15},{4,8},{5,9},{6,10},{7,11},{8,4},{9,5},... | collective-permute-start | bytes 110600 | tf_op jit(solution)/shard_map/ppermute | solution.py:30
  51.3 0.8 collective-permute-start.16
  52.1 1.5 %collective-permute-start.15 = (f32[72,128]{1,0:T(8,128)S(1)}, f32[72,128]{1,0:T(8,128)S(1)}, u32[]{:S(2)}, u32[]{:S(2)}) collective-permute-start(f32[72,128]{1,0:T(8,128)S(1)} %get-tuple-element.83), channel_id=1, source_target_pairs={{0,4},{1,5},{2,6},{3,7},{4,0},{5,1},{6,2},{7,3},{8,12},{9,13},{10,... | collective-permute-start | bytes 110600 | tf_op jit(solution)/shard_map/ppermute | solution.py:30
  53.6 0.0 collective-permute-done.18.r3
  53.6 1.4 %token_kernel.1 = bf16[2,128,512]{2,1,0:T(8,128)(2,1)S(1)} custom-call(s32[5]{0:T(128)S(1)} %stack.59.spot, bf16[128,512]{1,0:T(8,128)(2,1)S(1)} %get-tuple-element.44.r0, bf16[128,512]{1,0:T(8,128)(2,1)S(1)} %collective-permute-done.13.r1, bf16[128,512]{1,0:T(8,128)(2,1)S(1)} %collective-permute-done.14.r2, ...), custom_call_target="tpu_custom_call" | custom-call | flops 500000000 | bytes 4000000 | tf_op jit(solution)/shard_map/token_kernel/pallas_call | solution.py:321
  55.0 0.6 collective-permute-done.16.m2
  55.6 0.0 collective-permute-done.15.m1
  55.6 6.4 %collective-permute-start.24 = (bf16[2,4,8,512]{3,2,1,0:T(8,128)(2,1)S(1)}, bf16[2,4,8,512]{3,2,1,0:T(8,128)(2,1)S(1)}, u32[]{:S(2)}, u32[]{:S(2)}) collective-permute-start(bf16[2,4,8,512]{3,2,1,0:T(8,128)(2,1)S(1)} %get-tuple-element.87), channel_id=1, source_target_pairs={{0,241},{1,242},{2,243},{3,240},{4,245},{5,246},{6,247},{7,244},{8... | collective-permute-start | bytes 196616 | tf_op jit(solution)/shard_map/ppermute | solution.py:30
  62.0 4.5 %collective-permute-start.23 = (bf16[2,4,8,512]{3,2,1,0:T(8,128)(2,1)S(1)}, bf16[2,4,8,512]{3,2,1,0:T(8,128)(2,1)S(1)}, u32[]{:S(2)}, u32[]{:S(2)}) collective-permute-start(bf16[2,4,8,512]{3,2,1,0:T(8,128)(2,1)S(1)} %get-tuple-element.88), channel_id=1, source_target_pairs={{0,240},{1,241},{2,242},{3,243},{4,244},{5,245},{6,246},{7,247},{8... | collective-permute-start | bytes 196616 | tf_op jit(solution)/shard_map/ppermute | solution.py:30
  66.5 0.0 collective-permute-start.22
  66.5 0.7 z_parts_kernel.1
  67.2 0.1 collective-permute-start.19
  67.3 2.2 %collective-permute-start.20 = (f32[72,128]{1,0:T(8,128)S(1)}, f32[72,128]{1,0:T(8,128)S(1)}, u32[]{:S(2)}, u32[]{:S(2)}) collective-permute-start(f32[72,128]{1,0:T(8,128)S(1)} %get-tuple-element.63), channel_id=1, source_target_pairs={{0,128},{1,129},{2,130},{3,131},{4,132},{5,133},{6,134},{7,135},{8... | collective-permute-start | bytes 110600 | tf_op jit(solution)/shard_map/ppermute | solution.py:30
  69.5 0.0 collective-permute-done.24.other_low
  69.5 3.5 %collective-permute-start.21 = (f32[72,128]{1,0:T(8,128)S(1)}, f32[72,128]{1,0:T(8,128)S(1)}, u32[]{:S(2)}, u32[]{:S(2)}) collective-permute-start(f32[72,128]{1,0:T(8,128)S(1)} %get-tuple-element.64), channel_id=1, source_target_pairs={{0,192},{1,193},{2,194},{3,195},{4,196},{5,197},{6,198},{7,199},{8... | collective-permute-start | bytes 110600 | tf_op jit(solution)/shard_map/ppermute | solution.py:30
  73.0 0.0 collective-permute-done.23.other_high
  73.0 0.0 collective-permute-done.22.mine_low
  73.0 1.3 %merge_kernel.1 = (bf16[8,16,512]{2,1,0:T(8,128)(2,1)}, bf16[8,16,512]{2,1,0:T(8,128)(2,1)}) custom-call(s32[5]{0:T(128)S(1)} %stack.59.spot, bf16[8,16,512]{2,1,0:T(8,128)(2,1)S(1)} %bitcast.67, bf16[8,16,512]{2,1,0:T(8,128)(2,1)S(1)} %bitcast.69, bf16[2,4,8,512]{3,2,1,0:T(8,128)(2,1)S(1)} %get-tuple-element.90.mine_high, ...), custom_call_target="tpu_custom_call" | custom-call | tf_op jit(solution)/shard_map/merge_kernel/pallas_call | solution.py:321
  74.3 0.0 collective-permute-done.19
  74.3 0.0 collective-permute-done.20
  74.3 1.1 %collective-permute-done.21 = f32[72,128]{1,0:T(8,128)S(1)} collective-permute-done((f32[72,128]{1,0:T(8,128)S(1)}, f32[72,128]{1,0:T(8,128)S(1)}, u32[]{:S(2)}, u32[]{:S(2)}) %collective-permute-start.21) | collective-permute-done | bytes 36896 | tf_op jit(solution)/shard_map/ppermute | solution.py:30
  75.4 3.0 %collective-permute-start.27 = (f32[72,128]{1,0:T(8,128)S(1)}, f32[72,128]{1,0:T(8,128)S(1)}, u32[]{:S(2)}, u32[]{:S(2)}) collective-permute-start(f32[72,128]{1,0:T(8,128)S(1)} %add_add_fusion.near), channel_id=1, source_target_pairs={{0,3},{1,2},{2,1},{3,0},{4,7},{5,6},{6,5},{7,4},{8,11},{9,10},{10,... | collective-permute-start | bytes 110600 | tf_op jit(solution)/shard_map/ppermute | solution.py:30
  78.4 0.5 collective-permute-start.25
  78.9 1.1 %collective-permute-done.27.both_in = f32[72,128]{1,0:T(8,128)S(1)} collective-permute-done((f32[72,128]{1,0:T(8,128)S(1)}, f32[72,128]{1,0:T(8,128)S(1)}, u32[]{:S(2)}, u32[]{:S(2)}) %collective-permute-start.27) | collective-permute-done | bytes 36896 | tf_op jit(solution)/shard_map/ppermute | solution.py:30
  80.1 1.2 %collective-permute-done.26.z_in = f32[72,128]{1,0:T(8,128)S(1)} collective-permute-done((f32[72,128]{1,0:T(8,128)S(1)}, f32[72,128]{1,0:T(8,128)S(1)}, u32[]{:S(2)}, u32[]{:S(2)}) %collective-permute-start.26) | collective-permute-done | bytes 36896 | tf_op jit(solution)/shard_map/ppermute | solution.py:30
  81.2 1.2 %last_kernel.1 = (f32[24,512]{1,0:T(8,128)}, f32[8,512]{1,0:T(8,128)}, f32[2,8]{1,0:T(2,128)}) custom-call(s32[5]{0:T(128)S(1)} %stack.59.spot, f32[72,128]{1,0:T(8,128)S(1)} %add_add_fusion.near, f32[72,128]{1,0:T(8,128)S(1)} %collective-permute-done.25.core_in, f32[72,128]{1,0:T(8,128)S(1)} %collective-permute-done.26.z_in, ...), custom_call_target="tpu_custom_call" | custom-call | tf_op jit(solution)/shard_map/last_kernel/pallas_call | solution.py:321
  (27 shorter events, 0.2 us)
Async XLA Ops:
  0.6 22.4 %copy-start = (bf16[512,1536]{1,0:T(8,128)(2,1)S(1)}, bf16[512,1536]{1,0:T(8,128)(2,1)}, u32[]{:S(2)}) copy-start(bf16[512,1536]{1,0:T(8,128)(2,1)} %w_qkv.7) | copy-start | bytes 4718596
  0.6 22.4 %copy-start.5 = (f32[2,512]{1,0:T(2,128)S(1)}, f32[2,512]{1,0:T(2,128)}, u32[]{:S(2)}) copy-start(f32[2,512]{1,0:T(2,128)} %norm.5) | copy-start | bytes 12292
  1.9 10.6 %collective-permute-start = (bf16[2,4,8,512]{3,2,1,0:T(8,128)(2,1)S(1)}, bf16[2,4,8,512]{3,2,1,0:T(8,128)(2,1)S(1)}, u32[]{:S(2)}, u32[]{:S(2)}) collective-permute-start(bf16[2,4,8,512]{3,2,1,0:T(8,128)(2,1)S(1)} %get-tuple-element.94), channel_id=1, source_target_pairs={{0,3},{1,0},{2,1},{3,2},{4,7},{5,4},{6,5},{7,6},{8,11},{9,8},{10,9... | collective-permute-start | bytes 196616 | tf_op jit(solution)/shard_map/ppermute | solution.py:30
  5.3 10.8 %collective-permute-start.4 = (bf16[2,4,8,512]{3,2,1,0:T(8,128)(2,1)S(1)}, bf16[2,4,8,512]{3,2,1,0:T(8,128)(2,1)S(1)}, u32[]{:S(2)}, u32[]{:S(2)}) collective-permute-start(bf16[2,4,8,512]{3,2,1,0:T(8,128)(2,1)S(1)} %get-tuple-element.91), channel_id=1, source_target_pairs={{0,240},{1,241},{2,242},{3,243},{4,244},{5,245},{6,246},{7,247},{8... | collective-permute-start | bytes 196616 | tf_op jit(solution)/shard_map/ppermute | solution.py:30
  12.1 7.6 %collective-permute-start.5 = (bf16[2,4,8,512]{3,2,1,0:T(8,128)(2,1)S(1)}, bf16[2,4,8,512]{3,2,1,0:T(8,128)(2,1)S(1)}, u32[]{:S(2)}, u32[]{:S(2)}) collective-permute-start(bf16[2,4,8,512]{3,2,1,0:T(8,128)(2,1)S(1)} %get-tuple-element.92), channel_id=1, source_target_pairs={{0,243},{1,240},{2,241},{3,242},{4,247},{5,244},{6,245},{7,246},{8... | collective-permute-start | bytes 196616 | tf_op jit(solution)/shard_map/ppermute | solution.py:30
  12.6 10.2 %collective-permute-start.3 = (bf16[2,64,512]{2,1,0:T(8,128)(2,1)S(1)}, bf16[2,64,512]{2,1,0:T(8,128)(2,1)S(1)}, u32[]{:S(2)}, u32[]{:S(2)}) collective-permute-start(bf16[2,64,512]{2,1,0:T(8,128)(2,1)S(1)} %bitcast.70), channel_id=1, source_target_pairs={{0,12},{1,13},{2,14},{3,15},{4,8},{5,9},{6,10},{7,11},{8,4},{9,5},... | collective-permute-start | bytes 393224 | tf_op jit(solution)/shard_map/ppermute | solution.py:30
  15.1 7.9 %collective-permute-start.2 = (bf16[2,64,512]{2,1,0:T(8,128)(2,1)S(1)}, bf16[2,64,512]{2,1,0:T(8,128)(2,1)S(1)}, u32[]{:S(2)}, u32[]{:S(2)}) collective-permute-start(bf16[2,64,512]{2,1,0:T(8,128)(2,1)S(1)} %bitcast.71), channel_id=1, source_target_pairs={{0,8},{1,9},{2,10},{3,11},{4,12},{5,13},{6,14},{7,15},{8,0},{9,1},... | collective-permute-start | bytes 393224 | tf_op jit(solution)/shard_map/ppermute | solution.py:30
  15.7 7.4 %collective-permute-start.1 = (bf16[2,64,512]{2,1,0:T(8,128)(2,1)S(1)}, bf16[2,64,512]{2,1,0:T(8,128)(2,1)S(1)}, u32[]{:S(2)}, u32[]{:S(2)}) collective-permute-start(bf16[2,64,512]{2,1,0:T(8,128)(2,1)S(1)} %bitcast.72), channel_id=1, source_target_pairs={{0,4},{1,5},{2,6},{3,7},{4,0},{5,1},{6,2},{7,3},{8,12},{9,13},{10,... | collective-permute-start | bytes 393224 | tf_op jit(solution)/shard_map/ppermute | solution.py:30
  19.7 5.9 %collective-permute-start.8 = (bf16[2,64,512]{2,1,0:T(8,128)(2,1)S(1)}, bf16[2,64,512]{2,1,0:T(8,128)(2,1)S(1)}, u32[]{:S(2)}, u32[]{:S(2)}) collective-permute-start(bf16[2,64,512]{2,1,0:T(8,128)(2,1)S(1)} %bitcast.76), channel_id=1, source_target_pairs={{0,12},{1,13},{2,14},{3,15},{4,8},{5,9},{6,10},{7,11},{8,4},{9,5},... | collective-permute-start | bytes 393224 | tf_op jit(solution)/shard_map/ppermute | solution.py:30
  22.3 5.4 %collective-permute-start.7 = (bf16[2,64,512]{2,1,0:T(8,128)(2,1)S(1)}, bf16[2,64,512]{2,1,0:T(8,128)(2,1)S(1)}, u32[]{:S(2)}, u32[]{:S(2)}) collective-permute-start(bf16[2,64,512]{2,1,0:T(8,128)(2,1)S(1)} %bitcast.77), channel_id=1, source_target_pairs={{0,8},{1,9},{2,10},{3,11},{4,12},{5,13},{6,14},{7,15},{8,0},{9,1},... | collective-permute-start | bytes 393224 | tf_op jit(solution)/shard_map/ppermute | solution.py:30
  22.8 4.9 %collective-permute-start.6 = (bf16[2,64,512]{2,1,0:T(8,128)(2,1)S(1)}, bf16[2,64,512]{2,1,0:T(8,128)(2,1)S(1)}, u32[]{:S(2)}, u32[]{:S(2)}) collective-permute-start(bf16[2,64,512]{2,1,0:T(8,128)(2,1)S(1)} %bitcast.78), channel_id=1, source_target_pairs={{0,4},{1,5},{2,6},{3,7},{4,0},{5,1},{6,2},{7,3},{8,12},{9,13},{10,... | collective-permute-start | bytes 393224 | tf_op jit(solution)/shard_map/ppermute | solution.py:30
  23.1 1.0 %copy-start.3 = (bf16[512,512]{1,0:T(8,128)(2,1)S(1)}, bf16[512,512]{1,0:T(8,128)(2,1)}, u32[]{:S(2)}) copy-start(bf16[512,512]{1,0:T(8,128)(2,1)} %w_proj.5) | copy-start | bytes 1572868
  36.9 16.7 %copy-start.4 = (bf16[512,512]{1,0:T(8,128)(2,1)S(1)}, bf16[512,512]{1,0:T(8,128)(2,1)}, u32[]{:S(2)}) copy-start(bf16[512,512]{1,0:T(8,128)(2,1)} %w_proj.5) | copy-start | bytes 1572868
  36.9 6.8 %collective-permute-start.9 = (f32[16,72,128]{2,1,0:T(8,128)S(1)}, f32[16,72,128]{2,1,0:T(8,128)S(1)}, u32[]{:S(2)}, u32[]{:S(2)}) collective-permute-start(f32[16,72,128]{2,1,0:T(8,128)S(1)} %get-tuple-element.52), channel_id=1, source_target_pairs={{0,1},{1,0},{2,3},{3,2},{4,5},{5,4},{6,7},{7,6},{8,9},{9,8},{10,11... | collective-permute-start | bytes 1769480 | tf_op jit(solution)/shard_map/ppermute | solution.py:30
  40.8 6.3 %collective-permute-start.13 = (bf16[128,512]{1,0:T(8,128)(2,1)S(1)}, bf16[128,512]{1,0:T(8,128)(2,1)S(1)}, u32[]{:S(2)}, u32[]{:S(2)}) collective-permute-start(bf16[128,512]{1,0:T(8,128)(2,1)S(1)} %get-tuple-element.45.r1), channel_id=1, source_target_pairs={{0,4},{1,5},{2,6},{3,7},{4,0},{5,1},{6,2},{7,3},{8,12},{9,13},{10,... | collective-permute-start | bytes 393224 | tf_op jit(solution)/shard_map/ppermute | solution.py:30
  41.3 8.9 %collective-permute-start.14 = (bf16[128,512]{1,0:T(8,128)(2,1)S(1)}, bf16[128,512]{1,0:T(8,128)(2,1)S(1)}, u32[]{:S(2)}, u32[]{:S(2)}) collective-permute-start(bf16[128,512]{1,0:T(8,128)(2,1)S(1)} %get-tuple-element.46.r2), channel_id=1, source_target_pairs={{0,8},{1,9},{2,10},{3,11},{4,12},{5,13},{6,14},{7,15},{8,0},{9,1},... | collective-permute-start | bytes 393224 | tf_op jit(solution)/shard_map/ppermute | solution.py:30
  43.8 6.3 %collective-permute-start.12 = (bf16[4,72,128]{2,1,0:T(8,128)(2,1)S(1)}, bf16[4,72,128]{2,1,0:T(8,128)(2,1)S(1)}, u32[]{:S(2)}, u32[]{:S(2)}) collective-permute-start(bf16[4,72,128]{2,1,0:T(8,128)(2,1)S(1)} %get-tuple-element.77), channel_id=1, source_target_pairs={{0,48},{1,49},{2,50},{3,51},{4,52},{5,53},{6,54},{7,55},{8,56},{9,... | collective-permute-start | bytes 221192 | tf_op jit(solution)/shard_map/ppermute | solution.py:30
  43.9 6.2 %collective-permute-start.11 = (bf16[4,72,128]{2,1,0:T(8,128)(2,1)S(1)}, bf16[4,72,128]{2,1,0:T(8,128)(2,1)S(1)}, u32[]{:S(2)}, u32[]{:S(2)}) collective-permute-start(bf16[4,72,128]{2,1,0:T(8,128)(2,1)S(1)} %get-tuple-element.78), channel_id=1, source_target_pairs={{0,32},{1,33},{2,34},{3,35},{4,36},{5,37},{6,38},{7,39},{8,40},{9,... | collective-permute-start | bytes 221192 | tf_op jit(solution)/shard_map/ppermute | solution.py:30
  44.0 6.1 %collective-permute-start.10 = (bf16[4,72,128]{2,1,0:T(8,128)(2,1)S(1)}, bf16[4,72,128]{2,1,0:T(8,128)(2,1)S(1)}, u32[]{:S(2)}, u32[]{:S(2)}) collective-permute-start(bf16[4,72,128]{2,1,0:T(8,128)(2,1)S(1)} %get-tuple-element.79), channel_id=1, source_target_pairs={{0,16},{1,17},{2,18},{3,19},{4,20},{5,21},{6,22},{7,23},{8,24},{9,... | collective-permute-start | bytes 221192 | tf_op jit(solution)/shard_map/ppermute | solution.py:30
  47.2 6.4 %collective-permute-start.18 = (bf16[128,512]{1,0:T(8,128)(2,1)S(1)}, bf16[128,512]{1,0:T(8,128)(2,1)S(1)}, u32[]{:S(2)}, u32[]{:S(2)}) collective-permute-start(bf16[128,512]{1,0:T(8,128)(2,1)S(1)} %get-tuple-element.47.r3), channel_id=1, source_target_pairs={{0,12},{1,13},{2,14},{3,15},{4,8},{5,9},{6,10},{7,11},{8,4},{9,5},... | collective-permute-start | bytes 393224 | tf_op jit(solution)/shard_map/ppermute | solution.py:30
  50.3 4.7 %collective-permute-start.17 = (f32[72,128]{1,0:T(8,128)S(1)}, f32[72,128]{1,0:T(8,128)S(1)}, u32[]{:S(2)}, u32[]{:S(2)}) collective-permute-start(f32[72,128]{1,0:T(8,128)S(1)} %get-tuple-element.81), channel_id=1, source_target_pairs={{0,12},{1,13},{2,14},{3,15},{4,8},{5,9},{6,10},{7,11},{8,4},{9,5},... | collective-permute-start | bytes 110600 | tf_op jit(solution)/shard_map/ppermute | solution.py:30
  51.3 4.3 %collective-permute-start.16 = (f32[72,128]{1,0:T(8,128)S(1)}, f32[72,128]{1,0:T(8,128)S(1)}, u32[]{:S(2)}, u32[]{:S(2)}) collective-permute-start(f32[72,128]{1,0:T(8,128)S(1)} %get-tuple-element.82), channel_id=1, source_target_pairs={{0,8},{1,9},{2,10},{3,11},{4,12},{5,13},{6,14},{7,15},{8,0},{9,1},... | collective-permute-start | bytes 110600 | tf_op jit(solution)/shard_map/ppermute | solution.py:30
  52.1 20.9 %copy-start.1 = (bf16[1,1,8,16,512]{4,3,2,1,0:T(8,128)(2,1)S(1)}, bf16[1,1,8,16,512]{4,3,2,1,0:T(8,128)(2,1)}, u32[]{:S(2)}) copy-start(bf16[1,1,8,16,512]{4,3,2,1,0:T(8,128)(2,1)} %param.5) | copy-start | bytes 393220
  52.1 20.9 %copy-start.2 = (bf16[1,1,8,16,512]{4,3,2,1,0:T(8,128)(2,1)S(1)}, bf16[1,1,8,16,512]{4,3,2,1,0:T(8,128)(2,1)}, u32[]{:S(2)}) copy-start(bf16[1,1,8,16,512]{4,3,2,1,0:T(8,128)(2,1)} %param.9) | copy-start | bytes 393220
  52.1 3.5 %collective-permute-start.15 = (f32[72,128]{1,0:T(8,128)S(1)}, f32[72,128]{1,0:T(8,128)S(1)}, u32[]{:S(2)}, u32[]{:S(2)}) collective-permute-start(f32[72,128]{1,0:T(8,128)S(1)} %get-tuple-element.83), channel_id=1, source_target_pairs={{0,4},{1,5},{2,6},{3,7},{4,0},{5,1},{6,2},{7,3},{8,12},{9,13},{10,... | collective-permute-start | bytes 110600 | tf_op jit(solution)/shard_map/ppermute | solution.py:30
  55.6 13.9 %collective-permute-start.24 = (bf16[2,4,8,512]{3,2,1,0:T(8,128)(2,1)S(1)}, bf16[2,4,8,512]{3,2,1,0:T(8,128)(2,1)S(1)}, u32[]{:S(2)}, u32[]{:S(2)}) collective-permute-start(bf16[2,4,8,512]{3,2,1,0:T(8,128)(2,1)S(1)} %get-tuple-element.87), channel_id=1, source_target_pairs={{0,241},{1,242},{2,243},{3,240},{4,245},{5,246},{6,247},{7,244},{8... | collective-permute-start | bytes 196616 | tf_op jit(solution)/shard_map/ppermute | solution.py:30
  62.0 10.9 %collective-permute-start.23 = (bf16[2,4,8,512]{3,2,1,0:T(8,128)(2,1)S(1)}, bf16[2,4,8,512]{3,2,1,0:T(8,128)(2,1)S(1)}, u32[]{:S(2)}, u32[]{:S(2)}) collective-permute-start(bf16[2,4,8,512]{3,2,1,0:T(8,128)(2,1)S(1)} %get-tuple-element.88), channel_id=1, source_target_pairs={{0,240},{1,241},{2,242},{3,243},{4,244},{5,245},{6,246},{7,247},{8... | collective-permute-start | bytes 196616 | tf_op jit(solution)/shard_map/ppermute | solution.py:30
  66.5 6.5 %collective-permute-start.22 = (bf16[2,4,8,512]{3,2,1,0:T(8,128)(2,1)S(1)}, bf16[2,4,8,512]{3,2,1,0:T(8,128)(2,1)S(1)}, u32[]{:S(2)}, u32[]{:S(2)}) collective-permute-start(bf16[2,4,8,512]{3,2,1,0:T(8,128)(2,1)S(1)} %get-tuple-element.89), channel_id=1, source_target_pairs={{0,1},{1,2},{2,3},{3,0},{4,5},{5,6},{6,7},{7,4},{8,9},{9,10},{10,1... | collective-permute-start | bytes 196616 | tf_op jit(solution)/shard_map/ppermute | solution.py:30
  67.2 7.1 %collective-permute-start.19 = (f32[72,128]{1,0:T(8,128)S(1)}, f32[72,128]{1,0:T(8,128)S(1)}, u32[]{:S(2)}, u32[]{:S(2)}) collective-permute-start(f32[72,128]{1,0:T(8,128)S(1)} %get-tuple-element.62), channel_id=1, source_target_pairs={{0,64},{1,65},{2,66},{3,67},{4,68},{5,69},{6,70},{7,71},{8,72},{9,... | collective-permute-start | bytes 110600 | tf_op jit(solution)/shard_map/ppermute | solution.py:30
  67.3 7.0 %collective-permute-start.20 = (f32[72,128]{1,0:T(8,128)S(1)}, f32[72,128]{1,0:T(8,128)S(1)}, u32[]{:S(2)}, u32[]{:S(2)}) collective-permute-start(f32[72,128]{1,0:T(8,128)S(1)} %get-tuple-element.63), channel_id=1, source_target_pairs={{0,128},{1,129},{2,130},{3,131},{4,132},{5,133},{6,134},{7,135},{8... | collective-permute-start | bytes 110600 | tf_op jit(solution)/shard_map/ppermute | solution.py:30
  69.5 5.9 %collective-permute-start.21 = (f32[72,128]{1,0:T(8,128)S(1)}, f32[72,128]{1,0:T(8,128)S(1)}, u32[]{:S(2)}, u32[]{:S(2)}) collective-permute-start(f32[72,128]{1,0:T(8,128)S(1)} %get-tuple-element.64), channel_id=1, source_target_pairs={{0,192},{1,193},{2,194},{3,195},{4,196},{5,197},{6,198},{7,199},{8... | collective-permute-start | bytes 110600 | tf_op jit(solution)/shard_map/ppermute | solution.py:30
  75.4 4.6 %collective-permute-start.27 = (f32[72,128]{1,0:T(8,128)S(1)}, f32[72,128]{1,0:T(8,128)S(1)}, u32[]{:S(2)}, u32[]{:S(2)}) collective-permute-start(f32[72,128]{1,0:T(8,128)S(1)} %add_add_fusion.near), channel_id=1, source_target_pairs={{0,3},{1,2},{2,1},{3,0},{4,7},{5,6},{6,5},{7,4},{8,11},{9,10},{10,... | collective-permute-start | bytes 110600 | tf_op jit(solution)/shard_map/ppermute | solution.py:30
  78.4 2.8 %collective-permute-start.26 = (f32[72,128]{1,0:T(8,128)S(1)}, f32[72,128]{1,0:T(8,128)S(1)}, u32[]{:S(2)}, u32[]{:S(2)}) collective-permute-start(f32[72,128]{1,0:T(8,128)S(1)} %add_add_fusion.near), channel_id=1, source_target_pairs={{0,2},{1,3},{2,0},{3,1},{4,6},{5,7},{6,4},{7,5},{8,10},{9,11},{10,... | collective-permute-start | bytes 110600 | tf_op jit(solution)/shard_map/ppermute | solution.py:30
  78.4 2.8 %collective-permute-start.25 = (f32[72,128]{1,0:T(8,128)S(1)}, f32[72,128]{1,0:T(8,128)S(1)}, u32[]{:S(2)}, u32[]{:S(2)}) collective-permute-start(f32[72,128]{1,0:T(8,128)S(1)} %add_add_fusion.near), channel_id=1, source_target_pairs={{0,1},{1,0},{2,3},{3,2},{4,5},{5,4},{6,7},{7,6},{8,9},{9,8},{10,11... | collective-permute-start | bytes 110600 | tf_op jit(solution)/shard_map/ppermute | solution.py:30

commit v9 on v8

--- a/solution.py
+++ b/solution.py
@@ -222,7 +222,7 @@
                     out[block, 64:, :] = jnp.zeros((8, 128), F32)
 
 
-def z_parts_kernel(spot, m0, m1, m2, m3, *outs):
+def z_parts_kernel(spot, m0, m1, m2, m3, mark, *outs):
     x, y, z = spot[0], spot[1], spot[3]
     pieces = (m0, m1, m2, m3)
 
@@ -293,7 +293,7 @@
 
 
 def token_kernel(
-    spot, r0, r1, r2, r3, own0, own1, w_qkv, w_proj, norm, out
+    spot, r0, r1, r2, r3, own0, own1, w_qkv, w_proj, norm, out, mark
 ):
     x = spot[0]
     projected = jnp.zeros((SLAB, C), F32)
@@ -307,6 +307,7 @@
             lanes = slice(third * OWN, (third + 1) * OWN)
             columns = w_qkv[:, pl.ds(pl.multiple_of(start + C * third, OWN), OWN)]
             d_normed += dot_nt(rows[:, lanes], columns)
+    mark[...] = projected[:8, :128]
     out[0] = projected.astype(BF16)
     unit, inv_scale = unit_of(jnp.concatenate([own0[0], own1[0]], 0))
     d_unit = d_normed * norm[0:1, :]
@@ -396,11 +397,11 @@
     *from_y, returned[1], returned[2] = lax.optimization_barrier(
         (*from_y, returned[1], returned[2])
     )
-    (back,) = call(
+    back, mark = call(
         token_kernel,
         spot,
         (*returned, part0, part1, w_qkv, w_proj, norm_params),
-        [((2, SLAB, C), BF16)],
+        [((2, SLAB, C), BF16), ((8, 128), F32)],
         flops=500_000_000,
         moved=4_000_000,
     )
@@ -408,26 +409,28 @@
     sums = [piece.astype(F32) for piece in from_y]
     x_parts = [(sums[0][k] + sums[1][k]) + (sums[2][k] + sums[3][k]) for k in range(4)]
     from_x = [x_parts[0]] + [move(x_parts[mask], over_x(mask)) for mask in (1, 2, 3)]
-    from_x[1], from_x[2], from_x[3], back = lax.optimization_barrier(
-        (from_x[1], from_x[2], from_x[3], back)
+    from_x[1], from_x[2], from_x[3], mark = lax.optimization_barrier(
+        (from_x[1], from_x[2], from_x[3], mark)
     )
     back = back.reshape(2, 4, 4, 8, C)
-    lower = move(back[:, 1], lambda p, n: (p, n + 1))
-    other_upper = move(back[:, 2], lambda p, n: (partner_of(p), n))
-    other_lower = move(back[:, 3], lambda p, n: (partner_of(p), n + 1))
-    z_parts = call(z_parts_kernel, spot, from_x, [share] * 4)
+    crossed = move(back[:, 2:], lambda p, n: (partner_of(p), n))
+    z_parts = call(z_parts_kernel, spot, (*from_x, mark), [share] * 4)
+    line = [z_parts[0]] + [move(z_parts[mask], over_z(mask)) for mask in (1, 2, 3)]
+    line[1], line[2], line[3], crossed = lax.optimization_barrier(
+        (line[1], line[2], line[3], crossed)
+    )
+    line = (line[0] + line[1]) + (line[2] + line[3])
+    last = [line] + [move(line, over_narrow(mask)) for mask in (1, 2, 3)]
+    lower = move(jnp.stack([back[:, 1], crossed[:, 1]], 1), lambda p, n: (p, n + 1))
     output, grad_inputs = call(
         merge_kernel,
         spot,
-        (own_inputs, own_upstream, back[:, 0], lower, other_upper, other_lower),
+        (own_inputs, own_upstream, back[:, 0], lower[:, 0], crossed[:, 0], lower[:, 1]),
         [((8, 16, C), BF16)] * 2,
     )
-    line = [z_parts[0]] + [move(z_parts[mask], over_z(mask)) for mask in (1, 2, 3)]
-    line[1], line[2], line[3], output, grad_inputs = lax.optimization_barrier(
-        (line[1], line[2], line[3], output, grad_inputs)
-    )
-    line = (line[0] + line[1]) + (line[2] + line[3])
-    last = [line] + [move(line, over_narrow(mask)) for mask in (1, 2, 3)]
+    last[1], last[2], last[3], output, grad_inputs = lax.optimization_barrier(
+        (last[1], last[2], last[3], output, grad_inputs)
+    )
     grad_qkv, grad_proj, grad_norm = call(
         last_kernel, spot, last, [((24, C), F32), ((8, C), F32), ((2, 8), F32)]
     )

time: 82.6 us -> 78.3 us (0.948)
  starting transfers between devices: 51.8 us -> 49 us
  waiting for transfers between devices: 12.2 us -> 10.6 us
    ppermute x28 -> x27, starting transfers between devices: 51.8 us -> 49 us  [move(): return lax.ppermute(value, ('wide', 'narrow'), pairs)]
    ppermute x28 -> x27, waiting for transfers between devices: 12.2 us -> 10.6 us  [move(): return lax.ppermute(value, ('wide', 'narrow'), pairs)]
  transfers between devices with their start and end apart: 28 -> 27, of which waited for: 8 -> 7; matrix products, arithmetic and copies ran while one was open for 0% -> 1% of each run, Pallas kernels for 5% -> 6%
where the time goes in v9:
time: 78.3 us; the launch traced here: 78.1 us
  starting transfers between devices  49 us (63%)
  Pallas kernels  14.9 us (19%)
  waiting for transfers between devices  10.6 us (14%)
  other arithmetic  1.47 us (2%)
  local copies, waits for them, and re-layouts  1.23 us (2%)
  between operations  0.97 us (1%)
    ppermute x27, starting transfers between devices, move(): return lax.ppermute(value, ('wide', 'narrow'), pairs)  49 us
    pallas_call x7, Pallas kernels, call(): pl.pallas_call(kernel, out_shape=[jax.ShapeDtypeStruct(shape, dtype) for...  14.9 us
    ppermute x27, waiting for transfers between devices, move(): return lax.ppermute(value, ('wide', 'narrow'), pairs)  10.6 us
  transfers between devices with their start and end apart: 27, of which 7 were waited for; matrix products, arithmetic and copies ran while one was open for 1% of the time, Pallas kernels for 6%

profile of v9, /device:TPU:1, one launch (start us, length us, event | category | flops | bytes accessed | tf_op | source)
XLA Modules:
  0.0 78.1 jit_solution(6994151882179411885)
XLA Ops:
  0.7 1.2 %broadcast_select_fusion = (bf16[2,8,8,512]{3,2,1,0:T(8,128)(2,1)S(1)}, bf16[2,8,8,512]{3,2,1,0:T(8,128)(2,1)S(1)}) fusion(pred[8]{0:T(512)(128)(4,1)S(1)} %compare_compare_fusion, bf16[1,8,2,8,512]{4,3,2,1,0:T(8,128)(2,1)} %bitcast.63, bf16[1,8,2,8,512]{4,3,2,1,0:T(8,128)(2,1)} %bitcast.61), kind=kLoop, calls=%fused_computation.16 | loop fusion | flops 327680 | bytes 524296 | tf_op jit(solution)/shard_map/jit(_where)/select_n | solution.py:348
  1.9 3.3 %collective-permute-start = (bf16[2,4,8,512]{3,2,1,0:T(8,128)(2,1)S(1)}, bf16[2,4,8,512]{3,2,1,0:T(8,128)(2,1)S(1)}, u32[]{:S(2)}, u32[]{:S(2)}) collective-permute-start(bf16[2,4,8,512]{3,2,1,0:T(8,128)(2,1)S(1)} %get-tuple-element.108), channel_id=1, source_target_pairs={{0,3},{1,0},{2,1},{3,2},{4,7},{5,4},{6,5},{7,6},{8,11},{9,8},{10,9... | collective-permute-start | bytes 196616 | tf_op jit(solution)/shard_map/ppermute | solution.py:30
  5.3 6.8 %collective-permute-start.4 = (bf16[2,4,8,512]{3,2,1,0:T(8,128)(2,1)S(1)}, bf16[2,4,8,512]{3,2,1,0:T(8,128)(2,1)S(1)}, u32[]{:S(2)}, u32[]{:S(2)}) collective-permute-start(bf16[2,4,8,512]{3,2,1,0:T(8,128)(2,1)S(1)} %get-tuple-element.105), channel_id=1, source_target_pairs={{0,240},{1,241},{2,242},{3,243},{4,244},{5,245},{6,246},{7,247},{8... | collective-permute-start | bytes 196616 | tf_op jit(solution)/shard_map/ppermute | solution.py:30
  12.1 0.4 collective-permute-start.5
  12.5 0.0 collective-permute-done
  12.6 2.6 %collective-permute-start.3 = (bf16[2,64,512]{2,1,0:T(8,128)(2,1)S(1)}, bf16[2,64,512]{2,1,0:T(8,128)(2,1)S(1)}, u32[]{:S(2)}, u32[]{:S(2)}) collective-permute-start(bf16[2,64,512]{2,1,0:T(8,128)(2,1)S(1)} %bitcast.65), channel_id=1, source_target_pairs={{0,12},{1,13},{2,14},{3,15},{4,8},{5,9},{6,10},{7,11},{8,4},{9,5},... | collective-permute-start | bytes 393224 | tf_op jit(solution)/shard_map/ppermute | solution.py:30
  15.1 0.5 collective-permute-start.2
  15.7 0.3 collective-permute-start.1
  15.9 0.1 pad_add_fusion.flags
  16.0 0.1 stack.62.spot
  16.1 0.0 collective-permute-done.4
  16.1 3.6 %collective-permute-done.5 = bf16[2,4,8,512]{3,2,1,0:T(8,128)(2,1)S(1)} collective-permute-done((bf16[2,4,8,512]{3,2,1,0:T(8,128)(2,1)S(1)}, bf16[2,4,8,512]{3,2,1,0:T(8,128)(2,1)S(1)}, u32[]{:S(2)}, u32[]{:S(2)}) %collective-permute-start.5) | collective-permute-done | bytes 65568 | tf_op jit(solution)/shard_map/ppermute | solution.py:30
  19.7 2.6 %collective-permute-start.8 = (bf16[2,64,512]{2,1,0:T(8,128)(2,1)S(1)}, bf16[2,64,512]{2,1,0:T(8,128)(2,1)S(1)}, u32[]{:S(2)}, u32[]{:S(2)}) collective-permute-start(bf16[2,64,512]{2,1,0:T(8,128)(2,1)S(1)} %bitcast.71), channel_id=1, source_target_pairs={{0,12},{1,13},{2,14},{3,15},{4,8},{5,9},{6,10},{7,11},{8,4},{9,5},... | collective-permute-start | bytes 393224 | tf_op jit(solution)/shard_map/ppermute | solution.py:30
  22.3 0.5 collective-permute-start.7
  22.8 0.0 collective-permute-done.3.p3
  22.8 0.3 collective-permute-start.6
  23.1 0.0 collective-permute-done.2.p2
  23.1 0.0 copy-start.1
  23.1 1.0 %copy-done.1 = bf16[512,512]{1,0:T(8,128)(2,1)S(1)} copy-done((bf16[512,512]{1,0:T(8,128)(2,1)S(1)}, bf16[512,512]{1,0:T(8,128)(2,1)}, u32[]{:S(2)}) %copy-start.1) | copy-done | bytes 524312
  24.1 1.1 %first_kernel.1 = (bf16[256,512]{1,0:T(8,128)(2,1)S(1)}, bf16[256,384]{1,0:T(8,128)(2,1)S(1)}, bf16[256,128]{1,0:T(8,128)(2,1)S(1)}) custom-call(s32[4]{0:T(128)S(1)} %pad_add_fusion.flags, bf16[2,64,512]{2,1,0:T(8,128)(2,1)S(1)} %bitcast.68, bf16[2,64,512]{2,1,0:T(8,128)(2,1)S(1)} %collective-permute-done.1.p1, ...), custom_call_target="tpu_custom_call" | custom-call | flops 10000000000 | bytes 3000000 | tf_op jit(solution)/shard_map/first_kernel/pallas_call | solution.py:322
  25.2 0.4 collective-permute-done.8.p3.p7
  25.6 2.1 %collective-permute-done.7.p2.p6 = bf16[2,64,512]{2,1,0:T(8,128)(2,1)S(1)} collective-permute-done((bf16[2,64,512]{2,1,0:T(8,128)(2,1)S(1)}, bf16[2,64,512]{2,1,0:T(8,128)(2,1)S(1)}, u32[]{:S(2)}, u32[]{:S(2)}) %collective-permute-start.7) | collective-permute-done | bytes 131104 | tf_op jit(solution)/shard_map/ppermute | solution.py:30
  27.7 0.0 collective-permute-done.6.p1.p5
  27.7 6.7 %attention_kernel.1 = (bf16[128,512]{1,0:T(8,128)(2,1)S(1)}, bf16[128,512]{1,0:T(8,128)(2,1)S(1)}, bf16[128,512]{1,0:T(8,128)(2,1)S(1)}, bf16[128,512]{1,0:T(8,1...) custom-call(s32[4]{0:T(128)S(1)} %pad_add_fusion.flags, ...), custom_call_target="tpu_custom_call" | custom-call | flops 1200000000 | bytes 6000000 | tf_op jit(solution)/shard_map/attention_kernel/pallas_call | solution.py:322
  34.4 2.5 %gradient_kernel.1 = (f32[16,72,128]{2,1,0:T(8,128)S(1)}, f32[16,72,128]{2,1,0:T(8,128)S(1)}) custom-call(s32[5]{0:T(128)S(1)} %stack.62.spot, bf16[2,64,512]{2,1,0:T(8,128)(2,1)S(1)} %bitcast.69, bf16[2,64,512]{2,1,0:T(8,128)(2,1)S(1)} %collective-permute-done.1.p1, bf16[2,64,512]{2,1,0:T(8,128)(2,1)S(1)} %collective-permute-done.2.p2, ...), custom_call_target="tpu_custom_call" | custom-call | flops 20000000000 | bytes 6000000 | tf_op jit(solution)/shard_map/gradient_kernel/pallas_call | solution.py:322
  36.9 0.0 copy-start.2
  36.9 3.9 %collective-permute-start.9 = (f32[16,72,128]{2,1,0:T(8,128)S(1)}, f32[16,72,128]{2,1,0:T(8,128)S(1)}, u32[]{:S(2)}, u32[]{:S(2)}) collective-permute-start(f32[16,72,128]{2,1,0:T(8,128)S(1)} %get-tuple-element.58), channel_id=1, source_target_pairs={{0,1},{1,0},{2,3},{3,2},{4,5},{5,4},{6,7},{7,6},{8,9},{9,8},{10,11... | collective-permute-start | bytes 1769480 | tf_op jit(solution)/shard_map/ppermute | solution.py:30
  40.8 0.4 collective-permute-start.13
  41.3 2.5 %collective-permute-start.14 = (bf16[128,512]{1,0:T(8,128)(2,1)S(1)}, bf16[128,512]{1,0:T(8,128)(2,1)S(1)}, u32[]{:S(2)}, u32[]{:S(2)}) collective-permute-start(bf16[128,512]{1,0:T(8,128)(2,1)S(1)} %get-tuple-element.52.r2), channel_id=1, source_target_pairs={{0,8},{1,9},{2,10},{3,11},{4,12},{5,13},{6,14},{7,15},{8,0},{9,1},... | collective-permute-start | bytes 393224 | tf_op jit(solution)/shard_map/ppermute | solution.py:30
  43.8 0.0 collective-permute-done.9
  43.8 0.1 fusion
  43.8 0.1 collective-permute-start.12
  43.9 0.1 collective-permute-start.11
  44.0 3.1 %collective-permute-start.10 = (bf16[4,72,128]{2,1,0:T(8,128)(2,1)S(1)}, bf16[4,72,128]{2,1,0:T(8,128)(2,1)S(1)}, u32[]{:S(2)}, u32[]{:S(2)}) collective-permute-start(bf16[4,72,128]{2,1,0:T(8,128)(2,1)S(1)} %get-tuple-element.91), channel_id=1, source_target_pairs={{0,16},{1,17},{2,18},{3,19},{4,20},{5,21},{6,22},{7,23},{8,24},{9,... | collective-permute-start | bytes 221192 | tf_op jit(solution)/shard_map/ppermute | solution.py:30
  47.2 0.0 collective-permute-done.13.r1
  47.2 1.0 %collective-permute-start.18 = (bf16[128,512]{1,0:T(8,128)(2,1)S(1)}, bf16[128,512]{1,0:T(8,128)(2,1)S(1)}, u32[]{:S(2)}, u32[]{:S(2)}) collective-permute-start(bf16[128,512]{1,0:T(8,128)(2,1)S(1)} %get-tuple-element.53.r3), channel_id=1, source_target_pairs={{0,12},{1,13},{2,14},{3,15},{4,8},{5,9},{6,10},{7,11},{8,4},{9,5},... | collective-permute-start | bytes 393224 | tf_op jit(solution)/shard_map/ppermute | solution.py:30
  48.1 2.0 %collective-permute-done.14.r2 = bf16[128,512]{1,0:T(8,128)(2,1)S(1)} collective-permute-done((bf16[128,512]{1,0:T(8,128)(2,1)S(1)}, bf16[128,512]{1,0:T(8,128)(2,1)S(1)}, u32[]{:S(2)}, u32[]{:S(2)}) %collective-permute-start.14) | collective-permute-done | bytes 131104 | tf_op jit(solution)/shard_map/ppermute | solution.py:30
  50.1 0.0 collective-permute-done.12
  50.1 0.0 collective-permute-done.11
  50.3 1.0 %collective-permute-start.17 = (f32[72,128]{1,0:T(8,128)S(1)}, f32[72,128]{1,0:T(8,128)S(1)}, u32[]{:S(2)}, u32[]{:S(2)}) collective-permute-start(f32[72,128]{1,0:T(8,128)S(1)} %get-tuple-element.93), channel_id=1, source_target_pairs={{0,12},{1,13},{2,14},{3,15},{4,8},{5,9},{6,10},{7,11},{8,4},{9,5},... | collective-permute-start | bytes 110600 | tf_op jit(solution)/shard_map/ppermute | solution.py:30
  51.3 0.8 collective-permute-start.16
  52.1 1.5 %collective-permute-start.15 = (f32[72,128]{1,0:T(8,128)S(1)}, f32[72,128]{1,0:T(8,128)S(1)}, u32[]{:S(2)}, u32[]{:S(2)}) collective-permute-start(f32[72,128]{1,0:T(8,128)S(1)} %get-tuple-element.95), channel_id=1, source_target_pairs={{0,4},{1,5},{2,6},{3,7},{4,0},{5,1},{6,2},{7,3},{8,12},{9,13},{10,... | collective-permute-start | bytes 110600 | tf_op jit(solution)/shard_map/ppermute | solution.py:30
  53.6 0.0 collective-permute-done.18.r3
  53.6 1.3 %token_kernel.1 = (bf16[2,128,512]{2,1,0:T(8,128)(2,1)S(1)}, f32[8,128]{1,0:T(8,128)S(1)}) custom-call(s32[5]{0:T(128)S(1)} %stack.62.spot, bf16[128,512]{1,0:T(8,128)(2,1)S(1)} %get-tuple-element.50.r0, bf16[128,512]{1,0:T(8,128)(2,1)S(1)} %collective-permute-done.13.r1, bf16[128,512]{1,0:T(8,128)(2,1)S(1)} %collective-permute-done.14.r2, ...), custom_call_target="tpu_custom_call" | custom-call | flops 500000000 | bytes 4000000 | tf_op jit(solution)/shard_map/token_kernel/pallas_call | solution.py:322
  55.0 0.0 copy-start.3
  55.0 0.0 copy-start.4
  55.0 4.1 %collective-permute-start.22 = (bf16[2,2,4,8,512]{4,3,2,0,1:T(8,128)(2,1)S(1)}, bf16[2,2,4,8,512]{4,3,2,0,1:T(8,128)(2,1)S(1)}, u32[]{:S(2)}, u32[]{:S(2)}) collective-permute-start(bf16[2,2,4,8,512]{4,3,2,0,1:T(8,128)(2,1)S(1)} %copy.24), channel_id=1, source_target_pairs={{0,240},{1,241},{2,242},{3,243},{4,244},{5,245},{6,246},{7,247},{8... | collective-permute-start | bytes 393224 | tf_op jit(solution)/shard_map/ppermute | solution.py:30
  59.2 0.7 z_parts_kernel.1
  59.9 0.1 collective-permute-start.19
  60.0 2.0 %collective-permute-start.20 = (f32[72,128]{1,0:T(8,128)S(1)}, f32[72,128]{1,0:T(8,128)S(1)}, u32[]{:S(2)}, u32[]{:S(2)}) collective-permute-start(f32[72,128]{1,0:T(8,128)S(1)} %get-tuple-element.72), channel_id=1, source_target_pairs={{0,128},{1,129},{2,130},{3,131},{4,132},{5,133},{6,134},{7,135},{8... | collective-permute-start | bytes 110600 | tf_op jit(solution)/shard_map/ppermute | solution.py:30
  61.9 3.7 %collective-permute-start.21 = (f32[72,128]{1,0:T(8,128)S(1)}, f32[72,128]{1,0:T(8,128)S(1)}, u32[]{:S(2)}, u32[]{:S(2)}) collective-permute-start(f32[72,128]{1,0:T(8,128)S(1)} %get-tuple-element.73), channel_id=1, source_target_pairs={{0,192},{1,193},{2,194},{3,195},{4,196},{5,197},{6,198},{7,199},{8... | collective-permute-start | bytes 110600 | tf_op jit(solution)/shard_map/ppermute | solution.py:30
  65.6 0.0 collective-permute-done.19
  65.6 1.8 %collective-permute-done.20 = f32[72,128]{1,0:T(8,128)S(1)} collective-permute-done((f32[72,128]{1,0:T(8,128)S(1)}, f32[72,128]{1,0:T(8,128)S(1)}, u32[]{:S(2)}, u32[]{:S(2)}) %collective-permute-start.20) | collective-permute-done | bytes 36896 | tf_op jit(solution)/shard_map/ppermute | solution.py:30
  67.4 0.6 collective-permute-done.21
  68.1 5.2 %collective-permute-start.26 = (bf16[2,2,4,8,512]{4,3,2,0,1:T(8,128)(2,1)S(1)}, bf16[2,2,4,8,512]{4,3,2,0,1:T(8,128)(2,1)S(1)}, u32[]{:S(2)}, u32[]{:S(2)}) collective-permute-start(bf16[2,2,4,8,512]{4,3,2,0,1:T(8,128)(2,1)S(1)} %pad_maximum_fusion.3), channel_id=1, source_target_pairs={{0,1},{1,2},{2,3},{3,0},{4,5},{5,6},{6,7},{7,4},{8,9},{9,10},{10,1... | collective-permute-start | bytes 393224 | tf_op jit(solution)/shard_map/ppermute | solution.py:30
  73.3 0.1 collective-permute-start.25
  73.4 0.1 collective-permute-start.24
  73.5 2.0 %collective-permute-start.23 = (f32[72,128]{1,0:T(8,128)S(1)}, f32[72,128]{1,0:T(8,128)S(1)}, u32[]{:S(2)}, u32[]{:S(2)}) collective-permute-start(f32[72,128]{1,0:T(8,128)S(1)} %add_add_fusion.near), channel_id=1, source_target_pairs={{0,1},{1,0},{2,3},{3,2},{4,5},{5,4},{6,7},{7,6},{8,9},{9,8},{10,11... | collective-permute-start | bytes 110600 | tf_op jit(solution)/shard_map/ppermute | solution.py:30
  75.5 0.1 collective-permute-done.26
  75.6 1.3 %merge_kernel.1 = (bf16[8,16,512]{2,1,0:T(8,128)(2,1)}, bf16[8,16,512]{2,1,0:T(8,128)(2,1)}) custom-call(s32[5]{0:T(128)S(1)} %stack.62.spot, bf16[8,16,512]{2,1,0:T(8,128)(2,1)S(1)} %bitcast.62, bf16[8,16,512]{2,1,0:T(8,128)(2,1)S(1)} %bitcast.64, bf16[2,4,8,512]{3,2,1,0:T(8,128)(2,1)S(1)} %get-tuple-element.100.mine_high, ...), custom_call_target="tpu_custom_call" | custom-call | tf_op jit(solution)/shard_map/merge_kernel/pallas_call | solution.py:322
  76.9 0.0 collective-permute-done.25.both_in
  76.9 0.0 collective-permute-done.24.z_in
  76.9 0.0 collective-permute-done.23.core_in
  76.9 1.2 %last_kernel.1 = (f32[24,512]{1,0:T(8,128)}, f32[8,512]{1,0:T(8,128)}, f32[2,8]{1,0:T(2,128)}) custom-call(s32[5]{0:T(128)S(1)} %stack.62.spot, f32[72,128]{1,0:T(8,128)S(1)} %add_add_fusion.near, f32[72,128]{1,0:T(8,128)S(1)} %collective-permute-done.23.core_in, f32[72,128]{1,0:T(8,128)S(1)} %collective-permute-done.24.z_in, ...), custom_call_target="tpu_custom_call" | custom-call | tf_op jit(solution)/shard_map/last_kernel/pallas_call | solution.py:322
  (30 shorter events, 0.2 us)
Async XLA Ops:
  0.6 22.4 %copy-start = (bf16[512,1536]{1,0:T(8,128)(2,1)S(1)}, bf16[512,1536]{1,0:T(8,128)(2,1)}, u32[]{:S(2)}) copy-start(bf16[512,1536]{1,0:T(8,128)(2,1)} %w_qkv.7) | copy-start | bytes 4718596
  0.6 22.4 %copy-start.5 = (f32[2,512]{1,0:T(2,128)S(1)}, f32[2,512]{1,0:T(2,128)}, u32[]{:S(2)}) copy-start(f32[2,512]{1,0:T(2,128)} %norm.5) | copy-start | bytes 12292
  1.9 10.6 %collective-permute-start = (bf16[2,4,8,512]{3,2,1,0:T(8,128)(2,1)S(1)}, bf16[2,4,8,512]{3,2,1,0:T(8,128)(2,1)S(1)}, u32[]{:S(2)}, u32[]{:S(2)}) collective-permute-start(bf16[2,4,8,512]{3,2,1,0:T(8,128)(2,1)S(1)} %get-tuple-element.108), channel_id=1, source_target_pairs={{0,3},{1,0},{2,1},{3,2},{4,7},{5,4},{6,5},{7,6},{8,11},{9,8},{10,9... | collective-permute-start | bytes 196616 | tf_op jit(solution)/shard_map/ppermute | solution.py:30
  5.3 10.8 %collective-permute-start.4 = (bf16[2,4,8,512]{3,2,1,0:T(8,128)(2,1)S(1)}, bf16[2,4,8,512]{3,2,1,0:T(8,128)(2,1)S(1)}, u32[]{:S(2)}, u32[]{:S(2)}) collective-permute-start(bf16[2,4,8,512]{3,2,1,0:T(8,128)(2,1)S(1)} %get-tuple-element.105), channel_id=1, source_target_pairs={{0,240},{1,241},{2,242},{3,243},{4,244},{5,245},{6,246},{7,247},{8... | collective-permute-start | bytes 196616 | tf_op jit(solution)/shard_map/ppermute | solution.py:30
  12.1 7.6 %collective-permute-start.5 = (bf16[2,4,8,512]{3,2,1,0:T(8,128)(2,1)S(1)}, bf16[2,4,8,512]{3,2,1,0:T(8,128)(2,1)S(1)}, u32[]{:S(2)}, u32[]{:S(2)}) collective-permute-start(bf16[2,4,8,512]{3,2,1,0:T(8,128)(2,1)S(1)} %get-tuple-element.106), channel_id=1, source_target_pairs={{0,243},{1,240},{2,241},{3,242},{4,247},{5,244},{6,245},{7,246},{8... | collective-permute-start | bytes 196616 | tf_op jit(solution)/shard_map/ppermute | solution.py:30
  12.6 10.2 %collective-permute-start.3 = (bf16[2,64,512]{2,1,0:T(8,128)(2,1)S(1)}, bf16[2,64,512]{2,1,0:T(8,128)(2,1)S(1)}, u32[]{:S(2)}, u32[]{:S(2)}) collective-permute-start(bf16[2,64,512]{2,1,0:T(8,128)(2,1)S(1)} %bitcast.65), channel_id=1, source_target_pairs={{0,12},{1,13},{2,14},{3,15},{4,8},{5,9},{6,10},{7,11},{8,4},{9,5},... | collective-permute-start | bytes 393224 | tf_op jit(solution)/shard_map/ppermute | solution.py:30
  15.1 7.9 %collective-permute-start.2 = (bf16[2,64,512]{2,1,0:T(8,128)(2,1)S(1)}, bf16[2,64,512]{2,1,0:T(8,128)(2,1)S(1)}, u32[]{:S(2)}, u32[]{:S(2)}) collective-permute-start(bf16[2,64,512]{2,1,0:T(8,128)(2,1)S(1)} %bitcast.66), channel_id=1, source_target_pairs={{0,8},{1,9},{2,10},{3,11},{4,12},{5,13},{6,14},{7,15},{8,0},{9,1},... | collective-permute-start | bytes 393224 | tf_op jit(solution)/shard_map/ppermute | solution.py:30
  15.7 7.4 %collective-permute-start.1 = (bf16[2,64,512]{2,1,0:T(8,128)(2,1)S(1)}, bf16[2,64,512]{2,1,0:T(8,128)(2,1)S(1)}, u32[]{:S(2)}, u32[]{:S(2)}) collective-permute-start(bf16[2,64,512]{2,1,0:T(8,128)(2,1)S(1)} %bitcast.67), channel_id=1, source_target_pairs={{0,4},{1,5},{2,6},{3,7},{4,0},{5,1},{6,2},{7,3},{8,12},{9,13},{10,... | collective-permute-start | bytes 393224 | tf_op jit(solution)/shard_map/ppermute | solution.py:30
  19.7 5.9 %collective-permute-start.8 = (bf16[2,64,512]{2,1,0:T(8,128)(2,1)S(1)}, bf16[2,64,512]{2,1,0:T(8,128)(2,1)S(1)}, u32[]{:S(2)}, u32[]{:S(2)}) collective-permute-start(bf16[2,64,512]{2,1,0:T(8,128)(2,1)S(1)} %bitcast.71), channel_id=1, source_target_pairs={{0,12},{1,13},{2,14},{3,15},{4,8},{5,9},{6,10},{7,11},{8,4},{9,5},... | collective-permute-start | bytes 393224 | tf_op jit(solution)/shard_map/ppermute | solution.py:30
  22.3 5.4 %collective-permute-start.7 = (bf16[2,64,512]{2,1,0:T(8,128)(2,1)S(1)}, bf16[2,64,512]{2,1,0:T(8,128)(2,1)S(1)}, u32[]{:S(2)}, u32[]{:S(2)}) collective-permute-start(bf16[2,64,512]{2,1,0:T(8,128)(2,1)S(1)} %bitcast.72), channel_id=1, source_target_pairs={{0,8},{1,9},{2,10},{3,11},{4,12},{5,13},{6,14},{7,15},{8,0},{9,1},... | collective-permute-start | bytes 393224 | tf_op jit(solution)/shard_map/ppermute | solution.py:30
  22.8 4.9 %collective-permute-start.6 = (bf16[2,64,512]{2,1,0:T(8,128)(2,1)S(1)}, bf16[2,64,512]{2,1,0:T(8,128)(2,1)S(1)}, u32[]{:S(2)}, u32[]{:S(2)}) collective-permute-start(bf16[2,64,512]{2,1,0:T(8,128)(2,1)S(1)} %bitcast.73), channel_id=1, source_target_pairs={{0,4},{1,5},{2,6},{3,7},{4,0},{5,1},{6,2},{7,3},{8,12},{9,13},{10,... | collective-permute-start | bytes 393224 | tf_op jit(solution)/shard_map/ppermute | solution.py:30
  23.1 1.0 %copy-start.1 = (bf16[512,512]{1,0:T(8,128)(2,1)S(1)}, bf16[512,512]{1,0:T(8,128)(2,1)}, u32[]{:S(2)}) copy-start(bf16[512,512]{1,0:T(8,128)(2,1)} %w_proj.5) | copy-start | bytes 1572868
  36.9 16.7 %copy-start.2 = (bf16[512,512]{1,0:T(8,128)(2,1)S(1)}, bf16[512,512]{1,0:T(8,128)(2,1)}, u32[]{:S(2)}) copy-start(bf16[512,512]{1,0:T(8,128)(2,1)} %w_proj.5) | copy-start | bytes 1572868
  36.9 6.8 %collective-permute-start.9 = (f32[16,72,128]{2,1,0:T(8,128)S(1)}, f32[16,72,128]{2,1,0:T(8,128)S(1)}, u32[]{:S(2)}, u32[]{:S(2)}) collective-permute-start(f32[16,72,128]{2,1,0:T(8,128)S(1)} %get-tuple-element.58), channel_id=1, source_target_pairs={{0,1},{1,0},{2,3},{3,2},{4,5},{5,4},{6,7},{7,6},{8,9},{9,8},{10,11... | collective-permute-start | bytes 1769480 | tf_op jit(solution)/shard_map/ppermute | solution.py:30
  40.8 6.3 %collective-permute-start.13 = (bf16[128,512]{1,0:T(8,128)(2,1)S(1)}, bf16[128,512]{1,0:T(8,128)(2,1)S(1)}, u32[]{:S(2)}, u32[]{:S(2)}) collective-permute-start(bf16[128,512]{1,0:T(8,128)(2,1)S(1)} %get-tuple-element.51.r1), channel_id=1, source_target_pairs={{0,4},{1,5},{2,6},{3,7},{4,0},{5,1},{6,2},{7,3},{8,12},{9,13},{10,... | collective-permute-start | bytes 393224 | tf_op jit(solution)/shard_map/ppermute | solution.py:30
  41.3 8.9 %collective-permute-start.14 = (bf16[128,512]{1,0:T(8,128)(2,1)S(1)}, bf16[128,512]{1,0:T(8,128)(2,1)S(1)}, u32[]{:S(2)}, u32[]{:S(2)}) collective-permute-start(bf16[128,512]{1,0:T(8,128)(2,1)S(1)} %get-tuple-element.52.r2), channel_id=1, source_target_pairs={{0,8},{1,9},{2,10},{3,11},{4,12},{5,13},{6,14},{7,15},{8,0},{9,1},... | collective-permute-start | bytes 393224 | tf_op jit(solution)/shard_map/ppermute | solution.py:30
  43.8 6.3 %collective-permute-start.12 = (bf16[4,72,128]{2,1,0:T(8,128)(2,1)S(1)}, bf16[4,72,128]{2,1,0:T(8,128)(2,1)S(1)}, u32[]{:S(2)}, u32[]{:S(2)}) collective-permute-start(bf16[4,72,128]{2,1,0:T(8,128)(2,1)S(1)} %get-tuple-element.89), channel_id=1, source_target_pairs={{0,48},{1,49},{2,50},{3,51},{4,52},{5,53},{6,54},{7,55},{8,56},{9,... | collective-permute-start | bytes 221192 | tf_op jit(solution)/shard_map/ppermute | solution.py:30
  43.9 6.2 %collective-permute-start.11 = (bf16[4,72,128]{2,1,0:T(8,128)(2,1)S(1)}, bf16[4,72,128]{2,1,0:T(8,128)(2,1)S(1)}, u32[]{:S(2)}, u32[]{:S(2)}) collective-permute-start(bf16[4,72,128]{2,1,0:T(8,128)(2,1)S(1)} %get-tuple-element.90), channel_id=1, source_target_pairs={{0,32},{1,33},{2,34},{3,35},{4,36},{5,37},{6,38},{7,39},{8,40},{9,... | collective-permute-start | bytes 221192 | tf_op jit(solution)/shard_map/ppermute | solution.py:30
  44.0 6.1 %collective-permute-start.10 = (bf16[4,72,128]{2,1,0:T(8,128)(2,1)S(1)}, bf16[4,72,128]{2,1,0:T(8,128)(2,1)S(1)}, u32[]{:S(2)}, u32[]{:S(2)}) collective-permute-start(bf16[4,72,128]{2,1,0:T(8,128)(2,1)S(1)} %get-tuple-element.91), channel_id=1, source_target_pairs={{0,16},{1,17},{2,18},{3,19},{4,20},{5,21},{6,22},{7,23},{8,24},{9,... | collective-permute-start | bytes 221192 | tf_op jit(solution)/shard_map/ppermute | solution.py:30
  47.2 6.4 %collective-permute-start.18 = (bf16[128,512]{1,0:T(8,128)(2,1)S(1)}, bf16[128,512]{1,0:T(8,128)(2,1)S(1)}, u32[]{:S(2)}, u32[]{:S(2)}) collective-permute-start(bf16[128,512]{1,0:T(8,128)(2,1)S(1)} %get-tuple-element.53.r3), channel_id=1, source_target_pairs={{0,12},{1,13},{2,14},{3,15},{4,8},{5,9},{6,10},{7,11},{8,4},{9,5},... | collective-permute-start | bytes 393224 | tf_op jit(solution)/shard_map/ppermute | solution.py:30
  50.3 8.9 %collective-permute-start.17 = (f32[72,128]{1,0:T(8,128)S(1)}, f32[72,128]{1,0:T(8,128)S(1)}, u32[]{:S(2)}, u32[]{:S(2)}) collective-permute-start(f32[72,128]{1,0:T(8,128)S(1)} %get-tuple-element.93), channel_id=1, source_target_pairs={{0,12},{1,13},{2,14},{3,15},{4,8},{5,9},{6,10},{7,11},{8,4},{9,5},... | collective-permute-start | bytes 110600 | tf_op jit(solution)/shard_map/ppermute | solution.py:30
  51.3 7.9 %collective-permute-start.16 = (f32[72,128]{1,0:T(8,128)S(1)}, f32[72,128]{1,0:T(8,128)S(1)}, u32[]{:S(2)}, u32[]{:S(2)}) collective-permute-start(f32[72,128]{1,0:T(8,128)S(1)} %get-tuple-element.94), channel_id=1, source_target_pairs={{0,8},{1,9},{2,10},{3,11},{4,12},{5,13},{6,14},{7,15},{8,0},{9,1},... | collective-permute-start | bytes 110600 | tf_op jit(solution)/shard_map/ppermute | solution.py:30
  52.1 7.1 %collective-permute-start.15 = (f32[72,128]{1,0:T(8,128)S(1)}, f32[72,128]{1,0:T(8,128)S(1)}, u32[]{:S(2)}, u32[]{:S(2)}) collective-permute-start(f32[72,128]{1,0:T(8,128)S(1)} %get-tuple-element.95), channel_id=1, source_target_pairs={{0,4},{1,5},{2,6},{3,7},{4,0},{5,1},{6,2},{7,3},{8,12},{9,13},{10,... | collective-permute-start | bytes 110600 | tf_op jit(solution)/shard_map/ppermute | solution.py:30
  55.0 20.6 %copy-start.3 = (bf16[1,1,8,16,512]{4,3,2,1,0:T(8,128)(2,1)S(1)}, bf16[1,1,8,16,512]{4,3,2,1,0:T(8,128)(2,1)}, u32[]{:S(2)}) copy-start(bf16[1,1,8,16,512]{4,3,2,1,0:T(8,128)(2,1)} %param.5) | copy-start | bytes 393220
  55.0 20.6 %copy-start.4 = (bf16[1,1,8,16,512]{4,3,2,1,0:T(8,128)(2,1)S(1)}, bf16[1,1,8,16,512]{4,3,2,1,0:T(8,128)(2,1)}, u32[]{:S(2)}) copy-start(bf16[1,1,8,16,512]{4,3,2,1,0:T(8,128)(2,1)} %param.9) | copy-start | bytes 393220
  55.0 13.0 %collective-permute-start.22 = (bf16[2,2,4,8,512]{4,3,2,0,1:T(8,128)(2,1)S(1)}, bf16[2,2,4,8,512]{4,3,2,0,1:T(8,128)(2,1)S(1)}, u32[]{:S(2)}, u32[]{:S(2)}) collective-permute-start(bf16[2,2,4,8,512]{4,3,2,0,1:T(8,128)(2,1)S(1)} %copy.24), channel_id=1, source_target_pairs={{0,240},{1,241},{2,242},{3,243},{4,244},{5,245},{6,246},{7,247},{8... | collective-permute-start | bytes 393224 | tf_op jit(solution)/shard_map/ppermute | solution.py:30
  59.9 5.8 %collective-permute-start.19 = (f32[72,128]{1,0:T(8,128)S(1)}, f32[72,128]{1,0:T(8,128)S(1)}, u32[]{:S(2)}, u32[]{:S(2)}) collective-permute-start(f32[72,128]{1,0:T(8,128)S(1)} %get-tuple-element.71), channel_id=1, source_target_pairs={{0,64},{1,65},{2,66},{3,67},{4,68},{5,69},{6,70},{7,71},{8,72},{9,... | collective-permute-start | bytes 110600 | tf_op jit(solution)/shard_map/ppermute | solution.py:30
  60.0 7.4 %collective-permute-start.20 = (f32[72,128]{1,0:T(8,128)S(1)}, f32[72,128]{1,0:T(8,128)S(1)}, u32[]{:S(2)}, u32[]{:S(2)}) collective-permute-start(f32[72,128]{1,0:T(8,128)S(1)} %get-tuple-element.72), channel_id=1, source_target_pairs={{0,128},{1,129},{2,130},{3,131},{4,132},{5,133},{6,134},{7,135},{8... | collective-permute-start | bytes 110600 | tf_op jit(solution)/shard_map/ppermute | solution.py:30
  61.9 6.1 %collective-permute-start.21 = (f32[72,128]{1,0:T(8,128)S(1)}, f32[72,128]{1,0:T(8,128)S(1)}, u32[]{:S(2)}, u32[]{:S(2)}) collective-permute-start(f32[72,128]{1,0:T(8,128)S(1)} %get-tuple-element.73), channel_id=1, source_target_pairs={{0,192},{1,193},{2,194},{3,195},{4,196},{5,197},{6,198},{7,199},{8... | collective-permute-start | bytes 110600 | tf_op jit(solution)/shard_map/ppermute | solution.py:30
  68.1 7.5 %collective-permute-start.26 = (bf16[2,2,4,8,512]{4,3,2,0,1:T(8,128)(2,1)S(1)}, bf16[2,2,4,8,512]{4,3,2,0,1:T(8,128)(2,1)S(1)}, u32[]{:S(2)}, u32[]{:S(2)}) collective-permute-start(bf16[2,2,4,8,512]{4,3,2,0,1:T(8,128)(2,1)S(1)} %pad_maximum_fusion.3), channel_id=1, source_target_pairs={{0,1},{1,2},{2,3},{3,0},{4,5},{5,6},{6,7},{7,4},{8,9},{9,10},{10,1... | collective-permute-start | bytes 393224 | tf_op jit(solution)/shard_map/ppermute | solution.py:30
  73.3 3.6 %collective-permute-start.25 = (f32[72,128]{1,0:T(8,128)S(1)}, f32[72,128]{1,0:T(8,128)S(1)}, u32[]{:S(2)}, u32[]{:S(2)}) collective-permute-start(f32[72,128]{1,0:T(8,128)S(1)} %add_add_fusion.near), channel_id=1, source_target_pairs={{0,3},{1,2},{2,1},{3,0},{4,7},{5,6},{6,5},{7,4},{8,11},{9,10},{10,... | collective-permute-start | bytes 110600 | tf_op jit(solution)/shard_map/ppermute | solution.py:30
  73.4 3.5 %collective-permute-start.24 = (f32[72,128]{1,0:T(8,128)S(1)}, f32[72,128]{1,0:T(8,128)S(1)}, u32[]{:S(2)}, u32[]{:S(2)}) collective-permute-start(f32[72,128]{1,0:T(8,128)S(1)} %add_add_fusion.near), channel_id=1, source_target_pairs={{0,2},{1,3},{2,0},{3,1},{4,6},{5,7},{6,4},{7,5},{8,10},{9,11},{10,... | collective-permute-start | bytes 110600 | tf_op jit(solution)/shard_map/ppermute | solution.py:30
  73.5 3.4 %collective-permute-start.23 = (f32[72,128]{1,0:T(8,128)S(1)}, f32[72,128]{1,0:T(8,128)S(1)}, u32[]{:S(2)}, u32[]{:S(2)}) collective-permute-start(f32[72,128]{1,0:T(8,128)S(1)} %add_add_fusion.near), channel_id=1, source_target_pairs={{0,1},{1,0},{2,3},{3,2},{4,5},{5,4},{6,7},{7,6},{8,9},{9,8},{10,11... | collective-permute-start | bytes 110600 | tf_op jit(solution)/shard_map/ppermute | solution.py:30

commit v10 on v9

--- a/solution.py
+++ b/solution.py
@@ -124,13 +124,13 @@
     d_value = jnp.zeros((TOKENS, OWN), F32)
     for block in range(TOKENS // BLOCK):
         span = slice(block * BLOCK, (block + 1) * BLOCK)
-        allowed = key_label == query_label[:, span]
+        barred = jnp.where(key_label == query_label[:, span], 0.0, -1e30)
         for head in range(RING):
             chosen = head_of_lane == head
             rows = slice(head * HEAD_DIM, (head + 1) * HEAD_DIM)
             key_head = jnp.where(chosen, keys, jnp.zeros_like(keys))
             value_head = jnp.where(chosen, values, jnp.zeros_like(values))
-            scores = jnp.where(allowed, dot(key_head, queries_t[:, span]), -1e30)
+            scores = dot(key_head, queries_t[:, span]) + barred
             highest = jnp.max(scores, 0, keepdims=True)
             d_probs = dot(value_head, cotangent_t[:, span])
             weights = []
@@ -256,9 +256,9 @@
             outs[across][...] = jnp.where(ahead, block, outs[across][...]) if to_z else block
 
 
-def last_kernel(spot, near, core_in, z_in, both_in, g_out, p_out, n_out):
-    mine = near[...] + z_in[...]
-    theirs = core_in[...] + both_in[...]
+def last_kernel(spot, near, core_in, g_out, p_out, n_out):
+    mine = near[...]
+    theirs = core_in[...]
     swap = spot[2] == 1
     shares = (jnp.where(swap, theirs, mine), jnp.where(swap, mine, theirs))
     for core in range(2):
@@ -420,7 +420,7 @@
         (line[1], line[2], line[3], crossed)
     )
     line = (line[0] + line[1]) + (line[2] + line[3])
-    last = [line] + [move(line, over_narrow(mask)) for mask in (1, 2, 3)]
+    across = move(line, over_narrow(2))
     lower = move(jnp.stack([back[:, 1], crossed[:, 1]], 1), lambda p, n: (p, n + 1))
     output, grad_inputs = call(
         merge_kernel,
@@ -428,11 +428,13 @@
         (own_inputs, own_upstream, back[:, 0], lower[:, 0], crossed[:, 0], lower[:, 1]),
         [((8, 16, C), BF16)] * 2,
     )
-    last[1], last[2], last[3], output, grad_inputs = lax.optimization_barrier(
-        (last[1], last[2], last[3], output, grad_inputs)
-    )
+    across, output, grad_inputs = lax.optimization_barrier((across, output, grad_inputs))
+    line = line + across
     grad_qkv, grad_proj, grad_norm = call(
-        last_kernel, spot, last, [((24, C), F32), ((8, C), F32), ((2, 8), F32)]
+        last_kernel,
+        spot,
+        (line, move(line, over_narrow(1))),
+        [((24, C), F32), ((8, C), F32), ((2, 8), F32)],
     )
     return (
         output[None, None], grad_inputs[None, None], grad_qkv.T, grad_proj.T, grad_norm

time: 78.3 us -> 80.4 us (1.027)
  waiting for transfers between devices: 10.6 us -> 13.6 us
  starting transfers between devices: 49 us -> 48.1 us
    ppermute x27 -> x26, waiting for transfers between devices: 10.6 us -> 13.6 us  [move(): return lax.ppermute(value, ('wide', 'narrow'), pairs)]
    ppermute x27 -> x26, starting transfers between devices: 49 us -> 48.1 us  [move(): return lax.ppermute(value, ('wide', 'narrow'), pairs)]
  transfers between devices with their start and end apart: 27 -> 26, of which waited for: 7 -> 8; matrix products, arithmetic and copies ran while one was open for 1% -> 0% of each run, Pallas kernels for 6% -> 6%
where the time goes in v10:
time: 80.4 us; the launch traced here: 80.2 us
  starting transfers between devices  48.1 us (60%)
  Pallas kernels  14.9 us (19%)
  waiting for transfers between devices  13.6 us (17%)
  other arithmetic  1.48 us (2%)
  local copies, waits for them, and re-layouts  1.23 us (2%)
  between operations  0.97 us (1%)
    ppermute x26, starting transfers between devices, move(): return lax.ppermute(value, ('wide', 'narrow'), pairs)  48.1 us
    pallas_call x7, Pallas kernels, call(): pl.pallas_call(kernel, out_shape=[jax.ShapeDtypeStruct(shape, dtype) for...  14.9 us
    ppermute x26, waiting for transfers between devices, move(): return lax.ppermute(value, ('wide', 'narrow'), pairs)  13.6 us
  transfers between devices with their start and end apart: 26, of which 8 were waited for; matrix products, arithmetic and copies ran while one was open for 0% of the time, Pallas kernels for 6%

profile of v10, /device:TPU:1, one launch (start us, length us, event | category | flops | bytes accessed | tf_op | source)
XLA Modules:
  0.0 80.2 jit_solution(17390190997798903452)
XLA Ops:
  0.7 1.2 %broadcast_select_fusion = (bf16[2,8,8,512]{3,2,1,0:T(8,128)(2,1)S(1)}, bf16[2,8,8,512]{3,2,1,0:T(8,128)(2,1)S(1)}) fusion(pred[8]{0:T(512)(128)(4,1)S(1)} %compare_compare_fusion, bf16[1,8,2,8,512]{4,3,2,1,0:T(8,128)(2,1)} %bitcast.63, bf16[1,8,2,8,512]{4,3,2,1,0:T(8,128)(2,1)} %bitcast.61), kind=kLoop, calls=%fused_computation.16 | loop fusion | flops 327680 | bytes 524296 | tf_op jit(solution)/shard_map/jit(_where)/select_n | solution.py:348
  1.9 3.3 %collective-permute-start = (bf16[2,4,8,512]{3,2,1,0:T(8,128)(2,1)S(1)}, bf16[2,4,8,512]{3,2,1,0:T(8,128)(2,1)S(1)}, u32[]{:S(2)}, u32[]{:S(2)}) collective-permute-start(bf16[2,4,8,512]{3,2,1,0:T(8,128)(2,1)S(1)} %get-tuple-element.104), channel_id=1, source_target_pairs={{0,3},{1,0},{2,1},{3,2},{4,7},{5,4},{6,5},{7,6},{8,11},{9,8},{10,9... | collective-permute-start | bytes 196616 | tf_op jit(solution)/shard_map/ppermute | solution.py:30
  5.3 6.8 %collective-permute-start.4 = (bf16[2,4,8,512]{3,2,1,0:T(8,128)(2,1)S(1)}, bf16[2,4,8,512]{3,2,1,0:T(8,128)(2,1)S(1)}, u32[]{:S(2)}, u32[]{:S(2)}) collective-permute-start(bf16[2,4,8,512]{3,2,1,0:T(8,128)(2,1)S(1)} %get-tuple-element.101), channel_id=1, source_target_pairs={{0,240},{1,241},{2,242},{3,243},{4,244},{5,245},{6,246},{7,247},{8... | collective-permute-start | bytes 196616 | tf_op jit(solution)/shard_map/ppermute | solution.py:30
  12.1 0.4 collective-permute-start.5
  12.5 0.0 collective-permute-done
  12.6 2.6 %collective-permute-start.3 = (bf16[2,64,512]{2,1,0:T(8,128)(2,1)S(1)}, bf16[2,64,512]{2,1,0:T(8,128)(2,1)S(1)}, u32[]{:S(2)}, u32[]{:S(2)}) collective-permute-start(bf16[2,64,512]{2,1,0:T(8,128)(2,1)S(1)} %bitcast.65), channel_id=1, source_target_pairs={{0,12},{1,13},{2,14},{3,15},{4,8},{5,9},{6,10},{7,11},{8,4},{9,5},... | collective-permute-start | bytes 393224 | tf_op jit(solution)/shard_map/ppermute | solution.py:30
  15.1 0.5 collective-permute-start.2
  15.7 0.3 collective-permute-start.1
  15.9 0.1 pad_add_fusion.flags
  16.0 0.1 stack.62.spot
  16.1 0.0 collective-permute-done.4
  16.1 3.6 %collective-permute-done.5 = bf16[2,4,8,512]{3,2,1,0:T(8,128)(2,1)S(1)} collective-permute-done((bf16[2,4,8,512]{3,2,1,0:T(8,128)(2,1)S(1)}, bf16[2,4,8,512]{3,2,1,0:T(8,128)(2,1)S(1)}, u32[]{:S(2)}, u32[]{:S(2)}) %collective-permute-start.5) | collective-permute-done | bytes 65568 | tf_op jit(solution)/shard_map/ppermute | solution.py:30
  19.7 2.6 %collective-permute-start.8 = (bf16[2,64,512]{2,1,0:T(8,128)(2,1)S(1)}, bf16[2,64,512]{2,1,0:T(8,128)(2,1)S(1)}, u32[]{:S(2)}, u32[]{:S(2)}) collective-permute-start(bf16[2,64,512]{2,1,0:T(8,128)(2,1)S(1)} %bitcast.71), channel_id=1, source_target_pairs={{0,12},{1,13},{2,14},{3,15},{4,8},{5,9},{6,10},{7,11},{8,4},{9,5},... | collective-permute-start | bytes 393224 | tf_op jit(solution)/shard_map/ppermute | solution.py:30
  22.3 0.5 collective-permute-start.7
  22.8 0.0 collective-permute-done.3.p3
  22.8 0.3 collective-permute-start.6
  23.1 0.0 collective-permute-done.2.p2
  23.1 0.0 collective-permute-done.1.p1
  23.1 0.0 copy-start.1
  23.1 1.0 %copy-done.1 = bf16[512,512]{1,0:T(8,128)(2,1)S(1)} copy-done((bf16[512,512]{1,0:T(8,128)(2,1)S(1)}, bf16[512,512]{1,0:T(8,128)(2,1)}, u32[]{:S(2)}) %copy-start.1) | copy-done | bytes 524312
  24.1 1.1 %first_kernel.1 = (bf16[256,512]{1,0:T(8,128)(2,1)S(1)}, bf16[256,384]{1,0:T(8,128)(2,1)S(1)}, bf16[256,128]{1,0:T(8,128)(2,1)S(1)}) custom-call(s32[4]{0:T(128)S(1)} %pad_add_fusion.flags, bf16[2,64,512]{2,1,0:T(8,128)(2,1)S(1)} %bitcast.68, bf16[2,64,512]{2,1,0:T(8,128)(2,1)S(1)} %collective-permute-done.1.p1, ...), custom_call_target="tpu_custom_call" | custom-call | flops 10000000000 | bytes 3000000 | tf_op jit(solution)/shard_map/first_kernel/pallas_call | solution.py:322
  25.2 0.4 collective-permute-done.8.p3.p7
  25.6 2.1 %collective-permute-done.7.p2.p6 = bf16[2,64,512]{2,1,0:T(8,128)(2,1)S(1)} collective-permute-done((bf16[2,64,512]{2,1,0:T(8,128)(2,1)S(1)}, bf16[2,64,512]{2,1,0:T(8,128)(2,1)S(1)}, u32[]{:S(2)}, u32[]{:S(2)}) %collective-permute-start.7) | collective-permute-done | bytes 131104 | tf_op jit(solution)/shard_map/ppermute | solution.py:30
  27.7 0.0 collective-permute-done.6.p1.p5
  27.7 6.7 %attention_kernel.1 = (bf16[128,512]{1,0:T(8,128)(2,1)S(1)}, bf16[128,512]{1,0:T(8,128)(2,1)S(1)}, bf16[128,512]{1,0:T(8,128)(2,1)S(1)}, bf16[128,512]{1,0:T(8,1...) custom-call(s32[4]{0:T(128)S(1)} %pad_add_fusion.flags, ...), custom_call_target="tpu_custom_call" | custom-call | flops 1200000000 | bytes 6000000 | tf_op jit(solution)/shard_map/attention_kernel/pallas_call | solution.py:322
  34.4 2.5 %gradient_kernel.1 = (f32[16,72,128]{2,1,0:T(8,128)S(1)}, f32[16,72,128]{2,1,0:T(8,128)S(1)}) custom-call(s32[5]{0:T(128)S(1)} %stack.62.spot, bf16[2,64,512]{2,1,0:T(8,128)(2,1)S(1)} %bitcast.69, bf16[2,64,512]{2,1,0:T(8,128)(2,1)S(1)} %collective-permute-done.1.p1, bf16[2,64,512]{2,1,0:T(8,128)(2,1)S(1)} %collective-permute-done.2.p2, ...), custom_call_target="tpu_custom_call" | custom-call | flops 20000000000 | bytes 6000000 | tf_op jit(solution)/shard_map/gradient_kernel/pallas_call | solution.py:322
  37.0 0.0 copy-start.2
  37.0 3.9 %collective-permute-start.9 = (f32[16,72,128]{2,1,0:T(8,128)S(1)}, f32[16,72,128]{2,1,0:T(8,128)S(1)}, u32[]{:S(2)}, u32[]{:S(2)}) collective-permute-start(f32[16,72,128]{2,1,0:T(8,128)S(1)} %get-tuple-element.56), channel_id=1, source_target_pairs={{0,1},{1,0},{2,3},{3,2},{4,5},{5,4},{6,7},{7,6},{8,9},{9,8},{10,11... | collective-permute-start | bytes 1769480 | tf_op jit(solution)/shard_map/ppermute | solution.py:30
  40.8 0.4 collective-permute-start.13
  41.3 2.5 %collective-permute-start.14 = (bf16[128,512]{1,0:T(8,128)(2,1)S(1)}, bf16[128,512]{1,0:T(8,128)(2,1)S(1)}, u32[]{:S(2)}, u32[]{:S(2)}) collective-permute-start(bf16[128,512]{1,0:T(8,128)(2,1)S(1)} %get-tuple-element.50.r2), channel_id=1, source_target_pairs={{0,8},{1,9},{2,10},{3,11},{4,12},{5,13},{6,14},{7,15},{8,0},{9,1},... | collective-permute-start | bytes 393224 | tf_op jit(solution)/shard_map/ppermute | solution.py:30
  43.8 0.1 fusion
  43.8 0.1 collective-permute-start.12
  43.9 0.1 collective-permute-start.11
  44.0 3.1 %collective-permute-start.10 = (bf16[4,72,128]{2,1,0:T(8,128)(2,1)S(1)}, bf16[4,72,128]{2,1,0:T(8,128)(2,1)S(1)}, u32[]{:S(2)}, u32[]{:S(2)}) collective-permute-start(bf16[4,72,128]{2,1,0:T(8,128)(2,1)S(1)} %get-tuple-element.87), channel_id=1, source_target_pairs={{0,16},{1,17},{2,18},{3,19},{4,20},{5,21},{6,22},{7,23},{8,24},{9,... | collective-permute-start | bytes 221192 | tf_op jit(solution)/shard_map/ppermute | solution.py:30
  47.2 1.0 %collective-permute-start.18 = (bf16[128,512]{1,0:T(8,128)(2,1)S(1)}, bf16[128,512]{1,0:T(8,128)(2,1)S(1)}, u32[]{:S(2)}, u32[]{:S(2)}) collective-permute-start(bf16[128,512]{1,0:T(8,128)(2,1)S(1)} %get-tuple-element.51.r3), channel_id=1, source_target_pairs={{0,12},{1,13},{2,14},{3,15},{4,8},{5,9},{6,10},{7,11},{8,4},{9,5},... | collective-permute-start | bytes 393224 | tf_op jit(solution)/shard_map/ppermute | solution.py:30
  48.1 2.0 %collective-permute-done.14.r2 = bf16[128,512]{1,0:T(8,128)(2,1)S(1)} collective-permute-done((bf16[128,512]{1,0:T(8,128)(2,1)S(1)}, bf16[128,512]{1,0:T(8,128)(2,1)S(1)}, u32[]{:S(2)}, u32[]{:S(2)}) %collective-permute-start.14) | collective-permute-done | bytes 131104 | tf_op jit(solution)/shard_map/ppermute | solution.py:30
  50.2 0.0 collective-permute-done.12
  50.2 0.0 collective-permute-done.11
  50.2 0.0 collective-permute-done.10
  50.3 1.0 %collective-permute-start.17 = (f32[72,128]{1,0:T(8,128)S(1)}, f32[72,128]{1,0:T(8,128)S(1)}, u32[]{:S(2)}, u32[]{:S(2)}) collective-permute-start(f32[72,128]{1,0:T(8,128)S(1)} %get-tuple-element.89), channel_id=1, source_target_pairs={{0,12},{1,13},{2,14},{3,15},{4,8},{5,9},{6,10},{7,11},{8,4},{9,5},... | collective-permute-start | bytes 110600 | tf_op jit(solution)/shard_map/ppermute | solution.py:30
  51.3 0.8 collective-permute-start.16
  52.1 1.5 %collective-permute-start.15 = (f32[72,128]{1,0:T(8,128)S(1)}, f32[72,128]{1,0:T(8,128)S(1)}, u32[]{:S(2)}, u32[]{:S(2)}) collective-permute-start(f32[72,128]{1,0:T(8,128)S(1)} %get-tuple-element.91), channel_id=1, source_target_pairs={{0,4},{1,5},{2,6},{3,7},{4,0},{5,1},{6,2},{7,3},{8,12},{9,13},{10,... | collective-permute-start | bytes 110600 | tf_op jit(solution)/shard_map/ppermute | solution.py:30
  53.6 1.3 %token_kernel.1 = (bf16[2,128,512]{2,1,0:T(8,128)(2,1)S(1)}, f32[8,128]{1,0:T(8,128)S(1)}) custom-call(s32[5]{0:T(128)S(1)} %stack.62.spot, bf16[128,512]{1,0:T(8,128)(2,1)S(1)} %get-tuple-element.48.r0, bf16[128,512]{1,0:T(8,128)(2,1)S(1)} %collective-permute-done.13.r1, bf16[128,512]{1,0:T(8,128)(2,1)S(1)} %collective-permute-done.14.r2, ...), custom_call_target="tpu_custom_call" | custom-call | flops 500000000 | bytes 4000000 | tf_op jit(solution)/shard_map/token_kernel/pallas_call | solution.py:322
  55.0 0.0 copy-start.3
  55.0 0.0 copy-start.4
  55.0 4.1 %collective-permute-start.22 = (bf16[2,2,4,8,512]{4,3,2,0,1:T(8,128)(2,1)S(1)}, bf16[2,2,4,8,512]{4,3,2,0,1:T(8,128)(2,1)S(1)}, u32[]{:S(2)}, u32[]{:S(2)}) collective-permute-start(bf16[2,2,4,8,512]{4,3,2,0,1:T(8,128)(2,1)S(1)} %copy.24), channel_id=1, source_target_pairs={{0,240},{1,241},{2,242},{3,243},{4,244},{5,245},{6,246},{7,247},{8... | collective-permute-start | bytes 393224 | tf_op jit(solution)/shard_map/ppermute | solution.py:30
  59.2 0.0 collective-permute-done.17.m3
  59.2 0.0 collective-permute-done.16.m2
  59.2 0.0 collective-permute-done.15.m1
  59.2 0.7 z_parts_kernel.1
  59.9 0.1 collective-permute-start.19
  60.0 2.0 %collective-permute-start.20 = (f32[72,128]{1,0:T(8,128)S(1)}, f32[72,128]{1,0:T(8,128)S(1)}, u32[]{:S(2)}, u32[]{:S(2)}) collective-permute-start(f32[72,128]{1,0:T(8,128)S(1)} %get-tuple-element.70), channel_id=1, source_target_pairs={{0,128},{1,129},{2,130},{3,131},{4,132},{5,133},{6,134},{7,135},{8... | collective-permute-start | bytes 110600 | tf_op jit(solution)/shard_map/ppermute | solution.py:30
  62.0 3.7 %collective-permute-start.21 = (f32[72,128]{1,0:T(8,128)S(1)}, f32[72,128]{1,0:T(8,128)S(1)}, u32[]{:S(2)}, u32[]{:S(2)}) collective-permute-start(f32[72,128]{1,0:T(8,128)S(1)} %get-tuple-element.71), channel_id=1, source_target_pairs={{0,192},{1,193},{2,194},{3,195},{4,196},{5,197},{6,198},{7,199},{8... | collective-permute-start | bytes 110600 | tf_op jit(solution)/shard_map/ppermute | solution.py:30
  65.7 1.8 %collective-permute-done.20 = f32[72,128]{1,0:T(8,128)S(1)} collective-permute-done((f32[72,128]{1,0:T(8,128)S(1)}, f32[72,128]{1,0:T(8,128)S(1)}, u32[]{:S(2)}, u32[]{:S(2)}) %collective-permute-start.20) | collective-permute-done | bytes 36896 | tf_op jit(solution)/shard_map/ppermute | solution.py:30
  67.4 0.6 collective-permute-done.21
  68.0 0.0 collective-permute-done.22
  68.1 5.2 %collective-permute-start.24 = (bf16[2,2,4,8,512]{4,3,2,0,1:T(8,128)(2,1)S(1)}, bf16[2,2,4,8,512]{4,3,2,0,1:T(8,128)(2,1)S(1)}, u32[]{:S(2)}, u32[]{:S(2)}) collective-permute-start(bf16[2,2,4,8,512]{4,3,2,0,1:T(8,128)(2,1)S(1)} %pad_maximum_fusion.3), channel_id=1, source_target_pairs={{0,1},{1,2},{2,3},{3,0},{4,5},{5,6},{6,7},{7,4},{8,9},{9,10},{10,1... | collective-permute-start | bytes 393224 | tf_op jit(solution)/shard_map/ppermute | solution.py:30
  73.3 0.1 collective-permute-start.23
  73.4 2.2 %collective-permute-done.24 = bf16[2,2,4,8,512]{4,3,2,0,1:T(8,128)(2,1)S(1)} collective-permute-done((bf16[2,2,4,8,512]{4,3,2,0,1:T(8,128)(2,1)S(1)}, bf16[2,2,4,8,512]{4,3,2,0,1:T(8,128)(2,1)S(1)}, u32[]{:S(2)}, u32[]{:S(2)}) %collective-permute-start.24) | collective-permute-done | bytes 131104 | tf_op jit(solution)/shard_map/ppermute | solution.py:30
  75.6 1.3 %merge_kernel.1 = (bf16[8,16,512]{2,1,0:T(8,128)(2,1)}, bf16[8,16,512]{2,1,0:T(8,128)(2,1)}) custom-call(s32[5]{0:T(128)S(1)} %stack.62.spot, bf16[8,16,512]{2,1,0:T(8,128)(2,1)S(1)} %bitcast.62, bf16[8,16,512]{2,1,0:T(8,128)(2,1)S(1)} %bitcast.64, bf16[2,4,8,512]{3,2,1,0:T(8,128)(2,1)S(1)} %get-tuple-element.96.mine_high, ...), custom_call_target="tpu_custom_call" | custom-call | tf_op jit(solution)/shard_map/merge_kernel/pallas_call | solution.py:322
  76.9 0.0 collective-permute-done.23
  76.9 1.2 %collective-permute-start.25 = (f32[72,128]{1,0:T(8,128)S(1)}, f32[72,128]{1,0:T(8,128)S(1)}, u32[]{:S(2)}, u32[]{:S(2)}) collective-permute-start(f32[72,128]{1,0:T(8,128)S(1)} %add.127.near), channel_id=1, source_target_pairs={{0,1},{1,0},{2,3},{3,2},{4,5},{5,4},{6,7},{7,6},{8,9},{9,8},{10,11... | collective-permute-start | bytes 110600 | tf_op jit(solution)/shard_map/ppermute | solution.py:30
  78.1 0.9 %collective-permute-done.25.core_in = f32[72,128]{1,0:T(8,128)S(1)} collective-permute-done((f32[72,128]{1,0:T(8,128)S(1)}, f32[72,128]{1,0:T(8,128)S(1)}, u32[]{:S(2)}, u32[]{:S(2)}) %collective-permute-start.25) | collective-permute-done | bytes 36896 | tf_op jit(solution)/shard_map/ppermute | solution.py:30
  79.0 1.2 %last_kernel.1 = (f32[24,512]{1,0:T(8,128)}, f32[8,512]{1,0:T(8,128)}, f32[2,8]{1,0:T(2,128)}) custom-call(s32[5]{0:T(128)S(1)} %stack.62.spot, f32[72,128]{1,0:T(8,128)S(1)} %add.127.near, f32[72,128]{1,0:T(8,128)S(1)} %collective-permute-done.25.core_in), custom_call_target="tpu_custom_call" | custom-call | tf_op jit(solution)/shard_map/last_kernel/pallas_call | solution.py:322
  (29 shorter events, 0.2 us)
Async XLA Ops:
  0.6 22.4 %copy-start = (bf16[512,1536]{1,0:T(8,128)(2,1)S(1)}, bf16[512,1536]{1,0:T(8,128)(2,1)}, u32[]{:S(2)}) copy-start(bf16[512,1536]{1,0:T(8,128)(2,1)} %w_qkv.7) | copy-start | bytes 4718596
  0.6 22.4 %copy-start.5 = (f32[2,512]{1,0:T(2,128)S(1)}, f32[2,512]{1,0:T(2,128)}, u32[]{:S(2)}) copy-start(f32[2,512]{1,0:T(2,128)} %norm.5) | copy-start | bytes 12292
  1.9 10.6 %collective-permute-start = (bf16[2,4,8,512]{3,2,1,0:T(8,128)(2,1)S(1)}, bf16[2,4,8,512]{3,2,1,0:T(8,128)(2,1)S(1)}, u32[]{:S(2)}, u32[]{:S(2)}) collective-permute-start(bf16[2,4,8,512]{3,2,1,0:T(8,128)(2,1)S(1)} %get-tuple-element.104), channel_id=1, source_target_pairs={{0,3},{1,0},{2,1},{3,2},{4,7},{5,4},{6,5},{7,6},{8,11},{9,8},{10,9... | collective-permute-start | bytes 196616 | tf_op jit(solution)/shard_map/ppermute | solution.py:30
  5.3 10.8 %collective-permute-start.4 = (bf16[2,4,8,512]{3,2,1,0:T(8,128)(2,1)S(1)}, bf16[2,4,8,512]{3,2,1,0:T(8,128)(2,1)S(1)}, u32[]{:S(2)}, u32[]{:S(2)}) collective-permute-start(bf16[2,4,8,512]{3,2,1,0:T(8,128)(2,1)S(1)} %get-tuple-element.101), channel_id=1, source_target_pairs={{0,240},{1,241},{2,242},{3,243},{4,244},{5,245},{6,246},{7,247},{8... | collective-permute-start | bytes 196616 | tf_op jit(solution)/shard_map/ppermute | solution.py:30
  12.1 7.6 %collective-permute-start.5 = (bf16[2,4,8,512]{3,2,1,0:T(8,128)(2,1)S(1)}, bf16[2,4,8,512]{3,2,1,0:T(8,128)(2,1)S(1)}, u32[]{:S(2)}, u32[]{:S(2)}) collective-permute-start(bf16[2,4,8,512]{3,2,1,0:T(8,128)(2,1)S(1)} %get-tuple-element.102), channel_id=1, source_target_pairs={{0,243},{1,240},{2,241},{3,242},{4,247},{5,244},{6,245},{7,246},{8... | collective-permute-start | bytes 196616 | tf_op jit(solution)/shard_map/ppermute | solution.py:30
  12.6 10.2 %collective-permute-start.3 = (bf16[2,64,512]{2,1,0:T(8,128)(2,1)S(1)}, bf16[2,64,512]{2,1,0:T(8,128)(2,1)S(1)}, u32[]{:S(2)}, u32[]{:S(2)}) collective-permute-start(bf16[2,64,512]{2,1,0:T(8,128)(2,1)S(1)} %bitcast.65), channel_id=1, source_target_pairs={{0,12},{1,13},{2,14},{3,15},{4,8},{5,9},{6,10},{7,11},{8,4},{9,5},... | collective-permute-start | bytes 393224 | tf_op jit(solution)/shard_map/ppermute | solution.py:30
  15.1 7.9 %collective-permute-start.2 = (bf16[2,64,512]{2,1,0:T(8,128)(2,1)S(1)}, bf16[2,64,512]{2,1,0:T(8,128)(2,1)S(1)}, u32[]{:S(2)}, u32[]{:S(2)}) collective-permute-start(bf16[2,64,512]{2,1,0:T(8,128)(2,1)S(1)} %bitcast.66), channel_id=1, source_target_pairs={{0,8},{1,9},{2,10},{3,11},{4,12},{5,13},{6,14},{7,15},{8,0},{9,1},... | collective-permute-start | bytes 393224 | tf_op jit(solution)/shard_map/ppermute | solution.py:30
  15.7 7.4 %collective-permute-start.1 = (bf16[2,64,512]{2,1,0:T(8,128)(2,1)S(1)}, bf16[2,64,512]{2,1,0:T(8,128)(2,1)S(1)}, u32[]{:S(2)}, u32[]{:S(2)}) collective-permute-start(bf16[2,64,512]{2,1,0:T(8,128)(2,1)S(1)} %bitcast.67), channel_id=1, source_target_pairs={{0,4},{1,5},{2,6},{3,7},{4,0},{5,1},{6,2},{7,3},{8,12},{9,13},{10,... | collective-permute-start | bytes 393224 | tf_op jit(solution)/shard_map/ppermute | solution.py:30
  19.7 5.9 %collective-permute-start.8 = (bf16[2,64,512]{2,1,0:T(8,128)(2,1)S(1)}, bf16[2,64,512]{2,1,0:T(8,128)(2,1)S(1)}, u32[]{:S(2)}, u32[]{:S(2)}) collective-permute-start(bf16[2,64,512]{2,1,0:T(8,128)(2,1)S(1)} %bitcast.71), channel_id=1, source_target_pairs={{0,12},{1,13},{2,14},{3,15},{4,8},{5,9},{6,10},{7,11},{8,4},{9,5},... | collective-permute-start | bytes 393224 | tf_op jit(solution)/shard_map/ppermute | solution.py:30
  22.3 5.4 %collective-permute-start.7 = (bf16[2,64,512]{2,1,0:T(8,128)(2,1)S(1)}, bf16[2,64,512]{2,1,0:T(8,128)(2,1)S(1)}, u32[]{:S(2)}, u32[]{:S(2)}) collective-permute-start(bf16[2,64,512]{2,1,0:T(8,128)(2,1)S(1)} %bitcast.72), channel_id=1, source_target_pairs={{0,8},{1,9},{2,10},{3,11},{4,12},{5,13},{6,14},{7,15},{8,0},{9,1},... | collective-permute-start | bytes 393224 | tf_op jit(solution)/shard_map/ppermute | solution.py:30
  22.8 4.9 %collective-permute-start.6 = (bf16[2,64,512]{2,1,0:T(8,128)(2,1)S(1)}, bf16[2,64,512]{2,1,0:T(8,128)(2,1)S(1)}, u32[]{:S(2)}, u32[]{:S(2)}) collective-permute-start(bf16[2,64,512]{2,1,0:T(8,128)(2,1)S(1)} %bitcast.73), channel_id=1, source_target_pairs={{0,4},{1,5},{2,6},{3,7},{4,0},{5,1},{6,2},{7,3},{8,12},{9,13},{10,... | collective-permute-start | bytes 393224 | tf_op jit(solution)/shard_map/ppermute | solution.py:30
  23.1 1.0 %copy-start.1 = (bf16[512,512]{1,0:T(8,128)(2,1)S(1)}, bf16[512,512]{1,0:T(8,128)(2,1)}, u32[]{:S(2)}) copy-start(bf16[512,512]{1,0:T(8,128)(2,1)} %w_proj.5) | copy-start | bytes 1572868
  37.0 16.7 %copy-start.2 = (bf16[512,512]{1,0:T(8,128)(2,1)S(1)}, bf16[512,512]{1,0:T(8,128)(2,1)}, u32[]{:S(2)}) copy-start(bf16[512,512]{1,0:T(8,128)(2,1)} %w_proj.5) | copy-start | bytes 1572868
  37.0 6.8 %collective-permute-start.9 = (f32[16,72,128]{2,1,0:T(8,128)S(1)}, f32[16,72,128]{2,1,0:T(8,128)S(1)}, u32[]{:S(2)}, u32[]{:S(2)}) collective-permute-start(f32[16,72,128]{2,1,0:T(8,128)S(1)} %get-tuple-element.56), channel_id=1, source_target_pairs={{0,1},{1,0},{2,3},{3,2},{4,5},{5,4},{6,7},{7,6},{8,9},{9,8},{10,11... | collective-permute-start | bytes 1769480 | tf_op jit(solution)/shard_map/ppermute | solution.py:30
  40.8 6.3 %collective-permute-start.13 = (bf16[128,512]{1,0:T(8,128)(2,1)S(1)}, bf16[128,512]{1,0:T(8,128)(2,1)S(1)}, u32[]{:S(2)}, u32[]{:S(2)}) collective-permute-start(bf16[128,512]{1,0:T(8,128)(2,1)S(1)} %get-tuple-element.49.r1), channel_id=1, source_target_pairs={{0,4},{1,5},{2,6},{3,7},{4,0},{5,1},{6,2},{7,3},{8,12},{9,13},{10,... | collective-permute-start | bytes 393224 | tf_op jit(solution)/shard_map/ppermute | solution.py:30
  41.3 8.9 %collective-permute-start.14 = (bf16[128,512]{1,0:T(8,128)(2,1)S(1)}, bf16[128,512]{1,0:T(8,128)(2,1)S(1)}, u32[]{:S(2)}, u32[]{:S(2)}) collective-permute-start(bf16[128,512]{1,0:T(8,128)(2,1)S(1)} %get-tuple-element.50.r2), channel_id=1, source_target_pairs={{0,8},{1,9},{2,10},{3,11},{4,12},{5,13},{6,14},{7,15},{8,0},{9,1},... | collective-permute-start | bytes 393224 | tf_op jit(solution)/shard_map/ppermute | solution.py:30
  43.8 6.3 %collective-permute-start.12 = (bf16[4,72,128]{2,1,0:T(8,128)(2,1)S(1)}, bf16[4,72,128]{2,1,0:T(8,128)(2,1)S(1)}, u32[]{:S(2)}, u32[]{:S(2)}) collective-permute-start(bf16[4,72,128]{2,1,0:T(8,128)(2,1)S(1)} %get-tuple-element.85), channel_id=1, source_target_pairs={{0,48},{1,49},{2,50},{3,51},{4,52},{5,53},{6,54},{7,55},{8,56},{9,... | collective-permute-start | bytes 221192 | tf_op jit(solution)/shard_map/ppermute | solution.py:30
  43.9 6.2 %collective-permute-start.11 = (bf16[4,72,128]{2,1,0:T(8,128)(2,1)S(1)}, bf16[4,72,128]{2,1,0:T(8,128)(2,1)S(1)}, u32[]{:S(2)}, u32[]{:S(2)}) collective-permute-start(bf16[4,72,128]{2,1,0:T(8,128)(2,1)S(1)} %get-tuple-element.86), channel_id=1, source_target_pairs={{0,32},{1,33},{2,34},{3,35},{4,36},{5,37},{6,38},{7,39},{8,40},{9,... | collective-permute-start | bytes 221192 | tf_op jit(solution)/shard_map/ppermute | solution.py:30
  44.0 6.1 %collective-permute-start.10 = (bf16[4,72,128]{2,1,0:T(8,128)(2,1)S(1)}, bf16[4,72,128]{2,1,0:T(8,128)(2,1)S(1)}, u32[]{:S(2)}, u32[]{:S(2)}) collective-permute-start(bf16[4,72,128]{2,1,0:T(8,128)(2,1)S(1)} %get-tuple-element.87), channel_id=1, source_target_pairs={{0,16},{1,17},{2,18},{3,19},{4,20},{5,21},{6,22},{7,23},{8,24},{9,... | collective-permute-start | bytes 221192 | tf_op jit(solution)/shard_map/ppermute | solution.py:30
  47.2 6.4 %collective-permute-start.18 = (bf16[128,512]{1,0:T(8,128)(2,1)S(1)}, bf16[128,512]{1,0:T(8,128)(2,1)S(1)}, u32[]{:S(2)}, u32[]{:S(2)}) collective-permute-start(bf16[128,512]{1,0:T(8,128)(2,1)S(1)} %get-tuple-element.51.r3), channel_id=1, source_target_pairs={{0,12},{1,13},{2,14},{3,15},{4,8},{5,9},{6,10},{7,11},{8,4},{9,5},... | collective-permute-start | bytes 393224 | tf_op jit(solution)/shard_map/ppermute | solution.py:30
  50.3 8.9 %collective-permute-start.17 = (f32[72,128]{1,0:T(8,128)S(1)}, f32[72,128]{1,0:T(8,128)S(1)}, u32[]{:S(2)}, u32[]{:S(2)}) collective-permute-start(f32[72,128]{1,0:T(8,128)S(1)} %get-tuple-element.89), channel_id=1, source_target_pairs={{0,12},{1,13},{2,14},{3,15},{4,8},{5,9},{6,10},{7,11},{8,4},{9,5},... | collective-permute-start | bytes 110600 | tf_op jit(solution)/shard_map/ppermute | solution.py:30
  51.3 7.9 %collective-permute-start.16 = (f32[72,128]{1,0:T(8,128)S(1)}, f32[72,128]{1,0:T(8,128)S(1)}, u32[]{:S(2)}, u32[]{:S(2)}) collective-permute-start(f32[72,128]{1,0:T(8,128)S(1)} %get-tuple-element.90), channel_id=1, source_target_pairs={{0,8},{1,9},{2,10},{3,11},{4,12},{5,13},{6,14},{7,15},{8,0},{9,1},... | collective-permute-start | bytes 110600 | tf_op jit(solution)/shard_map/ppermute | solution.py:30
  52.1 7.1 %collective-permute-start.15 = (f32[72,128]{1,0:T(8,128)S(1)}, f32[72,128]{1,0:T(8,128)S(1)}, u32[]{:S(2)}, u32[]{:S(2)}) collective-permute-start(f32[72,128]{1,0:T(8,128)S(1)} %get-tuple-element.91), channel_id=1, source_target_pairs={{0,4},{1,5},{2,6},{3,7},{4,0},{5,1},{6,2},{7,3},{8,12},{9,13},{10,... | collective-permute-start | bytes 110600 | tf_op jit(solution)/shard_map/ppermute | solution.py:30
  55.0 20.6 %copy-start.3 = (bf16[1,1,8,16,512]{4,3,2,1,0:T(8,128)(2,1)S(1)}, bf16[1,1,8,16,512]{4,3,2,1,0:T(8,128)(2,1)}, u32[]{:S(2)}) copy-start(bf16[1,1,8,16,512]{4,3,2,1,0:T(8,128)(2,1)} %param.5) | copy-start | bytes 393220
  55.0 20.6 %copy-start.4 = (bf16[1,1,8,16,512]{4,3,2,1,0:T(8,128)(2,1)S(1)}, bf16[1,1,8,16,512]{4,3,2,1,0:T(8,128)(2,1)}, u32[]{:S(2)}) copy-start(bf16[1,1,8,16,512]{4,3,2,1,0:T(8,128)(2,1)} %param.9) | copy-start | bytes 393220
  55.0 13.0 %collective-permute-start.22 = (bf16[2,2,4,8,512]{4,3,2,0,1:T(8,128)(2,1)S(1)}, bf16[2,2,4,8,512]{4,3,2,0,1:T(8,128)(2,1)S(1)}, u32[]{:S(2)}, u32[]{:S(2)}) collective-permute-start(bf16[2,2,4,8,512]{4,3,2,0,1:T(8,128)(2,1)S(1)} %copy.24), channel_id=1, source_target_pairs={{0,240},{1,241},{2,242},{3,243},{4,244},{5,245},{6,246},{7,247},{8... | collective-permute-start | bytes 393224 | tf_op jit(solution)/shard_map/ppermute | solution.py:30
  59.9 5.8 %collective-permute-start.19 = (f32[72,128]{1,0:T(8,128)S(1)}, f32[72,128]{1,0:T(8,128)S(1)}, u32[]{:S(2)}, u32[]{:S(2)}) collective-permute-start(f32[72,128]{1,0:T(8,128)S(1)} %get-tuple-element.69), channel_id=1, source_target_pairs={{0,64},{1,65},{2,66},{3,67},{4,68},{5,69},{6,70},{7,71},{8,72},{9,... | collective-permute-start | bytes 110600 | tf_op jit(solution)/shard_map/ppermute | solution.py:30
  60.0 7.4 %collective-permute-start.20 = (f32[72,128]{1,0:T(8,128)S(1)}, f32[72,128]{1,0:T(8,128)S(1)}, u32[]{:S(2)}, u32[]{:S(2)}) collective-permute-start(f32[72,128]{1,0:T(8,128)S(1)} %get-tuple-element.70), channel_id=1, source_target_pairs={{0,128},{1,129},{2,130},{3,131},{4,132},{5,133},{6,134},{7,135},{8... | collective-permute-start | bytes 110600 | tf_op jit(solution)/shard_map/ppermute | solution.py:30
  62.0 6.1 %collective-permute-start.21 = (f32[72,128]{1,0:T(8,128)S(1)}, f32[72,128]{1,0:T(8,128)S(1)}, u32[]{:S(2)}, u32[]{:S(2)}) collective-permute-start(f32[72,128]{1,0:T(8,128)S(1)} %get-tuple-element.71), channel_id=1, source_target_pairs={{0,192},{1,193},{2,194},{3,195},{4,196},{5,197},{6,198},{7,199},{8... | collective-permute-start | bytes 110600 | tf_op jit(solution)/shard_map/ppermute | solution.py:30
  68.1 7.5 %collective-permute-start.24 = (bf16[2,2,4,8,512]{4,3,2,0,1:T(8,128)(2,1)S(1)}, bf16[2,2,4,8,512]{4,3,2,0,1:T(8,128)(2,1)S(1)}, u32[]{:S(2)}, u32[]{:S(2)}) collective-permute-start(bf16[2,2,4,8,512]{4,3,2,0,1:T(8,128)(2,1)S(1)} %pad_maximum_fusion.3), channel_id=1, source_target_pairs={{0,1},{1,2},{2,3},{3,0},{4,5},{5,6},{6,7},{7,4},{8,9},{9,10},{10,1... | collective-permute-start | bytes 393224 | tf_op jit(solution)/shard_map/ppermute | solution.py:30
  73.3 3.6 %collective-permute-start.23 = (f32[72,128]{1,0:T(8,128)S(1)}, f32[72,128]{1,0:T(8,128)S(1)}, u32[]{:S(2)}, u32[]{:S(2)}) collective-permute-start(f32[72,128]{1,0:T(8,128)S(1)} %add_add_fusion), channel_id=1, source_target_pairs={{0,2},{1,3},{2,0},{3,1},{4,6},{5,7},{6,4},{7,5},{8,10},{9,11},{10,... | collective-permute-start | bytes 110600 | tf_op jit(solution)/shard_map/ppermute | solution.py:30
  76.9 2.1 %collective-permute-start.25 = (f32[72,128]{1,0:T(8,128)S(1)}, f32[72,128]{1,0:T(8,128)S(1)}, u32[]{:S(2)}, u32[]{:S(2)}) collective-permute-start(f32[72,128]{1,0:T(8,128)S(1)} %add.127.near), channel_id=1, source_target_pairs={{0,1},{1,0},{2,3},{3,2},{4,5},{5,4},{6,7},{7,6},{8,9},{9,8},{10,11... | collective-permute-start | bytes 110600 | tf_op jit(solution)/shard_map/ppermute | solution.py:30

commit v11 on v9

--- a/solution.py
+++ b/solution.py
@@ -109,7 +109,6 @@
     cotangent_t = cotangent.T
     keys_t = keys.T
     values_t = values.T
-    head_of_lane = lax.broadcasted_iota(jnp.int32, (TOKENS, OWN), 1) // HEAD_DIM
 
     def label(shape, dim):
         token = lax.broadcasted_iota(jnp.int32, shape, dim)
@@ -120,16 +119,20 @@
 
     key_label = label((TOKENS, 1), 0)
     query_label = label((1, TOKENS), 1)
+    def heads_of(rows):
+        lane_head = lax.broadcasted_iota(jnp.int32, rows.shape, 1) // HEAD_DIM
+        return [jnp.where(lane_head == head, rows, jnp.zeros_like(rows)) for head in range(RING)]
+
+    key_heads, value_heads = heads_of(keys), heads_of(values)
     d_key = jnp.zeros((TOKENS, OWN), F32)
     d_value = jnp.zeros((TOKENS, OWN), F32)
     for block in range(TOKENS // BLOCK):
         span = slice(block * BLOCK, (block + 1) * BLOCK)
         allowed = key_label == query_label[:, span]
+        block_scores, block_probs = [], []
         for head in range(RING):
-            chosen = head_of_lane == head
             rows = slice(head * HEAD_DIM, (head + 1) * HEAD_DIM)
-            key_head = jnp.where(chosen, keys, jnp.zeros_like(keys))
-            value_head = jnp.where(chosen, values, jnp.zeros_like(values))
+            key_head, value_head = key_heads[head], value_heads[head]
             scores = jnp.where(allowed, dot(key_head, queries_t[:, span]), -1e30)
             highest = jnp.max(scores, 0, keepdims=True)
             d_probs = dot(value_head, cotangent_t[:, span])
@@ -154,12 +157,12 @@
             d_scores = jnp.concatenate(d_scores, 0)
             at_ref[rows, span] = dot(values_t[rows], probs_low).astype(BF16)
             dt_ref[rows, span] = dot(keys_t[rows], d_scores)
-            query_head = jnp.where(chosen[span], queries[span], jnp.zeros_like(queries[span]))
-            cotangent_head = jnp.where(
-                chosen[span], cotangent[span], jnp.zeros_like(cotangent[span])
-            )
-            d_key += dot(d_scores, query_head)
-            d_value += dot(probs_low, cotangent_head)
+            block_scores.append(d_scores)
+            block_probs.append(probs_low)
+        query_heads = jnp.concatenate(heads_of(queries[span]), 0)
+        cotangent_heads = jnp.concatenate(heads_of(cotangent[span]), 0)
+        d_key += dot(jnp.concatenate(block_scores, 1), query_heads)
+        d_value += dot(jnp.concatenate(block_probs, 1), cotangent_heads)
     dt_ref[OWN : 2 * OWN, :] = d_key.T
     dt_ref[2 * OWN :, :] = d_value.T
     d_query = dt_ref[:OWN, :].T.astype(BF16)

time: 78.3 us -> 78.1 us (level)
  no operation moved by 1% of the time
where the time goes in v11:
time: 78.1 us; the launch traced here: 78 us
  starting transfers between devices  49 us (63%)
  Pallas kernels  14.7 us (19%)
  waiting for transfers between devices  10.6 us (14%)
  other arithmetic  1.47 us (2%)
  local copies, waits for them, and re-layouts  1.23 us (2%)
  between operations  0.97 us (1%)
    ppermute x27, starting transfers between devices, move(): return lax.ppermute(value, ('wide', 'narrow'), pairs)  49 us
    pallas_call x7, Pallas kernels, call(): pl.pallas_call(kernel, out_shape=[jax.ShapeDtypeStruct(shape, dtype) for...  14.7 us
    ppermute x27, waiting for transfers between devices, move(): return lax.ppermute(value, ('wide', 'narrow'), pairs)  10.6 us
  transfers between devices with their start and end apart: 27, of which 7 were waited for; matrix products, arithmetic and copies ran while one was open for 1% of the time, Pallas kernels for 6%

profile of v11, /device:TPU:1, one launch (start us, length us, event | category | flops | bytes accessed | tf_op | source)
XLA Modules:
  0.0 78.0 jit_solution(13591078013347328828)
XLA Ops:
  0.7 1.2 %broadcast_select_fusion = (bf16[2,8,8,512]{3,2,1,0:T(8,128)(2,1)S(1)}, bf16[2,8,8,512]{3,2,1,0:T(8,128)(2,1)S(1)}) fusion(pred[8]{0:T(512)(128)(4,1)S(1)} %compare_compare_fusion, bf16[1,8,2,8,512]{4,3,2,1,0:T(8,128)(2,1)} %bitcast.63, bf16[1,8,2,8,512]{4,3,2,1,0:T(8,128)(2,1)} %bitcast.61), kind=kLoop, calls=%fused_computation.16 | loop fusion | flops 327680 | bytes 524296 | tf_op jit(solution)/shard_map/jit(_where)/select_n | solution.py:351
  1.9 3.3 %collective-permute-start = (bf16[2,4,8,512]{3,2,1,0:T(8,128)(2,1)S(1)}, bf16[2,4,8,512]{3,2,1,0:T(8,128)(2,1)S(1)}, u32[]{:S(2)}, u32[]{:S(2)}) collective-permute-start(bf16[2,4,8,512]{3,2,1,0:T(8,128)(2,1)S(1)} %get-tuple-element.108), channel_id=1, source_target_pairs={{0,3},{1,0},{2,1},{3,2},{4,7},{5,4},{6,5},{7,6},{8,11},{9,8},{10,9... | collective-permute-start | bytes 196616 | tf_op jit(solution)/shard_map/ppermute | solution.py:30
  5.3 6.8 %collective-permute-start.4 = (bf16[2,4,8,512]{3,2,1,0:T(8,128)(2,1)S(1)}, bf16[2,4,8,512]{3,2,1,0:T(8,128)(2,1)S(1)}, u32[]{:S(2)}, u32[]{:S(2)}) collective-permute-start(bf16[2,4,8,512]{3,2,1,0:T(8,128)(2,1)S(1)} %get-tuple-element.105), channel_id=1, source_target_pairs={{0,240},{1,241},{2,242},{3,243},{4,244},{5,245},{6,246},{7,247},{8... | collective-permute-start | bytes 196616 | tf_op jit(solution)/shard_map/ppermute | solution.py:30
  12.1 0.4 collective-permute-start.5
  12.5 0.0 collective-permute-done
  12.6 2.6 %collective-permute-start.3 = (bf16[2,64,512]{2,1,0:T(8,128)(2,1)S(1)}, bf16[2,64,512]{2,1,0:T(8,128)(2,1)S(1)}, u32[]{:S(2)}, u32[]{:S(2)}) collective-permute-start(bf16[2,64,512]{2,1,0:T(8,128)(2,1)S(1)} %bitcast.65), channel_id=1, source_target_pairs={{0,12},{1,13},{2,14},{3,15},{4,8},{5,9},{6,10},{7,11},{8,4},{9,5},... | collective-permute-start | bytes 393224 | tf_op jit(solution)/shard_map/ppermute | solution.py:30
  15.1 0.5 collective-permute-start.2
  15.7 0.3 collective-permute-start.1
  15.9 0.1 pad_add_fusion.flags
  16.0 0.1 stack.62.spot
  16.1 3.6 %collective-permute-done.5 = bf16[2,4,8,512]{3,2,1,0:T(8,128)(2,1)S(1)} collective-permute-done((bf16[2,4,8,512]{3,2,1,0:T(8,128)(2,1)S(1)}, bf16[2,4,8,512]{3,2,1,0:T(8,128)(2,1)S(1)}, u32[]{:S(2)}, u32[]{:S(2)}) %collective-permute-start.5) | collective-permute-done | bytes 65568 | tf_op jit(solution)/shard_map/ppermute | solution.py:30
  19.7 2.6 %collective-permute-start.8 = (bf16[2,64,512]{2,1,0:T(8,128)(2,1)S(1)}, bf16[2,64,512]{2,1,0:T(8,128)(2,1)S(1)}, u32[]{:S(2)}, u32[]{:S(2)}) collective-permute-start(bf16[2,64,512]{2,1,0:T(8,128)(2,1)S(1)} %bitcast.71), channel_id=1, source_target_pairs={{0,12},{1,13},{2,14},{3,15},{4,8},{5,9},{6,10},{7,11},{8,4},{9,5},... | collective-permute-start | bytes 393224 | tf_op jit(solution)/shard_map/ppermute | solution.py:30
  22.3 0.5 collective-permute-start.7
  22.8 0.0 collective-permute-done.3.p3
  22.8 0.3 collective-permute-start.6
  23.1 0.0 collective-permute-done.2.p2
  23.1 0.0 collective-permute-done.1.p1
  23.1 0.0 copy-start.1
  23.1 1.0 %copy-done.1 = bf16[512,512]{1,0:T(8,128)(2,1)S(1)} copy-done((bf16[512,512]{1,0:T(8,128)(2,1)S(1)}, bf16[512,512]{1,0:T(8,128)(2,1)}, u32[]{:S(2)}) %copy-start.1) | copy-done | bytes 524312
  24.1 1.1 %first_kernel.1 = (bf16[256,512]{1,0:T(8,128)(2,1)S(1)}, bf16[256,384]{1,0:T(8,128)(2,1)S(1)}, bf16[256,128]{1,0:T(8,128)(2,1)S(1)}) custom-call(s32[4]{0:T(128)S(1)} %pad_add_fusion.flags, bf16[2,64,512]{2,1,0:T(8,128)(2,1)S(1)} %bitcast.68, bf16[2,64,512]{2,1,0:T(8,128)(2,1)S(1)} %collective-permute-done.1.p1, ...), custom_call_target="tpu_custom_call" | custom-call | flops 10000000000 | bytes 3000000 | tf_op jit(solution)/shard_map/first_kernel/pallas_call | solution.py:325
  25.2 0.4 collective-permute-done.8.p3.p7
  25.6 2.1 %collective-permute-done.7.p2.p6 = bf16[2,64,512]{2,1,0:T(8,128)(2,1)S(1)} collective-permute-done((bf16[2,64,512]{2,1,0:T(8,128)(2,1)S(1)}, bf16[2,64,512]{2,1,0:T(8,128)(2,1)S(1)}, u32[]{:S(2)}, u32[]{:S(2)}) %collective-permute-start.7) | collective-permute-done | bytes 131104 | tf_op jit(solution)/shard_map/ppermute | solution.py:30
  27.7 0.0 collective-permute-done.6.p1.p5
  27.7 6.6 %attention_kernel.1 = (bf16[128,512]{1,0:T(8,128)(2,1)S(1)}, bf16[128,512]{1,0:T(8,128)(2,1)S(1)}, bf16[128,512]{1,0:T(8,128)(2,1)S(1)}, bf16[128,512]{1,0:T(8,1...) custom-call(s32[4]{0:T(128)S(1)} %pad_add_fusion.flags, ...), custom_call_target="tpu_custom_call" | custom-call | flops 1200000000 | bytes 6000000 | tf_op jit(solution)/shard_map/attention_kernel/pallas_call | solution.py:325
  34.3 2.5 %gradient_kernel.1 = (f32[16,72,128]{2,1,0:T(8,128)S(1)}, f32[16,72,128]{2,1,0:T(8,128)S(1)}) custom-call(s32[5]{0:T(128)S(1)} %stack.62.spot, bf16[2,64,512]{2,1,0:T(8,128)(2,1)S(1)} %bitcast.69, bf16[2,64,512]{2,1,0:T(8,128)(2,1)S(1)} %collective-permute-done.1.p1, bf16[2,64,512]{2,1,0:T(8,128)(2,1)S(1)} %collective-permute-done.2.p2, ...), custom_call_target="tpu_custom_call" | custom-call | flops 20000000000 | bytes 6000000 | tf_op jit(solution)/shard_map/gradient_kernel/pallas_call | solution.py:325
  36.8 0.0 copy-start.2
  36.8 3.9 %collective-permute-start.9 = (f32[16,72,128]{2,1,0:T(8,128)S(1)}, f32[16,72,128]{2,1,0:T(8,128)S(1)}, u32[]{:S(2)}, u32[]{:S(2)}) collective-permute-start(f32[16,72,128]{2,1,0:T(8,128)S(1)} %get-tuple-element.58), channel_id=1, source_target_pairs={{0,1},{1,0},{2,3},{3,2},{4,5},{5,4},{6,7},{7,6},{8,9},{9,8},{10,11... | collective-permute-start | bytes 1769480 | tf_op jit(solution)/shard_map/ppermute | solution.py:30
  40.7 0.4 collective-permute-start.13
  41.1 2.5 %collective-permute-start.14 = (bf16[128,512]{1,0:T(8,128)(2,1)S(1)}, bf16[128,512]{1,0:T(8,128)(2,1)S(1)}, u32[]{:S(2)}, u32[]{:S(2)}) collective-permute-start(bf16[128,512]{1,0:T(8,128)(2,1)S(1)} %get-tuple-element.52.r2), channel_id=1, source_target_pairs={{0,8},{1,9},{2,10},{3,11},{4,12},{5,13},{6,14},{7,15},{8,0},{9,1},... | collective-permute-start | bytes 393224 | tf_op jit(solution)/shard_map/ppermute | solution.py:30
  43.6 0.0 collective-permute-done.9
  43.6 0.1 fusion
  43.7 0.1 collective-permute-start.12
  43.8 0.1 collective-permute-start.11
  43.9 3.1 %collective-permute-start.10 = (bf16[4,72,128]{2,1,0:T(8,128)(2,1)S(1)}, bf16[4,72,128]{2,1,0:T(8,128)(2,1)S(1)}, u32[]{:S(2)}, u32[]{:S(2)}) collective-permute-start(bf16[4,72,128]{2,1,0:T(8,128)(2,1)S(1)} %get-tuple-element.91), channel_id=1, source_target_pairs={{0,16},{1,17},{2,18},{3,19},{4,20},{5,21},{6,22},{7,23},{8,24},{9,... | collective-permute-start | bytes 221192 | tf_op jit(solution)/shard_map/ppermute | solution.py:30
  47.0 1.0 %collective-permute-start.18 = (bf16[128,512]{1,0:T(8,128)(2,1)S(1)}, bf16[128,512]{1,0:T(8,128)(2,1)S(1)}, u32[]{:S(2)}, u32[]{:S(2)}) collective-permute-start(bf16[128,512]{1,0:T(8,128)(2,1)S(1)} %get-tuple-element.53.r3), channel_id=1, source_target_pairs={{0,12},{1,13},{2,14},{3,15},{4,8},{5,9},{6,10},{7,11},{8,4},{9,5},... | collective-permute-start | bytes 393224 | tf_op jit(solution)/shard_map/ppermute | solution.py:30
  48.0 2.0 %collective-permute-done.14.r2 = bf16[128,512]{1,0:T(8,128)(2,1)S(1)} collective-permute-done((bf16[128,512]{1,0:T(8,128)(2,1)S(1)}, bf16[128,512]{1,0:T(8,128)(2,1)S(1)}, u32[]{:S(2)}, u32[]{:S(2)}) %collective-permute-start.14) | collective-permute-done | bytes 131104 | tf_op jit(solution)/shard_map/ppermute | solution.py:30
  50.0 0.0 collective-permute-done.10
  50.1 1.1 %collective-permute-start.17 = (f32[72,128]{1,0:T(8,128)S(1)}, f32[72,128]{1,0:T(8,128)S(1)}, u32[]{:S(2)}, u32[]{:S(2)}) collective-permute-start(f32[72,128]{1,0:T(8,128)S(1)} %get-tuple-element.93), channel_id=1, source_target_pairs={{0,12},{1,13},{2,14},{3,15},{4,8},{5,9},{6,10},{7,11},{8,4},{9,5},... | collective-permute-start | bytes 110600 | tf_op jit(solution)/shard_map/ppermute | solution.py:30
  51.2 0.8 collective-permute-start.16
  51.9 1.5 %collective-permute-start.15 = (f32[72,128]{1,0:T(8,128)S(1)}, f32[72,128]{1,0:T(8,128)S(1)}, u32[]{:S(2)}, u32[]{:S(2)}) collective-permute-start(f32[72,128]{1,0:T(8,128)S(1)} %get-tuple-element.95), channel_id=1, source_target_pairs={{0,4},{1,5},{2,6},{3,7},{4,0},{5,1},{6,2},{7,3},{8,12},{9,13},{10,... | collective-permute-start | bytes 110600 | tf_op jit(solution)/shard_map/ppermute | solution.py:30
  53.4 0.0 collective-permute-done.18.r3
  53.4 1.3 %token_kernel.1 = (bf16[2,128,512]{2,1,0:T(8,128)(2,1)S(1)}, f32[8,128]{1,0:T(8,128)S(1)}) custom-call(s32[5]{0:T(128)S(1)} %stack.62.spot, bf16[128,512]{1,0:T(8,128)(2,1)S(1)} %get-tuple-element.50.r0, bf16[128,512]{1,0:T(8,128)(2,1)S(1)} %collective-permute-done.13.r1, bf16[128,512]{1,0:T(8,128)(2,1)S(1)} %collective-permute-done.14.r2, ...), custom_call_target="tpu_custom_call" | custom-call | flops 500000000 | bytes 4000000 | tf_op jit(solution)/shard_map/token_kernel/pallas_call | solution.py:325
  54.8 0.0 copy-start.3
  54.8 0.0 copy-start.4
  54.9 4.1 %collective-permute-start.22 = (bf16[2,2,4,8,512]{4,3,2,0,1:T(8,128)(2,1)S(1)}, bf16[2,2,4,8,512]{4,3,2,0,1:T(8,128)(2,1)S(1)}, u32[]{:S(2)}, u32[]{:S(2)}) collective-permute-start(bf16[2,2,4,8,512]{4,3,2,0,1:T(8,128)(2,1)S(1)} %copy.24), channel_id=1, source_target_pairs={{0,240},{1,241},{2,242},{3,243},{4,244},{5,245},{6,246},{7,247},{8... | collective-permute-start | bytes 393224 | tf_op jit(solution)/shard_map/ppermute | solution.py:30
  59.0 0.0 collective-permute-done.17.m3
  59.0 0.7 z_parts_kernel.1
  59.7 0.1 collective-permute-start.19
  59.8 2.0 %collective-permute-start.20 = (f32[72,128]{1,0:T(8,128)S(1)}, f32[72,128]{1,0:T(8,128)S(1)}, u32[]{:S(2)}, u32[]{:S(2)}) collective-permute-start(f32[72,128]{1,0:T(8,128)S(1)} %get-tuple-element.72), channel_id=1, source_target_pairs={{0,128},{1,129},{2,130},{3,131},{4,132},{5,133},{6,134},{7,135},{8... | collective-permute-start | bytes 110600 | tf_op jit(solution)/shard_map/ppermute | solution.py:30
  61.8 3.7 %collective-permute-start.21 = (f32[72,128]{1,0:T(8,128)S(1)}, f32[72,128]{1,0:T(8,128)S(1)}, u32[]{:S(2)}, u32[]{:S(2)}) collective-permute-start(f32[72,128]{1,0:T(8,128)S(1)} %get-tuple-element.73), channel_id=1, source_target_pairs={{0,192},{1,193},{2,194},{3,195},{4,196},{5,197},{6,198},{7,199},{8... | collective-permute-start | bytes 110600 | tf_op jit(solution)/shard_map/ppermute | solution.py:30
  65.5 0.0 collective-permute-done.19
  65.5 1.8 %collective-permute-done.20 = f32[72,128]{1,0:T(8,128)S(1)} collective-permute-done((f32[72,128]{1,0:T(8,128)S(1)}, f32[72,128]{1,0:T(8,128)S(1)}, u32[]{:S(2)}, u32[]{:S(2)}) %collective-permute-start.20) | collective-permute-done | bytes 36896 | tf_op jit(solution)/shard_map/ppermute | solution.py:30
  67.2 0.6 collective-permute-done.21
  67.9 0.0 collective-permute-done.22
  67.9 5.2 %collective-permute-start.26 = (bf16[2,2,4,8,512]{4,3,2,0,1:T(8,128)(2,1)S(1)}, bf16[2,2,4,8,512]{4,3,2,0,1:T(8,128)(2,1)S(1)}, u32[]{:S(2)}, u32[]{:S(2)}) collective-permute-start(bf16[2,2,4,8,512]{4,3,2,0,1:T(8,128)(2,1)S(1)} %pad_maximum_fusion.3), channel_id=1, source_target_pairs={{0,1},{1,2},{2,3},{3,0},{4,5},{5,6},{6,7},{7,4},{8,9},{9,10},{10,1... | collective-permute-start | bytes 393224 | tf_op jit(solution)/shard_map/ppermute | solution.py:30
  73.1 0.1 collective-permute-start.25
  73.3 0.1 collective-permute-start.24
  73.3 2.0 %collective-permute-start.23 = (f32[72,128]{1,0:T(8,128)S(1)}, f32[72,128]{1,0:T(8,128)S(1)}, u32[]{:S(2)}, u32[]{:S(2)}) collective-permute-start(f32[72,128]{1,0:T(8,128)S(1)} %add_add_fusion.near), channel_id=1, source_target_pairs={{0,1},{1,0},{2,3},{3,2},{4,5},{5,4},{6,7},{7,6},{8,9},{9,8},{10,11... | collective-permute-start | bytes 110600 | tf_op jit(solution)/shard_map/ppermute | solution.py:30
  75.4 0.1 collective-permute-done.26
  75.5 1.3 %merge_kernel.1 = (bf16[8,16,512]{2,1,0:T(8,128)(2,1)}, bf16[8,16,512]{2,1,0:T(8,128)(2,1)}) custom-call(s32[5]{0:T(128)S(1)} %stack.62.spot, bf16[8,16,512]{2,1,0:T(8,128)(2,1)S(1)} %bitcast.62, bf16[8,16,512]{2,1,0:T(8,128)(2,1)S(1)} %bitcast.64, bf16[2,4,8,512]{3,2,1,0:T(8,128)(2,1)S(1)} %get-tuple-element.100.mine_high, ...), custom_call_target="tpu_custom_call" | custom-call | tf_op jit(solution)/shard_map/merge_kernel/pallas_call | solution.py:325
  76.8 0.0 collective-permute-done.25.both_in
  76.8 0.0 collective-permute-done.24.z_in
  76.8 0.0 collective-permute-done.23.core_in
  76.8 1.2 %last_kernel.1 = (f32[24,512]{1,0:T(8,128)}, f32[8,512]{1,0:T(8,128)}, f32[2,8]{1,0:T(2,128)}) custom-call(s32[5]{0:T(128)S(1)} %stack.62.spot, f32[72,128]{1,0:T(8,128)S(1)} %add_add_fusion.near, f32[72,128]{1,0:T(8,128)S(1)} %collective-permute-done.23.core_in, f32[72,128]{1,0:T(8,128)S(1)} %collective-permute-done.24.z_in, ...), custom_call_target="tpu_custom_call" | custom-call | tf_op jit(solution)/shard_map/last_kernel/pallas_call | solution.py:325
  (30 shorter events, 0.2 us)
Async XLA Ops:
  0.6 22.4 %copy-start = (bf16[512,1536]{1,0:T(8,128)(2,1)S(1)}, bf16[512,1536]{1,0:T(8,128)(2,1)}, u32[]{:S(2)}) copy-start(bf16[512,1536]{1,0:T(8,128)(2,1)} %w_qkv.7) | copy-start | bytes 4718596
  0.6 22.4 %copy-start.5 = (f32[2,512]{1,0:T(2,128)S(1)}, f32[2,512]{1,0:T(2,128)}, u32[]{:S(2)}) copy-start(f32[2,512]{1,0:T(2,128)} %norm.5) | copy-start | bytes 12292
  1.9 10.6 %collective-permute-start = (bf16[2,4,8,512]{3,2,1,0:T(8,128)(2,1)S(1)}, bf16[2,4,8,512]{3,2,1,0:T(8,128)(2,1)S(1)}, u32[]{:S(2)}, u32[]{:S(2)}) collective-permute-start(bf16[2,4,8,512]{3,2,1,0:T(8,128)(2,1)S(1)} %get-tuple-element.108), channel_id=1, source_target_pairs={{0,3},{1,0},{2,1},{3,2},{4,7},{5,4},{6,5},{7,6},{8,11},{9,8},{10,9... | collective-permute-start | bytes 196616 | tf_op jit(solution)/shard_map/ppermute | solution.py:30
  5.3 10.8 %collective-permute-start.4 = (bf16[2,4,8,512]{3,2,1,0:T(8,128)(2,1)S(1)}, bf16[2,4,8,512]{3,2,1,0:T(8,128)(2,1)S(1)}, u32[]{:S(2)}, u32[]{:S(2)}) collective-permute-start(bf16[2,4,8,512]{3,2,1,0:T(8,128)(2,1)S(1)} %get-tuple-element.105), channel_id=1, source_target_pairs={{0,240},{1,241},{2,242},{3,243},{4,244},{5,245},{6,246},{7,247},{8... | collective-permute-start | bytes 196616 | tf_op jit(solution)/shard_map/ppermute | solution.py:30
  12.1 7.6 %collective-permute-start.5 = (bf16[2,4,8,512]{3,2,1,0:T(8,128)(2,1)S(1)}, bf16[2,4,8,512]{3,2,1,0:T(8,128)(2,1)S(1)}, u32[]{:S(2)}, u32[]{:S(2)}) collective-permute-start(bf16[2,4,8,512]{3,2,1,0:T(8,128)(2,1)S(1)} %get-tuple-element.106), channel_id=1, source_target_pairs={{0,243},{1,240},{2,241},{3,242},{4,247},{5,244},{6,245},{7,246},{8... | collective-permute-start | bytes 196616 | tf_op jit(solution)/shard_map/ppermute | solution.py:30
  12.6 10.2 %collective-permute-start.3 = (bf16[2,64,512]{2,1,0:T(8,128)(2,1)S(1)}, bf16[2,64,512]{2,1,0:T(8,128)(2,1)S(1)}, u32[]{:S(2)}, u32[]{:S(2)}) collective-permute-start(bf16[2,64,512]{2,1,0:T(8,128)(2,1)S(1)} %bitcast.65), channel_id=1, source_target_pairs={{0,12},{1,13},{2,14},{3,15},{4,8},{5,9},{6,10},{7,11},{8,4},{9,5},... | collective-permute-start | bytes 393224 | tf_op jit(solution)/shard_map/ppermute | solution.py:30
  15.1 7.9 %collective-permute-start.2 = (bf16[2,64,512]{2,1,0:T(8,128)(2,1)S(1)}, bf16[2,64,512]{2,1,0:T(8,128)(2,1)S(1)}, u32[]{:S(2)}, u32[]{:S(2)}) collective-permute-start(bf16[2,64,512]{2,1,0:T(8,128)(2,1)S(1)} %bitcast.66), channel_id=1, source_target_pairs={{0,8},{1,9},{2,10},{3,11},{4,12},{5,13},{6,14},{7,15},{8,0},{9,1},... | collective-permute-start | bytes 393224 | tf_op jit(solution)/shard_map/ppermute | solution.py:30
  15.7 7.4 %collective-permute-start.1 = (bf16[2,64,512]{2,1,0:T(8,128)(2,1)S(1)}, bf16[2,64,512]{2,1,0:T(8,128)(2,1)S(1)}, u32[]{:S(2)}, u32[]{:S(2)}) collective-permute-start(bf16[2,64,512]{2,1,0:T(8,128)(2,1)S(1)} %bitcast.67), channel_id=1, source_target_pairs={{0,4},{1,5},{2,6},{3,7},{4,0},{5,1},{6,2},{7,3},{8,12},{9,13},{10,... | collective-permute-start | bytes 393224 | tf_op jit(solution)/shard_map/ppermute | solution.py:30
  19.7 5.9 %collective-permute-start.8 = (bf16[2,64,512]{2,1,0:T(8,128)(2,1)S(1)}, bf16[2,64,512]{2,1,0:T(8,128)(2,1)S(1)}, u32[]{:S(2)}, u32[]{:S(2)}) collective-permute-start(bf16[2,64,512]{2,1,0:T(8,128)(2,1)S(1)} %bitcast.71), channel_id=1, source_target_pairs={{0,12},{1,13},{2,14},{3,15},{4,8},{5,9},{6,10},{7,11},{8,4},{9,5},... | collective-permute-start | bytes 393224 | tf_op jit(solution)/shard_map/ppermute | solution.py:30
  22.3 5.4 %collective-permute-start.7 = (bf16[2,64,512]{2,1,0:T(8,128)(2,1)S(1)}, bf16[2,64,512]{2,1,0:T(8,128)(2,1)S(1)}, u32[]{:S(2)}, u32[]{:S(2)}) collective-permute-start(bf16[2,64,512]{2,1,0:T(8,128)(2,1)S(1)} %bitcast.72), channel_id=1, source_target_pairs={{0,8},{1,9},{2,10},{3,11},{4,12},{5,13},{6,14},{7,15},{8,0},{9,1},... | collective-permute-start | bytes 393224 | tf_op jit(solution)/shard_map/ppermute | solution.py:30
  22.8 4.9 %collective-permute-start.6 = (bf16[2,64,512]{2,1,0:T(8,128)(2,1)S(1)}, bf16[2,64,512]{2,1,0:T(8,128)(2,1)S(1)}, u32[]{:S(2)}, u32[]{:S(2)}) collective-permute-start(bf16[2,64,512]{2,1,0:T(8,128)(2,1)S(1)} %bitcast.73), channel_id=1, source_target_pairs={{0,4},{1,5},{2,6},{3,7},{4,0},{5,1},{6,2},{7,3},{8,12},{9,13},{10,... | collective-permute-start | bytes 393224 | tf_op jit(solution)/shard_map/ppermute | solution.py:30
  23.1 1.0 %copy-start.1 = (bf16[512,512]{1,0:T(8,128)(2,1)S(1)}, bf16[512,512]{1,0:T(8,128)(2,1)}, u32[]{:S(2)}) copy-start(bf16[512,512]{1,0:T(8,128)(2,1)} %w_proj.5) | copy-start | bytes 1572868
  36.8 16.7 %copy-start.2 = (bf16[512,512]{1,0:T(8,128)(2,1)S(1)}, bf16[512,512]{1,0:T(8,128)(2,1)}, u32[]{:S(2)}) copy-start(bf16[512,512]{1,0:T(8,128)(2,1)} %w_proj.5) | copy-start | bytes 1572868
  36.8 6.8 %collective-permute-start.9 = (f32[16,72,128]{2,1,0:T(8,128)S(1)}, f32[16,72,128]{2,1,0:T(8,128)S(1)}, u32[]{:S(2)}, u32[]{:S(2)}) collective-permute-start(f32[16,72,128]{2,1,0:T(8,128)S(1)} %get-tuple-element.58), channel_id=1, source_target_pairs={{0,1},{1,0},{2,3},{3,2},{4,5},{5,4},{6,7},{7,6},{8,9},{9,8},{10,11... | collective-permute-start | bytes 1769480 | tf_op jit(solution)/shard_map/ppermute | solution.py:30
  40.7 6.3 %collective-permute-start.13 = (bf16[128,512]{1,0:T(8,128)(2,1)S(1)}, bf16[128,512]{1,0:T(8,128)(2,1)S(1)}, u32[]{:S(2)}, u32[]{:S(2)}) collective-permute-start(bf16[128,512]{1,0:T(8,128)(2,1)S(1)} %get-tuple-element.51.r1), channel_id=1, source_target_pairs={{0,4},{1,5},{2,6},{3,7},{4,0},{5,1},{6,2},{7,3},{8,12},{9,13},{10,... | collective-permute-start | bytes 393224 | tf_op jit(solution)/shard_map/ppermute | solution.py:30
  41.1 8.9 %collective-permute-start.14 = (bf16[128,512]{1,0:T(8,128)(2,1)S(1)}, bf16[128,512]{1,0:T(8,128)(2,1)S(1)}, u32[]{:S(2)}, u32[]{:S(2)}) collective-permute-start(bf16[128,512]{1,0:T(8,128)(2,1)S(1)} %get-tuple-element.52.r2), channel_id=1, source_target_pairs={{0,8},{1,9},{2,10},{3,11},{4,12},{5,13},{6,14},{7,15},{8,0},{9,1},... | collective-permute-start | bytes 393224 | tf_op jit(solution)/shard_map/ppermute | solution.py:30
  43.7 6.3 %collective-permute-start.12 = (bf16[4,72,128]{2,1,0:T(8,128)(2,1)S(1)}, bf16[4,72,128]{2,1,0:T(8,128)(2,1)S(1)}, u32[]{:S(2)}, u32[]{:S(2)}) collective-permute-start(bf16[4,72,128]{2,1,0:T(8,128)(2,1)S(1)} %get-tuple-element.89), channel_id=1, source_target_pairs={{0,48},{1,49},{2,50},{3,51},{4,52},{5,53},{6,54},{7,55},{8,56},{9,... | collective-permute-start | bytes 221192 | tf_op jit(solution)/shard_map/ppermute | solution.py:30
  43.8 6.2 %collective-permute-start.11 = (bf16[4,72,128]{2,1,0:T(8,128)(2,1)S(1)}, bf16[4,72,128]{2,1,0:T(8,128)(2,1)S(1)}, u32[]{:S(2)}, u32[]{:S(2)}) collective-permute-start(bf16[4,72,128]{2,1,0:T(8,128)(2,1)S(1)} %get-tuple-element.90), channel_id=1, source_target_pairs={{0,32},{1,33},{2,34},{3,35},{4,36},{5,37},{6,38},{7,39},{8,40},{9,... | collective-permute-start | bytes 221192 | tf_op jit(solution)/shard_map/ppermute | solution.py:30
  43.9 6.1 %collective-permute-start.10 = (bf16[4,72,128]{2,1,0:T(8,128)(2,1)S(1)}, bf16[4,72,128]{2,1,0:T(8,128)(2,1)S(1)}, u32[]{:S(2)}, u32[]{:S(2)}) collective-permute-start(bf16[4,72,128]{2,1,0:T(8,128)(2,1)S(1)} %get-tuple-element.91), channel_id=1, source_target_pairs={{0,16},{1,17},{2,18},{3,19},{4,20},{5,21},{6,22},{7,23},{8,24},{9,... | collective-permute-start | bytes 221192 | tf_op jit(solution)/shard_map/ppermute | solution.py:30
  47.0 6.4 %collective-permute-start.18 = (bf16[128,512]{1,0:T(8,128)(2,1)S(1)}, bf16[128,512]{1,0:T(8,128)(2,1)S(1)}, u32[]{:S(2)}, u32[]{:S(2)}) collective-permute-start(bf16[128,512]{1,0:T(8,128)(2,1)S(1)} %get-tuple-element.53.r3), channel_id=1, source_target_pairs={{0,12},{1,13},{2,14},{3,15},{4,8},{5,9},{6,10},{7,11},{8,4},{9,5},... | collective-permute-start | bytes 393224 | tf_op jit(solution)/shard_map/ppermute | solution.py:30
  50.1 8.9 %collective-permute-start.17 = (f32[72,128]{1,0:T(8,128)S(1)}, f32[72,128]{1,0:T(8,128)S(1)}, u32[]{:S(2)}, u32[]{:S(2)}) collective-permute-start(f32[72,128]{1,0:T(8,128)S(1)} %get-tuple-element.93), channel_id=1, source_target_pairs={{0,12},{1,13},{2,14},{3,15},{4,8},{5,9},{6,10},{7,11},{8,4},{9,5},... | collective-permute-start | bytes 110600 | tf_op jit(solution)/shard_map/ppermute | solution.py:30
  51.2 7.9 %collective-permute-start.16 = (f32[72,128]{1,0:T(8,128)S(1)}, f32[72,128]{1,0:T(8,128)S(1)}, u32[]{:S(2)}, u32[]{:S(2)}) collective-permute-start(f32[72,128]{1,0:T(8,128)S(1)} %get-tuple-element.94), channel_id=1, source_target_pairs={{0,8},{1,9},{2,10},{3,11},{4,12},{5,13},{6,14},{7,15},{8,0},{9,1},... | collective-permute-start | bytes 110600 | tf_op jit(solution)/shard_map/ppermute | solution.py:30
  51.9 7.1 %collective-permute-start.15 = (f32[72,128]{1,0:T(8,128)S(1)}, f32[72,128]{1,0:T(8,128)S(1)}, u32[]{:S(2)}, u32[]{:S(2)}) collective-permute-start(f32[72,128]{1,0:T(8,128)S(1)} %get-tuple-element.95), channel_id=1, source_target_pairs={{0,4},{1,5},{2,6},{3,7},{4,0},{5,1},{6,2},{7,3},{8,12},{9,13},{10,... | collective-permute-start | bytes 110600 | tf_op jit(solution)/shard_map/ppermute | solution.py:30
  54.8 20.6 %copy-start.3 = (bf16[1,1,8,16,512]{4,3,2,1,0:T(8,128)(2,1)S(1)}, bf16[1,1,8,16,512]{4,3,2,1,0:T(8,128)(2,1)}, u32[]{:S(2)}) copy-start(bf16[1,1,8,16,512]{4,3,2,1,0:T(8,128)(2,1)} %param.5) | copy-start | bytes 393220
  54.8 20.6 %copy-start.4 = (bf16[1,1,8,16,512]{4,3,2,1,0:T(8,128)(2,1)S(1)}, bf16[1,1,8,16,512]{4,3,2,1,0:T(8,128)(2,1)}, u32[]{:S(2)}) copy-start(bf16[1,1,8,16,512]{4,3,2,1,0:T(8,128)(2,1)} %param.9) | copy-start | bytes 393220
  54.9 13.0 %collective-permute-start.22 = (bf16[2,2,4,8,512]{4,3,2,0,1:T(8,128)(2,1)S(1)}, bf16[2,2,4,8,512]{4,3,2,0,1:T(8,128)(2,1)S(1)}, u32[]{:S(2)}, u32[]{:S(2)}) collective-permute-start(bf16[2,2,4,8,512]{4,3,2,0,1:T(8,128)(2,1)S(1)} %copy.24), channel_id=1, source_target_pairs={{0,240},{1,241},{2,242},{3,243},{4,244},{5,245},{6,246},{7,247},{8... | collective-permute-start | bytes 393224 | tf_op jit(solution)/shard_map/ppermute | solution.py:30
  59.7 5.8 %collective-permute-start.19 = (f32[72,128]{1,0:T(8,128)S(1)}, f32[72,128]{1,0:T(8,128)S(1)}, u32[]{:S(2)}, u32[]{:S(2)}) collective-permute-start(f32[72,128]{1,0:T(8,128)S(1)} %get-tuple-element.71), channel_id=1, source_target_pairs={{0,64},{1,65},{2,66},{3,67},{4,68},{5,69},{6,70},{7,71},{8,72},{9,... | collective-permute-start | bytes 110600 | tf_op jit(solution)/shard_map/ppermute | solution.py:30
  59.8 7.4 %collective-permute-start.20 = (f32[72,128]{1,0:T(8,128)S(1)}, f32[72,128]{1,0:T(8,128)S(1)}, u32[]{:S(2)}, u32[]{:S(2)}) collective-permute-start(f32[72,128]{1,0:T(8,128)S(1)} %get-tuple-element.72), channel_id=1, source_target_pairs={{0,128},{1,129},{2,130},{3,131},{4,132},{5,133},{6,134},{7,135},{8... | collective-permute-start | bytes 110600 | tf_op jit(solution)/shard_map/ppermute | solution.py:30
  61.8 6.1 %collective-permute-start.21 = (f32[72,128]{1,0:T(8,128)S(1)}, f32[72,128]{1,0:T(8,128)S(1)}, u32[]{:S(2)}, u32[]{:S(2)}) collective-permute-start(f32[72,128]{1,0:T(8,128)S(1)} %get-tuple-element.73), channel_id=1, source_target_pairs={{0,192},{1,193},{2,194},{3,195},{4,196},{5,197},{6,198},{7,199},{8... | collective-permute-start | bytes 110600 | tf_op jit(solution)/shard_map/ppermute | solution.py:30
  67.9 7.5 %collective-permute-start.26 = (bf16[2,2,4,8,512]{4,3,2,0,1:T(8,128)(2,1)S(1)}, bf16[2,2,4,8,512]{4,3,2,0,1:T(8,128)(2,1)S(1)}, u32[]{:S(2)}, u32[]{:S(2)}) collective-permute-start(bf16[2,2,4,8,512]{4,3,2,0,1:T(8,128)(2,1)S(1)} %pad_maximum_fusion.3), channel_id=1, source_target_pairs={{0,1},{1,2},{2,3},{3,0},{4,5},{5,6},{6,7},{7,4},{8,9},{9,10},{10,1... | collective-permute-start | bytes 393224 | tf_op jit(solution)/shard_map/ppermute | solution.py:30
  73.1 3.6 %collective-permute-start.25 = (f32[72,128]{1,0:T(8,128)S(1)}, f32[72,128]{1,0:T(8,128)S(1)}, u32[]{:S(2)}, u32[]{:S(2)}) collective-permute-start(f32[72,128]{1,0:T(8,128)S(1)} %add_add_fusion.near), channel_id=1, source_target_pairs={{0,3},{1,2},{2,1},{3,0},{4,7},{5,6},{6,5},{7,4},{8,11},{9,10},{10,... | collective-permute-start | bytes 110600 | tf_op jit(solution)/shard_map/ppermute | solution.py:30
  73.3 3.5 %collective-permute-start.24 = (f32[72,128]{1,0:T(8,128)S(1)}, f32[72,128]{1,0:T(8,128)S(1)}, u32[]{:S(2)}, u32[]{:S(2)}) collective-permute-start(f32[72,128]{1,0:T(8,128)S(1)} %add_add_fusion.near), channel_id=1, source_target_pairs={{0,2},{1,3},{2,0},{3,1},{4,6},{5,7},{6,4},{7,5},{8,10},{9,11},{10,... | collective-permute-start | bytes 110600 | tf_op jit(solution)/shard_map/ppermute | solution.py:30
  73.3 3.4 %collective-permute-start.23 = (f32[72,128]{1,0:T(8,128)S(1)}, f32[72,128]{1,0:T(8,128)S(1)}, u32[]{:S(2)}, u32[]{:S(2)}) collective-permute-start(f32[72,128]{1,0:T(8,128)S(1)} %add_add_fusion.near), channel_id=1, source_target_pairs={{0,1},{1,0},{2,3},{3,2},{4,5},{5,4},{6,7},{7,6},{8,9},{9,8},{10,11... | collective-permute-start | bytes 110600 | tf_op jit(solution)/shard_map/ppermute | solution.py:30

commit v12 on v11

--- a/solution.py
+++ b/solution.py
@@ -81,25 +81,31 @@
 
 
 def project(parts, norm, w_qkv, w_proj, member):
-    unit, _ = unit_of(jnp.concatenate([part[0] for part in parts], 0))
+    tokens = jnp.concatenate([part[0] for part in parts], 0)
+    unit, inv_scale = unit_of(tokens)
+    average = jnp.mean(tokens.astype(F32), -1, keepdims=True)
+    lane = lax.broadcasted_iota(jnp.int32, (tokens.shape[0], 128), 1)
+    stats = jnp.where(lane == 0, average, inv_scale)
     normed = (unit * norm[0:1, :] + norm[1:2, :]).astype(BF16)
     qkv = dot(normed, own_columns(w_qkv, member)).astype(BF16)
     rows = w_proj[pl.ds(pl.multiple_of(OWN * member, OWN), OWN), :]
     cotangent = dot_nt(jnp.concatenate([part[1] for part in parts], 0), rows).astype(BF16)
-    return normed, qkv, cotangent
-
-
-def first_kernel(flags, p0, p1, p2, p3, norm, w_qkv, w_proj, normed_ref, qkv_ref, up_ref):
-    normed_ref[...], qkv_ref[...], up_ref[...] = project(
+    return normed, qkv, cotangent, stats
+
+
+def first_kernel(
+    flags, p0, p1, p2, p3, norm, w_qkv, w_proj, normed_ref, qkv_ref, up_ref, stats
+):
+    normed_ref[...], qkv_ref[...], up_ref[...], stats[...] = project(
         (p0, p1, p2, p3), norm, w_qkv, w_proj, flags[3]
     )
 
 
 def attention_kernel(
     flags, p0, p1, p2, p3, normed0, qkv0, up0, norm, w_qkv, w_proj,
-    r0, r1, r2, r3, dt_ref, at_ref, normed1,
+    r0, r1, r2, r3, dt_ref, at_ref, normed1, stats,
 ):
-    normed1[...], qkv1, up1 = project((p0, p1, p2, p3), norm, w_qkv, w_proj, flags[3])
+    normed1[...], qkv1, up1, stats[...] = project((p0, p1, p2, p3), norm, w_qkv, w_proj, flags[3])
     qkv = jnp.concatenate([qkv0[...], qkv1], 0)
     cotangent = jnp.concatenate([up0[...], up1], 0)
     queries = qkv[:, :OWN]
@@ -178,8 +184,8 @@
 
 
 def gradient_kernel(
-    spot, p0, p1, p2, p3, p4, p5, p6, p7, r0, r1, r2, r3, dt_ref, at_ref, normed0, normed1, w_qkv,
-    keep, send, g_ref, p_ref, n_ref,
+    spot, p0, p1, p2, p3, p4, p5, p6, p7, r0, r1, r2, r3, dt_ref, at_ref, normed0, normed1,
+    stats0, stats1, w_qkv, keep, send, g_ref, p_ref, n_ref,
 ):
     x, y, core = spot[0], spot[1], spot[2]
     parts = (p0, p1, p2, p3, p4, p5, p6, p7)
@@ -191,9 +197,12 @@
     gain_row = jnp.zeros((1, C), F32)
     offset_row = jnp.zeros((1, C), F32)
     for member, r_ref in enumerate((r0, r1, r2, r3)):
-        rows = jnp.concatenate([parts[member][0], parts[4 + member][0]], 0)
+        rows = jnp.concatenate([parts[member][0], parts[4 + member][0]], 0).astype(F32)
+        place = slice(64 * member, 64 * member + 64)
+        stats = jnp.concatenate([stats0[place, :], stats1[place, :]], 0)
+        unit = (rows - stats[:, 0:1]) * stats[:, 1:2]
         d_normed = dot_nt(r_ref[:, : 3 * OWN], columns)
-        gain_row += jnp.sum(d_normed * unit_of(rows)[0], 0, keepdims=True)
+        gain_row += jnp.sum(d_normed * unit, 0, keepdims=True)
         offset_row += jnp.sum(d_normed, 0, keepdims=True)
     row = lax.broadcasted_iota(jnp.int32, (128, C), 0)
     n_ref[...] = jnp.where(row == 0, gain_row, jnp.where(row == 1, offset_row, 0.0)).T
@@ -358,20 +367,20 @@
     part1 = jnp.stack([other_in, cross_in], 1).reshape(2, SLAB // 2, C)
     parts1 = [part1] + [move(part1, over_x(mask)) for mask in (1, 2, 3)]
     half = TOKENS // 2
-    normed0, qkv0, up0 = call(
+    normed0, qkv0, up0, stats0 = call(
         first_kernel,
         flags,
         (*parts0, norm_params, w_qkv, w_proj),
-        [((half, C), BF16), ((half, 3 * OWN), BF16), ((half, OWN), BF16)],
+        [((half, C), BF16), ((half, 3 * OWN), BF16), ((half, OWN), BF16), ((half, 128), F32)],
         flops=10_000_000_000,
         moved=3_000_000,
     )
-    r0, r1, r2, r3, d_t, a_t, normed1 = call(
+    r0, r1, r2, r3, d_t, a_t, normed1, stats1 = call(
         attention_kernel,
         flags,
         (*parts1, normed0, qkv0, up0, norm_params, w_qkv, w_proj),
         [((SLAB, C), BF16)] * 4
-        + [((3 * OWN, TOKENS), F32), ((OWN, TOKENS), BF16), ((half, C), BF16)],
+        + [((3 * OWN, TOKENS), F32), ((OWN, TOKENS), BF16), ((half, C), BF16), ((half, 128), F32)],
         flops=1_200_000_000,
         moved=6_000_000,
     )
@@ -379,7 +388,7 @@
     keep, send = call(
         gradient_kernel,
         spot,
-        (*parts0, *parts1, r0, r1, r2, r3, d_t, a_t, normed0, normed1, w_qkv),
+        (*parts0, *parts1, r0, r1, r2, r3, d_t, a_t, normed0, normed1, stats0, stats1, w_qkv),
         [((16, 72, 128), F32)] * 2,
         scratch=[
             pltpu.VMEM((3 * OWN, C), F32),

time: 78.1 us -> 78.1 us (level)
  no operation moved by 1% of the time
where the time goes in v12:
time: 78.1 us; the launch traced here: 77.9 us
  starting transfers between devices  49 us (63%)
  Pallas kernels  14.7 us (19%)
  waiting for transfers between devices  10.6 us (14%)
  other arithmetic  1.47 us (2%)
  local copies, waits for them, and re-layouts  1.23 us (2%)
  between operations  0.97 us (1%)
    ppermute x27, starting transfers between devices, move(): return lax.ppermute(value, ('wide', 'narrow'), pairs)  49 us
    pallas_call x7, Pallas kernels, call(): pl.pallas_call(kernel, out_shape=[jax.ShapeDtypeStruct(shape, dtype) for...  14.7 us
    ppermute x27, waiting for transfers between devices, move(): return lax.ppermute(value, ('wide', 'narrow'), pairs)  10.6 us
  transfers between devices with their start and end apart: 27, of which 7 were waited for; matrix products, arithmetic and copies ran while one was open for 1% of the time, Pallas kernels for 6%

profile of v12, /device:TPU:1, one launch (start us, length us, event | category | flops | bytes accessed | tf_op | source)
XLA Modules:
  0.0 77.9 jit_solution(7970607649056836432)
XLA Ops:
  0.7 1.2 %broadcast_select_fusion = (bf16[2,8,8,512]{3,2,1,0:T(8,128)(2,1)S(1)}, bf16[2,8,8,512]{3,2,1,0:T(8,128)(2,1)S(1)}) fusion(pred[8]{0:T(512)(128)(4,1)S(1)} %compare_compare_fusion, bf16[1,8,2,8,512]{4,3,2,1,0:T(8,128)(2,1)} %bitcast.63, bf16[1,8,2,8,512]{4,3,2,1,0:T(8,128)(2,1)} %bitcast.61), kind=kLoop, calls=%fused_computation.16 | loop fusion | flops 327680 | bytes 524296 | tf_op jit(solution)/shard_map/jit(_where)/select_n | solution.py:360
  1.9 3.3 %collective-permute-start = (bf16[2,4,8,512]{3,2,1,0:T(8,128)(2,1)S(1)}, bf16[2,4,8,512]{3,2,1,0:T(8,128)(2,1)S(1)}, u32[]{:S(2)}, u32[]{:S(2)}) collective-permute-start(bf16[2,4,8,512]{3,2,1,0:T(8,128)(2,1)S(1)} %get-tuple-element.112), channel_id=1, source_target_pairs={{0,3},{1,0},{2,1},{3,2},{4,7},{5,4},{6,5},{7,6},{8,11},{9,8},{10,9... | collective-permute-start | bytes 196616 | tf_op jit(solution)/shard_map/ppermute | solution.py:30
  5.3 6.8 %collective-permute-start.4 = (bf16[2,4,8,512]{3,2,1,0:T(8,128)(2,1)S(1)}, bf16[2,4,8,512]{3,2,1,0:T(8,128)(2,1)S(1)}, u32[]{:S(2)}, u32[]{:S(2)}) collective-permute-start(bf16[2,4,8,512]{3,2,1,0:T(8,128)(2,1)S(1)} %get-tuple-element.109), channel_id=1, source_target_pairs={{0,240},{1,241},{2,242},{3,243},{4,244},{5,245},{6,246},{7,247},{8... | collective-permute-start | bytes 196616 | tf_op jit(solution)/shard_map/ppermute | solution.py:30
  12.1 0.4 collective-permute-start.5
  12.6 2.6 %collective-permute-start.3 = (bf16[2,64,512]{2,1,0:T(8,128)(2,1)S(1)}, bf16[2,64,512]{2,1,0:T(8,128)(2,1)S(1)}, u32[]{:S(2)}, u32[]{:S(2)}) collective-permute-start(bf16[2,64,512]{2,1,0:T(8,128)(2,1)S(1)} %bitcast.65), channel_id=1, source_target_pairs={{0,12},{1,13},{2,14},{3,15},{4,8},{5,9},{6,10},{7,11},{8,4},{9,5},... | collective-permute-start | bytes 393224 | tf_op jit(solution)/shard_map/ppermute | solution.py:30
  15.1 0.5 collective-permute-start.2
  15.7 0.3 collective-permute-start.1
  15.9 0.1 pad_add_fusion.flags
  16.0 0.1 stack.62.spot
  16.1 0.0 collective-permute-done.4
  16.1 3.6 %collective-permute-done.5 = bf16[2,4,8,512]{3,2,1,0:T(8,128)(2,1)S(1)} collective-permute-done((bf16[2,4,8,512]{3,2,1,0:T(8,128)(2,1)S(1)}, bf16[2,4,8,512]{3,2,1,0:T(8,128)(2,1)S(1)}, u32[]{:S(2)}, u32[]{:S(2)}) %collective-permute-start.5) | collective-permute-done | bytes 65568 | tf_op jit(solution)/shard_map/ppermute | solution.py:30
  19.7 2.6 %collective-permute-start.8 = (bf16[2,64,512]{2,1,0:T(8,128)(2,1)S(1)}, bf16[2,64,512]{2,1,0:T(8,128)(2,1)S(1)}, u32[]{:S(2)}, u32[]{:S(2)}) collective-permute-start(bf16[2,64,512]{2,1,0:T(8,128)(2,1)S(1)} %bitcast.71), channel_id=1, source_target_pairs={{0,12},{1,13},{2,14},{3,15},{4,8},{5,9},{6,10},{7,11},{8,4},{9,5},... | collective-permute-start | bytes 393224 | tf_op jit(solution)/shard_map/ppermute | solution.py:30
  22.3 0.5 collective-permute-start.7
  22.8 0.0 collective-permute-done.3.p3
  22.8 0.3 collective-permute-start.6
  23.1 0.0 collective-permute-done.2.p2
  23.1 0.0 collective-permute-done.1.p1
  23.1 0.0 copy-start.1
  23.1 1.0 %copy-done.1 = bf16[512,512]{1,0:T(8,128)(2,1)S(1)} copy-done((bf16[512,512]{1,0:T(8,128)(2,1)S(1)}, bf16[512,512]{1,0:T(8,128)(2,1)}, u32[]{:S(2)}) %copy-start.1) | copy-done | bytes 524312
  24.1 1.1 %first_kernel.1 = (bf16[256,512]{1,0:T(8,128)(2,1)S(1)}, bf16[256,384]{1,0:T(8,128)(2,1)S(1)}, bf16[256,128]{1,0:T(8,128)(2,1)S(1)}, f32[256,128]{1,0:T(8,128)S(1)}) custom-call(s32[4]{0:T(128)S(1)} %pad_add_fusion.flags, bf16[2,64,512]{2,1,0:T(8,128)(2,1)S(1)} %bitcast.68, bf16[2,64,512]{2,1,0:T(8,128)(2,1)S(1)} %collective-permute-done.1.p1, ...), custom_call_target="tpu_custom_call" | custom-call | flops 10000000000 | bytes 3000000 | tf_op jit(solution)/shard_map/first_kernel/pallas_call | solution.py:334
  25.3 0.3 collective-permute-done.8.p3.p7
  25.6 2.1 %collective-permute-done.7.p2.p6 = bf16[2,64,512]{2,1,0:T(8,128)(2,1)S(1)} collective-permute-done((bf16[2,64,512]{2,1,0:T(8,128)(2,1)S(1)}, bf16[2,64,512]{2,1,0:T(8,128)(2,1)S(1)}, u32[]{:S(2)}, u32[]{:S(2)}) %collective-permute-start.7) | collective-permute-done | bytes 131104 | tf_op jit(solution)/shard_map/ppermute | solution.py:30
  27.7 0.0 collective-permute-done.6.p1.p5
  27.7 6.5 %attention_kernel.1 = (bf16[128,512]{1,0:T(8,128)(2,1)S(1)}, bf16[128,512]{1,0:T(8,128)(2,1)S(1)}, bf16[128,512]{1,0:T(8,128)(2,1)S(1)}, bf16[128,512]{1,0:T(8,1...) custom-call(s32[4]{0:T(128)S(1)} %pad_add_fusion.flags, ...), custom_call_target="tpu_custom_call" | custom-call | flops 1200000000 | bytes 6000000 | tf_op jit(solution)/shard_map/attention_kernel/pallas_call | solution.py:334
  34.3 2.5 %gradient_kernel.1 = (f32[16,72,128]{2,1,0:T(8,128)S(1)}, f32[16,72,128]{2,1,0:T(8,128)S(1)}) custom-call(s32[5]{0:T(128)S(1)} %stack.62.spot, bf16[2,64,512]{2,1,0:T(8,128)(2,1)S(1)} %bitcast.69, bf16[2,64,512]{2,1,0:T(8,128)(2,1)S(1)} %collective-permute-done.1.p1, bf16[2,64,512]{2,1,0:T(8,128)(2,1)S(1)} %collective-permute-done.2.p2, ...), custom_call_target="tpu_custom_call" | custom-call | flops 20000000000 | bytes 6000000 | tf_op jit(solution)/shard_map/gradient_kernel/pallas_call | solution.py:334
  36.7 0.0 copy-start.2
  36.7 3.9 %collective-permute-start.9 = (f32[16,72,128]{2,1,0:T(8,128)S(1)}, f32[16,72,128]{2,1,0:T(8,128)S(1)}, u32[]{:S(2)}, u32[]{:S(2)}) collective-permute-start(f32[16,72,128]{2,1,0:T(8,128)S(1)} %get-tuple-element.62), channel_id=1, source_target_pairs={{0,1},{1,0},{2,3},{3,2},{4,5},{5,4},{6,7},{7,6},{8,9},{9,8},{10,11... | collective-permute-start | bytes 1769480 | tf_op jit(solution)/shard_map/ppermute | solution.py:30
  40.6 0.4 collective-permute-start.13
  41.1 2.5 %collective-permute-start.14 = (bf16[128,512]{1,0:T(8,128)(2,1)S(1)}, bf16[128,512]{1,0:T(8,128)(2,1)S(1)}, u32[]{:S(2)}, u32[]{:S(2)}) collective-permute-start(bf16[128,512]{1,0:T(8,128)(2,1)S(1)} %get-tuple-element.54.r2), channel_id=1, source_target_pairs={{0,8},{1,9},{2,10},{3,11},{4,12},{5,13},{6,14},{7,15},{8,0},{9,1},... | collective-permute-start | bytes 393224 | tf_op jit(solution)/shard_map/ppermute | solution.py:30
  43.6 0.1 fusion
  43.6 0.1 collective-permute-start.12
  43.7 0.1 collective-permute-start.11
  43.8 3.1 %collective-permute-start.10 = (bf16[4,72,128]{2,1,0:T(8,128)(2,1)S(1)}, bf16[4,72,128]{2,1,0:T(8,128)(2,1)S(1)}, u32[]{:S(2)}, u32[]{:S(2)}) collective-permute-start(bf16[4,72,128]{2,1,0:T(8,128)(2,1)S(1)} %get-tuple-element.95), channel_id=1, source_target_pairs={{0,16},{1,17},{2,18},{3,19},{4,20},{5,21},{6,22},{7,23},{8,24},{9,... | collective-permute-start | bytes 221192 | tf_op jit(solution)/shard_map/ppermute | solution.py:30
  47.0 0.0 collective-permute-done.13.r1
  47.0 1.0 %collective-permute-start.18 = (bf16[128,512]{1,0:T(8,128)(2,1)S(1)}, bf16[128,512]{1,0:T(8,128)(2,1)S(1)}, u32[]{:S(2)}, u32[]{:S(2)}) collective-permute-start(bf16[128,512]{1,0:T(8,128)(2,1)S(1)} %get-tuple-element.55.r3), channel_id=1, source_target_pairs={{0,12},{1,13},{2,14},{3,15},{4,8},{5,9},{6,10},{7,11},{8,4},{9,5},... | collective-permute-start | bytes 393224 | tf_op jit(solution)/shard_map/ppermute | solution.py:30
  47.9 2.0 %collective-permute-done.14.r2 = bf16[128,512]{1,0:T(8,128)(2,1)S(1)} collective-permute-done((bf16[128,512]{1,0:T(8,128)(2,1)S(1)}, bf16[128,512]{1,0:T(8,128)(2,1)S(1)}, u32[]{:S(2)}, u32[]{:S(2)}) %collective-permute-start.14) | collective-permute-done | bytes 131104 | tf_op jit(solution)/shard_map/ppermute | solution.py:30
  50.0 0.0 collective-permute-done.12
  50.0 0.0 collective-permute-done.11
  50.0 0.0 collective-permute-done.10
  50.1 1.0 %collective-permute-start.17 = (f32[72,128]{1,0:T(8,128)S(1)}, f32[72,128]{1,0:T(8,128)S(1)}, u32[]{:S(2)}, u32[]{:S(2)}) collective-permute-start(f32[72,128]{1,0:T(8,128)S(1)} %get-tuple-element.97), channel_id=1, source_target_pairs={{0,12},{1,13},{2,14},{3,15},{4,8},{5,9},{6,10},{7,11},{8,4},{9,5},... | collective-permute-start | bytes 110600 | tf_op jit(solution)/shard_map/ppermute | solution.py:30
  51.1 0.7 collective-permute-start.16
  51.9 1.5 %collective-permute-start.15 = (f32[72,128]{1,0:T(8,128)S(1)}, f32[72,128]{1,0:T(8,128)S(1)}, u32[]{:S(2)}, u32[]{:S(2)}) collective-permute-start(f32[72,128]{1,0:T(8,128)S(1)} %get-tuple-element.99), channel_id=1, source_target_pairs={{0,4},{1,5},{2,6},{3,7},{4,0},{5,1},{6,2},{7,3},{8,12},{9,13},{10,... | collective-permute-start | bytes 110600 | tf_op jit(solution)/shard_map/ppermute | solution.py:30
  53.4 1.3 %token_kernel.1 = (bf16[2,128,512]{2,1,0:T(8,128)(2,1)S(1)}, f32[8,128]{1,0:T(8,128)S(1)}) custom-call(s32[5]{0:T(128)S(1)} %stack.62.spot, bf16[128,512]{1,0:T(8,128)(2,1)S(1)} %get-tuple-element.52.r0, bf16[128,512]{1,0:T(8,128)(2,1)S(1)} %collective-permute-done.13.r1, bf16[128,512]{1,0:T(8,128)(2,1)S(1)} %collective-permute-done.14.r2, ...), custom_call_target="tpu_custom_call" | custom-call | flops 500000000 | bytes 4000000 | tf_op jit(solution)/shard_map/token_kernel/pallas_call | solution.py:334
  54.8 0.0 copy-start.3
  54.8 0.0 copy-start.4
  54.8 4.1 %collective-permute-start.22 = (bf16[2,2,4,8,512]{4,3,2,0,1:T(8,128)(2,1)S(1)}, bf16[2,2,4,8,512]{4,3,2,0,1:T(8,128)(2,1)S(1)}, u32[]{:S(2)}, u32[]{:S(2)}) collective-permute-start(bf16[2,2,4,8,512]{4,3,2,0,1:T(8,128)(2,1)S(1)} %copy.24), channel_id=1, source_target_pairs={{0,240},{1,241},{2,242},{3,243},{4,244},{5,245},{6,246},{7,247},{8... | collective-permute-start | bytes 393224 | tf_op jit(solution)/shard_map/ppermute | solution.py:30
  59.0 0.0 collective-permute-done.17.m3
  59.0 0.0 collective-permute-done.16.m2
  59.0 0.0 collective-permute-done.15.m1
  59.0 0.7 z_parts_kernel.1
  59.7 0.1 collective-permute-start.19
  59.8 2.0 %collective-permute-start.20 = (f32[72,128]{1,0:T(8,128)S(1)}, f32[72,128]{1,0:T(8,128)S(1)}, u32[]{:S(2)}, u32[]{:S(2)}) collective-permute-start(f32[72,128]{1,0:T(8,128)S(1)} %get-tuple-element.76), channel_id=1, source_target_pairs={{0,128},{1,129},{2,130},{3,131},{4,132},{5,133},{6,134},{7,135},{8... | collective-permute-start | bytes 110600 | tf_op jit(solution)/shard_map/ppermute | solution.py:30
  61.7 3.7 %collective-permute-start.21 = (f32[72,128]{1,0:T(8,128)S(1)}, f32[72,128]{1,0:T(8,128)S(1)}, u32[]{:S(2)}, u32[]{:S(2)}) collective-permute-start(f32[72,128]{1,0:T(8,128)S(1)} %get-tuple-element.77), channel_id=1, source_target_pairs={{0,192},{1,193},{2,194},{3,195},{4,196},{5,197},{6,198},{7,199},{8... | collective-permute-start | bytes 110600 | tf_op jit(solution)/shard_map/ppermute | solution.py:30
  65.4 1.8 %collective-permute-done.20 = f32[72,128]{1,0:T(8,128)S(1)} collective-permute-done((f32[72,128]{1,0:T(8,128)S(1)}, f32[72,128]{1,0:T(8,128)S(1)}, u32[]{:S(2)}, u32[]{:S(2)}) %collective-permute-start.20) | collective-permute-done | bytes 36896 | tf_op jit(solution)/shard_map/ppermute | solution.py:30
  67.2 0.6 collective-permute-done.21
  67.8 0.0 collective-permute-done.22
  67.9 5.2 %collective-permute-start.26 = (bf16[2,2,4,8,512]{4,3,2,0,1:T(8,128)(2,1)S(1)}, bf16[2,2,4,8,512]{4,3,2,0,1:T(8,128)(2,1)S(1)}, u32[]{:S(2)}, u32[]{:S(2)}) collective-permute-start(bf16[2,2,4,8,512]{4,3,2,0,1:T(8,128)(2,1)S(1)} %pad_maximum_fusion.3), channel_id=1, source_target_pairs={{0,1},{1,2},{2,3},{3,0},{4,5},{5,6},{6,7},{7,4},{8,9},{9,10},{10,1... | collective-permute-start | bytes 393224 | tf_op jit(solution)/shard_map/ppermute | solution.py:30
  73.1 0.1 collective-permute-start.25
  73.2 0.1 collective-permute-start.24
  73.3 2.0 %collective-permute-start.23 = (f32[72,128]{1,0:T(8,128)S(1)}, f32[72,128]{1,0:T(8,128)S(1)}, u32[]{:S(2)}, u32[]{:S(2)}) collective-permute-start(f32[72,128]{1,0:T(8,128)S(1)} %add_add_fusion.near), channel_id=1, source_target_pairs={{0,1},{1,0},{2,3},{3,2},{4,5},{5,4},{6,7},{7,6},{8,9},{9,8},{10,11... | collective-permute-start | bytes 110600 | tf_op jit(solution)/shard_map/ppermute | solution.py:30
  75.3 0.1 collective-permute-done.26
  75.4 1.3 %merge_kernel.1 = (bf16[8,16,512]{2,1,0:T(8,128)(2,1)}, bf16[8,16,512]{2,1,0:T(8,128)(2,1)}) custom-call(s32[5]{0:T(128)S(1)} %stack.62.spot, bf16[8,16,512]{2,1,0:T(8,128)(2,1)S(1)} %bitcast.62, bf16[8,16,512]{2,1,0:T(8,128)(2,1)S(1)} %bitcast.64, bf16[2,4,8,512]{3,2,1,0:T(8,128)(2,1)S(1)} %get-tuple-element.104.mine_high, ...), custom_call_target="tpu_custom_call" | custom-call | tf_op jit(solution)/shard_map/merge_kernel/pallas_call | solution.py:334
  76.7 0.0 collective-permute-done.25.both_in
  76.7 1.2 %last_kernel.1 = (f32[24,512]{1,0:T(8,128)}, f32[8,512]{1,0:T(8,128)}, f32[2,8]{1,0:T(2,128)}) custom-call(s32[5]{0:T(128)S(1)} %stack.62.spot, f32[72,128]{1,0:T(8,128)S(1)} %add_add_fusion.near, f32[72,128]{1,0:T(8,128)S(1)} %collective-permute-done.23.core_in, f32[72,128]{1,0:T(8,128)S(1)} %collective-permute-done.24.z_in, ...), custom_call_target="tpu_custom_call" | custom-call | tf_op jit(solution)/shard_map/last_kernel/pallas_call | solution.py:334
  (30 shorter events, 0.2 us)
Async XLA Ops:
  0.6 22.4 %copy-start = (bf16[512,1536]{1,0:T(8,128)(2,1)S(1)}, bf16[512,1536]{1,0:T(8,128)(2,1)}, u32[]{:S(2)}) copy-start(bf16[512,1536]{1,0:T(8,128)(2,1)} %w_qkv.7) | copy-start | bytes 4718596
  0.6 22.4 %copy-start.5 = (f32[2,512]{1,0:T(2,128)S(1)}, f32[2,512]{1,0:T(2,128)}, u32[]{:S(2)}) copy-start(f32[2,512]{1,0:T(2,128)} %norm.5) | copy-start | bytes 12292
  1.9 10.6 %collective-permute-start = (bf16[2,4,8,512]{3,2,1,0:T(8,128)(2,1)S(1)}, bf16[2,4,8,512]{3,2,1,0:T(8,128)(2,1)S(1)}, u32[]{:S(2)}, u32[]{:S(2)}) collective-permute-start(bf16[2,4,8,512]{3,2,1,0:T(8,128)(2,1)S(1)} %get-tuple-element.112), channel_id=1, source_target_pairs={{0,3},{1,0},{2,1},{3,2},{4,7},{5,4},{6,5},{7,6},{8,11},{9,8},{10,9... | collective-permute-start | bytes 196616 | tf_op jit(solution)/shard_map/ppermute | solution.py:30
  5.3 10.8 %collective-permute-start.4 = (bf16[2,4,8,512]{3,2,1,0:T(8,128)(2,1)S(1)}, bf16[2,4,8,512]{3,2,1,0:T(8,128)(2,1)S(1)}, u32[]{:S(2)}, u32[]{:S(2)}) collective-permute-start(bf16[2,4,8,512]{3,2,1,0:T(8,128)(2,1)S(1)} %get-tuple-element.109), channel_id=1, source_target_pairs={{0,240},{1,241},{2,242},{3,243},{4,244},{5,245},{6,246},{7,247},{8... | collective-permute-start | bytes 196616 | tf_op jit(solution)/shard_map/ppermute | solution.py:30
  12.1 7.6 %collective-permute-start.5 = (bf16[2,4,8,512]{3,2,1,0:T(8,128)(2,1)S(1)}, bf16[2,4,8,512]{3,2,1,0:T(8,128)(2,1)S(1)}, u32[]{:S(2)}, u32[]{:S(2)}) collective-permute-start(bf16[2,4,8,512]{3,2,1,0:T(8,128)(2,1)S(1)} %get-tuple-element.110), channel_id=1, source_target_pairs={{0,243},{1,240},{2,241},{3,242},{4,247},{5,244},{6,245},{7,246},{8... | collective-permute-start | bytes 196616 | tf_op jit(solution)/shard_map/ppermute | solution.py:30
  12.6 10.2 %collective-permute-start.3 = (bf16[2,64,512]{2,1,0:T(8,128)(2,1)S(1)}, bf16[2,64,512]{2,1,0:T(8,128)(2,1)S(1)}, u32[]{:S(2)}, u32[]{:S(2)}) collective-permute-start(bf16[2,64,512]{2,1,0:T(8,128)(2,1)S(1)} %bitcast.65), channel_id=1, source_target_pairs={{0,12},{1,13},{2,14},{3,15},{4,8},{5,9},{6,10},{7,11},{8,4},{9,5},... | collective-permute-start | bytes 393224 | tf_op jit(solution)/shard_map/ppermute | solution.py:30
  15.1 7.9 %collective-permute-start.2 = (bf16[2,64,512]{2,1,0:T(8,128)(2,1)S(1)}, bf16[2,64,512]{2,1,0:T(8,128)(2,1)S(1)}, u32[]{:S(2)}, u32[]{:S(2)}) collective-permute-start(bf16[2,64,512]{2,1,0:T(8,128)(2,1)S(1)} %bitcast.66), channel_id=1, source_target_pairs={{0,8},{1,9},{2,10},{3,11},{4,12},{5,13},{6,14},{7,15},{8,0},{9,1},... | collective-permute-start | bytes 393224 | tf_op jit(solution)/shard_map/ppermute | solution.py:30
  15.7 7.4 %collective-permute-start.1 = (bf16[2,64,512]{2,1,0:T(8,128)(2,1)S(1)}, bf16[2,64,512]{2,1,0:T(8,128)(2,1)S(1)}, u32[]{:S(2)}, u32[]{:S(2)}) collective-permute-start(bf16[2,64,512]{2,1,0:T(8,128)(2,1)S(1)} %bitcast.67), channel_id=1, source_target_pairs={{0,4},{1,5},{2,6},{3,7},{4,0},{5,1},{6,2},{7,3},{8,12},{9,13},{10,... | collective-permute-start | bytes 393224 | tf_op jit(solution)/shard_map/ppermute | solution.py:30
  19.7 5.9 %collective-permute-start.8 = (bf16[2,64,512]{2,1,0:T(8,128)(2,1)S(1)}, bf16[2,64,512]{2,1,0:T(8,128)(2,1)S(1)}, u32[]{:S(2)}, u32[]{:S(2)}) collective-permute-start(bf16[2,64,512]{2,1,0:T(8,128)(2,1)S(1)} %bitcast.71), channel_id=1, source_target_pairs={{0,12},{1,13},{2,14},{3,15},{4,8},{5,9},{6,10},{7,11},{8,4},{9,5},... | collective-permute-start | bytes 393224 | tf_op jit(solution)/shard_map/ppermute | solution.py:30
  22.3 5.4 %collective-permute-start.7 = (bf16[2,64,512]{2,1,0:T(8,128)(2,1)S(1)}, bf16[2,64,512]{2,1,0:T(8,128)(2,1)S(1)}, u32[]{:S(2)}, u32[]{:S(2)}) collective-permute-start(bf16[2,64,512]{2,1,0:T(8,128)(2,1)S(1)} %bitcast.72), channel_id=1, source_target_pairs={{0,8},{1,9},{2,10},{3,11},{4,12},{5,13},{6,14},{7,15},{8,0},{9,1},... | collective-permute-start | bytes 393224 | tf_op jit(solution)/shard_map/ppermute | solution.py:30
  22.8 4.9 %collective-permute-start.6 = (bf16[2,64,512]{2,1,0:T(8,128)(2,1)S(1)}, bf16[2,64,512]{2,1,0:T(8,128)(2,1)S(1)}, u32[]{:S(2)}, u32[]{:S(2)}) collective-permute-start(bf16[2,64,512]{2,1,0:T(8,128)(2,1)S(1)} %bitcast.73), channel_id=1, source_target_pairs={{0,4},{1,5},{2,6},{3,7},{4,0},{5,1},{6,2},{7,3},{8,12},{9,13},{10,... | collective-permute-start | bytes 393224 | tf_op jit(solution)/shard_map/ppermute | solution.py:30
  23.1 1.0 %copy-start.1 = (bf16[512,512]{1,0:T(8,128)(2,1)S(1)}, bf16[512,512]{1,0:T(8,128)(2,1)}, u32[]{:S(2)}) copy-start(bf16[512,512]{1,0:T(8,128)(2,1)} %w_proj.5) | copy-start | bytes 1572868
  36.7 16.7 %copy-start.2 = (bf16[512,512]{1,0:T(8,128)(2,1)S(1)}, bf16[512,512]{1,0:T(8,128)(2,1)}, u32[]{:S(2)}) copy-start(bf16[512,512]{1,0:T(8,128)(2,1)} %w_proj.5) | copy-start | bytes 1572868
  36.7 6.8 %collective-permute-start.9 = (f32[16,72,128]{2,1,0:T(8,128)S(1)}, f32[16,72,128]{2,1,0:T(8,128)S(1)}, u32[]{:S(2)}, u32[]{:S(2)}) collective-permute-start(f32[16,72,128]{2,1,0:T(8,128)S(1)} %get-tuple-element.62), channel_id=1, source_target_pairs={{0,1},{1,0},{2,3},{3,2},{4,5},{5,4},{6,7},{7,6},{8,9},{9,8},{10,11... | collective-permute-start | bytes 1769480 | tf_op jit(solution)/shard_map/ppermute | solution.py:30
  40.6 6.3 %collective-permute-start.13 = (bf16[128,512]{1,0:T(8,128)(2,1)S(1)}, bf16[128,512]{1,0:T(8,128)(2,1)S(1)}, u32[]{:S(2)}, u32[]{:S(2)}) collective-permute-start(bf16[128,512]{1,0:T(8,128)(2,1)S(1)} %get-tuple-element.53.r1), channel_id=1, source_target_pairs={{0,4},{1,5},{2,6},{3,7},{4,0},{5,1},{6,2},{7,3},{8,12},{9,13},{10,... | collective-permute-start | bytes 393224 | tf_op jit(solution)/shard_map/ppermute | solution.py:30
  41.1 8.9 %collective-permute-start.14 = (bf16[128,512]{1,0:T(8,128)(2,1)S(1)}, bf16[128,512]{1,0:T(8,128)(2,1)S(1)}, u32[]{:S(2)}, u32[]{:S(2)}) collective-permute-start(bf16[128,512]{1,0:T(8,128)(2,1)S(1)} %get-tuple-element.54.r2), channel_id=1, source_target_pairs={{0,8},{1,9},{2,10},{3,11},{4,12},{5,13},{6,14},{7,15},{8,0},{9,1},... | collective-permute-start | bytes 393224 | tf_op jit(solution)/shard_map/ppermute | solution.py:30
  43.6 6.3 %collective-permute-start.12 = (bf16[4,72,128]{2,1,0:T(8,128)(2,1)S(1)}, bf16[4,72,128]{2,1,0:T(8,128)(2,1)S(1)}, u32[]{:S(2)}, u32[]{:S(2)}) collective-permute-start(bf16[4,72,128]{2,1,0:T(8,128)(2,1)S(1)} %get-tuple-element.93), channel_id=1, source_target_pairs={{0,48},{1,49},{2,50},{3,51},{4,52},{5,53},{6,54},{7,55},{8,56},{9,... | collective-permute-start | bytes 221192 | tf_op jit(solution)/shard_map/ppermute | solution.py:30
  43.7 6.2 %collective-permute-start.11 = (bf16[4,72,128]{2,1,0:T(8,128)(2,1)S(1)}, bf16[4,72,128]{2,1,0:T(8,128)(2,1)S(1)}, u32[]{:S(2)}, u32[]{:S(2)}) collective-permute-start(bf16[4,72,128]{2,1,0:T(8,128)(2,1)S(1)} %get-tuple-element.94), channel_id=1, source_target_pairs={{0,32},{1,33},{2,34},{3,35},{4,36},{5,37},{6,38},{7,39},{8,40},{9,... | collective-permute-start | bytes 221192 | tf_op jit(solution)/shard_map/ppermute | solution.py:30
  43.8 6.1 %collective-permute-start.10 = (bf16[4,72,128]{2,1,0:T(8,128)(2,1)S(1)}, bf16[4,72,128]{2,1,0:T(8,128)(2,1)S(1)}, u32[]{:S(2)}, u32[]{:S(2)}) collective-permute-start(bf16[4,72,128]{2,1,0:T(8,128)(2,1)S(1)} %get-tuple-element.95), channel_id=1, source_target_pairs={{0,16},{1,17},{2,18},{3,19},{4,20},{5,21},{6,22},{7,23},{8,24},{9,... | collective-permute-start | bytes 221192 | tf_op jit(solution)/shard_map/ppermute | solution.py:30
  47.0 6.4 %collective-permute-start.18 = (bf16[128,512]{1,0:T(8,128)(2,1)S(1)}, bf16[128,512]{1,0:T(8,128)(2,1)S(1)}, u32[]{:S(2)}, u32[]{:S(2)}) collective-permute-start(bf16[128,512]{1,0:T(8,128)(2,1)S(1)} %get-tuple-element.55.r3), channel_id=1, source_target_pairs={{0,12},{1,13},{2,14},{3,15},{4,8},{5,9},{6,10},{7,11},{8,4},{9,5},... | collective-permute-start | bytes 393224 | tf_op jit(solution)/shard_map/ppermute | solution.py:30
  50.1 8.9 %collective-permute-start.17 = (f32[72,128]{1,0:T(8,128)S(1)}, f32[72,128]{1,0:T(8,128)S(1)}, u32[]{:S(2)}, u32[]{:S(2)}) collective-permute-start(f32[72,128]{1,0:T(8,128)S(1)} %get-tuple-element.97), channel_id=1, source_target_pairs={{0,12},{1,13},{2,14},{3,15},{4,8},{5,9},{6,10},{7,11},{8,4},{9,5},... | collective-permute-start | bytes 110600 | tf_op jit(solution)/shard_map/ppermute | solution.py:30
  51.1 7.8 %collective-permute-start.16 = (f32[72,128]{1,0:T(8,128)S(1)}, f32[72,128]{1,0:T(8,128)S(1)}, u32[]{:S(2)}, u32[]{:S(2)}) collective-permute-start(f32[72,128]{1,0:T(8,128)S(1)} %get-tuple-element.98), channel_id=1, source_target_pairs={{0,8},{1,9},{2,10},{3,11},{4,12},{5,13},{6,14},{7,15},{8,0},{9,1},... | collective-permute-start | bytes 110600 | tf_op jit(solution)/shard_map/ppermute | solution.py:30
  51.9 7.1 %collective-permute-start.15 = (f32[72,128]{1,0:T(8,128)S(1)}, f32[72,128]{1,0:T(8,128)S(1)}, u32[]{:S(2)}, u32[]{:S(2)}) collective-permute-start(f32[72,128]{1,0:T(8,128)S(1)} %get-tuple-element.99), channel_id=1, source_target_pairs={{0,4},{1,5},{2,6},{3,7},{4,0},{5,1},{6,2},{7,3},{8,12},{9,13},{10,... | collective-permute-start | bytes 110600 | tf_op jit(solution)/shard_map/ppermute | solution.py:30
  54.8 20.6 %copy-start.3 = (bf16[1,1,8,16,512]{4,3,2,1,0:T(8,128)(2,1)S(1)}, bf16[1,1,8,16,512]{4,3,2,1,0:T(8,128)(2,1)}, u32[]{:S(2)}) copy-start(bf16[1,1,8,16,512]{4,3,2,1,0:T(8,128)(2,1)} %param.5) | copy-start | bytes 393220
  54.8 20.6 %copy-start.4 = (bf16[1,1,8,16,512]{4,3,2,1,0:T(8,128)(2,1)S(1)}, bf16[1,1,8,16,512]{4,3,2,1,0:T(8,128)(2,1)}, u32[]{:S(2)}) copy-start(bf16[1,1,8,16,512]{4,3,2,1,0:T(8,128)(2,1)} %param.9) | copy-start | bytes 393220
  54.8 13.0 %collective-permute-start.22 = (bf16[2,2,4,8,512]{4,3,2,0,1:T(8,128)(2,1)S(1)}, bf16[2,2,4,8,512]{4,3,2,0,1:T(8,128)(2,1)S(1)}, u32[]{:S(2)}, u32[]{:S(2)}) collective-permute-start(bf16[2,2,4,8,512]{4,3,2,0,1:T(8,128)(2,1)S(1)} %copy.24), channel_id=1, source_target_pairs={{0,240},{1,241},{2,242},{3,243},{4,244},{5,245},{6,246},{7,247},{8... | collective-permute-start | bytes 393224 | tf_op jit(solution)/shard_map/ppermute | solution.py:30
  59.7 5.8 %collective-permute-start.19 = (f32[72,128]{1,0:T(8,128)S(1)}, f32[72,128]{1,0:T(8,128)S(1)}, u32[]{:S(2)}, u32[]{:S(2)}) collective-permute-start(f32[72,128]{1,0:T(8,128)S(1)} %get-tuple-element.75), channel_id=1, source_target_pairs={{0,64},{1,65},{2,66},{3,67},{4,68},{5,69},{6,70},{7,71},{8,72},{9,... | collective-permute-start | bytes 110600 | tf_op jit(solution)/shard_map/ppermute | solution.py:30
  59.8 7.4 %collective-permute-start.20 = (f32[72,128]{1,0:T(8,128)S(1)}, f32[72,128]{1,0:T(8,128)S(1)}, u32[]{:S(2)}, u32[]{:S(2)}) collective-permute-start(f32[72,128]{1,0:T(8,128)S(1)} %get-tuple-element.76), channel_id=1, source_target_pairs={{0,128},{1,129},{2,130},{3,131},{4,132},{5,133},{6,134},{7,135},{8... | collective-permute-start | bytes 110600 | tf_op jit(solution)/shard_map/ppermute | solution.py:30
  61.7 6.1 %collective-permute-start.21 = (f32[72,128]{1,0:T(8,128)S(1)}, f32[72,128]{1,0:T(8,128)S(1)}, u32[]{:S(2)}, u32[]{:S(2)}) collective-permute-start(f32[72,128]{1,0:T(8,128)S(1)} %get-tuple-element.77), channel_id=1, source_target_pairs={{0,192},{1,193},{2,194},{3,195},{4,196},{5,197},{6,198},{7,199},{8... | collective-permute-start | bytes 110600 | tf_op jit(solution)/shard_map/ppermute | solution.py:30
  67.9 7.5 %collective-permute-start.26 = (bf16[2,2,4,8,512]{4,3,2,0,1:T(8,128)(2,1)S(1)}, bf16[2,2,4,8,512]{4,3,2,0,1:T(8,128)(2,1)S(1)}, u32[]{:S(2)}, u32[]{:S(2)}) collective-permute-start(bf16[2,2,4,8,512]{4,3,2,0,1:T(8,128)(2,1)S(1)} %pad_maximum_fusion.3), channel_id=1, source_target_pairs={{0,1},{1,2},{2,3},{3,0},{4,5},{5,6},{6,7},{7,4},{8,9},{9,10},{10,1... | collective-permute-start | bytes 393224 | tf_op jit(solution)/shard_map/ppermute | solution.py:30
  73.1 3.6 %collective-permute-start.25 = (f32[72,128]{1,0:T(8,128)S(1)}, f32[72,128]{1,0:T(8,128)S(1)}, u32[]{:S(2)}, u32[]{:S(2)}) collective-permute-start(f32[72,128]{1,0:T(8,128)S(1)} %add_add_fusion.near), channel_id=1, source_target_pairs={{0,3},{1,2},{2,1},{3,0},{4,7},{5,6},{6,5},{7,4},{8,11},{9,10},{10,... | collective-permute-start | bytes 110600 | tf_op jit(solution)/shard_map/ppermute | solution.py:30
  73.2 3.5 %collective-permute-start.24 = (f32[72,128]{1,0:T(8,128)S(1)}, f32[72,128]{1,0:T(8,128)S(1)}, u32[]{:S(2)}, u32[]{:S(2)}) collective-permute-start(f32[72,128]{1,0:T(8,128)S(1)} %add_add_fusion.near), channel_id=1, source_target_pairs={{0,2},{1,3},{2,0},{3,1},{4,6},{5,7},{6,4},{7,5},{8,10},{9,11},{10,... | collective-permute-start | bytes 110600 | tf_op jit(solution)/shard_map/ppermute | solution.py:30
  73.3 3.4 %collective-permute-start.23 = (f32[72,128]{1,0:T(8,128)S(1)}, f32[72,128]{1,0:T(8,128)S(1)}, u32[]{:S(2)}, u32[]{:S(2)}) collective-permute-start(f32[72,128]{1,0:T(8,128)S(1)} %add_add_fusion.near), channel_id=1, source_target_pairs={{0,1},{1,0},{2,3},{3,2},{4,5},{5,4},{6,7},{7,6},{8,9},{9,8},{10,11... | collective-permute-start | bytes 110600 | tf_op jit(solution)/shard_map/ppermute | solution.py:30
